TPU v7x, 256 devices: a whole 4x4x8 slice. The times are simulated.
256 devices in a mesh: pipe: 16 (over y, x), tensor: 16 (over z, core).
Axes of the slice: x: 4, y: 4, z: 8, core: 2. Of those that a mesh axis runs over, the one named last changes fastest.
Arguments:
- segment_in: bfloat16 [16, 512, 4096], P('pipe'), may hold values from -8 to 8
- layer_weight: bfloat16 [16, 4096, 4096], P('pipe', None, 'tensor'), may hold values from -0.09375 to 0.09375
- layer_gain: float32 [16, 4096], P('pipe'), may hold values from 0.25 to 1.75
- final_gain: float32 [4096], replicated, may hold values from 0.25 to 1.75
- head_weight: bfloat16 [32000, 4096], P('pipe', 'tensor'), may hold values from -8 to 8
- exit_rows: int32 [16, 32], replicated, may hold values from 0 to 511, as said below
- exit_count: int32 [16], replicated, may hold values from 8 to 32, as said below
- exit_targets: int32 [16, 32], replicated, may hold values from 0 to 31999
- exit_scale: float32 [16], replicated, may hold values from 4 to 32
- out_grad: bfloat16 [16, 512, 4096], P('pipe'), may hold values from -6 to 6
Outputs:
- input_grad: bfloat16 [16, 512, 4096], P('pipe')
- weight_grad: bfloat16 [16, 4096, 4096], P('pipe', None, 'tensor')
- gain_grad: float32 [16, 4096], P('pipe')
- head_grad: bfloat16 [32000, 4096], P('pipe', 'tensor')
Inputs may be any that keep to these rules, and one draw needn't show every extreme that they name: `exit_rows`: in each section the entries are distinct token rows; only the first exit_count entries are live, the others are ignored rows. `exit_count`: some section has all 32 slots live in every draw.
All inputs are finite; a program needn't handle non-finite values.
Results may differ from a plain program's by a relative error of at most 0.006.
Values may be sent and summed in bfloat16 or wider, within the bound.
No kernel may reach another device: no remote copies, remote signals or barrier semaphores. Data moves between devices by JAX's collectives and lax.ppermute only.
A program may use at most 128 MiB of HBM per device.

v0:
```python
import jax
import jax.numpy as jnp
from jax import lax
from jax.sharding import PartitionSpec as P


def local(
    segment_in,
    layer_weight,
    layer_gain,
    final_gain,
    head_weight,
    exit_rows,
    exit_count,
    exit_targets,
    exit_scale,
    out_grad,
):
    epsilon = 1e-05
    tensor_pos = lax.axis_index("tensor")
    pipe_pos = lax.axis_index("pipe")
    tensor_count = lax.axis_size("tensor")
    inputs = segment_in[0].astype(jnp.float32)
    weight = layer_weight[0]
    gain = layer_gain[0]
    slab = weight.shape[1]
    exit_slots = exit_rows.shape[1]
    inv_rms = lax.rsqrt(jnp.mean(inputs * inputs, axis=-1, keepdims=True) + epsilon)
    unit = inputs * inv_rms
    normed = (unit * gain).astype(jnp.bfloat16)
    update_slab = jnp.dot(normed, weight, preferred_element_type=jnp.float32).astype(jnp.bfloat16)
    update = lax.all_gather(update_slab, "tensor", axis=1, tiled=True)
    hidden = (inputs + update.astype(jnp.float32)).astype(jnp.bfloat16)
    my_rows = exit_rows[pipe_pos]
    exit_hidden = hidden[my_rows].astype(jnp.float32)
    exit_inv = lax.rsqrt(jnp.mean(exit_hidden * exit_hidden, axis=-1, keepdims=True) + epsilon)
    exit_unit = exit_hidden * exit_inv
    exit_normed = (exit_unit * final_gain).astype(jnp.bfloat16)
    exit_slab = lax.dynamic_slice_in_dim(exit_normed, tensor_pos * slab, slab, 1)
    all_slabs = lax.all_gather(exit_slab, "pipe", axis=0, tiled=True)
    total_rows = all_slabs.shape[0]
    own_rows = total_rows // tensor_count
    piece = all_slabs
    logits = lax.psum_scatter(
        lax.dot_general(
            piece, head_weight, (((1,), (1,)), ((), ())), preferred_element_type=jnp.float32
        ),
        "tensor",
        scatter_dimension=0,
        tiled=True,
    )
    vocab_part = head_weight.shape[0]
    flat_index = tensor_pos * own_rows + jnp.arange(own_rows, dtype=jnp.int32)
    segment_ids = flat_index // exit_slots
    slot_ids = flat_index % exit_slots
    targets = exit_targets.reshape(-1)[flat_index]
    row_weight = jnp.where(
        slot_ids < exit_count[segment_ids], exit_scale[segment_ids], jnp.float32(0.0)
    )
    local_target = targets - pipe_pos * vocab_part
    onehot = (jnp.arange(vocab_part, dtype=jnp.int32)[None, :] == local_target[:, None]).astype(
        jnp.float32
    )
    row_top = lax.pmax(jnp.max(logits, axis=-1), "pipe")
    row_total = lax.psum(jnp.sum(jnp.exp(logits - row_top[:, None]), axis=-1), "pipe")
    probs = jnp.exp(logits - row_top[:, None]) / row_total[:, None]
    dlogits = (row_weight[:, None] * (probs - onehot)).astype(jnp.bfloat16)
    piece = lax.all_gather(dlogits, "tensor", axis=0, tiled=True)
    head_acc = lax.dot_general(
        piece, all_slabs, (((0,), (0,)), ((), ())), preferred_element_type=jnp.float32
    )
    exit_part = jnp.dot(piece, head_weight, preferred_element_type=jnp.float32)
    head_acc, exit_part = (head_acc, exit_part)
    head_grad = head_acc.astype(jnp.bfloat16)
    exit_grad_slab = lax.psum_scatter(exit_part, "pipe", scatter_dimension=0, tiled=True)
    exit_grad = lax.all_gather(exit_grad_slab, "tensor", axis=1, tiled=True)
    scaled = exit_grad * final_gain
    exit_back = (
        scaled - exit_unit * jnp.mean(scaled * exit_unit, axis=-1, keepdims=True)
    ) * exit_inv
    hidden_grad = out_grad[0].astype(jnp.float32).at[my_rows].add(exit_back)
    grad_rounded = hidden_grad.astype(jnp.bfloat16)
    grad_slab = lax.dynamic_slice_in_dim(grad_rounded, tensor_pos * slab, slab, 1)
    weight_grad = lax.dot_general(
        normed, grad_slab, (((0,), (0,)), ((), ())), preferred_element_type=jnp.float32
    ).astype(jnp.bfloat16)
    normed_part = lax.dot_general(
        grad_slab, weight, (((1,), (1,)), ((), ())), preferred_element_type=jnp.float32
    )
    normed_grad = lax.psum(normed_part, "tensor")
    gain_grad = jnp.sum(normed_grad * unit, axis=0)
    unit_grad = normed_grad * gain
    input_grad = (
        hidden_grad
        + (unit_grad - unit * jnp.mean(unit_grad * unit, axis=-1, keepdims=True)) * inv_rms
    ).astype(jnp.bfloat16)
    return (input_grad[None], weight_grad[None], gain_grad[None], head_grad)


def solution(mesh):
    in_specs = (
        P("pipe", None, None),
        P("pipe", None, "tensor"),
        P("pipe", None),
        P(),
        P("pipe", "tensor"),
        P(),
        P(),
        P(),
        P(),
        P("pipe", None, None),
    )
    out_specs = (
        P("pipe", None, None),
        P("pipe", None, "tensor"),
        P("pipe", None),
        P("pipe", "tensor"),
    )
    return jax.shard_map(local, mesh=mesh, in_specs=in_specs, out_specs=out_specs, check_vma=False)
```

profile of v0, /device:TPU:1, one launch (start us, length us, event | category | flops | bytes accessed | tf_op | source)
XLA Modules:
  0.0 545.9 jit_solution(8138788326033098541)
XLA Ops:
  7.2 3.2 fusion.14
  10.5 4.2 fusion.31
  14.8 0.7 fusion.53
  15.5 52.9 %all-gather.3.cloned.1.call-done = bf16[512,4096]{1,0:T(8,128)(2,1)} async-done(((bf16[512,256]{1,0:T(8,128)(2,1)}), bf16[512,4096]{1,0:T(8,128)(2,1)}) %all-gather.3.cloned.1.call-update) | async-done | bytes 4194320 | tf_op jit(solution)/shard_map/all_gather | solution.py:32
  68.5 7.2 %fusion.15 = bf16[512,4096]{1,0:T(8,128)(2,1)} fusion(bf16[1,512,4096]{2,1,0:T(8,128)(2,1)} %param.10, bf16[512,4096]{1,0:T(8,128)(2,1)} %all-gather.3.cloned.1.call-done), kind=kLoop, calls=%fused_computation.22 | loop fusion | flops 8388608 | bytes 12582912 | tf_op jit(solution)/shard_map/convert_element_type | solution.py:33
  75.7 3.7 gather_fusion.2
  79.4 0.2 fusion.36
  79.8 17.8 %all_gather.13 = bf16[512,256]{1,0:T(8,128)(2,1)S(1)} all-gather(bf16[32,256]{1,0:T(8,128)(2,1)S(1)} %fusion.46), channel_id=1, replica_groups=mesh['pipe'=16,'tensor'=16] {'pipe'}, dimensions={0}, use_global_device_ids=true | all-gather | bytes 278528 | tf_op jit(solution)/shard_map/all_gather | solution.py:40
  97.5 4.0 fusion.54
  101.6 0.7 gather_fusion
  102.3 0.7 gather_fusion.1
  103.1 0.7 gather_fusion.3
  103.8 59.7 %reduce-scatter.3.cloned.1.call-done = f32[32,2000]{1,0:T(8,128)} async-done(((f32[512,2000]{1,0:T(8,128)}), f32[32,2000]{1,0:T(8,128)}) %reduce-scatter.3.cloned.1.call-update) | async-done | bytes 256016 | tf_op jit(solution)/shard_map/reduce_scatter | solution.py:44
  163.5 1.1 reduce_max.9
  164.6 33.4 %pmax.7 = f32[32]{0:T(128)S(1)} all-reduce(f32[32]{0:T(128)S(1)} %reduce_max.9), channel_id=1, replica_groups=mesh['pipe'=16,'tensor'=16] {'pipe'}, use_global_device_ids=true, to_apply=%region_4.5 | all-reduce | flops 32 | bytes 256 | tf_op jit(solution)/shard_map/pmax | solution.py:64
  198.0 1.2 fusion.45
  199.1 28.7 %psum.14 = f32[32]{0:T(128)S(1)} all-reduce(f32[32]{0:T(128)S(1)} %fusion.45), channel_id=1, replica_groups=mesh['pipe'=16,'tensor'=16] {'pipe'}, use_global_device_ids=true, to_apply=%region_6.7 | all-reduce | flops 32 | bytes 256 | tf_op jit(solution)/shard_map/psum | solution.py:65
  227.8 1.8 multiply_convert_fusion
  229.7 52.1 %all-gather.5.cloned.1.call-done = bf16[512,2000]{1,0:T(8,128)(2,1)} async-done(((bf16[32,2000]{1,0:T(8,128)(2,1)}), bf16[512,2000]{1,0:T(8,128)(2,1)}) %all-gather.5.cloned.1.call-update) | async-done | bytes 2048016 | tf_op jit(solution)/shard_map/all_gather | solution.py:68
  281.8 3.4 fusion.55
  285.2 6.5 %bitcast_convert_fusion = f32[512,4096]{1,0:T(8,128)} fusion(bf16[1,512,4096]{2,1,0:T(8,128)(2,1)} %param.19), kind=kLoop, calls=%fused_computation.30 | loop fusion | flops 2097152 | bytes 12582912 | tf_op jit(solution)/shard_map/convert_element_type | solution.py:81
  291.7 67.6 %reduce-scatter.5.cloned.1.call-done = f32[32,256]{1,0:T(8,128)} async-done(((f32[512,256]{1,0:T(8,128)}), f32[32,256]{1,0:T(8,128)}) %reduce-scatter.5.cloned.1.call-update) | async-done | bytes 32784 | tf_op jit(solution)/shard_map/reduce_scatter | solution.py:75
  359.3 21.2 %all_gather.15 = f32[32,4096]{1,0:T(8,128)S(1)} all-gather(f32[32,256]{1,0:T(8,128)} %reduce-scatter.5.cloned.1.call-done), channel_id=1, replica_groups=mesh['pipe'=16,'tensor'=16] {'tensor'}, dimensions={1}, use_global_device_ids=true | all-gather | bytes 557056 | tf_op jit(solution)/shard_map/all_gather | solution.py:76
  380.6 0.3 multiply_reduce_fusion
  380.8 7.9 %scatter_custom_fusion = f32[512,4096]{1,0:T(8,128)} fusion(f32[512,4096]{1,0:T(8,128)} %bitcast_convert_fusion, s32[32]{0:T(128)S(1)} %fusion.53, f32[32,4096]{1,0:T(8,128)S(1)} %all_gather.15, f32[32]{0:T(128)S(1)} %broadcast_multiply_fusion.1, f32[4096]{0:T(1024)S(1)} %copy-done.5, f32[32]{0:T(128)S(1)} %add_rsqrt_fusion.1, ...), kind=kCustom, calls=%fused_computation.44 | custom fusion | flops 917504 | bytes 9192448 | tf_op jit(solution)/shard_map/scatter-add | solution.py:81
  388.8 5.5 %fusion.28 = f32[512,4096]{1,0:T(8,128)} fusion(bf16[1,4096,256]{2,1,0:T(8,128)(2,1)S(1)} %copy-done, f32[512,4096]{1,0:T(8,128)} %scatter_custom_fusion, s32[]{:T(128)S(6)} %select_n.76), kind=kOutput, calls=%fused_computation.36 | convolution fusion | flops 1073741824 | bytes 10747908 | tf_op jit(solution)/shard_map/dot_general | solution.py:87
  394.3 3.3 convolution_convert_fusion.1
  397.7 5.4 fusion.18
  403.1 121.4 %all-reduce.2.cloned.1.call-done = f32[512,4096]{1,0:T(8,128)} async-done(((f32[512,4096]{1,0:T(8,128)}), f32[512,4096]{1,0:T(8,128)}) %all-reduce.2.cloned.1.call-update) | async-done | bytes 8388624 | tf_op jit(solution)/shard_map/psum | solution.py:90
  524.5 7.3 %fusion.13 = (f32[4096]{0:T(1024)}, f32[512]{0:T(512)S(1)}) fusion(f32[512,4096]{1,0:T(8,128)} %all-reduce.2.cloned.1.call-done, bf16[1,512,4096]{2,1,0:T(8,128)(2,1)} %param.10, f32[512]{0:T(512)S(1)} %add_rsqrt_fusion, f32[4096]{0:T(1024)S(1)} %bitcast.78), kind=kLoop, calls=%fused_computation.20 | loop fusion | flops 14675456 | bytes 12619776 | tf_op jit(solution)/shard_map/reduce_sum | solution.py:91
  531.7 1.1 copy-done.4
  532.8 6.6 %fusion.23 = bf16[1,512,4096]{2,1,0:T(8,128)(2,1)} fusion(f32[512,4096]{1,0:T(8,128)} %scatter_custom_fusion, bf16[1,512,4096]{2,1,0:T(8,128)(2,1)S(1)} %copy-done.3, f32[512,4096]{1,0:T(8,128)S(1)} %copy-done.4, f32[512]{0:T(512)S(1)} %broadcast_multiply_fusion, f32[512]{0:T(512)S(1)} %add_rsqrt_fusion, f32[4096]{0:T(1024)S(1)} %bitcast.79), kind=kLoop, calls=%fused_computation.29 | loop fusion | flops 16777216 | bytes 25186304 | tf_op jit(solution)/shard_map/broadcast_in_dim | solution.py:97
  (39 shorter events, 0.7 us)
Async XLA Ops:
  7.2 3.3 copy-start
  7.2 7.6 %copy-start.5 = (f32[4096]{0:T(1024)S(1)}, f32[4096]{0:T(1024)}, u32[]{:S(2)}) copy-start(f32[4096]{0:T(1024)} %param.13) | copy-start | bytes 49156
  7.2 61.3 %all-gather.3.cloned.1.call-start = ((), (), s32[]{:S(2)}) async-start(), calls=%async_computation.2 | async-start | bytes 4456448 | tf_op jit(solution)/shard_map/all_gather | solution.py:32
  14.7 148.8 %reduce-scatter.3.cloned.1.call-start = ((), (), s32[]{:S(2)}) async-start(), calls=%async_computation.3 | async-start | bytes 4456448 | tf_op jit(solution)/shard_map/reduce_scatter | solution.py:44
  75.7 25.9 %copy-start.1 = (s32[16]{0:T(128)S(1)}, s32[16]{0:T(128)}, u32[]{:S(2)}) copy-start(s32[16]{0:T(128)} %param.16) | copy-start | bytes 196
  75.7 26.6 %copy-start.2 = (f32[16]{0:T(128)S(1)}, f32[16]{0:T(128)}, u32[]{:S(2)}) copy-start(f32[16]{0:T(128)} %param.18) | copy-start | bytes 196
  75.7 27.3 %copy-start.7 = (s32[16,32]{1,0:T(8,128)S(1)}, s32[16,32]{1,0:T(8,128)}, u32[]{:S(2)}) copy-start(s32[16,32]{1,0:T(8,128)} %param.17) | copy-start | bytes 6148
  101.5 180.3 %all-gather.5.cloned.1.call-start = ((), (), s32[]{:S(2)}) async-start(), calls=%async_computation.4 | async-start | bytes 2228224 | tf_op jit(solution)/shard_map/all_gather | solution.py:68
  229.6 129.7 %reduce-scatter.5.cloned.1.call-start = ((), (), s32[]{:S(2)}) async-start(), calls=%async_computation.5 | async-start | bytes 557056 | tf_op jit(solution)/shard_map/reduce_scatter | solution.py:75
  285.2 239.3 %all-reduce.2.cloned.1.call-start = ((), (), s32[]{:S(2)}) async-start(), calls=%async_computation.6 | async-start | bytes 16777216 | tf_op jit(solution)/shard_map/psum | solution.py:90
  394.3 3.3 copy-start.6
  524.5 7.3 %copy-start.3 = (bf16[1,512,4096]{2,1,0:T(8,128)(2,1)S(1)}, bf16[1,512,4096]{2,1,0:T(8,128)(2,1)}, u32[]{:S(2)}) copy-start(bf16[1,512,4096]{2,1,0:T(8,128)(2,1)} %param.10) | copy-start | bytes 12582916
  524.5 8.3 %copy-start.4 = (f32[512,4096]{1,0:T(8,128)S(1)}, f32[512,4096]{1,0:T(8,128)}, u32[]{:S(2)}) copy-start(f32[512,4096]{1,0:T(8,128)} %all-reduce.2.cloned.1.call-done) | copy-start | bytes 25165828
Sparse Core Ops, SparseCore 0:
  14.8 53.5 all-gather.2
  101.6 61.8 reduce-scatter.2
  229.7 52.0 all-gather.4
  285.7 73.5 reduce-scatter.4
  394.5 129.9 all-reduce.1
where the time goes:
time: 547 us; the launch traced here: 546 us
  waiting for transfers between devices  354 us (65%)
  blocking collectives  101 us (18%)
  other arithmetic  44.1 us (8%)
  matrix products  25.8 us (5%)
  between operations  13.9 us (3%)
  local copies, waits for them, and re-layouts  7.08 us (1%)
    psum x1, waiting for transfers between devices, local(): normed_grad = lax.psum(normed_part, 'tensor')  121 us
    reduce_scatter x1, waiting for transfers between devices, local(): lax.psum_scatter(exit_part, 'pipe', scatter_dimension=0, tiled=True)  67.6 us
    reduce_scatter x1, waiting for transfers between devices, local(): lax.psum_scatter(lax.dot_general(piece, head_weight, (((1,), (1,)), ((),...  59.7 us
    all_gather x1, waiting for transfers between devices, local(): update = lax.all_gather(update_slab, 'tensor', axis=1, tiled=True)  52.9 us
    all_gather x1, waiting for transfers between devices, local(): piece = lax.all_gather(dlogits, 'tensor', axis=0, tiled=True)  52.1 us
    pmax x1, blocking collectives, local(): row_top = lax.pmax(jnp.max(logits, axis=-1), 'pipe')  33.4 us
    psum x1, blocking collectives, local(): lax.psum(jnp.sum(jnp.exp(logits - row_top[:, None]), axis=-1), 'pipe')  28.7 us
    all_gather x1, blocking collectives, local(): exit_grad = lax.all_gather(exit_grad_slab, 'tensor', axis=1, tiled=True)  21.2 us
  transfers between devices with their start and end apart: 5, of which 5 were waited for; matrix products, arithmetic and copies ran while one was open for 3% of the time, Pallas kernels for 0%

commit v1 on v0

v1 whole, which is shorter than its diff:
```python
import jax
import jax.numpy as jnp
from jax import lax
from jax.sharding import Mesh, PartitionSpec as P

F32 = jnp.float32
BF16 = jnp.bfloat16
EPSILON = 1e-05


def rounded(values):
    return lax.reduce_precision(values, 8, 7)


def split3(values):
    first = rounded(values)
    rest = values - first
    second = rounded(rest)
    return [first, second, rest - second]


def spread(values, axis, count):
    return lax.all_to_all(jnp.broadcast_to(values[None], (count,) + values.shape), axis, 0, 0)


def swap(values):
    return lax.ppermute(values, "core", [(0, 1), (1, 0)])


def pair(mine, other, core, axis):
    first = jnp.where(core == 0, mine, other)
    second = jnp.where(core == 0, other, mine)
    return jnp.concatenate([first, second], axis=axis)


def local(
    segment_in,
    layer_weight,
    layer_gain,
    final_gain,
    head_weight,
    exit_rows,
    exit_count,
    exit_targets,
    exit_scale,
    out_grad,
):
    pipe = lax.axis_index("pipe")
    core = lax.axis_index("core")
    z = lax.axis_index("z")
    pipes = lax.axis_size("pipe")
    zs = lax.axis_size("z")
    block = z * 2 + core
    seg = segment_in[0]
    weight = layer_weight[0]
    gain = layer_gain[0]
    grad = out_grad[0]
    tokens, width = seg.shape
    slab = weight.shape[1]
    exits = exit_rows.shape[1]
    rows_all = pipes * exits
    vocab_part = head_weight.shape[0]
    half = vocab_part // 2
    padded = -(-(half + 6) // 128) * 128

    weight_other = swap(weight)
    head_mine = lax.dynamic_slice_in_dim(head_weight, core * half, half, 0)
    head_rest = lax.dynamic_slice_in_dim(head_weight, (1 - core) * half, half, 0)
    head_other = swap(head_rest)
    pad_rows = ((0, padded - half), (0, 0))
    head_mine = jnp.pad(head_mine, pad_rows)
    head_rest = jnp.pad(head_rest, pad_rows)
    head_other = jnp.pad(head_other, pad_rows)

    my_rows = exit_rows[pipe]
    pick = (my_rows[:, None] == jnp.arange(tokens, dtype=jnp.int32)[None, :]).astype(BF16)
    row_in = jnp.dot(pick, seg, preferred_element_type=F32)
    row_inv = lax.rsqrt(jnp.mean(row_in * row_in, axis=-1, keepdims=True) + EPSILON)
    row_unit = row_in * row_inv
    row_normed = (row_unit * gain).astype(BF16)
    row_update = rounded(jnp.dot(row_normed, weight, preferred_element_type=F32))
    row_block = lax.dynamic_slice_in_dim(row_in, block * slab, slab, 1)
    hidden = (row_block + row_update).astype(BF16)

    all_mine = spread(hidden, "pipe", pipes).reshape(rows_all, slab)
    all_other = swap(all_mine)
    gain_mine = lax.dynamic_slice_in_dim(final_gain, block * slab, slab, 0)
    gain_other = lax.dynamic_slice_in_dim(final_gain, (z * 2 + 1 - core) * slab, slab, 0)
    mine32 = all_mine.astype(F32)
    other32 = all_other.astype(F32)
    squares = jnp.sum(mine32 * mine32, axis=-1) + jnp.sum(other32 * other32, axis=-1)
    part = lax.dot_general(
        (mine32 * gain_mine).astype(BF16), head_mine, (((1,), (1,)), ((), ())), preferred_element_type=F32
    ) + lax.dot_general(
        (other32 * gain_other).astype(BF16), head_other, (((1,), (1,)), ((), ())), preferred_element_type=F32
    )
    column = lax.broadcasted_iota(jnp.int32, (1, padded), 1)
    for spot, piece in enumerate(split3(squares)):
        part = jnp.where(column == half + spot, piece[:, None], part)
    own = rows_all // zs
    parts = lax.all_to_all(part.astype(BF16).reshape(zs, own, padded), "z", 0, 0)
    sums = jnp.sum(parts.astype(F32), axis=0)
    own_inv = lax.rsqrt(jnp.sum(sums[:, half : half + 3], axis=-1, keepdims=True) / width + EPSILON)
    logits = sums * own_inv

    live_column = column < half
    index = z * own + jnp.arange(own, dtype=jnp.int32)
    section = index // exits
    target = exit_targets.reshape(-1)[index] - pipe * vocab_part - core * half
    row_weight = jnp.where(index % exits < exit_count[section], exit_scale[section], F32(0.0))[:, None]
    hit = (column == target[:, None]) & live_column
    top = jnp.max(jnp.where(live_column, logits, -jnp.inf), axis=-1)
    shifted = jnp.where(live_column, logits - top[:, None], -jnp.inf)
    expo = jnp.exp(shifted)
    total = jnp.sum(expo, axis=-1)
    along = jnp.sum(jnp.where(live_column, expo * shifted, 0.0), axis=-1)
    at_target = jnp.sum(jnp.where(hit, logits, 0.0), axis=-1)
    mine4 = jnp.stack([top, total, along, at_target])
    stats = jnp.concatenate([mine4, swap(mine4)])
    stats = spread(stats, "pipe", pipes).reshape(pipes * 2, 4, own)
    tops, totals, alongs, targets = [stats[:, i] for i in range(4)]
    row_top = jnp.max(tops, axis=0)
    lower = jnp.exp(tops - row_top)
    row_total = jnp.sum(totals * lower, axis=0)
    row_along = jnp.sum((alongs + (tops - row_top) * totals) * lower, axis=0) / row_total
    row_target = jnp.sum(targets, axis=0) - row_top
    back_mean = row_weight[:, 0] * (row_along - row_target) / width
    probs = jnp.exp(logits - row_top[:, None]) / row_total[:, None]
    dlogits = row_weight * (probs - hit.astype(F32))
    for spot, piece in enumerate(split3(own_inv[:, 0]) + split3(back_mean)):
        dlogits = jnp.where(column == half + spot, piece[:, None], dlogits)
    dl_mine = lax.all_gather(dlogits.astype(BF16), "z", axis=0, tiled=True)
    dl_other = swap(dl_mine)

    exit_part = jnp.dot(dl_mine, head_mine, preferred_element_type=F32) + jnp.dot(
        dl_other, head_rest, preferred_element_type=F32
    )
    extra = dl_mine[:, half : half + 6].astype(F32)
    exit_inv = jnp.sum(extra[:, :3], axis=-1, keepdims=True)
    exit_mean = jnp.sum(extra[:, 3:], axis=-1, keepdims=True)
    exit_normed = (mine32 * exit_inv * gain_mine).astype(BF16)
    over_rows = (((0,), (0,)), ((), ()))
    head_a = lax.dot_general(dl_mine, exit_normed, over_rows, preferred_element_type=F32).astype(BF16)[:half]
    head_b = lax.dot_general(dl_other, exit_normed, over_rows, preferred_element_type=F32).astype(BF16)[:half]
    head_grad = pair(head_a, head_b, core, 0)
    exit_grad = jnp.sum(lax.all_to_all(exit_part.reshape(pipes, exits, slab), "pipe", 0, 0), axis=0)
    my_inv = lax.dynamic_slice_in_dim(exit_inv, pipe * exits, exits, 0)
    my_mean = lax.dynamic_slice_in_dim(exit_mean, pipe * exits, exits, 0)
    exit_unit = hidden.astype(F32) * my_inv
    exit_back = (exit_grad * gain_mine - exit_unit * my_mean) * my_inv
    grad_slab = lax.dynamic_slice_in_dim(grad, block * slab, slab, 1)
    row_grad = jnp.dot(pick, grad_slab, preferred_element_type=F32) + exit_back
    row_rounded = row_grad.astype(BF16)

    inputs = seg.astype(F32)
    inv_rms = lax.rsqrt(jnp.mean(inputs * inputs, axis=-1, keepdims=True) + EPSILON)
    normed = (inputs * inv_rms * gain).astype(BF16)
    is_exit = jnp.any(pick > 0, axis=0)
    held = tokens // (zs * 2)

    def of_core(values):
        grouped = values.reshape((zs, 2, held) + values.shape[1:])
        return lax.dynamic_index_in_dim(grouped, core, 1, keepdims=False)

    grad_core = of_core(grad).reshape(zs * held, width)
    other_block = (z * 2 + 1 - core) * slab
    on_columns = (((1,), (1,)), ((), ()))
    main_part = lax.dot_general(
        lax.dynamic_slice_in_dim(grad_core, block * slab, slab, 1), weight, on_columns, preferred_element_type=F32
    ) + lax.dot_general(
        lax.dynamic_slice_in_dim(grad_core, other_block, slab, 1),
        weight_other,
        on_columns,
        preferred_element_type=F32,
    )
    main_grad = lax.psum_scatter(main_part, "z", scatter_dimension=0, tiled=True)
    first = block * held
    held_in = lax.dynamic_slice_in_dim(seg, first, held, 0).astype(F32)
    held_grad = lax.dynamic_slice_in_dim(grad, first, held, 0).astype(F32)
    held_exit = lax.dynamic_slice_in_dim(is_exit, first, held, 0)

    def layer_back(norm_grad, unit, inv, residual):
        unit_grad = norm_grad * gain
        centre = jnp.mean(unit_grad * unit, axis=-1, keepdims=True)
        return (residual + (unit_grad - unit * centre) * inv).astype(BF16)

    held_inv = lax.rsqrt(jnp.mean(held_in * held_in, axis=-1, keepdims=True) + EPSILON)
    held_unit = held_in * held_inv
    main_out = layer_back(main_grad, held_unit, held_inv, held_grad)
    gain_part = jnp.sum(jnp.where(held_exit[:, None], 0.0, main_grad * held_unit), axis=0)
    main_all = lax.all_gather(main_out, ("z", "core"), axis=0, tiled=True)

    put = pick.T
    slab_rounded = jnp.where(
        is_exit[:, None], jnp.dot(put, row_rounded, preferred_element_type=F32).astype(BF16), grad_slab
    )
    weight_grad = lax.dot_general(normed, slab_rounded, over_rows, preferred_element_type=F32).astype(BF16)
    core_rows = exits // 2
    share = core_rows // zs
    row_other = swap(lax.dynamic_slice_in_dim(row_grad, (1 - core) * core_rows, core_rows, 0))
    row_mine = lax.dynamic_slice_in_dim(row_grad, core * core_rows, core_rows, 0)
    row_part = lax.dot_general(
        row_mine.astype(BF16), weight, on_columns, preferred_element_type=F32
    ) + lax.dot_general(row_other.astype(BF16), weight_other, on_columns, preferred_element_type=F32)
    send = jnp.concatenate([row_part, pair(row_mine, row_other, core, 1)], axis=1)
    got = lax.all_to_all(send.reshape(zs, share, width + 2 * slab), "z", 0, 0)
    norm_grad = jnp.sum(got[:, :, :width], axis=0)
    residual = got[:, :, width:].transpose(1, 0, 2).reshape(share, width)
    at = core * core_rows + z * share
    share_unit = lax.dynamic_slice_in_dim(row_unit, at, share, 0)
    share_inv = lax.dynamic_slice_in_dim(row_inv, at, share, 0)
    share_out = layer_back(norm_grad, share_unit, share_inv, residual)
    gain_part = gain_part + jnp.sum(norm_grad * share_unit, axis=0)
    gain_first = rounded(gain_part)
    gain_rest = gain_part - gain_first
    last = jnp.concatenate([share_out, gain_first.astype(BF16)[None], gain_rest.astype(BF16)[None]])
    last = spread(last, ("z", "core"), zs * 2)
    gain_grad = jnp.sum(last[:, share:].astype(F32), axis=(0, 1))
    row_out = last[:, :share].reshape(zs, 2, share, width).transpose(1, 0, 2, 3).reshape(exits, width)
    input_grad = jnp.where(
        is_exit[:, None], jnp.dot(put, row_out, preferred_element_type=F32).astype(BF16), main_all
    )
    return (input_grad[None], weight_grad[None], gain_grad[None], head_grad)


def solution(mesh):
    pipes, tensors = mesh.devices.shape
    fine = Mesh(mesh.devices.reshape(pipes, tensors // 2, 2), ("pipe", "z", "core"))
    tensor = ("z", "core")
    in_specs = (
        P("pipe", None, None),
        P("pipe", None, tensor),
        P("pipe", None),
        P(),
        P("pipe", tensor),
        P(),
        P(),
        P(),
        P(),
        P("pipe", None, None),
    )
    out_specs = (
        P("pipe", None, None),
        P("pipe", None, tensor),
        P("pipe", None),
        P("pipe", tensor),
    )
    return jax.shard_map(local, mesh=fine, in_specs=in_specs, out_specs=out_specs, check_vma=False)
```

time: 547 us -> 272 us (0.50)
  waiting for transfers between devices: 354 us -> 138 us
  blocking collectives: 101 us -> 0 us
  starting transfers between devices: 0.21 us -> 46.3 us
  other arithmetic: 44.1 us -> 21.9 us
  local copies, waits for them, and re-layouts: 7.08 us -> 16.2 us
  matrix products: 25.8 us -> 33.8 us
    psum x1 -> x0, waiting for transfers between devices: 121 us -> none  [local(): normed_grad = lax.psum(normed_part, 'tensor')]
    all_gather x2, waiting for transfers between devices: 105 us -> 18.5 us  [the longest x1 18.5 us: local(): dl_mine = lax.all_gather(dlogits.astype(BF16), 'z', axis=0, tiled=True)]
    reduce_scatter x2 -> x1, waiting for transfers between devices: 127 us -> 56.3 us  [local(): lax.psum_scatter(main_part, 'z', scatter_dimension=0, tiled=True)]
    all_to_all x0 -> x6, waiting for transfers between devices: none -> 62.8 us  [the longest x1 27.2 us: local(): lax.all_to_all(part.astype(BF16).reshape(zs, own, padded), 'z', 0, 0)]
    all_gather x2 -> x0, blocking collectives: 39 us -> none  [the longest x1 21.2 us: local(): exit_grad = lax.all_gather(exit_grad_slab, 'tensor', axis=1, tiled=True)]
    all_to_all x0 -> x6, starting transfers between devices: none -> 34 us  [the longest x3 15.1 us: spread(): lax.all_to_all(jnp.broadcast_to(values[None], (count,) + values.shape), a...]
    pmax x1 -> x0, blocking collectives: 33.4 us -> none  [local(): row_top = lax.pmax(jnp.max(logits, axis=-1), 'pipe')]
    psum x1 -> x0, blocking collectives: 28.7 us -> none  [local(): lax.psum(jnp.sum(jnp.exp(logits - row_top[:, None]), axis=-1), 'pipe')]
  transfers between devices with their start and end apart: 5 -> 15, of which waited for: 5 -> 10; matrix products, arithmetic and copies ran while one was open for 3% -> 22% of each run, Pallas kernels for 0% -> 0%
where the time goes in v1:
time: 272 us; the launch traced here: 271 us
  waiting for transfers between devices  138 us (51%)
  starting transfers between devices  46.3 us (17%)
  matrix products  33.8 us (12%)
  other arithmetic  21.9 us (8%)
  local copies, waits for them, and re-layouts  16.2 us (6%)
  between operations  14.2 us (5%)
    reduce_scatter x1, waiting for transfers between devices, local(): lax.psum_scatter(main_part, 'z', scatter_dimension=0, tiled=True)  56.3 us
    all_to_all x1, waiting for transfers between devices, local(): lax.all_to_all(part.astype(BF16).reshape(zs, own, padded), 'z', 0, 0)  27.2 us
    all_to_all x3, waiting for transfers between devices, spread(): lax.all_to_all(jnp.broadcast_to(values[None], (count,) + values.shape), a...  20.1 us
    all_gather x1, waiting for transfers between devices, local(): dl_mine = lax.all_gather(dlogits.astype(BF16), 'z', axis=0, tiled=True)  18.5 us
    all_to_all x3, starting transfers between devices, spread(): lax.all_to_all(jnp.broadcast_to(values[None], (count,) + values.shape), a...  15.1 us
    ppermute x6, starting transfers between devices, swap(): return lax.ppermute(values, 'core', [(0, 1), (1, 0)])  12.2 us
    all_to_all x1, waiting for transfers between devices, local(): got = lax.all_to_all(send.reshape(zs, share, width + 2 * slab), 'z', 0, 0)  10.1 us
    all_to_all x1, starting transfers between devices, local(): lax.all_to_all(part.astype(BF16).reshape(zs, own, padded), 'z', 0, 0)  8.21 us
  transfers between devices with their start and end apart: 15, of which 10 were waited for; matrix products, arithmetic and copies ran while one was open for 22% of the time, Pallas kernels for 0%

profile of v1, /device:TPU:1, one launch (start us, length us, event | category | flops | bytes accessed | tf_op | source)
XLA Modules:
  0.0 270.7 jit_solution(9369262299353777747)
XLA Ops:
  7.9 3.1 %multiply_reduce_fusion.1 = (f32[32]{0:T(128)S(1)}, f32[32,4096]{1,0:T(8,128)S(1)}) fusion(bf16[1,512,4096]{2,1,0:T(8,128)(2,1)} %param.10, s32[32]{0:T(128)S(1)} %fusion.76), kind=kOutput, calls=%fused_computation.59 | convolution fusion | flops 134496224 | bytes 4718848 | tf_op jit(solution)/shard_map/dot_general | solution.py:77
  12.3 7.6 %all-to-all-start = ((bf16[16,32,256]{2,1,0:T(8,128)(2,1)}), bf16[16,32,256]{2,1,0:T(8,128)(2,1)S(1)}, u32[]{:S(2)}, u32[]{:S(2)}) async-start(bf16[16,32,256]{2,1,0:T(8,128)(2,1)} %broadcast_in_dim.233), calls=%async_computation | async-start | bytes 524288 | tf_op jit(solution)/shard_map/all_to_all | solution.py:23
  19.9 2.1 constant_dynamic-slice_fusion.2
  23.9 3.6 %all-to-all-done = bf16[16,32,256]{2,1,0:T(8,128)(2,1)S(1)} async-done(((bf16[16,32,256]{2,1,0:T(8,128)(2,1)}), bf16[16,32,256]{2,1,0:T(8,128)(2,1)S(1)}, u32[]{:S(2)}, u32[]{:S(2)}) %all-to-all-start) | async-done | bytes 262176 | tf_op jit(solution)/shard_map/all_to_all | solution.py:23
  27.5 2.1 collective-permute-start
  32.0 2.7 select_convert_fusion
  34.7 8.2 %all-to-all-start.1 = ((bf16[8,64,1024]{2,1,0:T(8,128)(2,1)}), bf16[8,64,1024]{2,1,0:T(8,128)(2,1)}, u32[]{:S(2)}, u32[]{:S(2)}) async-start(bf16[8,64,1024]{2,1,0:T(8,128)(2,1)} %bitcast.85), calls=%async_computation.1 | async-start | bytes 2097152 | tf_op jit(solution)/shard_map/all_to_all | solution.py:101
  45.1 27.2 %all-to-all-done.1 = bf16[8,64,1024]{2,1,0:T(8,128)(2,1)} async-done(((bf16[8,64,1024]{2,1,0:T(8,128)(2,1)}), bf16[8,64,1024]{2,1,0:T(8,128)(2,1)}, u32[]{:S(2)}, u32[]{:S(2)}) %all-to-all-start.1) | async-done | bytes 1048608 | tf_op jit(solution)/shard_map/all_to_all | solution.py:101
  79.5 3.5 %all-to-all-start.2 = ((f32[16,1,512]{2,1,0:T(1,128)}), f32[16,1,512]{2,1,0:T(1,128)S(1)}, u32[]{:S(2)}, u32[]{:S(2)}) async-start(f32[16,1,512]{2,1,0:T(1,128)} %reshape.398), calls=%async_computation.2 | async-start | bytes 65536 | tf_op jit(solution)/shard_map/all_to_all | solution.py:23
  83.6 5.8 %all-to-all-done.2 = f32[16,1,512]{2,1,0:T(1,128)S(1)} async-done(((f32[16,1,512]{2,1,0:T(1,128)}), f32[16,1,512]{2,1,0:T(1,128)S(1)}, u32[]{:S(2)}, u32[]{:S(2)}) %all-to-all-start.2) | async-done | bytes 32800 | tf_op jit(solution)/shard_map/all_to_all | solution.py:23
  93.6 1.7 select_convert_fusion.1
  95.4 1.8 constant_dynamic-slice_fusion
  98.0 4.4 %convolution_add_fusion = f32[256,4096]{1,0:T(8,128)} fusion(f32[256,4096]{1,0:T(8,128)S(1)} %fusion.51, bf16[4096,256]{1,0:T(8,128)(2,1)} %collective-permute-done.5, bf16[256,4096]{1,0:T(8,128)(2,1)S(1)} %bitcast.79, s32[]{:T(128)S(6)} %select_n.198), kind=kOutput, calls=%fused_computation.9 | convolution fusion | flops 537919488 | bytes 10616836 | tf_op jit(solution)/shard_map/dot_general | solution.py:170
  103.8 18.5 %all-gather.3.cloned.1.call-done = bf16[512,1024]{1,0:T(8,128)(2,1)} async-done(((bf16[64,1024]{1,0:T(8,128)(2,1)}), bf16[512,1024]{1,0:T(8,128)(2,1)}) %all-gather.3.cloned.1.call-update) | async-done | bytes 1048592 | tf_op jit(solution)/shard_map/all_gather | solution.py:132
  122.2 5.8 %collective-permute-start.3 = (bf16[512,1024]{1,0:T(8,128)(2,1)}, bf16[512,1024]{1,0:T(8,128)(2,1)}, u32[]{:S(2)}, u32[]{:S(2)}) collective-permute-start(bf16[512,1024]{1,0:T(8,128)(2,1)} %all-gather.3.cloned.1.call-done), channel_id=1, source_target_pairs={{0,1},{1,0},{2,3},{3,2},{4,5},{5,4},{6,7},{7,6},{8,9},{9,8},{10,11... | collective-permute-start | bytes 3145736 | tf_op jit(solution)/shard_map/ppermute | solution.py:27
  128.0 56.3 %reduce-scatter.2.cloned.1.call-done = f32[32,4096]{1,0:T(8,128)} async-done(((f32[256,4096]{1,0:T(8,128)}), f32[32,4096]{1,0:T(8,128)}) %reduce-scatter.2.cloned.1.call-update) | async-done | bytes 524304 | tf_op jit(solution)/shard_map/reduce_scatter | solution.py:176
  184.3 1.4 fusion.24
  185.7 2.1 fusion.29
  187.9 1.7 fusion.33
  189.6 2.6 convolution_add_fusion.2
  192.2 6.6 %all-to-all-start.3 = ((f32[16,32,256]{2,1,0:T(8,128)}), f32[16,32,256]{2,1,0:T(8,128)}, u32[]{:S(2)}, u32[]{:S(2)}) async-start(f32[16,32,256]{2,1,0:T(8,128)} %bitcast.18), calls=%async_computation.3 | async-start | bytes 1048576 | tf_op jit(solution)/shard_map/all_to_all | solution.py:146
  198.8 3.1 %fusion = f32[512]{0:T(512)S(1)} fusion(bf16[1,512,4096]{2,1,0:T(8,128)(2,1)} %param.10), kind=kLoop, calls=%fused_computation.5 | loop fusion | flops 6290944 | bytes 4196352 | tf_op jit(solution)/shard_map/reduce_sum | solution.py:156
  203.8 5.5 %all-to-all-done.3 = f32[16,32,256]{2,1,0:T(8,128)} async-done(((f32[16,32,256]{2,1,0:T(8,128)}), f32[16,32,256]{2,1,0:T(8,128)}, u32[]{:S(2)}, u32[]{:S(2)}) %all-to-all-start.3) | async-done | bytes 524320 | tf_op jit(solution)/shard_map/all_to_all | solution.py:146
  211.5 2.1 collective-permute-start.4
  214.5 2.4 convolution_add_fusion.1
  217.8 4.1 %all-to-all-start.4 = ((f32[8,2,4608]{2,1,0:T(2,128)}), f32[8,2,4608]{2,1,0:T(2,128)S(1)}, u32[]{:S(2)}, u32[]{:S(2)}) async-start(f32[8,2,4608]{2,1,0:T(2,128)} %reshape.367), calls=%async_computation.4 | async-start | bytes 589824 | tf_op jit(solution)/shard_map/all_to_all | solution.py:206
  222.4 1.8 fusion.53
  224.2 10.1 %all-to-all-done.4 = f32[8,2,4608]{2,1,0:T(2,128)S(1)} async-done(((f32[8,2,4608]{2,1,0:T(2,128)}), f32[8,2,4608]{2,1,0:T(2,128)S(1)}, u32[]{:S(2)}, u32[]{:S(2)}) %all-to-all-start.4) | async-done | bytes 294944 | tf_op jit(solution)/shard_map/all_to_all | solution.py:206
  235.8 4.0 %all-to-all-start.5 = ((bf16[16,4,4096]{2,1,0:T(4,128)(2,1)}), bf16[16,4,4096]{2,1,0:T(4,128)(2,1)S(1)}, u32[]{:S(2)}, u32[]{:S(2)}) async-start(bf16[16,4,4096]{2,1,0:T(4,128)(2,1)} %broadcast_in_dim.255), calls=%async_computation.6 | async-start | bytes 1048576 | tf_op jit(solution)/shard_map/all_to_all | solution.py:23
  240.9 5.5 %fusion.5 = bf16[1,4096,256]{2,1,0:T(8,128)(2,1)} fusion(bf16[1,512,4096]{2,1,0:T(8,128)(2,1)} %param.10, f32[4096]{0:T(1024)S(1)} %bitcast.92, f32[512]{0:T(512)S(1)} %add_rsqrt_fusion, pred[512]{0:T(512)(128)(4,1)S(1)} %compare_reduce_fusion, bf16[1,512,4096]{2,1,0:T(8,128)(2,1)} %param.19, s32[]{:T(128)S(6)} %select_n.192, s32[32]{0:T(128)S(1)} %fusion.76, ...), kind=kOutput, calls=%fused_computation.13 | convolution fusion | flops 1091854336 | bytes 6605444 | tf_op jit(solution)/shard_map/dot_general | solution.py:197
  246.4 10.7 %all-to-all-done.5 = bf16[16,4,4096]{2,1,0:T(4,128)(2,1)S(1)} async-done(((bf16[16,4,4096]{2,1,0:T(4,128)(2,1)}), bf16[16,4,4096]{2,1,0:T(4,128)(2,1)S(1)}, u32[]{:S(2)}, u32[]{:S(2)}) %all-to-all-start.5) | async-done | bytes 524320 | tf_op jit(solution)/shard_map/all_to_all | solution.py:23
  258.6 5.6 %fusion.4 = bf16[1,512,4096]{2,1,0:T(8,128)(2,1)} fusion(bf16[512,4096]{1,0:T(8,128)(2,1)} %all-gather.5.cloned.1.call-done, bf16[32,4096]{1,0:T(8,128)(2,1)S(1)} %reshape.371, pred[512]{0:T(512)(128)(4,1)S(1)} %compare_reduce_fusion, s32[32]{0:T(128)S(1)} %fusion.76), kind=kOutput, calls=%fused_computation.12 | convolution fusion | flops 138428416 | bytes 8651392 | tf_op jit(solution)/shard_map/dot_general | solution.py:221
  (129 shorter events, 32.9 us)
Async XLA Ops:
  7.2 0.7 copy-start
  7.2 4.0 %copy-start.7 = (f32[1,4096]{1,0:T(1,128)S(1)}, f32[1,4096]{1,0:T(1,128)}, u32[]{:S(2)}) copy-start(f32[1,4096]{1,0:T(1,128)} %param.12) | copy-start | bytes 49156
  7.2 4.0 %copy-start.3 = (bf16[1,4096,256]{2,1,0:T(8,128)(2,1)S(1)}, bf16[1,4096,256]{2,1,0:T(8,128)(2,1)}, u32[]{:S(2)}) copy-start(bf16[1,4096,256]{2,1,0:T(8,128)(2,1)} %param.11) | copy-start | bytes 6291460
  11.0 19.3 %copy-start.14 = (f32[32]{0:T(128)}, f32[32]{0:T(128)S(1)}, u32[]{:S(2)}) copy-start(f32[32]{0:T(128)S(1)} %add_rsqrt_fusion.3) | copy-start | bytes 388
  12.3 15.1 %all-to-all-start = ((bf16[16,32,256]{2,1,0:T(8,128)(2,1)}), bf16[16,32,256]{2,1,0:T(8,128)(2,1)S(1)}, u32[]{:S(2)}, u32[]{:S(2)}) async-start(bf16[16,32,256]{2,1,0:T(8,128)(2,1)} %broadcast_in_dim.233), calls=%async_computation | async-start | bytes 524288 | tf_op jit(solution)/shard_map/all_to_all | solution.py:23
  22.1 9.9 %collective-permute-start.1 = (bf16[1000,256]{1,0:T(8,128)(2,1)}, bf16[1000,256]{1,0:T(8,128)(2,1)}, u32[]{:S(2)}, u32[]{:S(2)}) collective-permute-start(bf16[1000,256]{1,0:T(8,128)(2,1)} %get-tuple-element.22), channel_id=1, source_target_pairs={{0,1},{1,0},{2,3},{3,2},{4,5},{5,4},{6,7},{7,6},{8,9},{9,8},{10,11... | collective-permute-start | bytes 1536008 | tf_op jit(solution)/shard_map/ppermute | solution.py:27
  23.0 11.7 %copy-start.13 = (pred[1024]{0:T(1024)(128)(4,1)}, pred[1024]{0:T(1024)(128)(4,1)S(1)}, u32[]{:S(2)}) copy-start(pred[1024]{0:T(1024)(128)(4,1)S(1)} %iota_compare_fusion.11) | copy-start | bytes 3076
  23.0 11.7 %copy-start.11 = (pred[1024]{0:T(1024)(128)(4,1)}, pred[1024]{0:T(1024)(128)(4,1)S(1)}, u32[]{:S(2)}) copy-start(pred[1024]{0:T(1024)(128)(4,1)S(1)} %get-tuple-element.45) | copy-start | bytes 3076
  23.0 11.7 %copy-start.12 = (pred[1024]{0:T(1024)(128)(4,1)}, pred[1024]{0:T(1024)(128)(4,1)S(1)}, u32[]{:S(2)}) copy-start(pred[1024]{0:T(1024)(128)(4,1)S(1)} %get-tuple-element.46) | copy-start | bytes 3076
  27.5 7.2 %copy-start.4 = (bf16[16,32,256]{2,1,0:T(8,128)(2,1)}, bf16[16,32,256]{2,1,0:T(8,128)(2,1)S(1)}, u32[]{:S(2)}) copy-start(bf16[16,32,256]{2,1,0:T(8,128)(2,1)S(1)} %all-to-all-done) | copy-start | bytes 786436
  27.5 3.4 %collective-permute-start = (bf16[512,256]{1,0:T(8,128)(2,1)S(1)}, bf16[512,256]{1,0:T(8,128)(2,1)}, u32[]{:S(2)}, u32[]{:S(2)}) collective-permute-start(bf16[512,256]{1,0:T(8,128)(2,1)S(1)} %bitcast.80), channel_id=1, source_target_pairs={{0,1},{1,0},{2,3},{3,2},{4,5},{5,4},{6,7},{7,6},{8,9},{9,8},{10,11... | collective-permute-start | bytes 786440 | tf_op jit(solution)/shard_map/ppermute | solution.py:27
  30.3 13.3 %copy-start.8 = (s32[16,32]{1,0:T(8,128)S(1)}, s32[16,32]{1,0:T(8,128)}, u32[]{:S(2)}) copy-start(s32[16,32]{1,0:T(8,128)} %param.17) | copy-start | bytes 6148
  32.0 44.1 %copy-start.1 = (s32[16]{0:T(128)S(1)}, s32[16]{0:T(128)}, u32[]{:S(2)}) copy-start(s32[16]{0:T(128)} %param.16) | copy-start | bytes 196
  32.0 45.5 %copy-start.2 = (f32[16]{0:T(128)S(1)}, f32[16]{0:T(128)}, u32[]{:S(2)}) copy-start(f32[16]{0:T(128)} %param.18) | copy-start | bytes 196
  34.7 37.5 %all-to-all-start.1 = ((bf16[8,64,1024]{2,1,0:T(8,128)(2,1)}), bf16[8,64,1024]{2,1,0:T(8,128)(2,1)}, u32[]{:S(2)}, u32[]{:S(2)}) async-start(bf16[8,64,1024]{2,1,0:T(8,128)(2,1)} %bitcast.85), calls=%async_computation.1 | async-start | bytes 2097152 | tf_op jit(solution)/shard_map/all_to_all | solution.py:101
  42.9 55.0 %collective-permute-start.5 = (bf16[4096,256]{1,0:T(8,128)(2,1)S(1)}, bf16[4096,256]{1,0:T(8,128)(2,1)}, u32[]{:S(2)}, u32[]{:S(2)}) collective-permute-start(bf16[4096,256]{1,0:T(8,128)(2,1)S(1)} %bitcast.77), channel_id=1, source_target_pairs={{0,1},{1,0},{2,3},{3,2},{4,5},{5,4},{6,7},{7,6},{8,9},{9,8},{10,11... | collective-permute-start | bytes 6291464 | tf_op jit(solution)/shard_map/ppermute | solution.py:27
  45.1 44.4 %copy-start.10 = (s32[64]{0:T(128)}, s32[64]{0:T(128)S(1)}, u32[]{:S(2)}) copy-start(s32[64]{0:T(128)S(1)} %subtract_subtract_fusion) | copy-start | bytes 772
  74.5 15.0 %copy-start.9 = (f32[64]{0:T(128)}, f32[64]{0:T(128)S(1)}, u32[]{:S(2)}) copy-start(f32[64]{0:T(128)S(1)} %get-tuple-element.19) | copy-start | bytes 772
  75.0 3.8 %collective-permute-start.2 = (f32[4,64]{1,0:T(4,128)S(1)}, f32[4,64]{1,0:T(4,128)S(1)}, u32[]{:S(2)}, u32[]{:S(2)}) collective-permute-start(f32[4,64]{1,0:T(4,128)S(1)} %pad_maximum_fusion.3), channel_id=1, source_target_pairs={{0,1},{1,0},{2,3},{3,2},{4,5},{5,4},{6,7},{7,6},{8,9},{9,8},{10,11... | collective-permute-start | bytes 3080 | tf_op jit(solution)/shard_map/ppermute | solution.py:27
  79.5 9.9 %all-to-all-start.2 = ((f32[16,1,512]{2,1,0:T(1,128)}), f32[16,1,512]{2,1,0:T(1,128)S(1)}, u32[]{:S(2)}, u32[]{:S(2)}) async-start(f32[16,1,512]{2,1,0:T(1,128)} %reshape.398), calls=%async_computation.2 | async-start | bytes 65536 | tf_op jit(solution)/shard_map/all_to_all | solution.py:23
  83.1 39.2 %all-gather.3.cloned.1.call-start = ((), (), s32[]{:S(2)}) async-start(), calls=%async_computation.7 | async-start | bytes 1179648 | tf_op jit(solution)/shard_map/all_gather | solution.py:132
  95.3 89.0 %reduce-scatter.2.cloned.1.call-start = ((), (), s32[]{:S(2)}) async-start(), calls=%async_computation.8 | async-start | bytes 4718592 | tf_op jit(solution)/shard_map/reduce_scatter | solution.py:176
  102.4 156.2 %all-gather.5.cloned.1.call-start = ((), (), s32[]{:S(2)}) async-start(), calls=%async_computation.9 | async-start | bytes 4456448 | tf_op jit(solution)/shard_map/all_gather | solution.py:191
  122.2 67.4 %collective-permute-start.3 = (bf16[512,1024]{1,0:T(8,128)(2,1)}, bf16[512,1024]{1,0:T(8,128)(2,1)}, u32[]{:S(2)}, u32[]{:S(2)}) collective-permute-start(bf16[512,1024]{1,0:T(8,128)(2,1)} %all-gather.3.cloned.1.call-done), channel_id=1, source_target_pairs={{0,1},{1,0},{2,3},{3,2},{4,5},{5,4},{6,7},{7,6},{8,9},{9,8},{10,11... | collective-permute-start | bytes 3145736 | tf_op jit(solution)/shard_map/ppermute | solution.py:27
  189.6 12.3 %copy-start.15 = (f32[32]{0:T(128)S(1)}, f32[32]{0:T(128)}, u32[]{:S(2)}) copy-start(f32[32]{0:T(128)} %copy-done.14) | copy-start | bytes 388
  192.2 17.1 %all-to-all-start.3 = ((f32[16,32,256]{2,1,0:T(8,128)}), f32[16,32,256]{2,1,0:T(8,128)}, u32[]{:S(2)}, u32[]{:S(2)}) async-start(f32[16,32,256]{2,1,0:T(8,128)} %bitcast.18), calls=%async_computation.3 | async-start | bytes 1048576 | tf_op jit(solution)/shard_map/all_to_all | solution.py:146
  201.8 20.0 %copy-start.5 = (bf16[16,32,256]{2,1,0:T(8,128)(2,1)S(1)}, bf16[16,32,256]{2,1,0:T(8,128)(2,1)}, u32[]{:S(2)}) copy-start(bf16[16,32,256]{2,1,0:T(8,128)(2,1)} %copy-done.4) | copy-start | bytes 786436
  211.5 3.0 %collective-permute-start.4 = (f32[16,256]{1,0:T(8,128)S(1)}, f32[16,256]{1,0:T(8,128)S(1)}, u32[]{:S(2)}, u32[]{:S(2)}) collective-permute-start(f32[16,256]{1,0:T(8,128)S(1)} %constant_dynamic-slice_fusion.1), channel_id=1, source_target_pairs={{0,1},{1,0},{2,3},{3,2},{4,5},{5,4},{6,7},{7,6},{8,9},{9,8},{10,11... | collective-permute-start | bytes 49160 | tf_op jit(solution)/shard_map/ppermute | solution.py:27
  214.3 7.6 %copy-start.6 = (bf16[512,1024]{1,0:T(8,128)(2,1)S(1)}, bf16[512,1024]{1,0:T(8,128)(2,1)}, u32[]{:S(2)}) copy-start(bf16[512,1024]{1,0:T(8,128)(2,1)} %all-gather.3.cloned.1.call-done) | copy-start | bytes 3145732
  216.9 17.7 %copy-start.16 = (f32[2]{0:T(128)S(1)}, f32[2]{0:T(128)}, u32[]{:S(2)}) copy-start(f32[2]{0:T(128)} %dynamic-slice.14) | copy-start | bytes 28
  217.8 16.5 %all-to-all-start.4 = ((f32[8,2,4608]{2,1,0:T(2,128)}), f32[8,2,4608]{2,1,0:T(2,128)S(1)}, u32[]{:S(2)}, u32[]{:S(2)}) async-start(f32[8,2,4608]{2,1,0:T(2,128)} %reshape.367), calls=%async_computation.4 | async-start | bytes 589824 | tf_op jit(solution)/shard_map/all_to_all | solution.py:206
  235.8 21.4 %all-to-all-start.5 = ((bf16[16,4,4096]{2,1,0:T(4,128)(2,1)}), bf16[16,4,4096]{2,1,0:T(4,128)(2,1)S(1)}, u32[]{:S(2)}, u32[]{:S(2)}) async-start(bf16[16,4,4096]{2,1,0:T(4,128)(2,1)} %broadcast_in_dim.255), calls=%async_computation.6 | async-start | bytes 1048576 | tf_op jit(solution)/shard_map/all_to_all | solution.py:23
Sparse Core Ops, SparseCore 0:
  95.4 26.7 all-gather.2
  125.3 58.9 reduce-scatter.1
  188.0 43.9 all-gather.4

commit v2 on v1

--- a/solution.py
+++ b/solution.py
@@ -83,6 +83,47 @@
     hidden = (row_block + row_update).astype(BF16)
 
     all_mine = spread(hidden, "pipe", pipes).reshape(rows_all, slab)
+
+    inputs = seg.astype(F32)
+    inv_rms = lax.rsqrt(jnp.mean(inputs * inputs, axis=-1, keepdims=True) + EPSILON)
+    normed = (inputs * inv_rms * gain).astype(BF16)
+    is_exit = jnp.any(pick > 0, axis=0)
+    held = tokens // (zs * 2)
+
+    def of_core(values):
+        grouped = values.reshape((zs, 2, held) + values.shape[1:])
+        return lax.dynamic_index_in_dim(grouped, core, 1, keepdims=False)
+
+    grad_core = of_core(grad).reshape(zs * held, width)
+    other_block = (z * 2 + 1 - core) * slab
+    on_columns = (((1,), (1,)), ((), ()))
+    main_part = lax.dot_general(
+        lax.dynamic_slice_in_dim(grad_core, block * slab, slab, 1), weight, on_columns, preferred_element_type=F32
+    ) + lax.dot_general(
+        lax.dynamic_slice_in_dim(grad_core, other_block, slab, 1),
+        weight_other,
+        on_columns,
+        preferred_element_type=F32,
+    )
+    all_mine, main_part = lax.optimization_barrier((all_mine, main_part))
+    main_grad = lax.psum_scatter(main_part, "z", scatter_dimension=0, tiled=True)
+    first = block * held
+    held_in = lax.dynamic_slice_in_dim(seg, first, held, 0).astype(F32)
+    held_grad = lax.dynamic_slice_in_dim(grad, first, held, 0).astype(F32)
+    held_exit = lax.dynamic_slice_in_dim(is_exit, first, held, 0)
+
+    def layer_back(norm_grad, unit, inv, residual):
+        unit_grad = norm_grad * gain
+        centre = jnp.mean(unit_grad * unit, axis=-1, keepdims=True)
+        return (residual + (unit_grad - unit * centre) * inv).astype(BF16)
+
+    held_inv = lax.rsqrt(jnp.mean(held_in * held_in, axis=-1, keepdims=True) + EPSILON)
+    held_unit = held_in * held_inv
+    main_out = layer_back(main_grad, held_unit, held_inv, held_grad)
+    gain_part = jnp.sum(jnp.where(held_exit[:, None], 0.0, main_grad * held_unit), axis=0)
+    main_all = lax.all_gather(main_out, ("z", "core"), axis=0, tiled=True)
+
+
     all_other = swap(all_mine)
     gain_mine = lax.dynamic_slice_in_dim(final_gain, block * slab, slab, 0)
     gain_other = lax.dynamic_slice_in_dim(final_gain, (z * 2 + 1 - core) * slab, slab, 0)
@@ -104,10 +145,14 @@
     logits = sums * own_inv
 
     live_column = column < half
-    index = z * own + jnp.arange(own, dtype=jnp.int32)
-    section = index // exits
-    target = exit_targets.reshape(-1)[index] - pipe * vocab_part - core * half
-    row_weight = jnp.where(index % exits < exit_count[section], exit_scale[section], F32(0.0))[:, None]
+    sections = own // exits
+    owned = z * sections
+    slot = jnp.arange(exits, dtype=jnp.int32)[None, :]
+    counts = lax.dynamic_slice_in_dim(exit_count, owned, sections, 0)[:, None]
+    scales = lax.dynamic_slice_in_dim(exit_scale, owned, sections, 0)[:, None]
+    row_weight = jnp.where(slot < counts, scales, F32(0.0)).reshape(own)
+    all_targets = exit_targets.reshape(rows_all)
+    target = lax.dynamic_slice_in_dim(all_targets, z * own, own, 0) - pipe * vocab_part - core * half
     hit = (column == target[:, None]) & live_column
     top = jnp.max(jnp.where(live_column, logits, -jnp.inf), axis=-1)
     shifted = jnp.where(live_column, logits - top[:, None], -jnp.inf)
@@ -115,29 +160,41 @@
     total = jnp.sum(expo, axis=-1)
     along = jnp.sum(jnp.where(live_column, expo * shifted, 0.0), axis=-1)
     at_target = jnp.sum(jnp.where(hit, logits, 0.0), axis=-1)
+    ex_mine = spread(expo.astype(BF16), "z", zs).reshape(rows_all, padded)
+    ex_other = swap(ex_mine)
     mine4 = jnp.stack([top, total, along, at_target])
-    stats = jnp.concatenate([mine4, swap(mine4)])
-    stats = spread(stats, "pipe", pipes).reshape(pipes * 2, 4, own)
+    other4 = swap(mine4)
+    stats = spread(jnp.concatenate([mine4, other4]), "pipe", pipes).reshape(pipes * 2, 4, own)
     tops, totals, alongs, targets = [stats[:, i] for i in range(4)]
     row_top = jnp.max(tops, axis=0)
     lower = jnp.exp(tops - row_top)
     row_total = jnp.sum(totals * lower, axis=0)
     row_along = jnp.sum((alongs + (tops - row_top) * totals) * lower, axis=0) / row_total
     row_target = jnp.sum(targets, axis=0) - row_top
-    back_mean = row_weight[:, 0] * (row_along - row_target) / width
-    probs = jnp.exp(logits - row_top[:, None]) / row_total[:, None]
-    dlogits = row_weight * (probs - hit.astype(F32))
-    for spot, piece in enumerate(split3(own_inv[:, 0]) + split3(back_mean)):
-        dlogits = jnp.where(column == half + spot, piece[:, None], dlogits)
-    dl_mine = lax.all_gather(dlogits.astype(BF16), "z", axis=0, tiled=True)
-    dl_other = swap(dl_mine)
+    back_mean = row_weight * (row_along - row_target) / width
+    known = jnp.stack(
+        [
+            row_weight * (jnp.exp(top - row_top) / row_total),
+            row_weight * (jnp.exp(other4[0] - row_top) / row_total),
+            row_weight * (jnp.exp(row_target) / row_total - 1.0),
+            back_mean,
+            own_inv[:, 0],
+        ]
+    )
+    known = spread(known, "z", zs).transpose(1, 0, 2).reshape(5, rows_all, 1)
+    factor_mine, factor_other, target_grad, exit_mean, exit_inv = [known[i] for i in range(5)]
+
+    def logit_grad(expo, factor, which):
+        spot = all_targets[:, None] - pipe * vocab_part - which * half
+        return jnp.where((column == spot) & live_column, target_grad, expo.astype(F32) * factor).astype(BF16)
+
+    ex_mine, main_out = lax.optimization_barrier((ex_mine, main_out))
+    dl_mine = logit_grad(ex_mine, factor_mine, core)
+    dl_other = logit_grad(ex_other, factor_other, 1 - core)
 
     exit_part = jnp.dot(dl_mine, head_mine, preferred_element_type=F32) + jnp.dot(
         dl_other, head_rest, preferred_element_type=F32
     )
-    extra = dl_mine[:, half : half + 6].astype(F32)
-    exit_inv = jnp.sum(extra[:, :3], axis=-1, keepdims=True)
-    exit_mean = jnp.sum(extra[:, 3:], axis=-1, keepdims=True)
     exit_normed = (mine32 * exit_inv * gain_mine).astype(BF16)
     over_rows = (((0,), (0,)), ((), ()))
     head_a = lax.dot_general(dl_mine, exit_normed, over_rows, preferred_element_type=F32).astype(BF16)[:half]
@@ -152,44 +209,6 @@
     row_grad = jnp.dot(pick, grad_slab, preferred_element_type=F32) + exit_back
     row_rounded = row_grad.astype(BF16)
 
-    inputs = seg.astype(F32)
-    inv_rms = lax.rsqrt(jnp.mean(inputs * inputs, axis=-1, keepdims=True) + EPSILON)
-    normed = (inputs * inv_rms * gain).astype(BF16)
-    is_exit = jnp.any(pick > 0, axis=0)
-    held = tokens // (zs * 2)
-
-    def of_core(values):
-        grouped = values.reshape((zs, 2, held) + values.shape[1:])
-        return lax.dynamic_index_in_dim(grouped, core, 1, keepdims=False)
-
-    grad_core = of_core(grad).reshape(zs * held, width)
-    other_block = (z * 2 + 1 - core) * slab
-    on_columns = (((1,), (1,)), ((), ()))
-    main_part = lax.dot_general(
-        lax.dynamic_slice_in_dim(grad_core, block * slab, slab, 1), weight, on_columns, preferred_element_type=F32
-    ) + lax.dot_general(
-        lax.dynamic_slice_in_dim(grad_core, other_block, slab, 1),
-        weight_other,
-        on_columns,
-        preferred_element_type=F32,
-    )
-    main_grad = lax.psum_scatter(main_part, "z", scatter_dimension=0, tiled=True)
-    first = block * held
-    held_in = lax.dynamic_slice_in_dim(seg, first, held, 0).astype(F32)
-    held_grad = lax.dynamic_slice_in_dim(grad, first, held, 0).astype(F32)
-    held_exit = lax.dynamic_slice_in_dim(is_exit, first, held, 0)
-
-    def layer_back(norm_grad, unit, inv, residual):
-        unit_grad = norm_grad * gain
-        centre = jnp.mean(unit_grad * unit, axis=-1, keepdims=True)
-        return (residual + (unit_grad - unit * centre) * inv).astype(BF16)
-
-    held_inv = lax.rsqrt(jnp.mean(held_in * held_in, axis=-1, keepdims=True) + EPSILON)
-    held_unit = held_in * held_inv
-    main_out = layer_back(main_grad, held_unit, held_inv, held_grad)
-    gain_part = jnp.sum(jnp.where(held_exit[:, None], 0.0, main_grad * held_unit), axis=0)
-    main_all = lax.all_gather(main_out, ("z", "core"), axis=0, tiled=True)
-
     put = pick.T
     slab_rounded = jnp.where(
         is_exit[:, None], jnp.dot(put, row_rounded, preferred_element_type=F32).astype(BF16), grad_slab
@@ -202,21 +221,32 @@
     row_part = lax.dot_general(
         row_mine.astype(BF16), weight, on_columns, preferred_element_type=F32
     ) + lax.dot_general(row_other.astype(BF16), weight_other, on_columns, preferred_element_type=F32)
-    send = jnp.concatenate([row_part, pair(row_mine, row_other, core, 1)], axis=1)
-    got = lax.all_to_all(send.reshape(zs, share, width + 2 * slab), "z", 0, 0)
-    norm_grad = jnp.sum(got[:, :, :width], axis=0)
-    residual = got[:, :, width:].transpose(1, 0, 2).reshape(share, width)
+    core_unit = lax.dynamic_slice_in_dim(row_unit, core * core_rows, core_rows, 0)
+    gain_part = gain_part + jnp.sum(row_part * core_unit, axis=0)
+    piece = slab * 2 // share
+    send = jnp.concatenate(
+        [
+            row_part.reshape(zs, share, width),
+            pair(row_mine, row_other, core, 1).reshape(zs, share, 2 * slab),
+            gain_part.reshape(zs, share, piece),
+        ],
+        axis=2,
+    )
+    got = lax.all_to_all(send, "z", 0, 0)
+    summed = jnp.sum(got, axis=0)
+    norm_grad = summed[:, :width]
+    residual = got[:, :, width : width + 2 * slab].transpose(1, 0, 2).reshape(share, width)
     at = core * core_rows + z * share
     share_unit = lax.dynamic_slice_in_dim(row_unit, at, share, 0)
     share_inv = lax.dynamic_slice_in_dim(row_inv, at, share, 0)
     share_out = layer_back(norm_grad, share_unit, share_inv, residual)
-    gain_part = gain_part + jnp.sum(norm_grad * share_unit, axis=0)
-    gain_first = rounded(gain_part)
-    gain_rest = gain_part - gain_first
-    last = jnp.concatenate([share_out, gain_first.astype(BF16)[None], gain_rest.astype(BF16)[None]])
-    last = spread(last, ("z", "core"), zs * 2)
-    gain_grad = jnp.sum(last[:, share:].astype(F32), axis=(0, 1))
-    row_out = last[:, :share].reshape(zs, 2, share, width).transpose(1, 0, 2, 3).reshape(exits, width)
+    gains = [values.astype(BF16) for values in split3(summed[:, width + 2 * slab :])]
+    last = spread(jnp.concatenate([share_out] + gains, axis=1), "z", zs)
+    last_other = swap(last)
+    gain_grad = jnp.sum(
+        (last[:, :, width:].astype(F32) + last_other[:, :, width:].astype(F32)).reshape(zs, share, 3, piece), axis=2
+    ).reshape(width)
+    row_out = pair(last, last_other, core, 0)[:, :, :width].reshape(exits, width)
     input_grad = jnp.where(
         is_exit[:, None], jnp.dot(put, row_out, preferred_element_type=F32).astype(BF16), main_all
     )

time: 272 us -> 248 us (0.912)
  waiting for transfers between devices: 138 us -> 95.6 us
  blocking collectives: 0 us -> 10.5 us
  local copies, waits for them, and re-layouts: 16.2 us -> 21.8 us
  other arithmetic: 21.9 us -> 25 us
    reduce_scatter x1, waiting for transfers between devices: 56.3 us -> 0.01 us  [local(): lax.psum_scatter(main_part, 'z', scatter_dimension=0, tiled=True)]
    all_gather x1 -> x0, waiting for transfers between devices: 18.5 us -> none  [local(): dl_mine = lax.all_gather(dlogits.astype(BF16), 'z', axis=0, tiled=True)]
    all_to_all x3 -> x4, waiting for transfers between devices: 20.1 us -> 37.5 us  [spread(): lax.all_to_all(jnp.broadcast_to(values[None], (count,) + values.shape), a...]
    all_to_all x1, waiting for transfers between devices: 27.2 us -> 39.5 us  [local(): lax.all_to_all(part.astype(BF16).reshape(zs, own, padded), 'z', 0, 0)]
    all_to_all x0 -> x1, blocking collectives: none -> 10.5 us  [spread(): lax.all_to_all(jnp.broadcast_to(values[None], (count,) + values.shape), a...]
    gather x3 -> x0, local copies, waits for them, and re-layouts: 3.45 us -> none  [the longest x1 1.36 us: local(): exit_count[section]]
    unnamed x37 -> x58, local copies, waits for them, and re-layouts: 1.63 us -> 5.04 us
    all_to_all x1, starting transfers between devices: 6.59 us -> 3.75 us  [local(): lax.all_to_all(exit_part.reshape(pipes, exits, slab), 'pipe', 0, 0)]
  transfers between devices with their start and end apart: 15 -> 16, of which waited for: 10 -> 9; matrix products, arithmetic and copies ran while one was open for 22% -> 30% of each run, Pallas kernels for 0% -> 0%
where the time goes in v2:
time: 248 us; the launch traced here: 246 us
  waiting for transfers between devices  95.6 us (39%)
  starting transfers between devices  46.1 us (19%)
  matrix products  32.3 us (13%)
  other arithmetic  25 us (10%)
  local copies, waits for them, and re-layouts  21.8 us (9%)
  between operations  14.7 us (6%)
  blocking collectives  10.5 us (4%)
    all_to_all x1, waiting for transfers between devices, local(): lax.all_to_all(part.astype(BF16).reshape(zs, own, padded), 'z', 0, 0)  39.5 us
    all_to_all x4, waiting for transfers between devices, spread(): lax.all_to_all(jnp.broadcast_to(values[None], (count,) + values.shape), a...  37.5 us
    all_to_all x4, starting transfers between devices, spread(): lax.all_to_all(jnp.broadcast_to(values[None], (count,) + values.shape), a...  17.8 us
    ppermute x7, starting transfers between devices, swap(): return lax.ppermute(values, 'core', [(0, 1), (1, 0)])  12.7 us
    all_to_all x1, blocking collectives, spread(): lax.all_to_all(jnp.broadcast_to(values[None], (count,) + values.shape), a...  10.5 us
    all_to_all x1, waiting for transfers between devices, local(): got = lax.all_to_all(send, 'z', 0, 0)  9.71 us
    all_to_all x1, starting transfers between devices, local(): lax.all_to_all(part.astype(BF16).reshape(zs, own, padded), 'z', 0, 0)  8.32 us
    all_to_all x1, waiting for transfers between devices, local(): lax.all_to_all(exit_part.reshape(pipes, exits, slab), 'pipe', 0, 0)  7.7 us
  transfers between devices with their start and end apart: 16, of which 9 were waited for; matrix products, arithmetic and copies ran while one was open for 30% of the time, Pallas kernels for 0%

profile of v2, /device:TPU:1, one launch (start us, length us, event | category | flops | bytes accessed | tf_op | source)
XLA Modules:
  0.0 245.9 jit_solution(15304313211204495754)
XLA Ops:
  7.2 3.3 %collective-permute-start = (bf16[4096,256]{1,0:T(8,128)(2,1)}, bf16[4096,256]{1,0:T(8,128)(2,1)}, u32[]{:S(2)}, u32[]{:S(2)}) collective-permute-start(bf16[4096,256]{1,0:T(8,128)(2,1)} %bitcast.119), channel_id=1, source_target_pairs={{0,1},{1,0},{2,3},{3,2},{4,5},{5,4},{6,7},{7,6},{8,9},{9,8},{10,11... | collective-permute-start | bytes 6291464 | tf_op jit(solution)/shard_map/ppermute | solution.py:27
  10.5 3.3 %multiply_reduce_fusion = (f32[32]{0:T(128)S(1)}, f32[32,4096]{1,0:T(8,128)S(1)}) fusion(bf16[1,512,4096]{2,1,0:T(8,128)(2,1)} %param.10, s32[32]{0:T(128)S(1)} %fusion.76), kind=kOutput, calls=%fused_computation.62 | convolution fusion | flops 134496224 | bytes 4718848 | tf_op jit(solution)/shard_map/dot_general | solution.py:77
  15.6 5.0 %all-to-all-start = ((bf16[16,32,256]{2,1,0:T(8,128)(2,1)}), bf16[16,32,256]{2,1,0:T(8,128)(2,1)S(1)}, u32[]{:S(2)}, u32[]{:S(2)}) async-start(bf16[16,32,256]{2,1,0:T(8,128)(2,1)} %broadcast_in_dim.184), calls=%async_computation | async-start | bytes 524288 | tf_op jit(solution)/shard_map/all_to_all | solution.py:23
  20.7 1.8 constant_dynamic-slice_fusion.5
  23.2 4.4 %convolution_add_fusion = f32[256,4096]{1,0:T(8,128)} fusion(f32[256,4096]{1,0:T(8,128)S(1)} %fusion.54, bf16[4096,256]{1,0:T(8,128)(2,1)} %collective-permute-done, bf16[256,4096]{1,0:T(8,128)(2,1)S(1)} %bitcast.121, s32[]{:T(128)S(6)} %select_n.167), kind=kOutput, calls=%fused_computation.6 | convolution fusion | flops 537919488 | bytes 10616836 | tf_op jit(solution)/shard_map/dot_general | solution.py:102
  29.8 1.9 collective-permute-start.2
  34.2 1.6 select_convert_fusion.2
  35.8 8.3 %all-to-all-start.1 = ((bf16[8,64,1024]{2,1,0:T(8,128)(2,1)}), bf16[8,64,1024]{2,1,0:T(8,128)(2,1)}, u32[]{:S(2)}, u32[]{:S(2)}) async-start(bf16[8,64,1024]{2,1,0:T(8,128)(2,1)} %bitcast.128), calls=%async_computation.1 | async-start | bytes 2097152 | tf_op jit(solution)/shard_map/all_to_all | solution.py:142
  44.8 39.5 %all-to-all-done.1 = bf16[8,64,1024]{2,1,0:T(8,128)(2,1)} async-done(((bf16[8,64,1024]{2,1,0:T(8,128)(2,1)}), bf16[8,64,1024]{2,1,0:T(8,128)(2,1)}, u32[]{:S(2)}, u32[]{:S(2)}) %all-to-all-start.1) | async-done | bytes 1048608 | tf_op jit(solution)/shard_map/all_to_all | solution.py:142
  95.0 5.0 %all-to-all-start.2 = ((f32[16,1,512]{2,1,0:T(1,128)}), f32[16,1,512]{2,1,0:T(1,128)}, u32[]{:S(2)}, u32[]{:S(2)}) async-start(f32[16,1,512]{2,1,0:T(1,128)} %reshape.443), calls=%async_computation.2 | async-start | bytes 65536 | tf_op jit(solution)/shard_map/all_to_all | solution.py:23
  101.4 5.2 %all-to-all-done.2 = f32[16,1,512]{2,1,0:T(1,128)} async-done(((f32[16,1,512]{2,1,0:T(1,128)}), f32[16,1,512]{2,1,0:T(1,128)}, u32[]{:S(2)}, u32[]{:S(2)}) %all-to-all-start.2) | async-done | bytes 32800 | tf_op jit(solution)/shard_map/all_to_all | solution.py:23
  107.1 2.1 reduce.24
  110.7 1.7 fusion.92
  119.2 10.5 %all_to_all.40 = f32[8,1,320]{2,1,0:T(1,128)} all-to-all(f32[8,1,320]{2,1,0:T(1,128)} %reshape.445), channel_id=1, replica_groups=mesh['pipe'=16,'z'=8,'core'=2] {'z'}, dimensions={0} | all-to-all | bytes 20480 | tf_op jit(solution)/shard_map/all_to_all | solution.py:23
  130.8 4.4 %all-to-all-start.4 = ((bf16[8,64,1024]{2,1,0:T(8,128)(2,1)}), bf16[8,64,1024]{2,1,0:T(8,128)(2,1)}, u32[]{:S(2)}, u32[]{:S(2)}) async-start(bf16[8,64,1024]{2,1,0:T(8,128)(2,1)} %broadcast_in_dim.196), calls=%async_computation.4 | async-start | bytes 2097152 | tf_op jit(solution)/shard_map/all_to_all | solution.py:23
  137.7 24.8 %all-to-all-done.4 = bf16[8,64,1024]{2,1,0:T(8,128)(2,1)} async-done(((bf16[8,64,1024]{2,1,0:T(8,128)(2,1)}), bf16[8,64,1024]{2,1,0:T(8,128)(2,1)}, u32[]{:S(2)}, u32[]{:S(2)}) %all-to-all-start.4) | async-done | bytes 1048608 | tf_op jit(solution)/shard_map/all_to_all | solution.py:23
  162.5 2.3 collective-permute-start.4
  166.3 2.1 fusion.26
  168.5 1.9 select_convert_fusion.1
  170.9 2.8 %convolution_add_fusion.2 = f32[512,256]{1,0:T(8,128)} fusion(f32[512,256]{1,0:T(8,128)S(1)} %fusion.36, bf16[1000,256]{1,0:T(8,128)(2,1)S(1)} %copy-done.5, bf16[512,1024]{1,0:T(8,128)(2,1)} %collective-permute-done.4, f32[512]{0:T(512)S(1)} %mul.347, s32[512]{0:T(512)S(1)} %get-tuple-element.44, bf16[512]{0:T(512)(128)(2,1)S(1)} %broadcast_in_dim.194, ...), kind=kOutput, calls=%fused_computation.25 | convolution fusion | flops 271187968 | bytes 2615296 | tf_op jit(solution)/shard_map/dot_general | solution.py:195
  173.7 3.8 %all-to-all-start.5 = ((f32[16,32,256]{2,1,0:T(8,128)}), f32[16,32,256]{2,1,0:T(8,128)S(1)}, u32[]{:S(2)}, u32[]{:S(2)}) async-start(f32[16,32,256]{2,1,0:T(8,128)} %bitcast.129), calls=%async_computation.6 | async-start | bytes 1048576 | tf_op jit(solution)/shard_map/all_to_all | solution.py:203
  177.5 3.2 %fusion = f32[512]{0:T(512)S(1)} fusion(bf16[1,512,4096]{2,1,0:T(8,128)(2,1)} %param.10), kind=kLoop, calls=%fused_computation.2 | loop fusion | flops 6290944 | bytes 4196352 | tf_op jit(solution)/shard_map/reduce_sum | solution.py:88
  181.1 7.7 %all-to-all-done.5 = f32[16,32,256]{2,1,0:T(8,128)S(1)} async-done(((f32[16,32,256]{2,1,0:T(8,128)}), f32[16,32,256]{2,1,0:T(8,128)S(1)}, u32[]{:S(2)}, u32[]{:S(2)}) %all-to-all-start.5) | async-done | bytes 524320 | tf_op jit(solution)/shard_map/all_to_all | solution.py:203
  192.1 2.3 multiply_reduce_fusion.1
  195.5 3.4 %all-to-all-start.6 = ((f32[8,2,4864]{2,1,0:T(2,128)}), f32[8,2,4864]{2,1,0:T(2,128)S(1)}, u32[]{:S(2)}, u32[]{:S(2)}) async-start(f32[8,2,4864]{2,1,0:T(2,128)} %pad_maximum_fusion.1), calls=%async_computation.7 | async-start | bytes 622592 | tf_op jit(solution)/shard_map/all_to_all | solution.py:235
  198.9 2.3 fusion.56
  201.8 9.7 %all-to-all-done.6 = f32[8,2,4864]{2,1,0:T(2,128)S(1)} async-done(((f32[8,2,4864]{2,1,0:T(2,128)}), f32[8,2,4864]{2,1,0:T(2,128)S(1)}, u32[]{:S(2)}, u32[]{:S(2)}) %all-to-all-start.6) | async-done | bytes 311328 | tf_op jit(solution)/shard_map/all_to_all | solution.py:235
  212.7 3.4 %all-to-all-start.7 = ((bf16[8,2,4864]{2,1,0:T(2,128)(2,1)}), bf16[8,2,4864]{2,1,0:T(2,128)(2,1)S(1)}, u32[]{:S(2)}, u32[]{:S(2)}) async-start(bf16[8,2,4864]{2,1,0:T(2,128)(2,1)} %broadcast_in_dim.199), calls=%async_computation.8 | async-start | bytes 311296 | tf_op jit(solution)/shard_map/all_to_all | solution.py:23
  217.2 6.8 %all-to-all-done.7 = bf16[8,2,4864]{2,1,0:T(2,128)(2,1)S(1)} async-done(((bf16[8,2,4864]{2,1,0:T(2,128)(2,1)}), bf16[8,2,4864]{2,1,0:T(2,128)(2,1)S(1)}, u32[]{:S(2)}, u32[]{:S(2)}) %all-to-all-start.7) | async-done | bytes 155680 | tf_op jit(solution)/shard_map/all_to_all | solution.py:23
  224.0 2.7 %collective-permute-start.6 = (bf16[8,2,4864]{2,0,1:T(8,128)(2,1)S(1)}, bf16[8,2,4864]{2,0,1:T(8,128)(2,1)S(1)}, u32[]{:S(2)}, u32[]{:S(2)}) collective-permute-start(bf16[8,2,4864]{2,0,1:T(8,128)(2,1)S(1)} %copy.50), channel_id=1, source_target_pairs={{0,1},{1,0},{2,3},{3,2},{4,5},{5,4},{6,7},{7,6},{8,9},{9,8},{10,11... | collective-permute-start | bytes 466952 | tf_op jit(solution)/shard_map/ppermute | solution.py:27
  226.7 5.5 %fusion.5 = bf16[1,4096,256]{2,1,0:T(8,128)(2,1)} fusion(bf16[1,512,4096]{2,1,0:T(8,128)(2,1)} %param.10, f32[4096]{0:T(1024)S(1)} %bitcast.135, f32[512]{0:T(512)S(1)} %add_rsqrt_fusion, pred[512]{0:T(512)(128)(4,1)S(1)} %copy-done.26, bf16[1,512,4096]{2,1,0:T(8,128)(2,1)} %param.19, s32[]{:T(128)S(6)} %select_n.162, s32[32]{0:T(128)S(1)} %copy-done.19, ...), kind=kOutput, calls=%fused_computation.10 | convolution fusion | flops 1091854336 | bytes 6605444 | tf_op jit(solution)/shard_map/dot_general | solution.py:216
  233.5 5.6 %fusion.4 = bf16[1,512,4096]{2,1,0:T(8,128)(2,1)} fusion(bf16[512,4096]{1,0:T(8,128)(2,1)} %all-gather.2.cloned.1.call-done, bf16[32,4096]{1,0:T(8,128)(2,1)S(1)} %reshape.409, pred[512]{0:T(512)(128)(4,1)S(1)} %copy-done.26, s32[32]{0:T(128)S(1)} %copy-done.19), kind=kOutput, calls=%fused_computation.9 | convolution fusion | flops 138428416 | bytes 8651392 | tf_op jit(solution)/shard_map/dot_general | solution.py:251
  (164 shorter events, 42.9 us)
Async XLA Ops:
  7.2 3.3 %copy-start = (s32[16,32]{1,0:T(8,128)S(1)}, s32[16,32]{1,0:T(8,128)}, u32[]{:S(2)}) copy-start(s32[16,32]{1,0:T(8,128)} %param.15) | copy-start | bytes 6148
  7.2 16.1 %collective-permute-start = (bf16[4096,256]{1,0:T(8,128)(2,1)}, bf16[4096,256]{1,0:T(8,128)(2,1)}, u32[]{:S(2)}, u32[]{:S(2)}) collective-permute-start(bf16[4096,256]{1,0:T(8,128)(2,1)} %bitcast.119), channel_id=1, source_target_pairs={{0,1},{1,0},{2,3},{3,2},{4,5},{5,4},{6,7},{7,6},{8,9},{9,8},{10,11... | collective-permute-start | bytes 6291464 | tf_op jit(solution)/shard_map/ppermute | solution.py:27
  10.5 3.3 %copy-start.18 = (s32[32]{0:T(128)}, s32[32]{0:T(128)S(1)}, u32[]{:S(2)}) copy-start(s32[32]{0:T(128)S(1)} %fusion.76) | copy-start | bytes 388
  10.5 3.9 %copy-start.1 = (bf16[1,4096,256]{2,1,0:T(8,128)(2,1)S(1)}, bf16[1,4096,256]{2,1,0:T(8,128)(2,1)}, u32[]{:S(2)}) copy-start(bf16[1,4096,256]{2,1,0:T(8,128)(2,1)} %param.11) | copy-start | bytes 6291460
  10.5 3.8 %copy-start.6 = (f32[1,4096]{1,0:T(1,128)S(1)}, f32[1,4096]{1,0:T(1,128)}, u32[]{:S(2)}) copy-start(f32[1,4096]{1,0:T(1,128)} %param.12) | copy-start | bytes 49156
  14.8 7.6 %copy-start.7 = (bf16[32,256]{1,0:T(8,128)(2,1)}, bf16[32,256]{1,0:T(8,128)(2,1)S(1)}, u32[]{:S(2)}) copy-start(bf16[32,256]{1,0:T(8,128)(2,1)S(1)} %fusion.16) | copy-start | bytes 49156
  15.6 12.9 %all-to-all-start = ((bf16[16,32,256]{2,1,0:T(8,128)(2,1)}), bf16[16,32,256]{2,1,0:T(8,128)(2,1)S(1)}, u32[]{:S(2)}, u32[]{:S(2)}) async-start(bf16[16,32,256]{2,1,0:T(8,128)(2,1)} %broadcast_in_dim.184), calls=%async_computation | async-start | bytes 524288 | tf_op jit(solution)/shard_map/all_to_all | solution.py:23
  20.6 144.3 %reduce-scatter.2.cloned.1.call-start = ((), (), s32[]{:S(2)}) async-start(), calls=%async_computation.9 | async-start | bytes 4718592 | tf_op jit(solution)/shard_map/reduce_scatter | solution.py:109
  29.8 4.3 %copy-start.4 = (bf16[1000,256]{1,0:T(8,128)(2,1)}, bf16[1000,256]{1,0:T(8,128)(2,1)S(1)}, u32[]{:S(2)}) copy-start(bf16[1000,256]{1,0:T(8,128)(2,1)S(1)} %get-tuple-element.24) | copy-start | bytes 1536004
  29.8 4.4 %collective-permute-start.2 = (bf16[1000,256]{1,0:T(8,128)(2,1)S(1)}, bf16[1000,256]{1,0:T(8,128)(2,1)S(1)}, u32[]{:S(2)}, u32[]{:S(2)}) collective-permute-start(bf16[1000,256]{1,0:T(8,128)(2,1)S(1)} %get-tuple-element.24), channel_id=1, source_target_pairs={{0,1},{1,0},{2,3},{3,2},{4,5},{5,4},{6,7},{7,6},{8,9},{9,8},{10,11... | collective-permute-start | bytes 1536008 | tf_op jit(solution)/shard_map/ppermute | solution.py:27
  32.5 1.6 collective-permute-start.1
  35.8 8.3 %copy-start.17 = (s32[16,32]{1,0:T(8,128)S(1)}, s32[16,32]{1,0:T(8,128)}, u32[]{:S(2)}) copy-start(s32[16,32]{1,0:T(8,128)} %param.17) | copy-start | bytes 6148
  35.8 48.5 %all-to-all-start.1 = ((bf16[8,64,1024]{2,1,0:T(8,128)(2,1)}), bf16[8,64,1024]{2,1,0:T(8,128)(2,1)}, u32[]{:S(2)}, u32[]{:S(2)}) async-start(bf16[8,64,1024]{2,1,0:T(8,128)(2,1)} %bitcast.128), calls=%async_computation.1 | async-start | bytes 2097152 | tf_op jit(solution)/shard_map/all_to_all | solution.py:142
  44.2 42.3 %copy-start.11 = (s32[512]{0:T(512)}, s32[512]{0:T(512)S(1)}, u32[]{:S(2)}) copy-start(s32[512]{0:T(512)S(1)} %broadcast_in_dim_reshape.7) | copy-start | bytes 6148
  44.8 47.3 %copy-start.13 = (pred[1024]{0:T(1024)(128)(4,1)}, pred[1024]{0:T(1024)(128)(4,1)S(1)}, u32[]{:S(2)}) copy-start(pred[1024]{0:T(1024)(128)(4,1)S(1)} %iota_compare_fusion.12) | copy-start | bytes 3076
  88.3 3.8 %collective-permute-start.3 = (f32[4,64]{1,0:T(4,128)}, f32[4,64]{1,0:T(4,128)}, u32[]{:S(2)}, u32[]{:S(2)}) collective-permute-start(f32[4,64]{1,0:T(4,128)} %pad_maximum_fusion.5), channel_id=1, source_target_pairs={{0,1},{1,0},{2,3},{3,2},{4,5},{5,4},{6,7},{7,6},{8,9},{9,8},{10,11... | collective-permute-start | bytes 3080 | tf_op jit(solution)/shard_map/ppermute | solution.py:27
  95.0 11.6 %all-to-all-start.2 = ((f32[16,1,512]{2,1,0:T(1,128)}), f32[16,1,512]{2,1,0:T(1,128)}, u32[]{:S(2)}, u32[]{:S(2)}) async-start(f32[16,1,512]{2,1,0:T(1,128)} %reshape.443), calls=%async_computation.2 | async-start | bytes 65536 | tf_op jit(solution)/shard_map/all_to_all | solution.py:23
  117.8 18.8 %copy-start.12 = (s32[512]{0:T(512)S(1)}, s32[512]{0:T(512)}, u32[]{:S(2)}) copy-start(s32[512]{0:T(512)} %copy-done.11) | copy-start | bytes 6148
  130.8 4.4 %copy-start.19 = (s32[32]{0:T(128)S(1)}, s32[32]{0:T(128)}, u32[]{:S(2)}) copy-start(s32[32]{0:T(128)} %copy-done.18) | copy-start | bytes 388
  130.8 5.8 %copy-start.9 = (f32[8,1,320]{2,1,0:T(1,128)S(1)}, f32[8,1,320]{2,1,0:T(1,128)}, u32[]{:S(2)}) copy-start(f32[8,1,320]{2,1,0:T(1,128)} %all_to_all.40) | copy-start | bytes 30724
  130.8 37.6 %copy-start.14 = (pred[1024]{0:T(1024)(128)(4,1)S(1)}, pred[1024]{0:T(1024)(128)(4,1)}, u32[]{:S(2)}) copy-start(pred[1024]{0:T(1024)(128)(4,1)} %copy-done.13) | copy-start | bytes 3076
  130.8 31.7 %all-to-all-start.4 = ((bf16[8,64,1024]{2,1,0:T(8,128)(2,1)}), bf16[8,64,1024]{2,1,0:T(8,128)(2,1)}, u32[]{:S(2)}, u32[]{:S(2)}) async-start(bf16[8,64,1024]{2,1,0:T(8,128)(2,1)} %broadcast_in_dim.196), calls=%async_computation.4 | async-start | bytes 2097152 | tf_op jit(solution)/shard_map/all_to_all | solution.py:23
  135.2 98.2 %all-gather.2.cloned.1.call-start = ((), (), s32[]{:S(2)}) async-start(), calls=%async_computation.10 | async-start | bytes 4456448 | tf_op jit(solution)/shard_map/all_gather | solution.py:124
  162.5 8.3 %collective-permute-start.4 = (bf16[512,1024]{1,0:T(8,128)(2,1)}, bf16[512,1024]{1,0:T(8,128)(2,1)}, u32[]{:S(2)}, u32[]{:S(2)}) collective-permute-start(bf16[512,1024]{1,0:T(8,128)(2,1)} %bitcast.24), channel_id=1, source_target_pairs={{0,1},{1,0},{2,3},{3,2},{4,5},{5,4},{6,7},{7,6},{8,9},{9,8},{10,11... | collective-permute-start | bytes 3145736 | tf_op jit(solution)/shard_map/ppermute | solution.py:27
  173.7 15.1 %all-to-all-start.5 = ((f32[16,32,256]{2,1,0:T(8,128)}), f32[16,32,256]{2,1,0:T(8,128)S(1)}, u32[]{:S(2)}, u32[]{:S(2)}) async-start(f32[16,32,256]{2,1,0:T(8,128)} %bitcast.129), calls=%async_computation.6 | async-start | bytes 1048576 | tf_op jit(solution)/shard_map/all_to_all | solution.py:203
  177.5 11.4 %copy-start.8 = (bf16[32,256]{1,0:T(8,128)(2,1)S(1)}, bf16[32,256]{1,0:T(8,128)(2,1)}, u32[]{:S(2)}) copy-start(bf16[32,256]{1,0:T(8,128)(2,1)} %copy-done.7) | copy-start | bytes 49156
  177.5 11.4 %copy-start.16 = (f32[256]{0:T(256)S(1)}, f32[256]{0:T(256)}, u32[]{:S(2)}) copy-start(f32[256]{0:T(256)} %copy-done.15) | copy-start | bytes 3076
  190.1 2.0 collective-permute-start.5
  195.5 16.1 %all-to-all-start.6 = ((f32[8,2,4864]{2,1,0:T(2,128)}), f32[8,2,4864]{2,1,0:T(2,128)S(1)}, u32[]{:S(2)}, u32[]{:S(2)}) async-start(f32[8,2,4864]{2,1,0:T(2,128)} %pad_maximum_fusion.1), calls=%async_computation.7 | async-start | bytes 622592 | tf_op jit(solution)/shard_map/all_to_all | solution.py:235
  212.7 11.3 %all-to-all-start.7 = ((bf16[8,2,4864]{2,1,0:T(2,128)(2,1)}), bf16[8,2,4864]{2,1,0:T(2,128)(2,1)S(1)}, u32[]{:S(2)}, u32[]{:S(2)}) async-start(bf16[8,2,4864]{2,1,0:T(2,128)(2,1)} %broadcast_in_dim.199), calls=%async_computation.8 | async-start | bytes 311296 | tf_op jit(solution)/shard_map/all_to_all | solution.py:23
  216.1 10.6 %copy-start.26 = (pred[512]{0:T(512)(128)(4,1)S(1)}, pred[512]{0:T(512)(128)(4,1)}, u32[]{:S(2)}) copy-start(pred[512]{0:T(512)(128)(4,1)} %copy-done.25) | copy-start | bytes 1540
  224.0 8.2 %collective-permute-start.6 = (bf16[8,2,4864]{2,0,1:T(8,128)(2,1)S(1)}, bf16[8,2,4864]{2,0,1:T(8,128)(2,1)S(1)}, u32[]{:S(2)}, u32[]{:S(2)}) collective-permute-start(bf16[8,2,4864]{2,0,1:T(8,128)(2,1)S(1)} %copy.50), channel_id=1, source_target_pairs={{0,1},{1,0},{2,3},{3,2},{4,5},{5,4},{6,7},{7,6},{8,9},{9,8},{10,11... | collective-permute-start | bytes 466952 | tf_op jit(solution)/shard_map/ppermute | solution.py:27
  (11 other events, 20.0 us)
Sparse Core Ops, SparseCore 0:
  28.6 80.3 reduce-scatter.1
  168.6 35.0 all-gather.1

commit v3 on v2

v3 whole, which is shorter than its diff:
```python
import functools

import jax
import jax.numpy as jnp
from jax import lax
from jax.experimental import pallas as pl
from jax.experimental.pallas import tpu as pltpu
from jax.sharding import Mesh, PartitionSpec as P

F32 = jnp.float32
BF16 = jnp.bfloat16
EPSILON = 1e-05
VMEM = 32 * 1024 * 1024


def rounded(values):
    return lax.reduce_precision(values, 8, 7)


def split3(values):
    first = rounded(values)
    rest = values - first
    second = rounded(rest)
    return [first, second, rest - second]


def spread(values, axis, count):
    return lax.all_to_all(jnp.broadcast_to(values[None], (count,) + values.shape), axis, 0, 0)


def swap(values):
    return lax.ppermute(values, "core", [(0, 1), (1, 0)])


def from_back(piece, count):
    return [piece(0)] + [
        lax.ppermute(piece(k), "z", [(i, (i + k) % count) for i in range(count)]) for k in range(1, count)
    ]


def pair(mine, other, core, axis):
    first = jnp.where(core == 0, mine, other)
    second = jnp.where(core == 0, other, mine)
    return jnp.concatenate([first, second], axis=axis)


def kernel_call(body, out, *operands):
    return pl.pallas_call(
        body,
        out_shape=out,
        in_specs=[
            pl.BlockSpec(memory_space=pltpu.SMEM if i == 0 else pltpu.VMEM) for i in range(len(operands))
        ],
        out_specs=jax.tree.map(lambda _: pl.BlockSpec(memory_space=pltpu.VMEM), out),
        compiler_params=pltpu.CompilerParams(vmem_limit_bytes=VMEM),
    )(*operands)


def shape(dims, dtype):
    return jax.ShapeDtypeStruct(dims, dtype)


def logits_kernel(place, rows, gains, *refs):
    heads, mine, other = refs[:-2], refs[-2], refs[-1]
    z, core = place[0], place[1]
    zs = len(heads)
    total = mine.shape[0] * 2
    part = jnp.zeros((total, heads[0].shape[0]), F32)
    squares = jnp.zeros((total, 1), F32)
    for k in range(zs):
        at = lax.rem(z - k + zs, zs)
        row = rows[:, at].reshape(total, rows.shape[3]).astype(F32)
        squares += jnp.sum(row * row, axis=-1, keepdims=True)
        part += lax.dot_general(
            (row * gains[pl.ds(at, 1), :]).astype(BF16),
            heads[k][...],
            (((1,), (1,)), ((), ())),
            preferred_element_type=F32,
        )
    whole = jnp.concatenate([part, jnp.broadcast_to(squares, (total, 128))], axis=1)
    low, high = whole[: total // 2], whole[total // 2 :]
    mine[...] = jnp.where(core == 0, low, high)
    other[...] = jnp.where(core == 0, high, low)


def softmax_kernel(width, vocab, place, mine, other, targets, expo_out, stats):
    z, start = place[0], place[2]
    columns = expo_out.shape[1]
    whole = mine[...] + other[...]
    inv = lax.rsqrt(whole[:, columns : columns + 1] / width + EPSILON)
    logits = whole[:, :columns] * inv
    column = lax.broadcasted_iota(jnp.int32, logits.shape, 1) + z * columns
    live = column < vocab
    top = jnp.max(jnp.where(live, logits, -jnp.inf), axis=-1, keepdims=True)
    shifted = jnp.where(live, logits - top, -jnp.inf)
    expo = jnp.exp(shifted)
    expo_out[...] = expo.astype(BF16)
    hit = live & (column == targets[...] - start)
    values = [
        top,
        jnp.sum(expo, axis=-1, keepdims=True),
        jnp.sum(jnp.where(live, expo * shifted, 0.0), axis=-1, keepdims=True),
        jnp.sum(jnp.where(hit, logits, 0.0), axis=-1, keepdims=True),
        inv,
    ]
    lane = lax.broadcasted_iota(jnp.int32, (logits.shape[0], 128), 1)
    table = jnp.zeros(lane.shape, F32)
    for i, value in enumerate(values):
        table = jnp.where(lane == i, value, table)
    stats[...] = table.T[: stats.shape[0]]


def merged(stats):
    tops, totals, alongs, hits = [stats[:, i] for i in range(4)]
    top = jnp.max(tops, axis=0, keepdims=True)
    lower = jnp.exp(tops - top)
    total = jnp.sum(totals * lower, axis=0, keepdims=True)
    along = jnp.sum((alongs + (tops - top) * totals) * lower, axis=0, keepdims=True)
    return top, total, along, jnp.sum(hits, axis=0, keepdims=True)


def merge_kernel(place, stats, out):
    values = merged(stats[...])
    out[...] = jnp.concatenate(list(values) + [jnp.zeros((out.shape[0] - 4, out.shape[1]), F32)])


def finish_kernel(width, place, stats, pieces, weights, known):
    top, total, along, hits = merged(stats[...])
    weight = weights[...]
    own = pieces[...]
    factors = weight * (jnp.exp(own[:, 0] - top) / total)
    target = weight * (jnp.exp(hits - top) / total - 1.0)
    mean = weight * (along / total - (hits - top)) / width
    rest = known.shape[0] - own.shape[0] - 3
    known[...] = jnp.concatenate(
        [factors, target, mean, own[0, 4:5], jnp.zeros((rest, known.shape[1]), F32)]
    )


def exit_kernel(zs, vocab, place, head, known_mine, known_other, targets_mine, targets_other, *refs):
    pieces, part, dlogits = refs[:-2], refs[-2], refs[-1]
    z, core, start = place[0], place[1], place[2]
    count, columns = pieces[0].shape
    for side, known, targets in ((0, known_mine, targets_mine), (1, known_other, targets_other)):
        table = known[...].T
        lane = lax.broadcasted_iota(jnp.int32, table.shape, 1)
        target_grad = table[:, zs : zs + 1]
        spot = targets[...] - start
        rows = pl.ds(pl.multiple_of(jnp.where(side == 0, core, 1 - core) * count, count), count)
        total = jnp.zeros((count, head.shape[2]), F32)
        for k in range(zs):
            at = lax.rem(z - k + zs, zs)
            factor = jnp.sum(jnp.where(lane == at, table, 0.0), axis=-1, keepdims=True)
            column = lax.broadcasted_iota(jnp.int32, (count, columns), 1) + at * columns
            hit = (column == spot) & (column < vocab)
            grad = jnp.where(hit, target_grad, pieces[side * zs + k][...].astype(F32) * factor).astype(BF16)
            dlogits[at, rows, :] = grad
            total += jnp.dot(grad, head[at], preferred_element_type=F32)
        part[rows, :] = total


def head_kernel(zs, place, rows, gain, known_mine, known_other, dlogits, out):
    z, core = place[0], place[1]
    count = dlogits.shape[1]
    columns = dlogits.shape[2]
    mine = known_mine[...].T[:, zs + 2 : zs + 3]
    other = known_other[...].T[:, zs + 2 : zs + 3]
    inv = jnp.concatenate([jnp.where(core == 0, mine, other), jnp.where(core == 0, other, mine)])
    row = rows[:, z].reshape(count, rows.shape[3]).astype(F32)
    normed = (row * inv * gain[...]).astype(BF16)
    for at in range(zs):
        held = min(columns, out.shape[0] - at * columns)
        piece = lax.dot_general(dlogits[at], normed, (((0,), (0,)), ((), ())), preferred_element_type=F32)
        out[at * columns : at * columns + held, :] = piece[:held].astype(BF16)


def local(
    segment_in,
    layer_weight,
    layer_gain,
    final_gain,
    head_weight,
    exit_rows,
    exit_count,
    exit_targets,
    exit_scale,
    out_grad,
):
    pipe = lax.axis_index("pipe")
    core = lax.axis_index("core")
    z = lax.axis_index("z")
    pipes = lax.axis_size("pipe")
    zs = lax.axis_size("z")
    block = z * 2 + core
    seg = segment_in[0]
    weight = layer_weight[0]
    gain = layer_gain[0]
    grad = out_grad[0]
    tokens, width = seg.shape
    slab = weight.shape[1]
    exits = exit_rows.shape[1]
    rows_all = pipes * exits
    vocab_part = head_weight.shape[0]
    columns = -(-vocab_part // (zs * 128)) * 128
    place = jnp.stack([z, core, pipe * vocab_part]).astype(jnp.int32)

    weight_other = swap(weight)
    head_pieces = jnp.pad(head_weight, ((0, zs * columns - vocab_part), (0, 0))).reshape(zs, columns, slab)
    heads = from_back(lambda k: lax.dynamic_index_in_dim(head_pieces, (z + k) % zs, 0, keepdims=False), zs)

    my_rows = exit_rows[pipe]
    pick = (my_rows[:, None] == jnp.arange(tokens, dtype=jnp.int32)[None, :]).astype(BF16)
    row_in = jnp.dot(pick, seg, preferred_element_type=F32)
    row_inv = lax.rsqrt(jnp.mean(row_in * row_in, axis=-1, keepdims=True) + EPSILON)
    row_unit = row_in * row_inv
    row_normed = (row_unit * gain).astype(BF16)
    row_update = rounded(jnp.dot(row_normed, weight, preferred_element_type=F32))
    row_block = lax.dynamic_slice_in_dim(row_in, block * slab, slab, 1)
    hidden = (row_block + row_update).astype(BF16)

    inputs = seg.astype(F32)
    inv_rms = lax.rsqrt(jnp.mean(inputs * inputs, axis=-1, keepdims=True) + EPSILON)
    normed = (inputs * inv_rms * gain).astype(BF16)
    is_exit = jnp.any(pick > 0, axis=0)
    grad_slab = lax.dynamic_slice_in_dim(grad, block * slab, slab, 1)
    held = tokens // (zs * 2)

    def of_core(values):
        grouped = values.reshape((zs, 2, held) + values.shape[1:])
        return lax.dynamic_index_in_dim(grouped, core, 1, keepdims=False)

    grad_core = of_core(grad).reshape(zs * held, width)
    other_block = (z * 2 + 1 - core) * slab
    on_columns = (((1,), (1,)), ((), ()))
    over_rows = (((0,), (0,)), ((), ()))
    main_part = lax.dot_general(
        lax.dynamic_slice_in_dim(grad_core, block * slab, slab, 1), weight, on_columns, preferred_element_type=F32
    ) + lax.dot_general(
        lax.dynamic_slice_in_dim(grad_core, other_block, slab, 1),
        weight_other,
        on_columns,
        preferred_element_type=F32,
    )
    column_rows = spread(hidden, "z", zs)
    column_rows, main_part = lax.optimization_barrier((column_rows, main_part))
    main_grad = lax.psum_scatter(main_part.astype(BF16), "z", scatter_dimension=0, tiled=True).astype(F32)
    first = block * held
    held_in = lax.dynamic_slice_in_dim(seg, first, held, 0).astype(F32)
    held_grad = lax.dynamic_slice_in_dim(grad, first, held, 0).astype(F32)
    held_exit = lax.dynamic_slice_in_dim(is_exit, first, held, 0)

    def layer_back(norm_grad, unit, inv, residual):
        unit_grad = norm_grad * gain
        centre = jnp.mean(unit_grad * unit, axis=-1, keepdims=True)
        return (residual + (unit_grad - unit * centre) * inv).astype(BF16)

    held_inv = lax.rsqrt(jnp.mean(held_in * held_in, axis=-1, keepdims=True) + EPSILON)
    held_unit = held_in * held_inv
    main_out = layer_back(main_grad, held_unit, held_inv, held_grad)
    gain_part = jnp.sum(jnp.where(held_exit[:, None], 0.0, main_grad * held_unit), axis=0)


    all_hidden = spread(column_rows, "pipe", pipes)
    gains = lax.dynamic_index_in_dim(final_gain.reshape(zs, 2, slab), core, 1, keepdims=False)
    own = rows_all // 2
    mine, other = kernel_call(
        logits_kernel, [shape((own, columns + 128), F32)] * 2, place, all_hidden, gains, *heads
    )

    all_targets = exit_targets.reshape(2, own, 1)
    targets_mine = lax.dynamic_index_in_dim(all_targets, core, 0, keepdims=False)
    targets_other = lax.dynamic_index_in_dim(all_targets, 1 - core, 0, keepdims=False)
    slot = jnp.arange(exits, dtype=jnp.int32)[None, :]
    weights = jnp.where(slot < exit_count[:, None], exit_scale[:, None], F32(0.0)).reshape(2, 1, own)
    weights = lax.dynamic_index_in_dim(weights, core, 0, keepdims=False)
    expo, stats = kernel_call(
        functools.partial(softmax_kernel, width, vocab_part),
        [shape((own, columns), BF16), shape((8, own), F32)],
        place,
        mine,
        swap(other),
        targets_mine,
    )
    ex_mine = from_back(lambda k: expo, zs)
    ex_other = [swap(piece) for piece in ex_mine]
    pieces = spread(stats, "z", zs)
    merged_stats = kernel_call(merge_kernel, shape((8, own), F32), place, pieces)
    known_mine = kernel_call(
        functools.partial(finish_kernel, width),
        shape((16, own), F32),
        place,
        spread(merged_stats, "pipe", pipes),
        pieces,
        weights,
    )
    known_other = swap(known_mine)

    exit_part, dlogits = kernel_call(
        functools.partial(exit_kernel, zs, vocab_part),
        [shape((rows_all, slab), F32), shape((zs, rows_all, columns), BF16)],
        place,
        head_pieces,
        known_mine,
        known_other,
        targets_mine,
        targets_other,
        *ex_mine,
        *ex_other,
    )
    exit_part, main_out = lax.optimization_barrier((exit_part, main_out))
    main_all = lax.all_gather(main_out, ("z", "core"), axis=0, tiled=True)
    gain_mine = lax.dynamic_slice_in_dim(final_gain, block * slab, slab, 0)
    head_grad = kernel_call(
        functools.partial(head_kernel, zs),
        shape((vocab_part, slab), BF16),
        place,
        all_hidden,
        gain_mine[None],
        known_mine,
        known_other,
        dlogits,
    )
    exit_grad = jnp.sum(lax.all_to_all(exit_part.reshape(pipes, exits, slab), "pipe", 0, 0), axis=0)
    known = pair(known_mine[zs + 1 : zs + 3], known_other[zs + 1 : zs + 3], core, 1)
    my_known = lax.dynamic_slice_in_dim(known, pipe * exits, exits, 1)
    my_mean = my_known[0][:, None]
    my_inv = my_known[1][:, None]
    exit_unit = hidden.astype(F32) * my_inv
    exit_back = (exit_grad * gain_mine - exit_unit * my_mean) * my_inv
    row_grad = jnp.dot(pick, grad_slab, preferred_element_type=F32) + exit_back
    row_rounded = row_grad.astype(BF16)

    put = pick.T
    slab_rounded = jnp.where(
        is_exit[:, None], jnp.dot(put, row_rounded, preferred_element_type=F32).astype(BF16), grad_slab
    )
    weight_grad = lax.dot_general(normed, slab_rounded, over_rows, preferred_element_type=F32).astype(BF16)
    core_rows = exits // 2
    share = core_rows // zs
    row_other = swap(lax.dynamic_slice_in_dim(row_grad, (1 - core) * core_rows, core_rows, 0))
    row_mine = lax.dynamic_slice_in_dim(row_grad, core * core_rows, core_rows, 0)
    row_part = lax.dot_general(
        row_mine.astype(BF16), weight, on_columns, preferred_element_type=F32
    ) + lax.dot_general(row_other.astype(BF16), weight_other, on_columns, preferred_element_type=F32)
    core_unit = lax.dynamic_slice_in_dim(row_unit, core * core_rows, core_rows, 0)
    gain_part = gain_part + jnp.sum(row_part * core_unit, axis=0)
    piece = slab * 2 // share
    send = jnp.concatenate(
        [
            row_part.reshape(zs, share, width),
            pair(row_mine, row_other, core, 1).reshape(zs, share, 2 * slab),
            gain_part.reshape(zs, share, piece),
        ],
        axis=2,
    )
    got = lax.all_to_all(send, "z", 0, 0)
    summed = jnp.sum(got, axis=0)
    norm_grad = summed[:, :width]
    residual = got[:, :, width : width + 2 * slab].transpose(1, 0, 2).reshape(share, width)
    at = core * core_rows + z * share
    share_unit = lax.dynamic_slice_in_dim(row_unit, at, share, 0)
    share_inv = lax.dynamic_slice_in_dim(row_inv, at, share, 0)
    share_out = layer_back(norm_grad, share_unit, share_inv, residual)
    gain_parts = [values.astype(BF16) for values in split3(summed[:, width + 2 * slab :])]
    last = spread(jnp.concatenate([share_out] + gain_parts, axis=1), "z", zs)
    last_other = swap(last)
    gain_grad = jnp.sum(
        (last[:, :, width:].astype(F32) + last_other[:, :, width:].astype(F32)).reshape(zs, share, 3, piece), axis=2
    ).reshape(width)
    row_out = pair(last, last_other, core, 0)[:, :, :width].reshape(exits, width)
    input_grad = jnp.where(
        is_exit[:, None], jnp.dot(put, row_out, preferred_element_type=F32).astype(BF16), main_all
    )
    return (input_grad[None], weight_grad[None], gain_grad[None], head_grad)


def solution(mesh):
    pipes, tensors = mesh.devices.shape
    fine = Mesh(mesh.devices.reshape(pipes, tensors // 2, 2), ("pipe", "z", "core"))
    tensor = ("z", "core")
    in_specs = (
        P("pipe", None, None),
        P("pipe", None, tensor),
        P("pipe", None),
        P(),
        P("pipe", tensor),
        P(),
        P(),
        P(),
        P(),
        P("pipe", None, None),
    )
    out_specs = (
        P("pipe", None, None),
        P("pipe", None, tensor),
        P("pipe", None),
        P("pipe", tensor),
    )
    return jax.shard_map(local, mesh=fine, in_specs=in_specs, out_specs=out_specs, check_vma=False)
```

time: 248 us -> 241 us (0.972)
  starting transfers between devices: 46.1 us -> 82.6 us
  waiting for transfers between devices: 95.6 us -> 68 us
  other arithmetic: 25 us -> 12.6 us
  Pallas kernels: 0 us -> 11.5 us
  blocking collectives: 10.5 us -> 0 us
  matrix products: 32.3 us -> 24.8 us
  local copies, waits for them, and re-layouts: 21.8 us -> 25.8 us
    all_to_all x1 -> x0, waiting for transfers between devices: 39.5 us -> none  [local(): lax.all_to_all(part.astype(BF16).reshape(zs, own, padded), 'z', 0, 0)]
    ppermute x0 -> x14, starting transfers between devices: none -> 25.4 us  [from_back(): lax.ppermute(piece(k), 'z', [(i, (i + k) % count) for i in range(count)])]
    ppermute x0 -> x14, waiting for transfers between devices: none -> 23.4 us  [from_back(): lax.ppermute(piece(k), 'z', [(i, (i + k) % count) for i in range(count)])]
    all_to_all x4 -> x5, waiting for transfers between devices: 37.5 us -> 16.2 us  [spread(): lax.all_to_all(jnp.broadcast_to(values[None], (count,) + values.shape), a...]
    pallas_call x0 -> x6, Pallas kernels: none -> 11.5 us  [kernel_call(): pl.pallas_call(body, out_shape=out, in_specs=[pl.BlockSpec(memory_space=p...]
    all_to_all x1 -> x0, blocking collectives: 10.5 us -> none  [spread(): lax.all_to_all(jnp.broadcast_to(values[None], (count,) + values.shape), a...]
    all_to_all x4 -> x5, starting transfers between devices: 17.8 us -> 28.3 us  [spread(): lax.all_to_all(jnp.broadcast_to(values[None], (count,) + values.shape), a...]
    all_to_all x1 -> x0, starting transfers between devices: 8.32 us -> none  [local(): lax.all_to_all(part.astype(BF16).reshape(zs, own, padded), 'z', 0, 0)]
  transfers between devices with their start and end apart: 16 -> 36, of which waited for: 9 -> 17; matrix products, arithmetic and copies ran while one was open for 30% -> 19% of each run, Pallas kernels for 0% -> 5%
where the time goes in v3:
time: 241 us; the launch traced here: 240 us
  starting transfers between devices  82.6 us (34%)
  waiting for transfers between devices  68 us (28%)
  local copies, waits for them, and re-layouts  25.8 us (11%)
  matrix products  24.8 us (10%)
  between operations  14.6 us (6%)
  other arithmetic  12.6 us (5%)
  Pallas kernels  11.5 us (5%)
    all_to_all x5, starting transfers between devices, spread(): lax.all_to_all(jnp.broadcast_to(values[None], (count,) + values.shape), a...  28.3 us
    ppermute x14, starting transfers between devices, from_back(): lax.ppermute(piece(k), 'z', [(i, (i + k) % count) for i in range(count)])  25.4 us
    ppermute x14, waiting for transfers between devices, from_back(): lax.ppermute(piece(k), 'z', [(i, (i + k) % count) for i in range(count)])  23.4 us
    ppermute x13, starting transfers between devices, swap(): return lax.ppermute(values, 'core', [(0, 1), (1, 0)])  17.3 us
    all_to_all x5, waiting for transfers between devices, spread(): lax.all_to_all(jnp.broadcast_to(values[None], (count,) + values.shape), a...  16.2 us
    all_to_all x1, waiting for transfers between devices, local(): got = lax.all_to_all(send, 'z', 0, 0)  16.2 us
    pallas_call x6, Pallas kernels, kernel_call(): pl.pallas_call(body, out_shape=out, in_specs=[pl.BlockSpec(memory_space=p...  11.5 us
    all_to_all x1, waiting for transfers between devices, local(): lax.all_to_all(exit_part.reshape(pipes, exits, slab), 'pipe', 0, 0)  10 us
  transfers between devices with their start and end apart: 36, of which 17 were waited for; matrix products, arithmetic and copies ran while one was open for 19% of the time, Pallas kernels for 5%

profile of v3, /device:TPU:1, one launch (start us, length us, event | category | flops | bytes accessed | tf_op | source)
XLA Modules:
  0.0 239.9 jit_solution(6976769590805751125)
XLA Ops:
  7.2 3.3 %collective-permute-start = (bf16[4096,256]{1,0:T(8,128)(2,1)}, bf16[4096,256]{1,0:T(8,128)(2,1)}, u32[]{:S(2)}, u32[]{:S(2)}) collective-permute-start(bf16[4096,256]{1,0:T(8,128)(2,1)} %bitcast.90), channel_id=1, source_target_pairs={{0,1},{1,0},{2,3},{3,2},{4,5},{5,4},{6,7},{7,6},{8,9},{9,8},{10,11... | collective-permute-start | bytes 6291464 | tf_op jit(solution)/shard_map/ppermute | solution.py:32
  11.1 3.1 %multiply_reduce_fusion = (f32[32]{0:T(128)S(1)}, f32[32,4096]{1,0:T(8,128)S(1)}) fusion(bf16[1,512,4096]{2,1,0:T(8,128)(2,1)} %param.10, s32[32]{0:T(128)S(1)} %fusion.55), kind=kOutput, calls=%fused_computation.38 | convolution fusion | flops 134496224 | bytes 4718848 | tf_op jit(solution)/shard_map/dot_general | solution.py:213
  16.9 6.5 %all-to-all-start = ((bf16[8,32,256]{2,1,0:T(8,128)(2,1)}), bf16[8,32,256]{2,1,0:T(8,128)(2,1)S(1)}, u32[]{:S(2)}, u32[]{:S(2)}) async-start(bf16[8,32,256]{2,1,0:T(8,128)(2,1)} %broadcast_in_dim.58), calls=%async_computation | async-start | bytes 262144 | tf_op jit(solution)/shard_map/all_to_all | solution.py:28
  25.9 3.7 %convolution_add_fusion = bf16[256,4096]{1,0:T(8,128)(2,1)} fusion(f32[256,4096]{1,0:T(8,128)S(1)} %fusion.33, bf16[4096,256]{1,0:T(8,128)(2,1)} %collective-permute-done, bf16[256,4096]{1,0:T(8,128)(2,1)S(1)} %bitcast.92, s32[]{:T(128)S(6)} %select_n.167), kind=kOutput, calls=%fused_computation.6 | convolution fusion | flops 538968064 | bytes 8519684 | tf_op jit(solution)/shard_map/dot_general | solution.py:238
  32.7 6.8 %all-to-all-start.1 = ((bf16[16,8,32,256]{3,2,1,0:T(8,128)(2,1)}), bf16[16,8,32,256]{3,2,1,0:T(8,128)(2,1)S(1)}, u32[]{:S(2)}, u32[]{:S(2)}) async-start(bf16[16,8,32,256]{3,2,1,0:T(8,128)(2,1)} %broadcast_in_dim.62), calls=%async_computation.1 | async-start | bytes 4194304 | tf_op jit(solution)/shard_map/all_to_all | solution.py:28
  43.8 2.4 collective-permute-start.3
  48.3 2.4 collective-permute-start.5
  52.0 3.3 %collective-permute-start.6 = (bf16[256,256]{1,0:T(8,128)(2,1)}, bf16[256,256]{1,0:T(8,128)(2,1)}, u32[]{:S(2)}, u32[]{:S(2)}) collective-permute-start(bf16[256,256]{1,0:T(8,128)(2,1)} %get-tuple-element.27), channel_id=1, source_target_pairs={{0,12},{2,14},{4,0},{6,2},{8,4},{10,6},{12,8},{14,10},{1,13},{3,15... | collective-permute-start | bytes 393224 | tf_op jit(solution)/shard_map/ppermute | solution.py:37
  57.9 4.9 %collective-permute-done.3.refs_3_ = bf16[256,256]{1,0:T(8,128)(2,1)} collective-permute-done((bf16[256,256]{1,0:T(8,128)(2,1)}, bf16[256,256]{1,0:T(8,128)(2,1)}, u32[]{:S(2)}, u32[]{:S(2)}) %collective-permute-start.3) | collective-permute-done | bytes 131104 | tf_op jit(solution)/shard_map/ppermute | solution.py:37
  62.8 6.5 %collective-permute-done.4.refs_4_ = bf16[256,256]{1,0:T(8,128)(2,1)} collective-permute-done((bf16[256,256]{1,0:T(8,128)(2,1)}, bf16[256,256]{1,0:T(8,128)(2,1)}, u32[]{:S(2)}, u32[]{:S(2)}) %collective-permute-start.4) | collective-permute-done | bytes 131104 | tf_op jit(solution)/shard_map/ppermute | solution.py:37
  69.2 2.4 collective-permute-done.5.refs_5_
  71.6 3.7 %collective-permute-done.6.refs_6_ = bf16[256,256]{1,0:T(8,128)(2,1)} collective-permute-done((bf16[256,256]{1,0:T(8,128)(2,1)}, bf16[256,256]{1,0:T(8,128)(2,1)}, u32[]{:S(2)}, u32[]{:S(2)}) %collective-permute-start.6) | collective-permute-done | bytes 131104 | tf_op jit(solution)/shard_map/ppermute | solution.py:37
  75.3 5.9 %collective-permute-done.7.refs_7_ = bf16[256,256]{1,0:T(8,128)(2,1)} collective-permute-done((bf16[256,256]{1,0:T(8,128)(2,1)}, bf16[256,256]{1,0:T(8,128)(2,1)}, u32[]{:S(2)}, u32[]{:S(2)}) %collective-permute-start.7) | collective-permute-done | bytes 131104 | tf_op jit(solution)/shard_map/ppermute | solution.py:37
  81.9 2.8 %shard_map.129 = (f32[256,384]{1,0:T(8,128)S(1)}, f32[256,384]{1,0:T(8,128)}) custom-call(s32[3]{0:T(128)S(1)} %copy-done.6, bf16[16,8,32,256]{3,2,1,0:T(8,128)(2,1)S(1)} %all-to-all-done.1.rows, f32[8,256]{1,0:T(8,128)S(1)} %bitcast.88, bf16[256,256]{1,0:T(8,128)(2,1)S(1)} %get-tuple-element.33.refs_0_, ...), custom_call_target="tpu_custom_call" | custom-call | tf_op jit(solution)/shard_map/pallas_call | solution.py:48
  85.5 3.3 %collective-permute-start.8 = (f32[256,384]{1,0:T(8,128)}, f32[256,384]{1,0:T(8,128)}, u32[]{:S(2)}, u32[]{:S(2)}) collective-permute-start(f32[256,384]{1,0:T(8,128)} %get-tuple-element.16), channel_id=1, source_target_pairs={{0,1},{1,0},{2,3},{3,2},{4,5},{5,4},{6,7},{7,6},{8,9},{9,8},{10,11... | collective-permute-start | bytes 1179656 | tf_op jit(solution)/shard_map/ppermute | solution.py:32
  99.1 3.8 %collective-permute-start.13 = (bf16[256,256]{1,0:T(8,128)(2,1)}, bf16[256,256]{1,0:T(8,128)(2,1)}, u32[]{:S(2)}, u32[]{:S(2)}) collective-permute-start(bf16[256,256]{1,0:T(8,128)(2,1)} %get-tuple-element.18.refs_0_), channel_id=1, source_target_pairs={{0,8},{2,10},{4,12},{6,14},{8,0},{10,2},{12,4},{14,6},{1,9},{3,11}... | collective-permute-start | bytes 393224 | tf_op jit(solution)/shard_map/ppermute | solution.py:37
  104.2 5.0 %all-to-all-start.2 = ((f32[8,8,256]{2,1,0:T(8,128)}), f32[8,8,256]{2,1,0:T(8,128)S(1)}, u32[]{:S(2)}, u32[]{:S(2)}) async-start(f32[8,8,256]{2,1,0:T(8,128)} %broadcast_in_dim.63), calls=%async_computation.2 | async-start | bytes 131072 | tf_op jit(solution)/shard_map/all_to_all | solution.py:28
  111.1 10.4 %all-to-all-done.2.stats.pieces = f32[8,8,256]{2,1,0:T(8,128)S(1)} async-done(((f32[8,8,256]{2,1,0:T(8,128)}), f32[8,8,256]{2,1,0:T(8,128)S(1)}, u32[]{:S(2)}, u32[]{:S(2)}) %all-to-all-start.2) | async-done | bytes 65568 | tf_op jit(solution)/shard_map/all_to_all | solution.py:28
  123.4 6.7 %all-to-all-start.3 = ((f32[16,8,256]{2,1,0:T(8,128)}), f32[16,8,256]{2,1,0:T(8,128)S(1)}, u32[]{:S(2)}, u32[]{:S(2)}) async-start(f32[16,8,256]{2,1,0:T(8,128)} %broadcast_in_dim.100), calls=%async_computation.3 | async-start | bytes 262144 | tf_op jit(solution)/shard_map/all_to_all | solution.py:28
  130.0 2.4 %collective-permute-start.15 = (bf16[256,256]{1,0:T(8,128)(2,1)}, bf16[256,256]{1,0:T(8,128)(2,1)}, u32[]{:S(2)}, u32[]{:S(2)}) collective-permute-start(bf16[256,256]{1,0:T(8,128)(2,1)} %get-tuple-element.18.refs_0_), channel_id=1, source_target_pairs={{0,12},{2,14},{4,0},{6,2},{8,4},{10,6},{12,8},{14,10},{1,13},{3,15... | collective-permute-start | bytes 393224 | tf_op jit(solution)/shard_map/ppermute | solution.py:37
  138.2 3.2 %collective-permute-start.9 = (f32[16,256]{1,0:T(8,128)S(1)}, f32[16,256]{1,0:T(8,128)S(1)}, u32[]{:S(2)}, u32[]{:S(2)}) collective-permute-start(f32[16,256]{1,0:T(8,128)S(1)} %shard_map.132.known_mine), channel_id=1, source_target_pairs={{0,1},{1,0},{2,3},{3,2},{4,5},{5,4},{6,7},{7,6},{8,9},{9,8},{10,11... | collective-permute-start | bytes 49160 | tf_op jit(solution)/shard_map/ppermute | solution.py:32
  148.2 3.1 %shard_map.133 = (f32[512,256]{1,0:T(8,128)S(1)}, bf16[8,512,256]{2,1,0:T(8,128)(2,1)S(1)}) custom-call(s32[3]{0:T(128)S(1)} %copy-done.10, bf16[8,256,256]{2,1,0:T(8,128)(2,1)S(1)} %bitcast.86, f32[16,256]{1,0:T(8,128)S(1)} %shard_map.132.known_mine, f32[16,256]{1,0:T(8,128)S(1)} %collective-permute-done.9.known_other, ...), custom_call_target="tpu_custom_call" | custom-call | tf_op jit(solution)/shard_map/pallas_call | solution.py:48
  156.8 6.6 %all-to-all-start.4 = ((f32[16,32,256]{2,1,0:T(8,128)}), f32[16,32,256]{2,1,0:T(8,128)S(1)}, u32[]{:S(2)}, u32[]{:S(2)}) async-start(f32[16,32,256]{2,1,0:T(8,128)} %bitcast.87), calls=%async_computation.5 | async-start | bytes 1048576 | tf_op jit(solution)/shard_map/all_to_all | solution.py:323
  164.3 10.0 %all-to-all-done.4 = f32[16,32,256]{2,1,0:T(8,128)S(1)} async-done(((f32[16,32,256]{2,1,0:T(8,128)}), f32[16,32,256]{2,1,0:T(8,128)S(1)}, u32[]{:S(2)}, u32[]{:S(2)}) %all-to-all-start.4) | async-done | bytes 524320 | tf_op jit(solution)/shard_map/all_to_all | solution.py:323
  182.9 4.7 %all-to-all-start.5 = ((f32[8,2,4864]{2,1,0:T(2,128)}), f32[8,2,4864]{2,1,0:T(2,128)S(1)}, u32[]{:S(2)}, u32[]{:S(2)}) async-start(f32[8,2,4864]{2,1,0:T(2,128)} %pad_maximum_fusion), calls=%async_computation.6 | async-start | bytes 622592 | tf_op jit(solution)/shard_map/all_to_all | solution.py:356
  187.6 16.2 %all-to-all-done.5 = f32[8,2,4864]{2,1,0:T(2,128)S(1)} async-done(((f32[8,2,4864]{2,1,0:T(2,128)}), f32[8,2,4864]{2,1,0:T(2,128)S(1)}, u32[]{:S(2)}, u32[]{:S(2)}) %all-to-all-start.5) | async-done | bytes 311328 | tf_op jit(solution)/shard_map/all_to_all | solution.py:356
  206.8 3.4 %all-to-all-start.6 = ((bf16[8,2,4864]{2,1,0:T(2,128)(2,1)}), bf16[8,2,4864]{2,1,0:T(2,128)(2,1)S(1)}, u32[]{:S(2)}, u32[]{:S(2)}) async-start(bf16[8,2,4864]{2,1,0:T(2,128)(2,1)} %broadcast_in_dim.107), calls=%async_computation.7 | async-start | bytes 311296 | tf_op jit(solution)/shard_map/all_to_all | solution.py:28
  210.2 3.2 %fusion = f32[512]{0:T(512)S(1)} fusion(bf16[1,512,4096]{2,1,0:T(8,128)(2,1)} %param.10), kind=kLoop, calls=%fused_computation.2 | loop fusion | flops 6290944 | bytes 4196352 | tf_op jit(solution)/shard_map/reduce_sum | solution.py:222
  213.5 2.5 %shard_map.134 = bf16[2000,256]{1,0:T(8,128)(2,1)} custom-call(s32[3]{0:T(128)S(1)} %copy-done.10, bf16[16,8,32,256]{3,2,1,0:T(8,128)(2,1)S(1)} %all-to-all-done.1.rows, f32[1,256]{1,0:T(1,128)S(1)} %bitcast.89, f32[16,256]{1,0:T(8,128)S(1)} %shard_map.132.known_mine, f32[16,256]{1,0:T(8,128)S(1)} %collective-permute-done.9.known_other, ...), custom_call_target="tpu_custom_call" | custom-call | tf_op jit(solution)/shard_map/pallas_call | solution.py:48
  218.2 2.5 %collective-permute-start.26 = (bf16[8,2,4864]{2,0,1:T(8,128)(2,1)S(1)}, bf16[8,2,4864]{2,0,1:T(8,128)(2,1)S(1)}, u32[]{:S(2)}, u32[]{:S(2)}) collective-permute-start(bf16[8,2,4864]{2,0,1:T(8,128)(2,1)S(1)} %copy.59), channel_id=1, source_target_pairs={{0,1},{1,0},{2,3},{3,2},{4,5},{5,4},{6,7},{7,6},{8,9},{9,8},{10,11... | collective-permute-start | bytes 466952 | tf_op jit(solution)/shard_map/ppermute | solution.py:32
  220.8 5.5 %fusion.5 = bf16[1,4096,256]{2,1,0:T(8,128)(2,1)} fusion(bf16[1,512,4096]{2,1,0:T(8,128)(2,1)} %param.10, f32[4096]{0:T(1024)S(1)} %bitcast.99, f32[512]{0:T(512)S(1)} %add_rsqrt_fusion, pred[512]{0:T(512)(128)(4,1)S(1)} %compare_reduce_fusion, bf16[1,512,4096]{2,1,0:T(8,128)(2,1)} %param.19, s32[]{:T(128)S(6)} %select_n.165, s32[32]{0:T(128)S(1)} %copy-done.18, ...), kind=kOutput, calls=%fused_computation.10 | convolution fusion | flops 1091854336 | bytes 6605444 | tf_op jit(solution)/shard_map/dot_general | solution.py:337
  227.5 5.6 %fusion.4 = bf16[1,512,4096]{2,1,0:T(8,128)(2,1)} fusion(bf16[512,4096]{1,0:T(8,128)(2,1)} %all-gather.2.cloned.1.call-done, bf16[32,4096]{1,0:T(8,128)(2,1)S(1)} %reshape.175, pred[512]{0:T(512)(128)(4,1)S(1)} %compare_reduce_fusion, s32[32]{0:T(128)S(1)} %copy-done.18), kind=kOutput, calls=%fused_computation.9 | convolution fusion | flops 138428416 | bytes 8651392 | tf_op jit(solution)/shard_map/dot_general | solution.py:372
  (167 shorter events, 69.6 us)
Async XLA Ops:
  7.2 18.7 %collective-permute-start = (bf16[4096,256]{1,0:T(8,128)(2,1)}, bf16[4096,256]{1,0:T(8,128)(2,1)}, u32[]{:S(2)}, u32[]{:S(2)}) collective-permute-start(bf16[4096,256]{1,0:T(8,128)(2,1)} %bitcast.90), channel_id=1, source_target_pairs={{0,1},{1,0},{2,3},{3,2},{4,5},{5,4},{6,7},{7,6},{8,9},{9,8},{10,11... | collective-permute-start | bytes 6291464 | tf_op jit(solution)/shard_map/ppermute | solution.py:32
  16.9 14.2 %all-to-all-start = ((bf16[8,32,256]{2,1,0:T(8,128)(2,1)}), bf16[8,32,256]{2,1,0:T(8,128)(2,1)S(1)}, u32[]{:S(2)}, u32[]{:S(2)}) async-start(bf16[8,32,256]{2,1,0:T(8,128)(2,1)} %broadcast_in_dim.58), calls=%async_computation | async-start | bytes 262144 | tf_op jit(solution)/shard_map/all_to_all | solution.py:28
  23.3 130.1 %reduce-scatter.2.cloned.1.call-start = ((), (), s32[]{:S(2)}) async-start(), calls=%async_computation.8 | async-start | bytes 2359296 | tf_op jit(solution)/shard_map/reduce_scatter | solution.py:246
  32.7 48.5 %all-to-all-start.1 = ((bf16[16,8,32,256]{3,2,1,0:T(8,128)(2,1)}), bf16[16,8,32,256]{3,2,1,0:T(8,128)(2,1)S(1)}, u32[]{:S(2)}, u32[]{:S(2)}) async-start(bf16[16,8,32,256]{3,2,1,0:T(8,128)(2,1)} %broadcast_in_dim.62), calls=%async_computation.1 | async-start | bytes 4194304 | tf_op jit(solution)/shard_map/all_to_all | solution.py:28
  41.8 10.2 %collective-permute-start.1 = (bf16[256,256]{1,0:T(8,128)(2,1)}, bf16[256,256]{1,0:T(8,128)(2,1)S(1)}, u32[]{:S(2)}, u32[]{:S(2)}) collective-permute-start(bf16[256,256]{1,0:T(8,128)(2,1)} %get-tuple-element.32), channel_id=1, source_target_pairs={{0,2},{2,4},{4,6},{6,8},{8,10},{10,12},{12,14},{14,0},{1,3},{3,5},... | collective-permute-start | bytes 393224 | tf_op jit(solution)/shard_map/ppermute | solution.py:37
  42.3 13.0 %collective-permute-start.2 = (bf16[256,256]{1,0:T(8,128)(2,1)}, bf16[256,256]{1,0:T(8,128)(2,1)S(1)}, u32[]{:S(2)}, u32[]{:S(2)}) collective-permute-start(bf16[256,256]{1,0:T(8,128)(2,1)} %get-tuple-element.31), channel_id=1, source_target_pairs={{0,4},{2,6},{4,8},{6,10},{8,12},{10,14},{12,0},{14,2},{1,5},{3,7},... | collective-permute-start | bytes 393224 | tf_op jit(solution)/shard_map/ppermute | solution.py:37
  43.8 18.9 %collective-permute-start.3 = (bf16[256,256]{1,0:T(8,128)(2,1)}, bf16[256,256]{1,0:T(8,128)(2,1)}, u32[]{:S(2)}, u32[]{:S(2)}) collective-permute-start(bf16[256,256]{1,0:T(8,128)(2,1)} %get-tuple-element.30), channel_id=1, source_target_pairs={{0,6},{2,8},{4,10},{6,12},{8,14},{10,0},{12,2},{14,4},{1,7},{3,9},... | collective-permute-start | bytes 393224 | tf_op jit(solution)/shard_map/ppermute | solution.py:37
  46.2 23.1 %collective-permute-start.4 = (bf16[256,256]{1,0:T(8,128)(2,1)}, bf16[256,256]{1,0:T(8,128)(2,1)}, u32[]{:S(2)}, u32[]{:S(2)}) collective-permute-start(bf16[256,256]{1,0:T(8,128)(2,1)} %get-tuple-element.29), channel_id=1, source_target_pairs={{0,8},{2,10},{4,12},{6,14},{8,0},{10,2},{12,4},{14,6},{1,9},{3,11}... | collective-permute-start | bytes 393224 | tf_op jit(solution)/shard_map/ppermute | solution.py:37
  48.3 23.4 %collective-permute-start.5 = (bf16[256,256]{1,0:T(8,128)(2,1)}, bf16[256,256]{1,0:T(8,128)(2,1)}, u32[]{:S(2)}, u32[]{:S(2)}) collective-permute-start(bf16[256,256]{1,0:T(8,128)(2,1)} %get-tuple-element.28), channel_id=1, source_target_pairs={{0,10},{2,12},{4,14},{6,0},{8,2},{10,4},{12,6},{14,8},{1,11},{3,13... | collective-permute-start | bytes 393224 | tf_op jit(solution)/shard_map/ppermute | solution.py:37
  52.0 23.3 %collective-permute-start.6 = (bf16[256,256]{1,0:T(8,128)(2,1)}, bf16[256,256]{1,0:T(8,128)(2,1)}, u32[]{:S(2)}, u32[]{:S(2)}) collective-permute-start(bf16[256,256]{1,0:T(8,128)(2,1)} %get-tuple-element.27), channel_id=1, source_target_pairs={{0,12},{2,14},{4,0},{6,2},{8,4},{10,6},{12,8},{14,10},{1,13},{3,15... | collective-permute-start | bytes 393224 | tf_op jit(solution)/shard_map/ppermute | solution.py:37
  55.3 25.9 %collective-permute-start.7 = (bf16[256,256]{1,0:T(8,128)(2,1)}, bf16[256,256]{1,0:T(8,128)(2,1)}, u32[]{:S(2)}, u32[]{:S(2)}) collective-permute-start(bf16[256,256]{1,0:T(8,128)(2,1)} %get-tuple-element.26), channel_id=1, source_target_pairs={{0,14},{2,0},{4,2},{6,4},{8,6},{10,8},{12,10},{14,12},{1,15},{3,1}... | collective-permute-start | bytes 393224 | tf_op jit(solution)/shard_map/ppermute | solution.py:37
  85.5 5.0 %collective-permute-start.8 = (f32[256,384]{1,0:T(8,128)}, f32[256,384]{1,0:T(8,128)}, u32[]{:S(2)}, u32[]{:S(2)}) collective-permute-start(f32[256,384]{1,0:T(8,128)} %get-tuple-element.16), channel_id=1, source_target_pairs={{0,1},{1,0},{2,3},{3,2},{4,5},{5,4},{6,7},{7,6},{8,9},{9,8},{10,11... | collective-permute-start | bytes 1179656 | tf_op jit(solution)/shard_map/ppermute | solution.py:32
  94.1 35.9 %collective-permute-start.10 = (bf16[256,256]{1,0:T(8,128)(2,1)}, bf16[256,256]{1,0:T(8,128)(2,1)}, u32[]{:S(2)}, u32[]{:S(2)}) collective-permute-start(bf16[256,256]{1,0:T(8,128)(2,1)} %get-tuple-element.18.refs_0_), channel_id=1, source_target_pairs={{0,2},{2,4},{4,6},{6,8},{8,10},{10,12},{12,14},{14,0},{1,3},{3,5},... | collective-permute-start | bytes 393224 | tf_op jit(solution)/shard_map/ppermute | solution.py:37
  95.5 37.0 %collective-permute-start.11 = (bf16[256,256]{1,0:T(8,128)(2,1)}, bf16[256,256]{1,0:T(8,128)(2,1)}, u32[]{:S(2)}, u32[]{:S(2)}) collective-permute-start(bf16[256,256]{1,0:T(8,128)(2,1)} %get-tuple-element.18.refs_0_), channel_id=1, source_target_pairs={{0,4},{2,6},{4,8},{6,10},{8,12},{10,14},{12,0},{14,2},{1,5},{3,7},... | collective-permute-start | bytes 393224 | tf_op jit(solution)/shard_map/ppermute | solution.py:37
  97.5 35.3 %collective-permute-start.12 = (bf16[256,256]{1,0:T(8,128)(2,1)}, bf16[256,256]{1,0:T(8,128)(2,1)}, u32[]{:S(2)}, u32[]{:S(2)}) collective-permute-start(bf16[256,256]{1,0:T(8,128)(2,1)} %get-tuple-element.18.refs_0_), channel_id=1, source_target_pairs={{0,6},{2,8},{4,10},{6,12},{8,14},{10,0},{12,2},{14,4},{1,7},{3,9},... | collective-permute-start | bytes 393224 | tf_op jit(solution)/shard_map/ppermute | solution.py:37
  99.1 35.2 %collective-permute-start.13 = (bf16[256,256]{1,0:T(8,128)(2,1)}, bf16[256,256]{1,0:T(8,128)(2,1)}, u32[]{:S(2)}, u32[]{:S(2)}) collective-permute-start(bf16[256,256]{1,0:T(8,128)(2,1)} %get-tuple-element.18.refs_0_), channel_id=1, source_target_pairs={{0,8},{2,10},{4,12},{6,14},{8,0},{10,2},{12,4},{14,6},{1,9},{3,11}... | collective-permute-start | bytes 393224 | tf_op jit(solution)/shard_map/ppermute | solution.py:37
  102.9 31.5 %collective-permute-start.14 = (bf16[256,256]{1,0:T(8,128)(2,1)}, bf16[256,256]{1,0:T(8,128)(2,1)}, u32[]{:S(2)}, u32[]{:S(2)}) collective-permute-start(bf16[256,256]{1,0:T(8,128)(2,1)} %get-tuple-element.18.refs_0_), channel_id=1, source_target_pairs={{0,10},{2,12},{4,14},{6,0},{8,2},{10,4},{12,6},{14,8},{1,11},{3,13... | collective-permute-start | bytes 393224 | tf_op jit(solution)/shard_map/ppermute | solution.py:37
  104.2 17.3 %all-to-all-start.2 = ((f32[8,8,256]{2,1,0:T(8,128)}), f32[8,8,256]{2,1,0:T(8,128)S(1)}, u32[]{:S(2)}, u32[]{:S(2)}) async-start(f32[8,8,256]{2,1,0:T(8,128)} %broadcast_in_dim.63), calls=%async_computation.2 | async-start | bytes 131072 | tf_op jit(solution)/shard_map/all_to_all | solution.py:28
  123.4 13.5 %all-to-all-start.3 = ((f32[16,8,256]{2,1,0:T(8,128)}), f32[16,8,256]{2,1,0:T(8,128)S(1)}, u32[]{:S(2)}, u32[]{:S(2)}) async-start(f32[16,8,256]{2,1,0:T(8,128)} %broadcast_in_dim.100), calls=%async_computation.3 | async-start | bytes 262144 | tf_op jit(solution)/shard_map/all_to_all | solution.py:28
  130.0 8.1 %collective-permute-start.15 = (bf16[256,256]{1,0:T(8,128)(2,1)}, bf16[256,256]{1,0:T(8,128)(2,1)}, u32[]{:S(2)}, u32[]{:S(2)}) collective-permute-start(bf16[256,256]{1,0:T(8,128)(2,1)} %get-tuple-element.18.refs_0_), channel_id=1, source_target_pairs={{0,12},{2,14},{4,0},{6,2},{8,4},{10,6},{12,8},{14,10},{1,13},{3,15... | collective-permute-start | bytes 393224 | tf_op jit(solution)/shard_map/ppermute | solution.py:37
  132.5 12.3 %collective-permute-start.16 = (bf16[256,256]{1,0:T(8,128)(2,1)}, bf16[256,256]{1,0:T(8,128)(2,1)}, u32[]{:S(2)}, u32[]{:S(2)}) collective-permute-start(bf16[256,256]{1,0:T(8,128)(2,1)} %get-tuple-element.18.refs_0_), channel_id=1, source_target_pairs={{0,14},{2,0},{4,2},{6,4},{8,6},{10,8},{12,10},{14,12},{1,15},{3,1}... | collective-permute-start | bytes 393224 | tf_op jit(solution)/shard_map/ppermute | solution.py:37
  132.8 12.2 %collective-permute-start.17 = (bf16[256,256]{1,0:T(8,128)(2,1)}, bf16[256,256]{1,0:T(8,128)(2,1)}, u32[]{:S(2)}, u32[]{:S(2)}) collective-permute-start(bf16[256,256]{1,0:T(8,128)(2,1)} %get-tuple-element.18.refs_0_), channel_id=1, source_target_pairs={{0,1},{1,0},{2,3},{3,2},{4,5},{5,4},{6,7},{7,6},{8,9},{9,8},{10,11... | collective-permute-start | bytes 393224 | tf_op jit(solution)/shard_map/ppermute | solution.py:32
  134.3 11.3 %collective-permute-start.18 = (bf16[256,256]{1,0:T(8,128)(2,1)}, bf16[256,256]{1,0:T(8,128)(2,1)}, u32[]{:S(2)}, u32[]{:S(2)}) collective-permute-start(bf16[256,256]{1,0:T(8,128)(2,1)} %collective-permute-done.10.refs_1_), channel_id=1, source_target_pairs={{0,1},{1,0},{2,3},{3,2},{4,5},{5,4},{6,7},{7,6},{8,9},{9,8},{10,11... | collective-permute-start | bytes 393224 | tf_op jit(solution)/shard_map/ppermute | solution.py:32
  134.4 11.6 %collective-permute-start.19 = (bf16[256,256]{1,0:T(8,128)(2,1)}, bf16[256,256]{1,0:T(8,128)(2,1)}, u32[]{:S(2)}, u32[]{:S(2)}) collective-permute-start(bf16[256,256]{1,0:T(8,128)(2,1)} %collective-permute-done.11.refs_2_), channel_id=1, source_target_pairs={{0,1},{1,0},{2,3},{3,2},{4,5},{5,4},{6,7},{7,6},{8,9},{9,8},{10,11... | collective-permute-start | bytes 393224 | tf_op jit(solution)/shard_map/ppermute | solution.py:32
  138.2 7.3 %collective-permute-start.9 = (f32[16,256]{1,0:T(8,128)S(1)}, f32[16,256]{1,0:T(8,128)S(1)}, u32[]{:S(2)}, u32[]{:S(2)}) collective-permute-start(f32[16,256]{1,0:T(8,128)S(1)} %shard_map.132.known_mine), channel_id=1, source_target_pairs={{0,1},{1,0},{2,3},{3,2},{4,5},{5,4},{6,7},{7,6},{8,9},{9,8},{10,11... | collective-permute-start | bytes 49160 | tf_op jit(solution)/shard_map/ppermute | solution.py:32
  144.9 1.7 collective-permute-start.21
  156.8 17.5 %all-to-all-start.4 = ((f32[16,32,256]{2,1,0:T(8,128)}), f32[16,32,256]{2,1,0:T(8,128)S(1)}, u32[]{:S(2)}, u32[]{:S(2)}) async-start(f32[16,32,256]{2,1,0:T(8,128)} %bitcast.87), calls=%async_computation.5 | async-start | bytes 1048576 | tf_op jit(solution)/shard_map/all_to_all | solution.py:323
  163.4 64.1 %all-gather.2.cloned.1.call-start = ((), (), s32[]{:S(2)}) async-start(), calls=%async_computation.9 | async-start | bytes 4456448 | tf_op jit(solution)/shard_map/all_gather | solution.py:311
  175.5 3.9 %collective-permute-start.25 = (f32[16,256]{1,0:T(8,128)S(1)}, f32[16,256]{1,0:T(8,128)S(1)}, u32[]{:S(2)}, u32[]{:S(2)}) collective-permute-start(f32[16,256]{1,0:T(8,128)S(1)} %constant_dynamic-slice_fusion.2), channel_id=1, source_target_pairs={{0,1},{1,0},{2,3},{3,2},{4,5},{5,4},{6,7},{7,6},{8,9},{9,8},{10,11... | collective-permute-start | bytes 49160 | tf_op jit(solution)/shard_map/ppermute | solution.py:32
  182.9 21.0 %all-to-all-start.5 = ((f32[8,2,4864]{2,1,0:T(2,128)}), f32[8,2,4864]{2,1,0:T(2,128)S(1)}, u32[]{:S(2)}, u32[]{:S(2)}) async-start(f32[8,2,4864]{2,1,0:T(2,128)} %pad_maximum_fusion), calls=%async_computation.6 | async-start | bytes 622592 | tf_op jit(solution)/shard_map/all_to_all | solution.py:356
  206.8 11.4 %all-to-all-start.6 = ((bf16[8,2,4864]{2,1,0:T(2,128)(2,1)}), bf16[8,2,4864]{2,1,0:T(2,128)(2,1)S(1)}, u32[]{:S(2)}, u32[]{:S(2)}) async-start(bf16[8,2,4864]{2,1,0:T(2,128)(2,1)} %broadcast_in_dim.107), calls=%async_computation.7 | async-start | bytes 311296 | tf_op jit(solution)/shard_map/all_to_all | solution.py:28
  218.2 8.1 %collective-permute-start.26 = (bf16[8,2,4864]{2,0,1:T(8,128)(2,1)S(1)}, bf16[8,2,4864]{2,0,1:T(8,128)(2,1)S(1)}, u32[]{:S(2)}, u32[]{:S(2)}) collective-permute-start(bf16[8,2,4864]{2,0,1:T(8,128)(2,1)S(1)} %copy.59), channel_id=1, source_target_pairs={{0,1},{1,0},{2,3},{3,2},{4,5},{5,4},{6,7},{7,6},{8,9},{9,8},{10,11... | collective-permute-start | bytes 466952 | tf_op jit(solution)/shard_map/ppermute | solution.py:32
  (25 other events, 301.4 us)
Sparse Core Ops, SparseCore 0:
  31.2 60.5 reduce-scatter.1
  166.1 46.5 all-gather.1

commit v4 on v3

--- a/solution.py
+++ b/solution.py
@@ -138,22 +138,19 @@
 
 
 def exit_kernel(zs, vocab, place, head, known_mine, known_other, targets_mine, targets_other, *refs):
-    pieces, part, dlogits = refs[:-2], refs[-2], refs[-1]
-    z, core, start = place[0], place[1], place[2]
-    count, columns = pieces[0].shape
+    part, dlogits = refs[2:]
+    core, start = place[1], place[2]
+    count, columns = refs[0].shape[1:]
     for side, known, targets in ((0, known_mine, targets_mine), (1, known_other, targets_other)):
         table = known[...].T
-        lane = lax.broadcasted_iota(jnp.int32, table.shape, 1)
         target_grad = table[:, zs : zs + 1]
         spot = targets[...] - start
         rows = pl.ds(pl.multiple_of(jnp.where(side == 0, core, 1 - core) * count, count), count)
         total = jnp.zeros((count, head.shape[2]), F32)
-        for k in range(zs):
-            at = lax.rem(z - k + zs, zs)
-            factor = jnp.sum(jnp.where(lane == at, table, 0.0), axis=-1, keepdims=True)
+        for at in range(zs):
             column = lax.broadcasted_iota(jnp.int32, (count, columns), 1) + at * columns
             hit = (column == spot) & (column < vocab)
-            grad = jnp.where(hit, target_grad, pieces[side * zs + k][...].astype(F32) * factor).astype(BF16)
+            grad = jnp.where(hit, target_grad, refs[side][at].astype(F32) * table[:, at : at + 1]).astype(BF16)
             dlogits[at, rows, :] = grad
             total += jnp.dot(grad, head[at], preferred_element_type=F32)
         part[rows, :] = total
@@ -233,6 +230,7 @@
     other_block = (z * 2 + 1 - core) * slab
     on_columns = (((1,), (1,)), ((), ()))
     over_rows = (((0,), (0,)), ((), ()))
+    over_rows = (((0,), (0,)), ((), ()))
     main_part = lax.dot_general(
         lax.dynamic_slice_in_dim(grad_core, block * slab, slab, 1), weight, on_columns, preferred_element_type=F32
     ) + lax.dot_general(
@@ -241,13 +239,15 @@
         on_columns,
         preferred_element_type=F32,
     )
-    column_rows = spread(hidden, "z", zs)
-    column_rows, main_part = lax.optimization_barrier((column_rows, main_part))
+    hidden_ready, heads[1], heads[7] = lax.optimization_barrier((hidden, heads[1], heads[7]))
+    column_rows = spread(hidden_ready, "z", zs)
+    column_rows, main_part, heads[2], heads[6], heads[3] = lax.optimization_barrier(
+        (column_rows, main_part, heads[2], heads[6], heads[3])
+    )
     main_grad = lax.psum_scatter(main_part.astype(BF16), "z", scatter_dimension=0, tiled=True).astype(F32)
     first = block * held
     held_in = lax.dynamic_slice_in_dim(seg, first, held, 0).astype(F32)
     held_grad = lax.dynamic_slice_in_dim(grad, first, held, 0).astype(F32)
-    held_exit = lax.dynamic_slice_in_dim(is_exit, first, held, 0)
 
     def layer_back(norm_grad, unit, inv, residual):
         unit_grad = norm_grad * gain
@@ -256,11 +256,12 @@
 
     held_inv = lax.rsqrt(jnp.mean(held_in * held_in, axis=-1, keepdims=True) + EPSILON)
     held_unit = held_in * held_inv
-    main_out = layer_back(main_grad, held_unit, held_inv, held_grad)
-    gain_part = jnp.sum(jnp.where(held_exit[:, None], 0.0, main_grad * held_unit), axis=0)
+    unit_core = of_core(jnp.where(is_exit[:, None], 0.0, inputs * inv_rms)).reshape(zs * held, width)
+    gain_part = jnp.sum(main_part * unit_core, axis=0)
 
 
     all_hidden = spread(column_rows, "pipe", pipes)
+    all_hidden, gain_part, normed = lax.optimization_barrier((all_hidden, gain_part, normed))
     gains = lax.dynamic_index_in_dim(final_gain.reshape(zs, 2, slab), core, 1, keepdims=False)
     own = rows_all // 2
     mine, other = kernel_call(
@@ -281,9 +282,12 @@
         swap(other),
         targets_mine,
     )
-    ex_mine = from_back(lambda k: expo, zs)
-    ex_other = [swap(piece) for piece in ex_mine]
+    expo, main_grad = lax.optimization_barrier((expo, main_grad))
+    main_out = layer_back(main_grad, held_unit, held_inv, held_grad)
+    ex_mine = lax.all_gather(expo, "z", axis=0)
+    ex_other = swap(ex_mine)
     pieces = spread(stats, "z", zs)
+    pieces, main_out = lax.optimization_barrier((pieces, main_out))
     merged_stats = kernel_call(merge_kernel, shape((8, own), F32), place, pieces)
     known_mine = kernel_call(
         functools.partial(finish_kernel, width),
@@ -304,10 +308,10 @@
         known_other,
         targets_mine,
         targets_other,
-        *ex_mine,
-        *ex_other,
-    )
-    exit_part, main_out = lax.optimization_barrier((exit_part, main_out))
+        ex_mine,
+        ex_other,
+    )
+    main_out, _ = lax.optimization_barrier((main_out, ex_mine))
     main_all = lax.all_gather(main_out, ("z", "core"), axis=0, tiled=True)
     gain_mine = lax.dynamic_slice_in_dim(final_gain, block * slab, slab, 0)
     head_grad = kernel_call(
@@ -361,6 +365,7 @@
     share_unit = lax.dynamic_slice_in_dim(row_unit, at, share, 0)
     share_inv = lax.dynamic_slice_in_dim(row_inv, at, share, 0)
     share_out = layer_back(norm_grad, share_unit, share_inv, residual)
+    share_out, weight_grad, head_grad = lax.optimization_barrier((share_out, weight_grad, head_grad))
     gain_parts = [values.astype(BF16) for values in split3(summed[:, width + 2 * slab :])]
     last = spread(jnp.concatenate([share_out] + gain_parts, axis=1), "z", zs)
     last_other = swap(last)

time: 241 us -> 259 us (1.075)
  starting transfers between devices: 82.6 us -> 56.1 us
  other arithmetic: 12.6 us -> 33.9 us
  blocking collectives: 0 us -> 10.6 us
  waiting for transfers between devices: 68 us -> 76.2 us
  matrix products: 24.8 us -> 30.2 us
    all_gather x0 -> x1, waiting for transfers between devices: none -> 25.9 us  [local(): ex_mine = lax.all_gather(expo, 'z', axis=0)]
    ppermute x14 -> x7, waiting for transfers between devices: 23.4 us -> 1.11 us  [from_back(): lax.ppermute(piece(k), 'z', [(i, (i + k) % count) for i in range(count)])]
    convert_element_type x0 -> x4, other arithmetic: none -> 21.4 us  [the longest x1 7.25 us: local(): main_part.astype(BF16)]
    all_to_all x5 -> x4, waiting for transfers between devices: 16.2 us -> 32.3 us  [spread(): lax.all_to_all(jnp.broadcast_to(values[None], (count,) + values.shape), a...]
    ppermute x14 -> x7, starting transfers between devices: 25.4 us -> 13 us  [from_back(): lax.ppermute(piece(k), 'z', [(i, (i + k) % count) for i in range(count)])]
    all_to_all x1, waiting for transfers between devices: 16.2 us -> 4.12 us  [local(): got = lax.all_to_all(send, 'z', 0, 0)]
    all_to_all x0 -> x1, blocking collectives: none -> 10.6 us  [spread(): lax.all_to_all(jnp.broadcast_to(values[None], (count,) + values.shape), a...]
    all_to_all x5 -> x4, starting transfers between devices: 28.3 us -> 22.2 us  [spread(): lax.all_to_all(jnp.broadcast_to(values[None], (count,) + values.shape), a...]
  transfers between devices with their start and end apart: 36 -> 22, of which waited for: 17 -> 9; matrix products, arithmetic and copies ran while one was open for 19% -> 24% of each run, Pallas kernels for 5% -> 4%
where the time goes in v4:
time: 259 us; the launch traced here: 257 us
  waiting for transfers between devices  76.2 us (29%)
  starting transfers between devices  56.1 us (22%)
  other arithmetic  33.9 us (13%)
  matrix products  30.2 us (12%)
  local copies, waits for them, and re-layouts  25 us (10%)
  between operations  14.4 us (6%)
  Pallas kernels  11 us (4%)
  blocking collectives  10.6 us (4%)
    all_to_all x4, waiting for transfers between devices, spread(): lax.all_to_all(jnp.broadcast_to(values[None], (count,) + values.shape), a...  32.3 us
    all_gather x1, waiting for transfers between devices, local(): ex_mine = lax.all_gather(expo, 'z', axis=0)  25.9 us
    all_to_all x4, starting transfers between devices, spread(): lax.all_to_all(jnp.broadcast_to(values[None], (count,) + values.shape), a...  22.2 us
    ppermute x7, starting transfers between devices, from_back(): lax.ppermute(piece(k), 'z', [(i, (i + k) % count) for i in range(count)])  13 us
    ppermute x6, starting transfers between devices, swap(): return lax.ppermute(values, 'core', [(0, 1), (1, 0)])  12.9 us
    pallas_call x6, Pallas kernels, kernel_call(): pl.pallas_call(body, out_shape=out, in_specs=[pl.BlockSpec(memory_space=p...  11 us
    all_to_all x1, waiting for transfers between devices, local(): lax.all_to_all(exit_part.reshape(pipes, exits, slab), 'pipe', 0, 0)  11 us
    all_to_all x1, blocking collectives, spread(): lax.all_to_all(jnp.broadcast_to(values[None], (count,) + values.shape), a...  10.6 us
  transfers between devices with their start and end apart: 22, of which 9 were waited for; matrix products, arithmetic and copies ran while one was open for 24% of the time, Pallas kernels for 4%

profile of v4, /device:TPU:1, one launch (start us, length us, event | category | flops | bytes accessed | tf_op | source)
XLA Modules:
  0.0 257.4 jit_solution(211252037307318926)
XLA Ops:
  9.4 2.5 collective-permute-start
  11.8 3.9 %collective-permute-start.1 = (bf16[256,256]{1,0:T(8,128)(2,1)S(1)}, bf16[256,256]{1,0:T(8,128)(2,1)S(1)}, u32[]{:S(2)}, u32[]{:S(2)}) collective-permute-start(bf16[256,256]{1,0:T(8,128)(2,1)S(1)} %get-tuple-element.62), channel_id=1, source_target_pairs={{0,14},{2,0},{4,2},{6,4},{8,6},{10,8},{12,10},{14,12},{1,15},{3,1}... | collective-permute-start | bytes 393224 | tf_op jit(solution)/shard_map/ppermute | solution.py:37
  15.8 3.6 %collective-permute-start.4 = (bf16[256,256]{1,0:T(8,128)(2,1)S(1)}, bf16[256,256]{1,0:T(8,128)(2,1)S(1)}, u32[]{:S(2)}, u32[]{:S(2)}) collective-permute-start(bf16[256,256]{1,0:T(8,128)(2,1)S(1)} %get-tuple-element.60), channel_id=1, source_target_pairs={{0,12},{2,14},{4,0},{6,2},{8,4},{10,6},{12,8},{14,10},{1,13},{3,15... | collective-permute-start | bytes 393224 | tf_op jit(solution)/shard_map/ppermute | solution.py:37
  21.0 3.3 %multiply_reduce_fusion = (f32[32]{0:T(128)S(1)}, f32[32,4096]{1,0:T(8,128)S(1)}) fusion(bf16[1,512,4096]{2,1,0:T(8,128)(2,1)} %param.10, s32[32]{0:T(128)S(1)} %fusion.49), kind=kOutput, calls=%fused_computation.34 | convolution fusion | flops 134496224 | bytes 4718848 | tf_op jit(solution)/shard_map/dot_general | solution.py:210
  25.4 3.1 %constant_dynamic-slice_fusion.11 = bf16[8,1,32,4096]{3,2,1,0:T(8,128)(2,1)} fusion(bf16[8,2,32,4096]{3,2,1,0:T(8,128)(2,1)} %bitcast.99, s32[]{:T(128)S(6)} %select_n.172), kind=kLoop, calls=%fused_computation.93 | loop fusion | bytes 4194308 | tf_op jit(solution)/shard_map/jit(dynamic_index_in_dim)/dynamic_slice | solution.py:227
  28.6 6.6 %convert.4 = f32[8,2,32,4096]{3,2,1,0:T(8,128)} convert(bf16[8,2,32,4096]{3,2,1,0:T(8,128)(2,1)} %bitcast.95) | non-fusion elementwise | flops 2097152 | bytes 12582912 | tf_op jit(solution)/shard_map/convert_element_type | solution.py:218
  35.2 4.4 %fusion.27 = f32[256,4096]{1,0:T(8,128)} fusion(bf16[256,4096]{1,0:T(8,128)(2,1)} %bitcast.97, s32[]{:T(128)S(6)} %select_n.167, bf16[1,4096,256]{2,1,0:T(8,128)(2,1)} %param.11), kind=kOutput, calls=%fused_computation.54 | convolution fusion | flops 536870912 | bytes 6422532 | tf_op jit(solution)/shard_map/dot_general | solution.py:234
  39.7 5.2 %fusion.5 = f32[8,1,32,4096]{3,2,0,1:T(8,128)} fusion(f32[8,1,32]{2,0,1:T(8,128)S(1)} %constant_dynamic-slice_fusion.2, pred[8,1,32]{2,0,1:T(8,128)(4,1)S(1)} %constant_dynamic-slice_fusion.10, f32[8,2,32,4096]{3,2,1,0:T(8,128)} %convert.4, s32[]{:T(128)S(6)} %select_n.172), kind=kLoop, calls=%fused_computation.12 | loop fusion | flops 2097152 | bytes 8389892 | tf_op jit(solution)/shard_map/jit(_where)/select_n | solution.py:259
  46.5 5.4 %all-to-all-start = ((bf16[8,32,256]{2,1,0:T(8,128)(2,1)}), bf16[8,32,256]{2,1,0:T(8,128)(2,1)S(1)}, u32[]{:S(2)}, u32[]{:S(2)}) async-start(bf16[8,32,256]{2,1,0:T(8,128)(2,1)} %broadcast_in_dim.63), calls=%async_computation | async-start | bytes 262144 | tf_op jit(solution)/shard_map/all_to_all | solution.py:28
  52.0 5.6 %convolution_add_fusion = f32[256,4096]{1,0:T(8,128)} fusion(f32[256,4096]{1,0:T(8,128)} %fusion.27, bf16[4096,256]{1,0:T(8,128)(2,1)} %collective-permute-done.2, bf16[256,4096]{1,0:T(8,128)(2,1)} %bitcast.98, s32[]{:T(128)S(6)} %select_n.173), kind=kOutput, calls=%fused_computation.6 | convolution fusion | flops 537919488 | bytes 10616836 | tf_op jit(solution)/shard_map/dot_general | solution.py:236
  58.8 3.4 %all-to-all-done = bf16[8,32,256]{2,1,0:T(8,128)(2,1)S(1)} async-done(((bf16[8,32,256]{2,1,0:T(8,128)(2,1)}), bf16[8,32,256]{2,1,0:T(8,128)(2,1)S(1)}, u32[]{:S(2)}, u32[]{:S(2)}) %all-to-all-start) | async-done | bytes 131104 | tf_op jit(solution)/shard_map/all_to_all | solution.py:28
  62.2 7.2 %fusion.53 = (bf16[256,4096]{1,0:T(8,128)(2,1)}, f32[4096]{0:T(1024)}) fusion(f32[256,4096]{1,0:T(8,128)} %convolution_add_fusion, f32[8,1,32,4096]{3,2,0,1:T(8,128)} %fusion.5), kind=kLoop, calls=%fused_computation.120 | loop fusion | flops 3141632 | bytes 10502144 | tf_op jit(solution)/shard_map/convert_element_type | solution.py:247
  71.1 6.8 %all-to-all-start.1 = ((bf16[16,8,32,256]{3,2,1,0:T(8,128)(2,1)}), bf16[16,8,32,256]{3,2,1,0:T(8,128)(2,1)S(1)}, u32[]{:S(2)}, u32[]{:S(2)}) async-start(bf16[16,8,32,256]{3,2,1,0:T(8,128)(2,1)} %broadcast_in_dim.100), calls=%async_computation.1 | async-start | bytes 4194304 | tf_op jit(solution)/shard_map/all_to_all | solution.py:28
  81.8 5.8 %fusion.2 = bf16[512,4096]{1,0:T(8,128)(2,1)} fusion(bf16[1,512,4096]{2,1,0:T(8,128)(2,1)} %param.10, f32[4096]{0:T(1024)} %bitcast.100, f32[512]{0:T(512)S(1)} %add_rsqrt_fusion), kind=kLoop, calls=%fused_computation.4 | loop fusion | flops 8388608 | bytes 8407040 | tf_op jit(solution)/shard_map/convert_element_type | solution.py:220
  87.7 21.8 %all-to-all-done.1.rows = bf16[16,8,32,256]{3,2,1,0:T(8,128)(2,1)S(1)} async-done(((bf16[16,8,32,256]{3,2,1,0:T(8,128)(2,1)}), bf16[16,8,32,256]{3,2,1,0:T(8,128)(2,1)S(1)}, u32[]{:S(2)}, u32[]{:S(2)}) %all-to-all-start.1) | async-done | bytes 2097184 | tf_op jit(solution)/shard_map/all_to_all | solution.py:28
  112.2 2.6 %shard_map.129 = (f32[256,384]{1,0:T(8,128)S(1)}, f32[256,384]{1,0:T(8,128)}) custom-call(s32[3]{0:T(128)S(1)} %pad_add_fusion.place, bf16[16,8,32,256]{3,2,1,0:T(8,128)(2,1)S(1)} %all-to-all-done.1.rows, f32[8,256]{1,0:T(8,128)S(1)} %bitcast.93, bf16[256,256]{1,0:T(8,128)(2,1)S(1)} %get-tuple-element.58.refs_0_, ...), custom_call_target="tpu_custom_call" | custom-call | tf_op jit(solution)/shard_map/pallas_call | solution.py:48
  125.3 3.4 %all-to-all-start.2 = ((f32[8,8,256]{2,1,0:T(8,128)}), f32[8,8,256]{2,1,0:T(8,128)S(1)}, u32[]{:S(2)}, u32[]{:S(2)}) async-start(f32[8,8,256]{2,1,0:T(8,128)} %broadcast_in_dim.104), calls=%async_computation.2 | async-start | bytes 131072 | tf_op jit(solution)/shard_map/all_to_all | solution.py:28
  130.1 25.9 %all-gather.6.cloned.1.call-done = bf16[2048,256]{1,0:T(8,128)(2,1)} async-done(((bf16[256,256]{1,0:T(8,128)(2,1)}), bf16[2048,256]{1,0:T(8,128)(2,1)}) %all-gather.6.cloned.1.call-update) | async-done | bytes 1048592 | tf_op jit(solution)/shard_map/all_gather | solution.py:287
  156.0 4.7 %collective-permute-start.10 = (bf16[8,256,256]{2,1,0:T(8,128)(2,1)}, bf16[8,256,256]{2,1,0:T(8,128)(2,1)}, u32[]{:S(2)}, u32[]{:S(2)}) collective-permute-start(bf16[8,256,256]{2,1,0:T(8,128)(2,1)} %bitcast.90), channel_id=1, source_target_pairs={{0,1},{1,0},{2,3},{3,2},{4,5},{5,4},{6,7},{7,6},{8,9},{9,8},{10,11... | collective-permute-start | bytes 3145736 | tf_op jit(solution)/shard_map/ppermute | solution.py:32
  166.0 6.6 %all-to-all-start.3 = ((f32[16,8,256]{2,1,0:T(8,128)}), f32[16,8,256]{2,1,0:T(8,128)S(1)}, u32[]{:S(2)}, u32[]{:S(2)}) async-start(f32[16,8,256]{2,1,0:T(8,128)} %broadcast_in_dim.105), calls=%async_computation.4 | async-start | bytes 262144 | tf_op jit(solution)/shard_map/all_to_all | solution.py:28
  172.7 7.1 %all-to-all-done.3.stats = f32[16,8,256]{2,1,0:T(8,128)S(1)} async-done(((f32[16,8,256]{2,1,0:T(8,128)}), f32[16,8,256]{2,1,0:T(8,128)S(1)}, u32[]{:S(2)}, u32[]{:S(2)}) %all-to-all-start.3) | async-done | bytes 131104 | tf_op jit(solution)/shard_map/all_to_all | solution.py:28
  183.8 2.8 %shard_map.133 = (f32[512,256]{1,0:T(8,128)S(1)}, bf16[8,512,256]{2,1,0:T(8,128)(2,1)S(1)}) custom-call(s32[3]{0:T(128)S(1)} %pad_add_fusion.place, bf16[8,256,256]{2,1,0:T(8,128)(2,1)S(1)} %bitcast.89, f32[16,256]{1,0:T(8,128)S(1)} %shard_map.132.known_mine, f32[16,256]{1,0:T(8,128)S(1)} %collective-permute-done.9.known_other, ...), custom_call_target="tpu_custom_call" | custom-call | tf_op jit(solution)/shard_map/pallas_call | solution.py:48
  188.7 3.7 %all-to-all-start.4 = ((f32[16,32,256]{2,1,0:T(8,128)}), f32[16,32,256]{2,1,0:T(8,128)S(1)}, u32[]{:S(2)}, u32[]{:S(2)}) async-start(f32[16,32,256]{2,1,0:T(8,128)} %bitcast.92), calls=%async_computation.5 | async-start | bytes 1048576 | tf_op jit(solution)/shard_map/all_to_all | solution.py:327
  192.5 11.0 %all-to-all-done.4 = f32[16,32,256]{2,1,0:T(8,128)S(1)} async-done(((f32[16,32,256]{2,1,0:T(8,128)}), f32[16,32,256]{2,1,0:T(8,128)S(1)}, u32[]{:S(2)}, u32[]{:S(2)}) %all-to-all-start.4) | async-done | bytes 524320 | tf_op jit(solution)/shard_map/all_to_all | solution.py:327
  208.5 2.3 multiply_reduce_fusion.1
  211.9 4.2 %all-to-all-start.5 = ((f32[8,2,4864]{2,1,0:T(2,128)}), f32[8,2,4864]{2,1,0:T(2,128)S(1)}, u32[]{:S(2)}, u32[]{:S(2)}) async-start(f32[8,2,4864]{2,1,0:T(2,128)} %pad_maximum_fusion), calls=%async_computation.6 | async-start | bytes 622592 | tf_op jit(solution)/shard_map/all_to_all | solution.py:360
  217.7 2.5 shard_map.134
  220.2 5.1 %convolution_convert_fusion.1 = bf16[4096,256]{1,0:T(8,128)(2,1)} fusion(bf16[512,4096]{1,0:T(8,128)(2,1)} %fusion.2, pred[512]{0:T(512)(128)(4,1)S(1)} %copy-done.27, bf16[1,512,4096]{2,1,0:T(8,128)(2,1)} %param.19, s32[]{:T(128)S(6)} %select_n.167, s32[32]{0:T(128)S(1)} %copy-done.25, f32[32,256]{1,0:T(8,128)S(1)} %convolution_add_fusion.2), kind=kOutput, calls=%fused_computation.7 | convolution fusion | flops 1083465728 | bytes 6587012 | tf_op jit(solution)/shard_map/dot_general | solution.py:341
  225.4 4.1 %all-to-all-done.5 = f32[8,2,4864]{2,1,0:T(2,128)S(1)} async-done(((f32[8,2,4864]{2,1,0:T(2,128)}), f32[8,2,4864]{2,1,0:T(2,128)S(1)}, u32[]{:S(2)}, u32[]{:S(2)}) %all-to-all-start.5) | async-done | bytes 311328 | tf_op jit(solution)/shard_map/all_to_all | solution.py:360
  230.0 10.6 %all_to_all.35 = bf16[8,2,4864]{2,1,0:T(2,128)(2,1)S(1)} all-to-all(bf16[8,2,4864]{2,1,0:T(2,128)(2,1)S(1)} %broadcast_in_dim.112), channel_id=1, replica_groups=mesh['pipe'=16,'z'=8,'core'=2] {'z'}, dimensions={0} | all-to-all | bytes 311296 | tf_op jit(solution)/shard_map/all_to_all | solution.py:28
  240.6 2.4 collective-permute-start.12
  245.3 5.6 %fusion.4 = bf16[1,512,4096]{2,1,0:T(8,128)(2,1)} fusion(bf16[512,4096]{1,0:T(8,128)(2,1)} %all-gather.4.cloned.1.call-done, bf16[32,4096]{1,0:T(8,128)(2,1)S(1)} %reshape.198, pred[512]{0:T(512)(128)(4,1)S(1)} %copy-done.27, s32[32]{0:T(128)S(1)} %copy-done.25), kind=kOutput, calls=%fused_computation.9 | convolution fusion | flops 138428416 | bytes 8651392 | tf_op jit(solution)/shard_map/dot_general | solution.py:377
  (169 shorter events, 49.8 us)
Async XLA Ops:
  7.2 13.7 %copy-start = (s32[16,32]{1,0:T(8,128)S(1)}, s32[16,32]{1,0:T(8,128)}, u32[]{:S(2)}) copy-start(s32[16,32]{1,0:T(8,128)} %param.15) | copy-start | bytes 6148
  9.4 36.0 %collective-permute-start = (bf16[256,256]{1,0:T(8,128)(2,1)S(1)}, bf16[256,256]{1,0:T(8,128)(2,1)S(1)}, u32[]{:S(2)}, u32[]{:S(2)}) collective-permute-start(bf16[256,256]{1,0:T(8,128)(2,1)S(1)} %get-tuple-element.63), channel_id=1, source_target_pairs={{0,2},{2,4},{4,6},{6,8},{8,10},{10,12},{12,14},{14,0},{1,3},{3,5},... | collective-permute-start | bytes 393224 | tf_op jit(solution)/shard_map/ppermute | solution.py:37
  11.8 34.0 %collective-permute-start.1 = (bf16[256,256]{1,0:T(8,128)(2,1)S(1)}, bf16[256,256]{1,0:T(8,128)(2,1)S(1)}, u32[]{:S(2)}, u32[]{:S(2)}) collective-permute-start(bf16[256,256]{1,0:T(8,128)(2,1)S(1)} %get-tuple-element.62), channel_id=1, source_target_pairs={{0,14},{2,0},{4,2},{6,4},{8,6},{10,8},{12,10},{14,12},{1,15},{3,1}... | collective-permute-start | bytes 393224 | tf_op jit(solution)/shard_map/ppermute | solution.py:37
  15.8 41.9 %collective-permute-start.3 = (bf16[256,256]{1,0:T(8,128)(2,1)S(1)}, bf16[256,256]{1,0:T(8,128)(2,1)S(1)}, u32[]{:S(2)}, u32[]{:S(2)}) collective-permute-start(bf16[256,256]{1,0:T(8,128)(2,1)S(1)} %get-tuple-element.61), channel_id=1, source_target_pairs={{0,4},{2,6},{4,8},{6,10},{8,12},{10,14},{12,0},{14,2},{1,5},{3,7},... | collective-permute-start | bytes 393224 | tf_op jit(solution)/shard_map/ppermute | solution.py:37
  15.8 41.9 %collective-permute-start.4 = (bf16[256,256]{1,0:T(8,128)(2,1)S(1)}, bf16[256,256]{1,0:T(8,128)(2,1)S(1)}, u32[]{:S(2)}, u32[]{:S(2)}) collective-permute-start(bf16[256,256]{1,0:T(8,128)(2,1)S(1)} %get-tuple-element.60), channel_id=1, source_target_pairs={{0,12},{2,14},{4,0},{6,2},{8,4},{10,6},{12,8},{14,10},{1,13},{3,15... | collective-permute-start | bytes 393224 | tf_op jit(solution)/shard_map/ppermute | solution.py:37
  19.4 32.7 %collective-permute-start.2 = (bf16[4096,256]{1,0:T(8,128)(2,1)}, bf16[4096,256]{1,0:T(8,128)(2,1)}, u32[]{:S(2)}, u32[]{:S(2)}) collective-permute-start(bf16[4096,256]{1,0:T(8,128)(2,1)} %bitcast.96), channel_id=1, source_target_pairs={{0,1},{1,0},{2,3},{3,2},{4,5},{5,4},{6,7},{7,6},{8,9},{9,8},{10,11... | collective-permute-start | bytes 6291464 | tf_op jit(solution)/shard_map/ppermute | solution.py:32
  25.3 14.3 %copy-start.28 = (f32[32]{0:T(128)}, f32[32]{0:T(128)S(1)}, u32[]{:S(2)}) copy-start(f32[32]{0:T(128)S(1)} %add_rsqrt_fusion.2) | copy-start | bytes 388
  45.4 12.3 %copy-start.20 = (bf16[32,256]{1,0:T(8,128)(2,1)}, bf16[32,256]{1,0:T(8,128)(2,1)S(1)}, u32[]{:S(2)}) copy-start(bf16[32,256]{1,0:T(8,128)(2,1)S(1)} %fusion.11) | copy-start | bytes 49156
  45.4 13.4 %collective-permute-start.5 = (bf16[256,256]{1,0:T(8,128)(2,1)S(1)}, bf16[256,256]{1,0:T(8,128)(2,1)S(1)}, u32[]{:S(2)}, u32[]{:S(2)}) collective-permute-start(bf16[256,256]{1,0:T(8,128)(2,1)S(1)} %get-tuple-element.59), channel_id=1, source_target_pairs={{0,6},{2,8},{4,10},{6,12},{8,14},{10,0},{12,2},{14,4},{1,7},{3,9},... | collective-permute-start | bytes 393224 | tf_op jit(solution)/shard_map/ppermute | solution.py:37
  46.5 15.7 %all-to-all-start = ((bf16[8,32,256]{2,1,0:T(8,128)(2,1)}), bf16[8,32,256]{2,1,0:T(8,128)(2,1)S(1)}, u32[]{:S(2)}, u32[]{:S(2)}) async-start(bf16[8,32,256]{2,1,0:T(8,128)(2,1)} %broadcast_in_dim.63), calls=%async_computation | async-start | bytes 262144 | tf_op jit(solution)/shard_map/all_to_all | solution.py:28
  52.0 69.8 %reduce-scatter.2.cloned.1.call-start = ((), (), s32[]{:S(2)}) async-start(), calls=%async_computation.8 | async-start | bytes 2359296 | tf_op jit(solution)/shard_map/reduce_scatter | solution.py:247
  57.7 11.8 %copy-start.8 = (bf16[256,256]{1,0:T(8,128)(2,1)}, bf16[256,256]{1,0:T(8,128)(2,1)S(1)}, u32[]{:S(2)}) copy-start(bf16[256,256]{1,0:T(8,128)(2,1)S(1)} %collective-permute-done.3.refs_2_) | copy-start | bytes 393220
  57.7 11.8 %copy-start.10 = (bf16[256,256]{1,0:T(8,128)(2,1)}, bf16[256,256]{1,0:T(8,128)(2,1)S(1)}, u32[]{:S(2)}) copy-start(bf16[256,256]{1,0:T(8,128)(2,1)S(1)} %collective-permute-done.4.refs_6_) | copy-start | bytes 393220
  71.1 38.3 %all-to-all-start.1 = ((bf16[16,8,32,256]{3,2,1,0:T(8,128)(2,1)}), bf16[16,8,32,256]{3,2,1,0:T(8,128)(2,1)S(1)}, u32[]{:S(2)}, u32[]{:S(2)}) async-start(bf16[16,8,32,256]{3,2,1,0:T(8,128)(2,1)} %broadcast_in_dim.100), calls=%async_computation.1 | async-start | bytes 4194304 | tf_op jit(solution)/shard_map/all_to_all | solution.py:28
  77.9 78.1 %all-gather.6.cloned.1.call-start = ((), (), s32[]{:S(2)}) async-start(), calls=%async_computation.10 | async-start | bytes 1179648 | tf_op jit(solution)/shard_map/all_gather | solution.py:287
  77.9 31.5 %collective-permute-start.6 = (bf16[256,256]{1,0:T(8,128)(2,1)}, bf16[256,256]{1,0:T(8,128)(2,1)}, u32[]{:S(2)}, u32[]{:S(2)}) collective-permute-start(bf16[256,256]{1,0:T(8,128)(2,1)} %get-tuple-element.57), channel_id=1, source_target_pairs={{0,8},{2,10},{4,12},{6,14},{8,0},{10,2},{12,4},{14,6},{1,9},{3,11}... | collective-permute-start | bytes 393224 | tf_op jit(solution)/shard_map/ppermute | solution.py:37
  79.3 30.1 %collective-permute-start.7 = (bf16[256,256]{1,0:T(8,128)(2,1)}, bf16[256,256]{1,0:T(8,128)(2,1)}, u32[]{:S(2)}, u32[]{:S(2)}) collective-permute-start(bf16[256,256]{1,0:T(8,128)(2,1)} %get-tuple-element.56), channel_id=1, source_target_pairs={{0,10},{2,12},{4,14},{6,0},{8,2},{10,4},{12,6},{14,8},{1,11},{3,13... | collective-permute-start | bytes 393224 | tf_op jit(solution)/shard_map/ppermute | solution.py:37
  115.6 3.3 %collective-permute-start.8 = (f32[256,384]{1,0:T(8,128)}, f32[256,384]{1,0:T(8,128)}, u32[]{:S(2)}, u32[]{:S(2)}) collective-permute-start(f32[256,384]{1,0:T(8,128)} %get-tuple-element.39), channel_id=1, source_target_pairs={{0,1},{1,0},{2,3},{3,2},{4,5},{5,4},{6,7},{7,6},{8,9},{9,8},{10,11... | collective-permute-start | bytes 1179656 | tf_op jit(solution)/shard_map/ppermute | solution.py:32
  125.3 37.5 %all-to-all-start.2 = ((f32[8,8,256]{2,1,0:T(8,128)}), f32[8,8,256]{2,1,0:T(8,128)S(1)}, u32[]{:S(2)}, u32[]{:S(2)}) async-start(f32[8,8,256]{2,1,0:T(8,128)} %broadcast_in_dim.104), calls=%async_computation.2 | async-start | bytes 131072 | tf_op jit(solution)/shard_map/all_to_all | solution.py:28
  128.7 74.8 %copy-start.21 = (bf16[32,256]{1,0:T(8,128)(2,1)S(1)}, bf16[32,256]{1,0:T(8,128)(2,1)}, u32[]{:S(2)}) copy-start(bf16[32,256]{1,0:T(8,128)(2,1)} %copy-done.20) | copy-start | bytes 49156
  128.7 74.8 %copy-start.25 = (s32[32]{0:T(128)S(1)}, s32[32]{0:T(128)}, u32[]{:S(2)}) copy-start(s32[32]{0:T(128)} %copy-done.24) | copy-start | bytes 388
  128.7 116.6 %all-gather.4.cloned.1.call-start = ((), (), s32[]{:S(2)}) async-start(), calls=%async_computation.9 | async-start | bytes 4456448 | tf_op jit(solution)/shard_map/all_gather | solution.py:315
  156.0 26.5 %collective-permute-start.10 = (bf16[8,256,256]{2,1,0:T(8,128)(2,1)}, bf16[8,256,256]{2,1,0:T(8,128)(2,1)}, u32[]{:S(2)}, u32[]{:S(2)}) collective-permute-start(bf16[8,256,256]{2,1,0:T(8,128)(2,1)} %bitcast.90), channel_id=1, source_target_pairs={{0,1},{1,0},{2,3},{3,2},{4,5},{5,4},{6,7},{7,6},{8,9},{9,8},{10,11... | collective-permute-start | bytes 3145736 | tf_op jit(solution)/shard_map/ppermute | solution.py:32
  166.0 13.8 %all-to-all-start.3 = ((f32[16,8,256]{2,1,0:T(8,128)}), f32[16,8,256]{2,1,0:T(8,128)S(1)}, u32[]{:S(2)}, u32[]{:S(2)}) async-start(f32[16,8,256]{2,1,0:T(8,128)} %broadcast_in_dim.105), calls=%async_computation.4 | async-start | bytes 262144 | tf_op jit(solution)/shard_map/all_to_all | solution.py:28
  180.4 2.1 collective-permute-start.9
  188.7 19.7 %copy-start.17 = (f32[32,4096]{1,0:T(8,128)S(1)}, f32[32,4096]{1,0:T(8,128)}, u32[]{:S(2)}) copy-start(f32[32,4096]{1,0:T(8,128)} %copy-done.16) | copy-start | bytes 1572868
  188.7 22.2 %copy-start.22 = (f32[4096]{0:T(1024)S(1)}, f32[4096]{0:T(1024)}, u32[]{:S(2)}) copy-start(f32[4096]{0:T(1024)} %get-tuple-element.46) | copy-start | bytes 49156
  188.7 14.8 %all-to-all-start.4 = ((f32[16,32,256]{2,1,0:T(8,128)}), f32[16,32,256]{2,1,0:T(8,128)S(1)}, u32[]{:S(2)}, u32[]{:S(2)}) async-start(f32[16,32,256]{2,1,0:T(8,128)} %bitcast.92), calls=%async_computation.5 | async-start | bytes 1048576 | tf_op jit(solution)/shard_map/all_to_all | solution.py:327
  192.4 23.6 %copy-start.29 = (f32[32]{0:T(128)S(1)}, f32[32]{0:T(128)}, u32[]{:S(2)}) copy-start(f32[32]{0:T(128)} %copy-done.28) | copy-start | bytes 388
  204.7 3.7 %collective-permute-start.11 = (f32[16,256]{1,0:T(8,128)S(1)}, f32[16,256]{1,0:T(8,128)S(1)}, u32[]{:S(2)}, u32[]{:S(2)}) collective-permute-start(f32[16,256]{1,0:T(8,128)S(1)} %constant_dynamic-slice_fusion.4), channel_id=1, source_target_pairs={{0,1},{1,0},{2,3},{3,2},{4,5},{5,4},{6,7},{7,6},{8,9},{9,8},{10,11... | collective-permute-start | bytes 49160 | tf_op jit(solution)/shard_map/ppermute | solution.py:32
  211.9 17.6 %all-to-all-start.5 = ((f32[8,2,4864]{2,1,0:T(2,128)}), f32[8,2,4864]{2,1,0:T(2,128)S(1)}, u32[]{:S(2)}, u32[]{:S(2)}) async-start(f32[8,2,4864]{2,1,0:T(2,128)} %pad_maximum_fusion), calls=%async_computation.6 | async-start | bytes 622592 | tf_op jit(solution)/shard_map/all_to_all | solution.py:360
  240.6 3.4 %collective-permute-start.12 = (bf16[8,2,4864]{2,0,1:T(8,128)(2,1)S(1)}, bf16[8,2,4864]{2,0,1:T(8,128)(2,1)S(1)}, u32[]{:S(2)}, u32[]{:S(2)}) collective-permute-start(bf16[8,2,4864]{2,0,1:T(8,128)(2,1)S(1)} %copy.78), channel_id=1, source_target_pairs={{0,1},{1,0},{2,3},{3,2},{4,5},{5,4},{6,7},{7,6},{8,9},{9,8},{10,11... | collective-permute-start | bytes 466952 | tf_op jit(solution)/shard_map/ppermute | solution.py:32
  (20 other events, 78.1 us)
Sparse Core Ops, SparseCore 0:
  69.6 47.1 reduce-scatter.1
  123.7 32.2 all-gather.5
  163.0 41.0 all-gather.3

commit v5 on v1

v5 whole, which is shorter than its diff:
```python
import functools

import jax
import jax.numpy as jnp
from jax import lax
from jax.experimental import pallas as pl
from jax.experimental.pallas import tpu as pltpu
from jax.sharding import Mesh, PartitionSpec as P

F32 = jnp.float32
BF16 = jnp.bfloat16
EPSILON = 1e-05
VMEM = 32 * 1024 * 1024


def rounded(values):
    return lax.reduce_precision(values, 8, 7)


def split3(values):
    first = rounded(values)
    rest = values - first
    second = rounded(rest)
    return [first, second, rest - second]


def spread(values, axis, count):
    return lax.all_to_all(jnp.broadcast_to(values[None], (count,) + values.shape), axis, 0, 0)


def swap(values):
    return lax.ppermute(values, "core", [(0, 1), (1, 0)])


def pair(mine, other, core, axis):
    first = jnp.where(core == 0, mine, other)
    second = jnp.where(core == 0, other, mine)
    return jnp.concatenate([first, second], axis=axis)


def kernel_call(body, out, *operands):
    return pl.pallas_call(
        body,
        out_shape=out,
        in_specs=[
            pl.BlockSpec(memory_space=pltpu.SMEM if i == 0 else pltpu.VMEM) for i in range(len(operands))
        ],
        out_specs=jax.tree.map(lambda _: pl.BlockSpec(memory_space=pltpu.VMEM), out),
        compiler_params=pltpu.CompilerParams(vmem_limit_bytes=VMEM),
    )(*operands)


def vmem_call(body, out, *operands):
    return pl.pallas_call(
        body,
        out_shape=out,
        compiler_params=pltpu.CompilerParams(vmem_limit_bytes=VMEM),
    )(*operands)


def shape(dims, dtype):
    return jax.ShapeDtypeStruct(dims, dtype)


def after(values, done):
    return lax.optimization_barrier((values, done))[0]


def pieces3(values):
    first = values.astype(BF16).astype(F32)
    rest = values - first
    second = rest.astype(BF16).astype(F32)
    return [first, second, rest - second]


def logits_kernel(half, mine, other, gain_mine, gain_other, head_mine, head_other, out):
    squares = 0.0
    part = 0.0
    for row, gain, head in ((mine, gain_mine, head_mine), (other, gain_other, head_other)):
        row = row[...].reshape(-1, row.shape[-1]).astype(F32)
        squares += jnp.sum(row * row, axis=-1, keepdims=True)
        part += lax.dot_general(
            (row * gain[...]).astype(BF16), head[...], (((1,), (1,)), ((), ())), preferred_element_type=F32
        )
    column = lax.broadcasted_iota(jnp.int32, part.shape, 1)
    for i, piece in enumerate(pieces3(squares)):
        part = jnp.where(column == half + i, piece, part)
    out[...] = part.astype(BF16).reshape(out.shape)


def softmax_kernel(width, half, vocab, place, parts, targets, logits_out, stats):
    core, start = place[0], place[1]
    total = parts[0].astype(F32)
    for i in range(1, parts.shape[0]):
        total += parts[i].astype(F32)
    inv = lax.rsqrt(jnp.sum(total[:, half : half + 3], axis=-1, keepdims=True) / width + EPSILON)
    logits = total * inv
    logits_out[...] = logits
    column = lax.broadcasted_iota(jnp.int32, logits.shape, 1)
    live = (column < half) & (column + core * half < vocab)
    top = jnp.max(jnp.where(live, logits, -jnp.inf), axis=-1, keepdims=True)
    shifted = jnp.where(live, logits - top, -jnp.inf)
    expo = jnp.exp(shifted)
    hit = live & (column == targets[...] - start)
    values = [
        top,
        jnp.sum(expo, axis=-1, keepdims=True),
        jnp.sum(jnp.where(live, expo * shifted, 0.0), axis=-1, keepdims=True),
        jnp.sum(jnp.where(hit, logits, 0.0), axis=-1, keepdims=True),
        inv,
    ]
    lane = lax.broadcasted_iota(jnp.int32, (logits.shape[0], 128), 1)
    table = jnp.zeros(lane.shape, F32)
    for i, value in enumerate(values):
        table = jnp.where(lane == i, value, table)
    table = jnp.concatenate([table, jnp.zeros((128 - table.shape[0], 128), F32)])
    stats[...] = table.T[: stats.shape[0]]


def dlogits_kernel(width, half, vocab, place, logits_in, targets, weights, stats, own, out):
    core, start = place[0], place[1]
    tops, totals, alongs, hits = [stats[:, i] for i in range(4)]
    top = jnp.max(tops, axis=0, keepdims=True)
    lower = jnp.exp(tops - top)
    total = jnp.sum(totals * lower, axis=0, keepdims=True)
    along = jnp.sum((alongs + (tops - top) * totals) * lower, axis=0, keepdims=True)
    target = jnp.sum(hits, axis=0, keepdims=True) - top
    weight = weights[...]
    mean = weight * (along / total - target) / width
    table = jnp.concatenate([top, total, weight, mean, own[4:5], jnp.zeros((3, 128), F32)]).T
    rows = logits_in.shape[0]
    top, total, weight, mean, inv = [table[:rows, i : i + 1] for i in range(5)]
    column = lax.broadcasted_iota(jnp.int32, logits_in.shape, 1)
    live = (column < half) & (column + core * half < vocab)
    hit = column == targets[...] - start
    probs = jnp.exp(jnp.where(live, logits_in[...] - top, -jnp.inf)) / total
    grad = jnp.where(live, weight * (probs - jnp.where(hit, 1.0, 0.0)), 0.0)
    for i, piece in enumerate(pieces3(inv) + pieces3(mean)):
        grad = jnp.where(column == half + i, piece, grad)
    out[...] = jnp.broadcast_to(grad.astype(BF16)[None], out.shape)


def exit_kernel(dl_mine, dl_other, head_mine, head_rest, part):
    rows = part.shape[0] * part.shape[1]
    total = jnp.dot(dl_mine[...].reshape(rows, -1), head_mine[...], preferred_element_type=F32)
    total += jnp.dot(dl_other[...].reshape(rows, -1), head_rest[...], preferred_element_type=F32)
    part[...] = total.reshape(part.shape)


def head_kernel(half, place, mine, gain, dl_mine, dl_other, out):
    core = place[0]
    row = mine[...].reshape(-1, mine.shape[-1]).astype(F32)
    low = dl_mine[...].reshape(row.shape[0], -1)
    high = dl_other[...].reshape(row.shape[0], -1)
    inv = jnp.sum(low[:, half : half + 3].astype(F32), axis=-1, keepdims=True)
    normed = (row * inv * gain[...]).astype(BF16)
    over_rows = (((0,), (0,)), ((), ()))
    low = lax.dot_general(low, normed, over_rows, preferred_element_type=F32)
    high = lax.dot_general(high, normed, over_rows, preferred_element_type=F32)
    out[:half, :] = jnp.where(core == 0, low, high)[:half].astype(BF16)
    out[half:, :] = jnp.where(core == 0, high, low)[: out.shape[0] - half].astype(BF16)


def first_kernel(chunks, place, seg, ids, gain, weight, unit_out, inv_out, hidden_out, held):
    step = pl.program_id(0)
    token = lax.broadcasted_iota(jnp.int32, (ids.shape[0], seg.shape[0]), 1)
    pick = (ids[...] == token).astype(BF16)
    chunk = seg.shape[1]
    held[:, pl.ds(pl.multiple_of(step * chunk, chunk), chunk)] = jnp.dot(
        pick, seg[...], preferred_element_type=F32
    )

    @pl.when(step == chunks - 1)
    def _():
        rows = held[...]
        inv = lax.rsqrt(jnp.mean(rows * rows, axis=-1, keepdims=True) + EPSILON)
        unit = rows * inv
        unit_out[...] = unit
        inv_out[...] = jnp.broadcast_to(inv, inv_out.shape)
        update = jnp.dot((unit * gain[...]).astype(BF16), weight[...], preferred_element_type=F32)
        slab = weight.shape[1]
        own = held[:, pl.ds(pl.multiple_of(place[2] * slab, slab), slab)]
        hidden = (own + update.astype(BF16).astype(F32)).astype(BF16)
        hidden_out[...] = jnp.broadcast_to(hidden[None], hidden_out.shape)


def row_kernel(at, place, got, hidden, extra, gain, grad_rows, mine, other, whole):
    core = place[0]
    total = got[0]
    for i in range(1, got.shape[0]):
        total += got[i]
    inv = jnp.sum(extra[:, at : at + 3].astype(F32), axis=-1, keepdims=True)
    mean = jnp.sum(extra[:, at + 3 : at + 6].astype(F32), axis=-1, keepdims=True)
    back = (total * gain[...] - hidden[...].astype(F32) * inv * mean) * inv
    rows = grad_rows[...] + back
    whole[...] = rows.astype(BF16)
    half = mine.shape[0]
    mine[...] = jnp.where(core == 0, rows[:half], rows[half:])
    other[...] = jnp.where(core == 0, rows[half:], rows[:half])


def send_kernel(place, mine, other, weight, weight_other, unit, gain_part, out):
    core = place[0]
    columns = (((1,), (1,)), ((), ()))
    part = lax.dot_general(mine[...].astype(BF16), weight[...], columns, preferred_element_type=F32)
    part += lax.dot_general(other[...].astype(BF16), weight_other[...], columns, preferred_element_type=F32)
    gain = gain_part[...] + jnp.sum(part * unit[...], axis=0, keepdims=True)
    low = jnp.where(core == 0, mine[...], other[...])
    high = jnp.where(core == 0, other[...], mine[...])
    count, share, _ = out.shape
    width, slab = weight.shape
    piece = width // (count * share)
    for i in range(count):
        rows = slice(i * share, (i + 1) * share)
        out[i, :, :width] = part[rows]
        out[i, :, width : width + slab] = low[rows]
        out[i, :, width + slab : width + 2 * slab] = high[rows]
        for j in range(share):
            at = (i * share + j) * piece
            out[i, j : j + 1, width + 2 * slab :] = gain[:, at : at + piece]


def share_kernel(slabs, got, gain, unit, inv, out):
    total = got[0]
    for i in range(1, got.shape[0]):
        total += got[i]
    width = gain.shape[1]
    residual = jnp.concatenate([got[i, :, width : width + slabs] for i in range(got.shape[0])], axis=1)
    unit_grad = total[:, :width] * gain[...]
    centre = jnp.mean(unit_grad * unit[...], axis=-1, keepdims=True)
    rows = residual + (unit_grad - unit[...] * centre) * inv[...]
    whole = jnp.concatenate([rows] + pieces3(total[:, width + slabs :]), axis=1)
    out[...] = jnp.broadcast_to(whole.astype(BF16)[None], out.shape)


def last_kernel(main, rows, ids, out):
    count = main.shape[0]
    token = lax.broadcasted_iota(jnp.int32, (count, ids.shape[1]), 0) + pl.program_id(0) * count
    put = token == ids[...]
    placed = jnp.dot(put.astype(BF16), rows[...], preferred_element_type=F32).astype(BF16)
    found = jnp.max(put.astype(F32), axis=-1, keepdims=True) > 0.0
    out[...] = jnp.where(found, placed, main[...])


def local(
    segment_in,
    layer_weight,
    layer_gain,
    final_gain,
    head_weight,
    exit_rows,
    exit_count,
    exit_targets,
    exit_scale,
    out_grad,
):
    pipe = lax.axis_index("pipe")
    core = lax.axis_index("core")
    z = lax.axis_index("z")
    pipes = lax.axis_size("pipe")
    zs = lax.axis_size("z")
    block = z * 2 + core
    seg = segment_in[0]
    weight = layer_weight[0]
    gain = layer_gain[0]
    grad = out_grad[0]
    tokens, width = seg.shape
    slab = weight.shape[1]
    exits = exit_rows.shape[1]
    rows_all = pipes * exits
    vocab_part = head_weight.shape[0]
    half = -(-vocab_part // 32) * 16
    padded = -(-(half + 6) // 128) * 128
    place = jnp.stack([core, pipe * vocab_part + core * half, block]).astype(jnp.int32)

    weight_other = swap(weight)
    halves = jnp.pad(head_weight, ((0, 2 * half - vocab_part), (0, 0))).reshape(2, half, slab)
    halves = jnp.pad(halves, ((0, 0), (0, padded - half), (0, 0)))
    head_mine = lax.dynamic_index_in_dim(halves, core, 0, keepdims=False)
    head_rest = lax.dynamic_index_in_dim(halves, 1 - core, 0, keepdims=False)
    head_other = swap(head_rest)

    my_rows = exit_rows[pipe]
    pick = (my_rows[:, None] == jnp.arange(tokens, dtype=jnp.int32)[None, :]).astype(BF16)
    chunks = 8
    whole = lambda *dims: pl.BlockSpec(dims, lambda i: (0,) * len(dims))
    row_unit, row_inv, hidden_copies = pl.pallas_call(
        functools.partial(first_kernel, chunks),
        grid=(chunks,),
        in_specs=[
            pl.BlockSpec(memory_space=pltpu.SMEM),
            pl.BlockSpec((tokens, width // chunks), lambda i: (0, i)),
            whole(exits, 1),
            whole(1, width),
            whole(width, slab),
        ],
        out_specs=[whole(exits, width), whole(exits, 128), whole(pipes, exits, slab)],
        out_shape=[
            shape((exits, width), F32),
            shape((exits, 128), F32),
            shape((pipes, exits, slab), BF16),
        ],
        scratch_shapes=[pltpu.VMEM((exits, width), F32)],
        compiler_params=pltpu.CompilerParams(vmem_limit_bytes=VMEM),
    )(place, seg, my_rows[:, None], gain[None], weight)
    hidden = hidden_copies[0]

    all_mine = lax.all_to_all(hidden_copies, "pipe", 0, 0)
    held = tokens // (zs * 2)
    on_columns = (((1,), (1,)), ((), ()))
    over_rows = (((0,), (0,)), ((), ()))

    def of_core(values):
        grouped = values.reshape((zs, 2, held) + values.shape[1:])
        return lax.dynamic_index_in_dim(grouped, core, 1, keepdims=False).reshape((zs * held,) + values.shape[1:])

    core_grad = of_core(grad)
    main_part = lax.dot_general(
        lax.dynamic_slice_in_dim(core_grad, block * slab, slab, 1), weight, on_columns, preferred_element_type=F32
    ) + lax.dot_general(
        lax.dynamic_slice_in_dim(core_grad, (z * 2 + 1 - core) * slab, slab, 1),
        weight_other,
        on_columns,
        preferred_element_type=F32,
    )
    main_sent = main_part.astype(BF16)
    all_mine, main_part, main_sent = lax.optimization_barrier((all_mine, main_part, main_sent))
    main_grad = lax.psum_scatter(main_sent, "z", scatter_dimension=0, tiled=True)
    all_other = swap(all_mine)
    gain_mine = lax.dynamic_slice_in_dim(final_gain, block * slab, slab, 0)[None]
    gain_other = lax.dynamic_slice_in_dim(final_gain, (z * 2 + 1 - core) * slab, slab, 0)[None]
    own = rows_all // zs
    part = vmem_call(
        functools.partial(logits_kernel, half),
        shape((zs, own, padded), BF16),
        all_mine,
        all_other,
        gain_mine,
        gain_other,
        head_mine,
        head_other,
    )
    parts = lax.all_to_all(part, "z", 0, 0)

    is_exit = jnp.any(pick > 0, axis=0)
    core_in = of_core(after(seg, part)).astype(F32)
    core_inv = lax.rsqrt(jnp.mean(core_in * core_in, axis=-1, keepdims=True) + EPSILON)
    core_inv = jnp.where(of_core(is_exit)[:, None], 0.0, core_inv)
    gain_part = jnp.sum(main_part * (core_in * core_inv), axis=0)
    grad_slab = lax.dynamic_slice_in_dim(after(grad, part), block * slab, slab, 1)
    grad_rows = jnp.dot(pick, grad_slab, preferred_element_type=F32)
    core_rows = exits // 2
    core_unit = lax.dynamic_slice_in_dim(row_unit, core * core_rows, core_rows, 0)
    all_targets = exit_targets.reshape(rows_all, 1)
    targets = lax.dynamic_slice_in_dim(all_targets, z * own, own, 0)
    slot = jnp.arange(exits, dtype=jnp.int32)[None, :]
    weights = jnp.where(slot < exit_count[:, None], exit_scale[:, None], F32(0.0)).reshape(1, rows_all)
    weights = jnp.pad(lax.dynamic_slice_in_dim(weights, z * own, own, 1), ((0, 0), (0, 128 - own)))
    parts, gain_part, grad_rows = lax.optimization_barrier((parts, gain_part, grad_rows))

    logits, stats = kernel_call(
        functools.partial(softmax_kernel, width, half, vocab_part),
        [shape((own, padded), F32), shape((8, 128), F32)],
        place,
        parts,
        targets,
    )
    all_stats = spread(jnp.stack([stats, swap(stats)]), "pipe", pipes).reshape(pipes * 2, 8, 128)
    dlogits = kernel_call(
        functools.partial(dlogits_kernel, width, half, vocab_part),
        shape((zs, own, padded), BF16),
        place,
        logits,
        targets,
        weights,
        all_stats,
        stats,
    )
    dl_mine = lax.all_to_all(dlogits, "z", 0, 0)

    def layer_back(norm_grad, unit, inv, residual):
        unit_grad = norm_grad * gain
        centre = jnp.mean(unit_grad * unit, axis=-1, keepdims=True)
        return (residual + (unit_grad - unit * centre) * inv).astype(BF16)

    first = block * held
    held_in = lax.dynamic_slice_in_dim(after(seg, dlogits), first, held, 0).astype(F32)
    held_grad = lax.dynamic_slice_in_dim(after(grad, dlogits), first, held, 0).astype(F32)
    held_inv = lax.rsqrt(jnp.mean(held_in * held_in, axis=-1, keepdims=True) + EPSILON)
    main_out = layer_back(main_grad.astype(F32), held_in * held_inv, held_inv, held_grad)
    inputs = after(seg, dlogits).astype(F32)
    inv_rms = lax.rsqrt(jnp.mean(inputs * inputs, axis=-1, keepdims=True) + EPSILON)
    normed = (inputs * inv_rms * gain).astype(BF16)
    dl_mine, main_out, normed = lax.optimization_barrier((dl_mine, main_out, normed))
    main_all = lax.all_gather(main_out, ("z", "core"), axis=0, tiled=True)
    dl_other = swap(dl_mine)

    exit_part = vmem_call(
        exit_kernel, shape((pipes, exits, slab), F32), dl_mine, dl_other, head_mine, head_rest
    )
    exit_got = lax.all_to_all(exit_part, "pipe", 0, 0)
    head_grad = kernel_call(
        functools.partial(head_kernel, half),
        shape((vocab_part, slab), BF16),
        place,
        all_mine,
        gain_mine,
        after(dl_mine, exit_part),
        dl_other,
    )
    tail = half // 128 * 128
    extra = lax.dynamic_slice_in_dim(
        dl_mine.reshape(rows_all, padded)[:, tail : tail + 128], pipe * exits, exits, 0
    )
    exit_got, head_grad, extra = lax.optimization_barrier((exit_got, head_grad, extra))
    row_mine, row_send, row_rounded = kernel_call(
        functools.partial(row_kernel, half - tail),
        [shape((core_rows, slab), F32)] * 2 + [shape((exits, slab), BF16)],
        place,
        exit_got,
        hidden,
        extra,
        gain_mine,
        grad_rows,
    )

    put = pick.T
    share = core_rows // zs
    piece = slab * 2 // share
    send = kernel_call(
        send_kernel,
        shape((zs, share, width + 2 * slab + piece), F32),
        place,
        row_mine,
        swap(row_send),
        weight,
        weight_other,
        core_unit,
        gain_part[None],
    )
    got = lax.all_to_all(send, "z", 0, 0)
    slab_rounded = jnp.where(
        is_exit[:, None], jnp.dot(put, after(row_rounded, send), preferred_element_type=F32).astype(BF16), grad_slab
    )
    weight_grad = lax.dot_general(normed, slab_rounded, over_rows, preferred_element_type=F32).astype(BF16)
    got, weight_grad = lax.optimization_barrier((got, weight_grad))
    at = core * core_rows + z * share
    last = vmem_call(
        functools.partial(share_kernel, 2 * slab),
        shape((zs, share, width + 3 * piece), BF16),
        got,
        gain[None],
        lax.dynamic_slice_in_dim(row_unit, at, share, 0),
        lax.dynamic_slice_in_dim(row_inv[:, :1], at, share, 0),
    )
    last = lax.all_to_all(last, "z", 0, 0)
    last_other = swap(last)
    gain_grad = jnp.sum(
        (last[:, :, width:].astype(F32) + last_other[:, :, width:].astype(F32)).reshape(zs, share, 3, piece), axis=2
    ).reshape(width)
    row_out = pair(last, last_other, core, 0)[:, :, :width].reshape(exits, width)
    steps = 8
    input_grad = pl.pallas_call(
        last_kernel,
        grid=(steps,),
        in_specs=[
            pl.BlockSpec((tokens // steps, width), lambda i: (i, 0)),
            whole(exits, width),
            whole(1, exits),
        ],
        out_specs=pl.BlockSpec((tokens // steps, width), lambda i: (i, 0)),
        out_shape=shape((tokens, width), BF16),
        compiler_params=pltpu.CompilerParams(vmem_limit_bytes=VMEM),
    )(main_all, row_out, my_rows[None])
    return (input_grad[None], weight_grad[None], gain_grad[None], head_grad)


def solution(mesh):
    pipes, tensors = mesh.devices.shape
    fine = Mesh(mesh.devices.reshape(pipes, tensors // 2, 2), ("pipe", "z", "core"))
    tensor = ("z", "core")
    in_specs = (
        P("pipe", None, None),
        P("pipe", None, tensor),
        P("pipe", None),
        P(),
        P("pipe", tensor),
        P(),
        P(),
        P(),
        P(),
        P("pipe", None, None),
    )
    out_specs = (
        P("pipe", None, None),
        P("pipe", None, tensor),
        P("pipe", None),
        P("pipe", tensor),
    )
    return jax.shard_map(local, mesh=fine, in_specs=in_specs, out_specs=out_specs, check_vma=False)
```

time: 272 us -> 219 us (0.81)
  waiting for transfers between devices: 138 us -> 73.5 us
  Pallas kernels: 0 us -> 22.6 us
  matrix products: 33.8 us -> 12.3 us
  blocking collectives: 0 us -> 11.2 us
  local copies, waits for them, and re-layouts: 16.2 us -> 25.6 us
  other arithmetic: 21.9 us -> 16.3 us
  starting transfers between devices: 46.3 us -> 41.8 us
    reduce_scatter x1, waiting for transfers between devices: 56.3 us -> 0.02 us  [local(): lax.psum_scatter(main_sent, 'z', scatter_dimension=0, tiled=True)]
    pallas_call x0 -> x10, Pallas kernels: none -> 22.6 us  [the longest x5 9.96 us: kernel_call(): pl.pallas_call(body, out_shape=out, in_specs=[pl.BlockSpec(memory_space=p...]
    dot_general x14 -> x3, matrix products: 28.3 us -> 7.13 us  [the longest x1 5.09 us: local(): lax.dot_general(lax.dynamic_slice_in_dim(core_grad, (z * 2 + 1 - core) *...]
    all_to_all x3 -> x5, waiting for transfers between devices: 42.7 us -> 63.3 us  [the longest x1 31 us: local(): parts = lax.all_to_all(part, 'z', 0, 0)]
    all_gather x1 -> x0, waiting for transfers between devices: 18.5 us -> none  [local(): dl_mine = lax.all_gather(dlogits.astype(BF16), 'z', axis=0, tiled=True)]
    unnamed x37 -> x52, local copies, waits for them, and re-layouts: 1.63 us -> 15.7 us
    all_to_all x3 -> x1, waiting for transfers between devices: 20.1 us -> 6.58 us  [spread(): lax.all_to_all(jnp.broadcast_to(values[None], (count,) + values.shape), a...]
    all_to_all x0 -> x1, blocking collectives: none -> 11.2 us  [local(): last = lax.all_to_all(last, 'z', 0, 0)]
  transfers between devices with their start and end apart: 15 -> 15, of which waited for: 10 -> 8; matrix products, arithmetic and copies ran while one was open for 22% -> 18% of each run, Pallas kernels for 0% -> 8%
where the time goes in v5:
time: 219 us; the launch traced here: 218 us
  waiting for transfers between devices  73.5 us (34%)
  starting transfers between devices  41.8 us (19%)
  local copies, waits for them, and re-layouts  25.6 us (12%)
  Pallas kernels  22.6 us (10%)
  other arithmetic  16.3 us (7%)
  between operations  14.5 us (7%)
  matrix products  12.3 us (6%)
  blocking collectives  11.2 us (5%)
    all_to_all x1, waiting for transfers between devices, local(): parts = lax.all_to_all(part, 'z', 0, 0)  31 us
    all_to_all x1, waiting for transfers between devices, local(): dl_mine = lax.all_to_all(dlogits, 'z', 0, 0)  18.2 us
    unnamed x52, local copies, waits for them, and re-layouts  15.7 us
    all_to_all x1, blocking collectives, local(): last = lax.all_to_all(last, 'z', 0, 0)  11.2 us
    pallas_call x5, Pallas kernels, kernel_call(): pl.pallas_call(body, out_shape=out, in_specs=[pl.BlockSpec(memory_space=p...  9.96 us
    ppermute x7, starting transfers between devices, swap(): return lax.ppermute(values, 'core', [(0, 1), (1, 0)])  9.92 us
    all_to_all x1, starting transfers between devices, local(): parts = lax.all_to_all(part, 'z', 0, 0)  8.19 us
    all_to_all x1, waiting for transfers between devices, local(): got = lax.all_to_all(send, 'z', 0, 0)  8.16 us
  transfers between devices with their start and end apart: 15, of which 8 were waited for; matrix products, arithmetic and copies ran while one was open for 18% of the time, Pallas kernels for 8%

profile of v5, /device:TPU:1, one launch (start us, length us, event | category | flops | bytes accessed | tf_op | source)
XLA Modules:
  0.0 217.6 jit_solution(5728103472312642751)
XLA Ops:
  7.2 3.3 %collective-permute-start = (bf16[4096,256]{1,0:T(8,128)(2,1)}, bf16[4096,256]{1,0:T(8,128)(2,1)}, u32[]{:S(2)}, u32[]{:S(2)}) collective-permute-start(bf16[4096,256]{1,0:T(8,128)(2,1)} %bitcast.60), channel_id=1, source_target_pairs={{0,1},{1,0},{2,3},{3,2},{4,5},{5,4},{6,7},{7,6},{8,9},{9,8},{10,11... | collective-permute-start | bytes 6291464 | tf_op jit(solution)/shard_map/ppermute | solution.py:32
  10.7 2.2 %copy-done.1 = bf16[1,512,4096]{2,1,0:T(8,128)(2,1)S(1)} copy-done((bf16[1,512,4096]{2,1,0:T(8,128)(2,1)S(1)}, bf16[1,512,4096]{2,1,0:T(8,128)(2,1)}, u32[]{:S(2)}) %copy-start.1) | copy-done | bytes 4194328
  15.2 4.1 %shard_map.129 = (f32[32,4096]{1,0:T(8,128)S(1)}, f32[32,128]{1,0:T(8,128)S(1)}, bf16[16,32,256]{2,1,0:T(8,128)(2,1)}) custom-call(s32[3]{0:T(128)S(1)} %pad_add_fusion.place, bf16[512,4096]{1,0:T(8,128)(2,1)S(1)} %bitcast.57, s32[32,1]{1,0:T(8,128)S(1)} %copy.34.ids, f32[1,4096]{1,0:T(1,128)S(1)} %copy-done.14, bf16[4096,256]{1,0:T(8,128)(2,1)S(1)} %bitcast.61), custom_call_target="tpu_custom_call" | custom-call | tf_op jit(solution)/shard_map/pallas_call | solution.py:287
  20.1 5.0 %all-to-all-start = ((bf16[16,32,256]{2,1,0:T(8,128)(2,1)}), bf16[16,32,256]{2,1,0:T(8,128)(2,1)S(1)}, u32[]{:S(2)}, u32[]{:S(2)}) async-start(bf16[16,32,256]{2,1,0:T(8,128)(2,1)} %get-tuple-element.32), calls=%async_computation | async-start | bytes 524288 | tf_op jit(solution)/shard_map/all_to_all | solution.py:308
  26.4 1.7 constant_dynamic-slice_fusion.6
  28.9 5.1 %fusion.34 = (bf16[256,4096]{1,0:T(8,128)(2,1)}, f32[256,4096]{1,0:T(8,128)}) fusion(f32[256,4096]{1,0:T(8,128)S(1)} %fusion.21, bf16[4096,256]{1,0:T(8,128)(2,1)} %collective-permute-done.weight_other, bf16[256,4096]{1,0:T(8,128)(2,1)S(1)} %bitcast.78, s32[]{:T(128)S(6)} %select_n.84), kind=kOutput, calls=%fused_computation.70 | convolution fusion | flops 538968064 | bytes 12713988 | tf_op jit(solution)/shard_map/dot_general | solution.py:320
  37.5 1.9 shard_map.130
  40.4 8.2 %all-to-all-start.1 = ((bf16[8,64,1024]{2,1,0:T(8,128)(2,1)}), bf16[8,64,1024]{2,1,0:T(8,128)(2,1)S(1)}, u32[]{:S(2)}, u32[]{:S(2)}) async-start(bf16[8,64,1024]{2,1,0:T(8,128)(2,1)} %copy-done.9), calls=%async_computation.1 | async-start | bytes 2097152 | tf_op jit(solution)/shard_map/all_to_all | solution.py:343
  49.3 2.1 multiply_reduce_fusion
  52.8 2.1 bitcast_convert_fusion
  56.0 31.0 %all-to-all-done.1.parts = bf16[8,64,1024]{2,1,0:T(8,128)(2,1)S(1)} async-done(((bf16[8,64,1024]{2,1,0:T(8,128)(2,1)}), bf16[8,64,1024]{2,1,0:T(8,128)(2,1)S(1)}, u32[]{:S(2)}, u32[]{:S(2)}) %all-to-all-start.1) | async-done | bytes 1048608 | tf_op jit(solution)/shard_map/all_to_all | solution.py:343
  91.0 7.2 %all-to-all-start.2 = ((f32[16,2,8,128]{3,2,1,0:T(8,128)}), f32[16,2,8,128]{3,2,1,0:T(8,128)S(1)}, u32[]{:S(2)}, u32[]{:S(2)}) async-start(f32[16,2,8,128]{3,2,1,0:T(8,128)} %broadcast_in_dim.59), calls=%async_computation.2 | async-start | bytes 262144 | tf_op jit(solution)/shard_map/all_to_all | solution.py:28
  98.5 6.6 %all-to-all-done.2 = f32[16,2,8,128]{3,2,1,0:T(8,128)S(1)} async-done(((f32[16,2,8,128]{3,2,1,0:T(8,128)}), f32[16,2,8,128]{3,2,1,0:T(8,128)S(1)}, u32[]{:S(2)}, u32[]{:S(2)}) %all-to-all-start.2) | async-done | bytes 131104 | tf_op jit(solution)/shard_map/all_to_all | solution.py:28
  107.8 3.6 %all-to-all-start.3 = ((bf16[8,64,1024]{2,1,0:T(8,128)(2,1)}), bf16[8,64,1024]{2,1,0:T(8,128)(2,1)S(1)}, u32[]{:S(2)}, u32[]{:S(2)}) async-start(bf16[8,64,1024]{2,1,0:T(8,128)(2,1)} %copy-done.7), calls=%async_computation.3 | async-start | bytes 2097152 | tf_op jit(solution)/shard_map/all_to_all | solution.py:379
  111.7 3.2 %fusion = f32[512]{0:T(512)S(1)} fusion(bf16[512,4096]{1,0:T(8,128)(2,1)} %bitcast.54), kind=kLoop, calls=%fused_computation.2 | loop fusion | flops 6290944 | bytes 4196352 | tf_op jit(solution)/shard_map/reduce_sum | solution.py:392
  115.1 3.6 %fusion.2 = bf16[512,4096]{1,0:T(8,128)(2,1)} fusion(bf16[512,4096]{1,0:T(8,128)(2,1)S(1)} %bitcast.58, f32[4096]{0:T(1024)S(1)} %bitcast.65, f32[512]{0:T(512)S(1)} %add_rsqrt_fusion.1), kind=kLoop, calls=%fused_computation.4 | loop fusion | flops 8388608 | bytes 8407040 | tf_op jit(solution)/shard_map/convert_element_type | solution.py:393
  120.2 2.0 fusion.12
  122.3 18.2 %all-to-all-done.3.dl_mine = bf16[8,64,1024]{2,1,0:T(8,128)(2,1)S(1)} async-done(((bf16[8,64,1024]{2,1,0:T(8,128)(2,1)}), bf16[8,64,1024]{2,1,0:T(8,128)(2,1)S(1)}, u32[]{:S(2)}, u32[]{:S(2)}) %all-to-all-start.3) | async-done | bytes 1048608 | tf_op jit(solution)/shard_map/all_to_all | solution.py:379
  141.8 1.7 collective-permute-done.4.dl_other
  145.6 2.0 shard_map.133
  148.4 4.2 %all-to-all-start.4 = ((f32[16,32,256]{2,1,0:T(8,128)}), f32[16,32,256]{2,1,0:T(8,128)}, u32[]{:S(2)}, u32[]{:S(2)}) async-start(f32[16,32,256]{2,1,0:T(8,128)} %copy-done.10), calls=%async_computation.5 | async-start | bytes 1048576 | tf_op jit(solution)/shard_map/all_to_all | solution.py:401
  152.6 1.7 constant_dynamic-slice_fusion.2.unit
  154.4 3.2 %shard_map.134 = bf16[2000,256]{1,0:T(8,128)(2,1)} custom-call(s32[3]{0:T(128)S(1)} %pad_add_fusion.place, bf16[16,32,256]{2,1,0:T(8,128)(2,1)S(1)} %all-to-all-done.mine, f32[1,256]{1,0:T(1,128)S(1)} %bitcast.70, bf16[8,64,1024]{2,1,0:T(8,128)(2,1)S(1)} %all-to-all-done.3.dl_mine, bf16[8,64,1024]{2,1,0:T(8,128)(2,1)} %collective-permute-done.4.dl_other), custom_call_target="tpu_custom_call" | custom-call | tf_op jit(solution)/shard_map/pallas_call | solution.py:42
  157.6 5.9 %all-to-all-done.4.got = f32[16,32,256]{2,1,0:T(8,128)} async-done(((f32[16,32,256]{2,1,0:T(8,128)}), f32[16,32,256]{2,1,0:T(8,128)}, u32[]{:S(2)}, u32[]{:S(2)}) %all-to-all-start.4) | async-done | bytes 524320 | tf_op jit(solution)/shard_map/all_to_all | solution.py:401
  168.3 3.6 %shard_map.136 = f32[8,2,4864]{2,1,0:T(2,128)} custom-call(s32[3]{0:T(128)S(1)} %pad_add_fusion.place, f32[16,256]{1,0:T(8,128)S(1)} %get-tuple-element.49.mine, f32[16,256]{1,0:T(8,128)S(1)} %collective-permute-done.5.other, bf16[4096,256]{1,0:T(8,128)(2,1)S(1)} %bitcast.62, bf16[4096,256]{1,0:T(8,128)(2,1)} %collective-permute-done.weight_other, ...), custom_call_target="tpu_custom_call" | custom-call | tf_op jit(solution)/shard_map/pallas_call | solution.py:42
  171.9 3.4 %all-to-all-start.5 = ((f32[8,2,4864]{2,1,0:T(2,128)}), f32[8,2,4864]{2,1,0:T(2,128)S(1)}, u32[]{:S(2)}, u32[]{:S(2)}) async-start(f32[8,2,4864]{2,1,0:T(2,128)} %shard_map.136), calls=%async_computation.6 | async-start | bytes 622592 | tf_op jit(solution)/shard_map/all_to_all | solution.py:441
  175.4 5.1 %convolution_convert_fusion = bf16[4096,256]{1,0:T(8,128)(2,1)} fusion(bf16[512,4096]{1,0:T(8,128)(2,1)} %fusion.2, bf16[32,256]{1,0:T(8,128)(2,1)S(1)} %get-tuple-element.55, pred[512]{0:T(512)(128)(4,1)S(1)} %copy-done.25, bf16[512,4096]{1,0:T(8,128)(2,1)} %bitcast.82, s32[]{:T(128)S(6)} %select_n.83, s32[32]{0:T(128)S(1)} %fusion.38), kind=kOutput, calls=%fused_computation.6 | convolution fusion | flops 1083457536 | bytes 6570628 | tf_op jit(solution)/shard_map/dot_general | solution.py:445
  180.5 8.2 %all-to-all-done.5.got = f32[8,2,4864]{2,1,0:T(2,128)S(1)} async-done(((f32[8,2,4864]{2,1,0:T(2,128)}), f32[8,2,4864]{2,1,0:T(2,128)S(1)}, u32[]{:S(2)}, u32[]{:S(2)}) %all-to-all-start.5) | async-done | bytes 311328 | tf_op jit(solution)/shard_map/all_to_all | solution.py:441
  188.8 11.2 %all_to_all.35 = bf16[8,2,4864]{2,1,0:T(2,128)(2,1)S(1)} all-to-all(bf16[8,2,4864]{2,1,0:T(2,128)(2,1)S(1)} %shard_map.137), channel_id=1, replica_groups=mesh['pipe'=16,'z'=8,'core'=2] {'z'}, dimensions={0} | all-to-all | bytes 311296 | tf_op jit(solution)/shard_map/all_to_all | solution.py:456
  200.0 1.7 collective-permute-start.6
  204.0 2.2 %copy-done.8 = bf16[512,4096]{1,0:T(8,128)(2,1)S(1)} copy-done((bf16[512,4096]{1,0:T(8,128)(2,1)S(1)}, bf16[512,4096]{1,0:T(8,128)(2,1)}, u32[]{:S(2)}) %copy-start.8) | copy-done | bytes 4194328
  206.2 4.5 %shard_map.138 = bf16[512,4096]{1,0:T(8,128)(2,1)} custom-call(bf16[512,4096]{1,0:T(8,128)(2,1)S(1)} %copy-done.8, bf16[32,4096]{1,0:T(8,128)(2,1)S(1)} %reshape.136.rows, s32[1,32]{1,0:T(1,128)S(1)} %constant_dynamic-slice_fusion.7.ids), custom_call_target="tpu_custom_call" | custom-call | tf_op jit(solution)/shard_map/pallas_call | solution.py:463
  (117 shorter events, 33.2 us)
Async XLA Ops:
  7.2 3.3 %copy-start = (s32[16,32]{1,0:T(8,128)S(1)}, s32[16,32]{1,0:T(8,128)}, u32[]{:S(2)}) copy-start(s32[16,32]{1,0:T(8,128)} %param.15) | copy-start | bytes 6148
  7.2 21.7 %collective-permute-start = (bf16[4096,256]{1,0:T(8,128)(2,1)}, bf16[4096,256]{1,0:T(8,128)(2,1)}, u32[]{:S(2)}, u32[]{:S(2)}) collective-permute-start(bf16[4096,256]{1,0:T(8,128)(2,1)} %bitcast.60), channel_id=1, source_target_pairs={{0,1},{1,0},{2,3},{3,2},{4,5},{5,4},{6,7},{7,6},{8,9},{9,8},{10,11... | collective-permute-start | bytes 6291464 | tf_op jit(solution)/shard_map/ppermute | solution.py:32
  10.7 2.2 %copy-start.1 = (bf16[1,512,4096]{2,1,0:T(8,128)(2,1)S(1)}, bf16[1,512,4096]{2,1,0:T(8,128)(2,1)}, u32[]{:S(2)}) copy-start(bf16[1,512,4096]{2,1,0:T(8,128)(2,1)} %param.10) | copy-start | bytes 12582916
  12.9 1.6 copy-start.3
  15.2 10.0 %copy-start.20 = (bf16[2000,256]{1,0:T(8,128)(2,1)S(1)}, bf16[2000,256]{1,0:T(8,128)(2,1)}, u32[]{:S(2)}) copy-start(bf16[2000,256]{1,0:T(8,128)(2,1)} %param.14) | copy-start | bytes 3072004
  20.1 13.9 %all-to-all-start = ((bf16[16,32,256]{2,1,0:T(8,128)(2,1)}), bf16[16,32,256]{2,1,0:T(8,128)(2,1)S(1)}, u32[]{:S(2)}, u32[]{:S(2)}) async-start(bf16[16,32,256]{2,1,0:T(8,128)(2,1)} %get-tuple-element.32), calls=%async_computation | async-start | bytes 524288 | tf_op jit(solution)/shard_map/all_to_all | solution.py:308
  25.1 3.0 %copy-start.4 = (bf16[1,4096,256]{2,1,0:T(8,128)(2,1)S(1)}, bf16[1,4096,256]{2,1,0:T(8,128)(2,1)}, u32[]{:S(2)}) copy-start(bf16[1,4096,256]{2,1,0:T(8,128)(2,1)} %param.11) | copy-start | bytes 6291460
  25.1 93.8 %reduce-scatter.2.cloned.1.call-start = ((), (), s32[]{:S(2)}) async-start(), calls=%async_computation.8 | async-start | bytes 2359296 | tf_op jit(solution)/shard_map/reduce_scatter | solution.py:328
  25.4 3.5 %copy-start.11 = (bf16[1024,256]{1,0:T(8,128)(2,1)}, bf16[1024,256]{1,0:T(8,128)(2,1)S(1)}, u32[]{:S(2)}) copy-start(bf16[1024,256]{1,0:T(8,128)(2,1)S(1)} %get-tuple-element.60.head_rest) | copy-start | bytes 1572868
  25.4 12.1 %copy-start.5 = (bf16[1024,256]{1,0:T(8,128)(2,1)}, bf16[1024,256]{1,0:T(8,128)(2,1)S(1)}, u32[]{:S(2)}) copy-start(bf16[1024,256]{1,0:T(8,128)(2,1)S(1)} %get-tuple-element.61.head_mine) | copy-start | bytes 1572868
  25.4 12.1 %collective-permute-start.2 = (bf16[1024,256]{1,0:T(8,128)(2,1)S(1)}, bf16[1024,256]{1,0:T(8,128)(2,1)}, u32[]{:S(2)}, u32[]{:S(2)}) collective-permute-start(bf16[1024,256]{1,0:T(8,128)(2,1)S(1)} %get-tuple-element.60.head_rest), channel_id=1, source_target_pairs={{0,1},{1,0},{2,3},{3,2},{4,5},{5,4},{6,7},{7,6},{8,9},{9,8},{10,11... | collective-permute-start | bytes 1572872 | tf_op jit(solution)/shard_map/ppermute | solution.py:32
  28.9 6.8 %copy-start.21 = (s32[16,32]{1,0:T(8,128)S(1)}, s32[16,32]{1,0:T(8,128)}, u32[]{:S(2)}) copy-start(s32[16,32]{1,0:T(8,128)} %param.17) | copy-start | bytes 6148
  34.0 3.5 %collective-permute-start.1 = (bf16[16,32,256]{2,1,0:T(8,128)(2,1)S(1)}, bf16[16,32,256]{2,1,0:T(8,128)(2,1)}, u32[]{:S(2)}, u32[]{:S(2)}) collective-permute-start(bf16[16,32,256]{2,1,0:T(8,128)(2,1)S(1)} %all-to-all-done.mine), channel_id=1, source_target_pairs={{0,1},{1,0},{2,3},{3,2},{4,5},{5,4},{6,7},{7,6},{8,9},{9,8},{10,11... | collective-permute-start | bytes 786440 | tf_op jit(solution)/shard_map/ppermute | solution.py:32
  40.4 46.6 %all-to-all-start.1 = ((bf16[8,64,1024]{2,1,0:T(8,128)(2,1)}), bf16[8,64,1024]{2,1,0:T(8,128)(2,1)S(1)}, u32[]{:S(2)}, u32[]{:S(2)}) async-start(bf16[8,64,1024]{2,1,0:T(8,128)(2,1)} %copy-done.9), calls=%async_computation.1 | async-start | bytes 2097152 | tf_op jit(solution)/shard_map/all_to_all | solution.py:343
  51.5 3.5 %copy-start.19 = (f32[256,4096]{1,0:T(8,128)S(1)}, f32[256,4096]{1,0:T(8,128)}, u32[]{:S(2)}) copy-start(f32[256,4096]{1,0:T(8,128)} %get-tuple-element.34) | copy-start | bytes 12582916
  55.0 43.2 %copy-start.22 = (f32[16]{0:T(128)S(1)}, f32[16]{0:T(128)}, u32[]{:S(2)}) copy-start(f32[16]{0:T(128)} %param.18) | copy-start | bytes 196
  55.0 43.2 %copy-start.23 = (s32[16]{0:T(128)S(1)}, s32[16]{0:T(128)}, u32[]{:S(2)}) copy-start(s32[16]{0:T(128)} %param.16) | copy-start | bytes 196
  88.7 26.2 %copy-start.15 = (f32[1,4096]{1,0:T(1,128)S(1)}, f32[1,4096]{1,0:T(1,128)}, u32[]{:S(2)}) copy-start(f32[1,4096]{1,0:T(1,128)} %gain.3) | copy-start | bytes 49156
  88.7 1.7 collective-permute-start.3
  91.0 14.0 %all-to-all-start.2 = ((f32[16,2,8,128]{3,2,1,0:T(8,128)}), f32[16,2,8,128]{3,2,1,0:T(8,128)S(1)}, u32[]{:S(2)}, u32[]{:S(2)}) async-start(f32[16,2,8,128]{3,2,1,0:T(8,128)} %broadcast_in_dim.59), calls=%async_computation.2 | async-start | bytes 262144 | tf_op jit(solution)/shard_map/all_to_all | solution.py:28
  107.8 32.7 %all-to-all-start.3 = ((bf16[8,64,1024]{2,1,0:T(8,128)(2,1)}), bf16[8,64,1024]{2,1,0:T(8,128)(2,1)S(1)}, u32[]{:S(2)}, u32[]{:S(2)}) async-start(bf16[8,64,1024]{2,1,0:T(8,128)(2,1)} %copy-done.7), calls=%async_computation.3 | async-start | bytes 2097152 | tf_op jit(solution)/shard_map/all_to_all | solution.py:379
  111.4 92.6 %all-gather.2.cloned.1.call-start = ((), (), s32[]{:S(2)}) async-start(), calls=%async_computation.9 | async-start | bytes 4456448 | tf_op jit(solution)/shard_map/all_gather | solution.py:395
  111.6 3.5 %copy-start.2 = (bf16[1,512,4096]{2,1,0:T(8,128)(2,1)S(1)}, bf16[1,512,4096]{2,1,0:T(8,128)(2,1)}, u32[]{:S(2)}) copy-start(bf16[1,512,4096]{2,1,0:T(8,128)(2,1)} %param.10) | copy-start | bytes 12582916
  140.5 3.0 %collective-permute-start.4 = (bf16[8,64,1024]{2,1,0:T(8,128)(2,1)S(1)}, bf16[8,64,1024]{2,1,0:T(8,128)(2,1)}, u32[]{:S(2)}, u32[]{:S(2)}) collective-permute-start(bf16[8,64,1024]{2,1,0:T(8,128)(2,1)S(1)} %all-to-all-done.3.dl_mine), channel_id=1, source_target_pairs={{0,1},{1,0},{2,3},{3,2},{4,5},{5,4},{6,7},{7,6},{8,9},{9,8},{10,11... | collective-permute-start | bytes 3145736 | tf_op jit(solution)/shard_map/ppermute | solution.py:32
  143.5 1.0 copy-start.6
  144.6 1.0 copy-start.12
  148.4 15.1 %all-to-all-start.4 = ((f32[16,32,256]{2,1,0:T(8,128)}), f32[16,32,256]{2,1,0:T(8,128)}, u32[]{:S(2)}, u32[]{:S(2)}) async-start(f32[16,32,256]{2,1,0:T(8,128)} %copy-done.10), calls=%async_computation.5 | async-start | bytes 1048576 | tf_op jit(solution)/shard_map/all_to_all | solution.py:401
  154.4 21.0 %copy-start.25 = (pred[512]{0:T(512)(128)(4,1)S(1)}, pred[512]{0:T(512)(128)(4,1)}, u32[]{:S(2)}) copy-start(pred[512]{0:T(512)(128)(4,1)} %copy-done.24) | copy-start | bytes 1540
  164.8 2.6 %collective-permute-start.5 = (f32[16,256]{1,0:T(8,128)S(1)}, f32[16,256]{1,0:T(8,128)S(1)}, u32[]{:S(2)}, u32[]{:S(2)}) collective-permute-start(f32[16,256]{1,0:T(8,128)S(1)} %get-tuple-element.50), channel_id=1, source_target_pairs={{0,1},{1,0},{2,3},{3,2},{4,5},{5,4},{6,7},{7,6},{8,9},{9,8},{10,11... | collective-permute-start | bytes 49160 | tf_op jit(solution)/shard_map/ppermute | solution.py:32
  171.9 16.8 %all-to-all-start.5 = ((f32[8,2,4864]{2,1,0:T(2,128)}), f32[8,2,4864]{2,1,0:T(2,128)S(1)}, u32[]{:S(2)}, u32[]{:S(2)}) async-start(f32[8,2,4864]{2,1,0:T(2,128)} %shard_map.136), calls=%async_computation.6 | async-start | bytes 622592 | tf_op jit(solution)/shard_map/all_to_all | solution.py:441
  200.0 2.8 %collective-permute-start.6 = (bf16[8,2,4864]{2,1,0:T(2,128)(2,1)S(1)}, bf16[8,2,4864]{2,1,0:T(2,128)(2,1)S(1)}, u32[]{:S(2)}, u32[]{:S(2)}) collective-permute-start(bf16[8,2,4864]{2,1,0:T(2,128)(2,1)S(1)} %all_to_all.35), channel_id=1, source_target_pairs={{0,1},{1,0},{2,3},{3,2},{4,5},{5,4},{6,7},{7,6},{8,9},{9,8},{10,11... | collective-permute-start | bytes 466952 | tf_op jit(solution)/shard_map/ppermute | solution.py:32
  204.0 2.2 %copy-start.8 = (bf16[512,4096]{1,0:T(8,128)(2,1)S(1)}, bf16[512,4096]{1,0:T(8,128)(2,1)}, u32[]{:S(2)}) copy-start(bf16[512,4096]{1,0:T(8,128)(2,1)} %all-gather.2.cloned.1.call-done.main) | copy-start | bytes 12582916
  (9 other events, 7.5 us)
Sparse Core Ops, SparseCore 0:
  37.6 59.3 reduce-scatter.1
  140.7 35.3 all-gather.1

commit v6 on v4

v6 whole, which is shorter than its diff:
```python
import functools

import jax
import jax.numpy as jnp
from jax import lax
from jax.experimental import pallas as pl
from jax.experimental.pallas import tpu as pltpu
from jax.sharding import Mesh, PartitionSpec as P

F32 = jnp.float32
BF16 = jnp.bfloat16
EPSILON = 1e-05
VMEM = 32 * 1024 * 1024
LARGE = 56 * 1024 * 1024


def spread(values, axis, count):
    return lax.all_to_all(jnp.broadcast_to(values[None], (count,) + values.shape), axis, 0, 0)


def swap(values):
    return lax.ppermute(values, "core", [(0, 1), (1, 0)])


def pair(mine, other, core, axis):
    first = jnp.where(core == 0, mine, other)
    second = jnp.where(core == 0, other, mine)
    return jnp.concatenate([first, second], axis=axis)


def kernel_call(body, out, *operands):
    return pl.pallas_call(
        body,
        out_shape=out,
        in_specs=[
            pl.BlockSpec(memory_space=pltpu.SMEM if i == 0 else pltpu.VMEM) for i in range(len(operands))
        ],
        out_specs=jax.tree.map(lambda _: pl.BlockSpec(memory_space=pltpu.VMEM), out),
        compiler_params=pltpu.CompilerParams(vmem_limit_bytes=VMEM),
    )(*operands)


def vmem_call(body, out, *operands):
    return pl.pallas_call(
        body,
        out_shape=out,
        compiler_params=pltpu.CompilerParams(vmem_limit_bytes=VMEM),
    )(*operands)


def shape(dims, dtype):
    return jax.ShapeDtypeStruct(dims, dtype)


def after(values, done):
    return lax.optimization_barrier((values, done))[0]


def pieces3(values):
    first = values.astype(BF16).astype(F32)
    rest = values - first
    second = rest.astype(BF16).astype(F32)
    return [first, second, rest - second]


def first_kernel(chunks, place, seg, ids, gain, weight, head, unit_out, inv_out, sent, held):
    step = pl.program_id(0)
    token = lax.broadcasted_iota(jnp.int32, (ids.shape[0], seg.shape[0]), 1)
    pick = (ids[...] == token).astype(BF16)
    chunk = seg.shape[1]
    held[:, pl.ds(pl.multiple_of(step * chunk, chunk), chunk)] = jnp.dot(
        pick, seg[...], preferred_element_type=F32
    )
    count, rows_sent, slab = sent.shape
    exits = ids.shape[0]
    columns = rows_sent - exits

    @pl.when(step == 0)
    def _():
        for i in range(count):
            live = min(columns, head.shape[0] - i * columns)
            sent[i, exits : exits + live, :] = head[i * columns : i * columns + live, :]
            if live < columns:
                sent[i, exits + live :, :] = jnp.zeros((columns - live, slab), BF16)

    @pl.when(step == chunks - 1)
    def _():
        rows = held[...]
        inv = lax.rsqrt(jnp.mean(rows * rows, axis=-1, keepdims=True) + EPSILON)
        unit = rows * inv
        unit_out[...] = unit
        inv_out[...] = jnp.broadcast_to(inv, inv_out.shape)
        update = jnp.dot((unit * gain[...]).astype(BF16), weight[...], preferred_element_type=F32)
        own = held[:, pl.ds(pl.multiple_of(place[3] * slab, slab), slab)]
        hidden = (own + update.astype(BF16).astype(F32)).astype(BF16)
        for i in range(count):
            sent[i, :exits, :] = hidden


def main_kernel(place, grad, seg, ids, weight, weight_other, sent, gain_out, inverse):
    core = place[1]
    step = pl.program_id(0)
    count, _, held, width = seg.shape
    tokens = count * held
    rows = seg[...].reshape(tokens, width)

    @pl.when(step == 0)
    def _():
        full = rows.astype(F32)
        inv = lax.rsqrt(jnp.mean(full * full, axis=-1, keepdims=True) + EPSILON)
        index = lax.broadcasted_iota(jnp.int32, (tokens, ids.shape[1]), 0)
        index = (index // held * 2 + core) * held + index % held
        found = jnp.max((index == ids[...]).astype(F32), axis=-1, keepdims=True) > 0.0
        inverse[...] = jnp.broadcast_to(jnp.where(found, 0.0, inv), inverse.shape)

    columns = (((1,), (1,)), ((), ()))
    slab = weight.shape[1]
    low = grad[:, 0, :, :slab].reshape(tokens, slab)
    high = grad[:, 0, :, slab:].reshape(tokens, slab)
    part = lax.dot_general(jnp.where(core == 0, low, high), weight[...], columns, preferred_element_type=F32)
    part += lax.dot_general(jnp.where(core == 0, high, low), weight_other[...], columns, preferred_element_type=F32)
    sent[...] = part.astype(BF16)
    chunk = part.shape[1]
    unit = seg[:, 0, :, pl.ds(pl.multiple_of(step * chunk, chunk), chunk)].reshape(tokens, chunk).astype(F32)
    gain_out[...] = jnp.sum(part * (unit * inverse[:, :1]), axis=0, keepdims=True)


def logits_kernel(place, rows, gains, heads, mine, other):
    core = place[1]
    total = mine.shape[0] * 2
    skip = heads.shape[1] - (mine.shape[1] - 128)
    part = jnp.zeros((total, mine.shape[1] - 128), F32)
    squares = jnp.zeros((total, 1), F32)
    for at in range(heads.shape[0]):
        row = rows[:, at].reshape(total, rows.shape[3]).astype(F32)
        squares += jnp.sum(row * row, axis=-1, keepdims=True)
        part += lax.dot_general(
            (row * gains[at : at + 1, :]).astype(BF16),
            heads[at, skip:, :],
            (((1,), (1,)), ((), ())),
            preferred_element_type=F32,
        )
    whole = jnp.concatenate([part, jnp.broadcast_to(squares, (total, 128))], axis=1)
    low, high = whole[: total // 2], whole[total // 2 :]
    mine[...] = jnp.where(core == 0, low, high)
    other[...] = jnp.where(core == 0, high, low)


def softmax_kernel(width, vocab, place, mine, other, targets, expo_out, stats):
    z, start = place[0], place[2]
    columns = expo_out.shape[1]
    whole = mine[...] + other[...]
    inv = lax.rsqrt(whole[:, columns : columns + 1] / width + EPSILON)
    logits = whole[:, :columns] * inv
    column = lax.broadcasted_iota(jnp.int32, logits.shape, 1) + z * columns
    live = column < vocab
    top = jnp.max(jnp.where(live, logits, -jnp.inf), axis=-1, keepdims=True)
    shifted = jnp.where(live, logits - top, -jnp.inf)
    expo = jnp.exp(shifted)
    expo_out[...] = expo.astype(BF16)
    hit = live & (column == targets[...] - start)
    values = [
        top,
        jnp.sum(expo, axis=-1, keepdims=True),
        jnp.sum(jnp.where(live, expo * shifted, 0.0), axis=-1, keepdims=True),
        jnp.sum(jnp.where(hit, logits, 0.0), axis=-1, keepdims=True),
        inv,
    ]
    lane = lax.broadcasted_iota(jnp.int32, (logits.shape[0], 128), 1)
    table = jnp.zeros(lane.shape, F32)
    for i, value in enumerate(values):
        table = jnp.where(lane == i, value, table)
    stats[...] = jnp.broadcast_to(table.T[: stats.shape[1]][None], stats.shape)


def merged(stats):
    tops, totals, alongs, hits = [stats[:, i] for i in range(4)]
    top = jnp.max(tops, axis=0, keepdims=True)
    lower = jnp.exp(tops - top)
    total = jnp.sum(totals * lower, axis=0, keepdims=True)
    along = jnp.sum((alongs + (tops - top) * totals) * lower, axis=0, keepdims=True)
    return top, total, along, jnp.sum(hits, axis=0, keepdims=True)


def merge_kernel(place, stats, out):
    values = merged(stats[...])
    whole = jnp.concatenate(list(values) + [jnp.zeros((out.shape[1] - 4, out.shape[2]), F32)])
    out[...] = jnp.broadcast_to(whole[None], out.shape)


def finish_kernel(width, place, stats, pieces, weights, known):
    top, total, along, hits = merged(stats[...])
    weight = weights[...]
    own = pieces[...]
    factors = weight * (jnp.exp(own[:, 0] - top) / total)
    target = weight * (jnp.exp(hits - top) / total - 1.0)
    mean = weight * (along / total - (hits - top)) / width
    rest = known.shape[0] - own.shape[0] - 3
    known[...] = jnp.concatenate(
        [factors, target, mean, own[0, 4:5], jnp.zeros((rest, known.shape[1]), F32)]
    )


def exit_kernel(zs, vocab, place, head, known_mine, known_other, targets_mine, targets_other, *refs):
    part, dlogits, kept = refs[2:]
    core, start = place[1], place[2]
    count, columns = refs[0].shape[1:]
    for side, known, targets in ((0, known_mine, targets_mine), (1, known_other, targets_other)):
        table = known[...].T
        target_grad = table[:, zs : zs + 1]
        spot = targets[...] - start
        rows = pl.ds(pl.multiple_of(jnp.where(side == 0, core, 1 - core) * count, count), count)
        total = jnp.zeros((count, head.shape[2]), F32)
        for at in range(zs):
            column = lax.broadcasted_iota(jnp.int32, (count, columns), 1) + at * columns
            hit = (column == spot) & (column < vocab)
            grad = jnp.where(hit, target_grad, refs[side][at].astype(F32) * table[:, at : at + 1]).astype(BF16)
            dlogits[at, rows, :] = grad
            total += jnp.dot(grad, head[at], preferred_element_type=F32)
        part[rows, :] = total
        lane = lax.broadcasted_iota(jnp.int32, (count, 128), 1)
        kept[rows, :] = jnp.where(lane == 0, table[:, zs + 1 : zs + 2], table[:, zs + 2 : zs + 3])


def head_kernel(zs, place, rows, gain, known_mine, known_other, dlogits, out):
    z, core = place[0], place[1]
    count = dlogits.shape[1]
    columns = dlogits.shape[2]
    mine = known_mine[...].T[:, zs + 2 : zs + 3]
    other = known_other[...].T[:, zs + 2 : zs + 3]
    inv = jnp.concatenate([jnp.where(core == 0, mine, other), jnp.where(core == 0, other, mine)])
    row = rows[:, z].reshape(count, rows.shape[3]).astype(F32)
    normed = (row * inv * gain[...]).astype(BF16)
    for at in range(zs):
        held = min(columns, out.shape[0] - at * columns)
        piece = lax.dot_general(dlogits[at], normed, (((0,), (0,)), ((), ())), preferred_element_type=F32)
        out[at * columns : at * columns + held, :] = piece[:held].astype(BF16)


def row_kernel(place, got, hidden, kept, gain, grad_rows, mine, other, whole):
    core = place[1]
    total = got[0]
    for i in range(1, got.shape[0]):
        total += got[i]
    mean, inv = kept[:, 0:1], kept[:, 1:2]
    back = (total * gain[...] - hidden[...].astype(F32) * inv * mean) * inv
    rows = grad_rows[...] + back
    whole[...] = rows.astype(BF16)
    half = mine.shape[0]
    mine[...] = jnp.where(core == 0, rows[:half], rows[half:])
    other[...] = jnp.where(core == 0, rows[half:], rows[:half])


def send_kernel(place, mine, other, weight, weight_other, unit, gain_part, out):
    core = place[1]
    columns = (((1,), (1,)), ((), ()))
    part = lax.dot_general(mine[...].astype(BF16), weight[...], columns, preferred_element_type=F32)
    part += lax.dot_general(other[...].astype(BF16), weight_other[...], columns, preferred_element_type=F32)
    gain = gain_part[...] + jnp.sum(part * unit[...], axis=0, keepdims=True)
    low = jnp.where(core == 0, mine[...], other[...])
    high = jnp.where(core == 0, other[...], mine[...])
    count, share, _ = out.shape
    width, slab = weight.shape
    piece = width // (count * share)
    for i in range(count):
        rows = slice(i * share, (i + 1) * share)
        out[i, :, :width] = part[rows]
        out[i, :, width : width + slab] = low[rows]
        out[i, :, width + slab : width + 2 * slab] = high[rows]
        for j in range(share):
            at = (i * share + j) * piece
            out[i, j : j + 1, width + 2 * slab :] = gain[:, at : at + piece]


def share_kernel(slabs, got, gain, unit, inv, out):
    total = got[0]
    for i in range(1, got.shape[0]):
        total += got[i]
    width = gain.shape[1]
    residual = jnp.concatenate([got[i, :, width : width + slabs] for i in range(got.shape[0])], axis=1)
    unit_grad = total[:, :width] * gain[...]
    centre = jnp.mean(unit_grad * unit[...], axis=-1, keepdims=True)
    rows = residual + (unit_grad - unit[...] * centre) * inv[...]
    whole = jnp.concatenate([rows] + pieces3(total[:, width + slabs :]), axis=1)
    out[...] = jnp.broadcast_to(whole.astype(BF16)[None], out.shape)


def last_kernel(main, rows, ids, out):
    count = main.shape[0]
    token = lax.broadcasted_iota(jnp.int32, (count, ids.shape[1]), 0) + pl.program_id(0) * count
    put = token == ids[...]
    placed = jnp.dot(put.astype(BF16), rows[...], preferred_element_type=F32).astype(BF16)
    found = jnp.max(put.astype(F32), axis=-1, keepdims=True) > 0.0
    out[...] = jnp.where(found, placed, main[...])


def local(
    segment_in,
    layer_weight,
    layer_gain,
    final_gain,
    head_weight,
    exit_rows,
    exit_count,
    exit_targets,
    exit_scale,
    out_grad,
):
    pipe = lax.axis_index("pipe")
    core = lax.axis_index("core")
    z = lax.axis_index("z")
    pipes = lax.axis_size("pipe")
    zs = lax.axis_size("z")
    block = z * 2 + core
    seg = segment_in[0]
    weight = layer_weight[0]
    gain = layer_gain[0]
    grad = out_grad[0]
    tokens, width = seg.shape
    slab = weight.shape[1]
    exits = exit_rows.shape[1]
    rows_all = pipes * exits
    vocab_part = head_weight.shape[0]
    columns = -(-vocab_part // (zs * 128)) * 128
    place = jnp.stack([z, core, pipe * vocab_part, block]).astype(jnp.int32)
    my_rows = exit_rows[pipe]
    weight_other = swap(weight)
    whole = lambda *dims: pl.BlockSpec(dims, lambda i, *_: (0,) * len(dims))

    chunks = 8
    row_unit, row_inv, sent = pl.pallas_call(
        functools.partial(first_kernel, chunks),
        grid=(chunks,),
        in_specs=[
            pl.BlockSpec(memory_space=pltpu.SMEM),
            pl.BlockSpec((tokens, width // chunks), lambda i: (0, i)),
            whole(exits, 1),
            whole(1, width),
            whole(width, slab),
            whole(vocab_part, slab),
        ],
        out_specs=[whole(exits, width), whole(exits, 128), whole(zs, exits + columns, slab)],
        out_shape=[
            shape((exits, width), F32),
            shape((exits, 128), F32),
            shape((zs, exits + columns, slab), BF16),
        ],
        scratch_shapes=[pltpu.VMEM((exits, width), F32)],
        compiler_params=pltpu.CompilerParams(vmem_limit_bytes=LARGE),
    )(place, seg, my_rows[:, None], gain[None], weight, head_weight)
    hidden = sent[0, :exits]
    got_first = lax.all_to_all(sent, "z", 0, 0)

    held = tokens // (zs * 2)
    steps = 4
    chunk = width // steps
    main_sent, gain_part = pl.pallas_call(
        main_kernel,
        grid_spec=pltpu.PrefetchScalarGridSpec(
            num_scalar_prefetch=1,
            grid=(steps,),
            in_specs=[
                pl.BlockSpec((zs, 1, held, 2 * slab), lambda i, at: (0, at[1], 0, at[0])),
                pl.BlockSpec((zs, 1, held, width), lambda i, at: (0, at[1], 0, 0)),
                whole(1, exits),
                pl.BlockSpec((chunk, slab), lambda i, at: (i, 0)),
                pl.BlockSpec((chunk, slab), lambda i, at: (i, 0)),
            ],
            out_specs=[
                pl.BlockSpec((zs * held, chunk), lambda i, at: (0, i)),
                pl.BlockSpec((1, chunk), lambda i, at: (0, i)),
            ],
            scratch_shapes=[pltpu.VMEM((zs * held, 128), F32)],
        ),
        out_shape=[shape((zs * held, width), BF16), shape((1, width), F32)],
        compiler_params=pltpu.CompilerParams(vmem_limit_bytes=LARGE),
    )(
        place,
        grad.reshape(zs, 2, held, width),
        seg.reshape(zs, 2, held, width),
        my_rows[None],
        weight,
        weight_other,
    )
    got_first, main_sent = lax.optimization_barrier((got_first, main_sent))
    main_grad = lax.psum_scatter(main_sent, "z", scatter_dimension=0, tiled=True)

    gathered = jnp.broadcast_to(got_first[None, :, :exits], (pipes, zs, exits, slab))
    all_hidden = lax.all_to_all(gathered, "pipe", 0, 0)
    own = rows_all // 2
    pick = (my_rows[:, None] == jnp.arange(tokens, dtype=jnp.int32)[None, :]).astype(BF16)
    is_exit = jnp.any(pick > 0, axis=0)
    inputs = after(seg, gathered).astype(F32)
    inv_rms = lax.rsqrt(jnp.mean(inputs * inputs, axis=-1, keepdims=True) + EPSILON)
    normed = (inputs * inv_rms * gain).astype(BF16)
    grad_slab = lax.dynamic_slice_in_dim(after(grad, gathered), block * slab, slab, 1)
    grad_rows = jnp.dot(pick, grad_slab, preferred_element_type=F32)
    core_rows = exits // 2
    share = core_rows // zs
    core_unit = lax.dynamic_slice_in_dim(row_unit, core * core_rows, core_rows, 0)
    share_at = core * core_rows + z * share
    share_unit = lax.dynamic_slice_in_dim(row_unit, share_at, share, 0)
    share_inv = lax.dynamic_slice_in_dim(row_inv[:, :1], share_at, share, 0)
    gains = lax.dynamic_index_in_dim(final_gain.reshape(zs, 2, slab), core, 1, keepdims=False)
    gain_mine = lax.dynamic_slice_in_dim(final_gain, block * slab, slab, 0)[None]
    all_targets = exit_targets.reshape(2, own, 1)
    targets_mine = lax.dynamic_index_in_dim(all_targets, core, 0, keepdims=False)
    targets_other = lax.dynamic_index_in_dim(all_targets, 1 - core, 0, keepdims=False)
    slot = jnp.arange(exits, dtype=jnp.int32)[None, :]
    weights = jnp.where(slot < exit_count[:, None], exit_scale[:, None], F32(0.0)).reshape(2, 1, own)
    weights = lax.dynamic_index_in_dim(weights, core, 0, keepdims=False)
    (
        all_hidden,
        normed,
        grad_rows,
        core_unit,
        share_unit,
        share_inv,
        targets_mine,
        targets_other,
        weights,
        is_exit,
    ) = lax.optimization_barrier(
        (
            all_hidden,
            normed,
            grad_rows,
            core_unit,
            share_unit,
            share_inv,
            targets_mine,
            targets_other,
            weights,
            is_exit,
        )
    )
    mine, other = kernel_call(
        logits_kernel, [shape((own, columns + 128), F32)] * 2, place, all_hidden, gains, got_first
    )

    expo, stats = kernel_call(
        functools.partial(softmax_kernel, width, vocab_part),
        [shape((own, columns), BF16), shape((zs, 8, own), F32)],
        place,
        mine,
        swap(other),
        targets_mine,
    )
    expo, stats, main_grad = lax.optimization_barrier((expo, stats, main_grad))
    ex_mine = lax.all_gather(expo, "z", axis=0)
    pieces = lax.all_to_all(stats, "z", 0, 0)
    merged_stats = kernel_call(merge_kernel, shape((pipes, 8, own), F32), place, pieces)
    all_stats = lax.all_to_all(merged_stats, "pipe", 0, 0)

    first = block * held
    held_in = lax.dynamic_slice_in_dim(after(seg, stats), first, held, 0).astype(F32)
    held_grad = lax.dynamic_slice_in_dim(after(grad, stats), first, held, 0).astype(F32)
    held_inv = lax.rsqrt(jnp.mean(held_in * held_in, axis=-1, keepdims=True) + EPSILON)
    held_unit = held_in * held_inv
    unit_grad = main_grad.astype(F32) * gain
    centre = jnp.mean(unit_grad * held_unit, axis=-1, keepdims=True)
    main_out = (held_grad + (unit_grad - held_unit * centre) * held_inv).astype(BF16)
    all_stats, main_out = lax.optimization_barrier((all_stats, main_out))
    known_mine = kernel_call(
        functools.partial(finish_kernel, width), shape((16, own), F32), place, all_stats, pieces, weights
    )
    known_other = swap(known_mine)
    ex_mine, main_out = lax.optimization_barrier((after(ex_mine, all_stats), main_out))
    main_all = lax.all_gather(main_out, ("z", "core"), axis=0, tiled=True)
    ex_other = swap(ex_mine)

    exit_part, dlogits, kept = kernel_call(
        functools.partial(exit_kernel, zs, vocab_part),
        [
            shape((rows_all, slab), F32),
            shape((zs, rows_all, columns), BF16),
            shape((rows_all, 128), F32),
        ],
        place,
        sent[:, exits:],
        known_mine,
        known_other,
        targets_mine,
        targets_other,
        ex_mine,
        ex_other,
    )
    exit_got = lax.all_to_all(exit_part.reshape(pipes, exits, slab), "pipe", 0, 0)
    head_grad = kernel_call(
        functools.partial(head_kernel, zs),
        shape((vocab_part, slab), BF16),
        place,
        all_hidden,
        gain_mine,
        known_mine,
        known_other,
        after(dlogits, exit_part),
    )
    kept = lax.dynamic_slice_in_dim(kept, pipe * exits, exits, 0)
    exit_got, head_grad, kept = lax.optimization_barrier((exit_got, head_grad, kept))
    row_mine, row_send, row_rounded = kernel_call(
        row_kernel,
        [shape((core_rows, slab), F32)] * 2 + [shape((exits, slab), BF16)],
        place,
        exit_got,
        hidden,
        kept,
        gain_mine,
        grad_rows,
    )

    piece = slab * 2 // share
    send = kernel_call(
        send_kernel,
        shape((zs, share, width + 2 * slab + piece), F32),
        place,
        row_mine,
        swap(row_send),
        weight,
        weight_other,
        core_unit,
        gain_part,
    )
    got = lax.all_to_all(send, "z", 0, 0)
    put = pick.T
    slab_rounded = jnp.where(
        is_exit[:, None], jnp.dot(put, after(row_rounded, send), preferred_element_type=F32).astype(BF16), grad_slab
    )
    over_rows = (((0,), (0,)), ((), ()))
    weight_grad = lax.dot_general(normed, slab_rounded, over_rows, preferred_element_type=F32).astype(BF16)
    got, weight_grad = lax.optimization_barrier((got, weight_grad))
    last = vmem_call(
        functools.partial(share_kernel, 2 * slab),
        shape((zs, share, width + 3 * piece), BF16),
        got,
        gain[None],
        share_unit,
        share_inv,
    )
    last = lax.all_to_all(last, "z", 0, 0)
    last_other = swap(last)
    gain_grad = jnp.sum(
        (last[:, :, width:].astype(F32) + last_other[:, :, width:].astype(F32)).reshape(zs, share, 3, piece), axis=2
    ).reshape(width)
    row_out = pair(last, last_other, core, 0)[:, :, :width].reshape(exits, width)
    steps = 8
    input_grad = pl.pallas_call(
        last_kernel,
        grid=(steps,),
        in_specs=[
            pl.BlockSpec((tokens // steps, width), lambda i: (i, 0)),
            whole(exits, width),
            whole(1, exits),
        ],
        out_specs=pl.BlockSpec((tokens // steps, width), lambda i: (i, 0)),
        out_shape=shape((tokens, width), BF16),
        compiler_params=pltpu.CompilerParams(vmem_limit_bytes=LARGE),
    )(main_all, row_out, my_rows[None])
    return (input_grad[None], weight_grad[None], gain_grad[None], head_grad)


def solution(mesh):
    pipes, tensors = mesh.devices.shape
    fine = Mesh(mesh.devices.reshape(pipes, tensors // 2, 2), ("pipe", "z", "core"))
    tensor = ("z", "core")
    in_specs = (
        P("pipe", None, None),
        P("pipe", None, tensor),
        P("pipe", None),
        P(),
        P("pipe", tensor),
        P(),
        P(),
        P(),
        P(),
        P("pipe", None, None),
    )
    out_specs = (
        P("pipe", None, None),
        P("pipe", None, tensor),
        P("pipe", None),
        P("pipe", tensor),
    )
    return jax.shard_map(local, mesh=fine, in_specs=in_specs, out_specs=out_specs, check_vma=False)
```

time: 259 us -> 233 us (0.90)
  Pallas kernels: 11 us -> 39.4 us
  matrix products: 30.2 us -> 6.9 us
  other arithmetic: 33.9 us -> 13.6 us
  starting transfers between devices: 56.1 us -> 44.6 us
  local copies, waits for them, and re-layouts: 25 us -> 30.4 us
  waiting for transfers between devices: 76.2 us -> 72.1 us
    pallas_call x0 -> x4, Pallas kernels: none -> 23.6 us  [the longest x1 8.31 us: local(): pl.pallas_call(functools.partial(first_kernel, chunks), grid=(chunks,), i...]
    dot_general x8 -> x1, matrix products: 25 us -> 1.76 us  [local(): grad_rows = jnp.dot(pick, grad_slab, preferred_element_type=F32)]
    all_to_all x4, waiting for transfers between devices: 32.3 us -> 53.3 us  [the longest x1 22.5 us: local(): got_first = lax.all_to_all(sent, 'z', 0, 0)]
    all_gather x1, waiting for transfers between devices: 25.9 us -> 4.91 us  [local(): ex_mine = lax.all_gather(expo, 'z', axis=0)]
    convert_element_type x6 -> x1, other arithmetic: 17.8 us -> 2.04 us  [local(): (held_grad + (unit_grad - held_unit * centre) * held_inv).astype(BF16)]
    ppermute x7 -> x0, starting transfers between devices: 13 us -> none  [from_back(): lax.ppermute(piece(k), 'z', [(i, (i + k) % count) for i in range(count)])]
    all_to_all x1, waiting for transfers between devices: 11 us -> 3.13 us  [local(): lax.all_to_all(exit_part.reshape(pipes, exits, slab), 'pipe', 0, 0)]
    unnamed x61, local copies, waits for them, and re-layouts: 9.55 us -> 16 us
  transfers between devices with their start and end apart: 22 -> 15, of which waited for: 9 -> 10; matrix products, arithmetic and copies ran while one was open for 24% -> 16% of each run, Pallas kernels for 4% -> 14%
where the time goes in v6:
time: 233 us; the launch traced here: 232 us
  waiting for transfers between devices  72.1 us (31%)
  starting transfers between devices  44.6 us (19%)
  Pallas kernels  39.4 us (17%)
  local copies, waits for them, and re-layouts  30.4 us (13%)
  between operations  14 us (6%)
  other arithmetic  13.6 us (6%)
  blocking collectives  10.7 us (5%)
  matrix products  6.9 us (3%)
    all_to_all x1, waiting for transfers between devices, local(): got_first = lax.all_to_all(sent, 'z', 0, 0)  22.5 us
    all_to_all x1, waiting for transfers between devices, local(): all_hidden = lax.all_to_all(gathered, 'pipe', 0, 0)  20.6 us
    unnamed x61, local copies, waits for them, and re-layouts  16 us
    pallas_call x8, Pallas kernels, kernel_call(): pl.pallas_call(body, out_shape=out, in_specs=[pl.BlockSpec(memory_space=p...  15.8 us
    ppermute x6, starting transfers between devices, swap(): return lax.ppermute(values, 'core', [(0, 1), (1, 0)])  14.1 us
    all_to_all x1, blocking collectives, local(): last = lax.all_to_all(last, 'z', 0, 0)  10.7 us
    pallas_call x1, Pallas kernels, local(): pl.pallas_call(functools.partial(first_kernel, chunks), grid=(chunks,), i...  8.31 us
    all_to_all x1, waiting for transfers between devices, local(): got = lax.all_to_all(send, 'z', 0, 0)  8 us
  transfers between devices with their start and end apart: 15, of which 10 were waited for; matrix products, arithmetic and copies ran while one was open for 16% of the time, Pallas kernels for 14%

profile of v6, /device:TPU:1, one launch (start us, length us, event | category | flops | bytes accessed | tf_op | source)
XLA Modules:
  0.0 231.7 jit_solution(9690215068444313365)
XLA Ops:
  7.2 3.3 %collective-permute-start = (bf16[4096,256]{1,0:T(8,128)(2,1)}, bf16[4096,256]{1,0:T(8,128)(2,1)S(1)}, u32[]{:S(2)}, u32[]{:S(2)}) collective-permute-start(bf16[4096,256]{1,0:T(8,128)(2,1)} %bitcast.39), channel_id=1, source_target_pairs={{0,1},{1,0},{2,3},{3,2},{4,5},{5,4},{6,7},{7,6},{8,9},{9,8},{10,11... | collective-permute-start | bytes 6291464 | tf_op jit(solution)/shard_map/ppermute | solution.py:22
  11.8 8.3 %shard_map.129 = (f32[32,4096]{1,0:T(8,128)}, f32[32,128]{1,0:T(8,128)}, bf16[8,288,256]{2,1,0:T(8,128)(2,1)}) custom-call(s32[4]{0:T(128)} %pad_add_fusion.place, bf16[512,4096]{1,0:T(8,128)(2,1)} %bitcast.51, s32[32,1]{1,0:T(8,128)} %copy.45.ids, f32[1,4096]{1,0:T(1,128)} %gain.3, bf16[4096,256]{1,0:T(8,128)(2,1)} %bitcast.40, bf16[2000,256]{1,0:T(8,128)(2,1)} %head.1), custom_call_target="tpu_custom_call" | custom-call | tf_op jit(solution)/shard_map/pallas_call | solution.py:331
  20.1 6.5 %all-to-all-start = ((bf16[8,288,256]{2,1,0:T(8,128)(2,1)}), bf16[8,288,256]{2,1,0:T(8,128)(2,1)S(1)}, u32[]{:S(2)}, u32[]{:S(2)}) async-start(bf16[8,288,256]{2,1,0:T(8,128)(2,1)} %get-tuple-element.50), calls=%async_computation | async-start | bytes 2359296 | tf_op jit(solution)/shard_map/all_to_all | solution.py:352
  28.5 7.6 %shard_map.130 = (bf16[256,4096]{1,0:T(8,128)(2,1)}, f32[1,4096]{1,0:T(1,128)}) custom-call(s32[4]{0:T(128)} %pad_add_fusion.place, bf16[8,2,32,4096]{3,2,1,0:T(8,128)(2,1)} %bitcast.58, bf16[8,2,32,4096]{3,2,1,0:T(8,128)(2,1)} %bitcast.52, s32[1,32]{1,0:T(1,128)} %constant_dynamic-slice_fusion.9.ids, bf16[4096,256]{1,0:T(8,128)(2,1)} %bitcast.41, ...), custom_call_target="tpu_custom_call" | custom-call | tf_op jit(solution)/shard_map/pallas_call | solution.py:357
  36.1 22.5 %all-to-all-done.heads = bf16[8,288,256]{2,1,0:T(8,128)(2,1)S(1)} async-done(((bf16[8,288,256]{2,1,0:T(8,128)(2,1)}), bf16[8,288,256]{2,1,0:T(8,128)(2,1)S(1)}, u32[]{:S(2)}, u32[]{:S(2)}) %all-to-all-start) | async-done | bytes 1179680 | tf_op jit(solution)/shard_map/all_to_all | solution.py:352
  65.9 6.8 %all-to-all-start.1 = ((bf16[16,8,32,256]{3,2,1,0:T(8,128)(2,1)}), bf16[16,8,32,256]{3,2,1,0:T(8,128)(2,1)S(1)}, u32[]{:S(2)}, u32[]{:S(2)}) async-start(bf16[16,8,32,256]{3,2,1,0:T(8,128)(2,1)} %broadcast_in_dim.47), calls=%async_computation.1 | async-start | bytes 4194304 | tf_op jit(solution)/shard_map/all_to_all | solution.py:389
  74.7 3.3 %fusion = f32[512]{0:T(512)S(1)} fusion(bf16[512,4096]{1,0:T(8,128)(2,1)} %bitcast.53), kind=kLoop, calls=%fused_computation.2 | loop fusion | flops 6290944 | bytes 4196352 | tf_op jit(solution)/shard_map/reduce_sum | solution.py:394
  78.0 1.8 fusion.14.grad_rows
  79.8 3.6 %fusion.2 = bf16[512,4096]{1,0:T(8,128)(2,1)} fusion(bf16[512,4096]{1,0:T(8,128)(2,1)S(1)} %bitcast.57, f32[4096]{0:T(1024)S(1)} %bitcast.47, f32[512]{0:T(512)S(1)} %add_rsqrt_fusion), kind=kLoop, calls=%fused_computation.4 | loop fusion | flops 8388608 | bytes 8407040 | tf_op jit(solution)/shard_map/convert_element_type | solution.py:395
  83.4 20.6 %all-to-all-done.1.rows = bf16[16,8,32,256]{3,2,1,0:T(8,128)(2,1)S(1)} async-done(((bf16[16,8,32,256]{3,2,1,0:T(8,128)(2,1)}), bf16[16,8,32,256]{3,2,1,0:T(8,128)(2,1)S(1)}, u32[]{:S(2)}, u32[]{:S(2)}) %all-to-all-start.1) | async-done | bytes 2097184 | tf_op jit(solution)/shard_map/all_to_all | solution.py:389
  104.8 2.2 shard_map.131
  113.6 1.6 shard_map.132
  115.3 3.4 %all-to-all-start.2 = ((f32[8,8,256]{2,1,0:T(8,128)}), f32[8,8,256]{2,1,0:T(8,128)S(1)}, u32[]{:S(2)}, u32[]{:S(2)}) async-start(f32[8,8,256]{2,1,0:T(8,128)} %get-tuple-element.65), calls=%async_computation.3 | async-start | bytes 131072 | tf_op jit(solution)/shard_map/all_to_all | solution.py:451
  121.1 5.4 %all-to-all-done.2.stats.pieces = f32[8,8,256]{2,1,0:T(8,128)S(1)} async-done(((f32[8,8,256]{2,1,0:T(8,128)}), f32[8,8,256]{2,1,0:T(8,128)S(1)}, u32[]{:S(2)}, u32[]{:S(2)}) %all-to-all-start.2) | async-done | bytes 65568 | tf_op jit(solution)/shard_map/all_to_all | solution.py:451
  127.7 3.5 %all-to-all-start.3 = ((f32[16,8,256]{2,1,0:T(8,128)}), f32[16,8,256]{2,1,0:T(8,128)S(1)}, u32[]{:S(2)}, u32[]{:S(2)}) async-start(f32[16,8,256]{2,1,0:T(8,128)} %shard_map.133), calls=%async_computation.4 | async-start | bytes 262144 | tf_op jit(solution)/shard_map/all_to_all | solution.py:453
  131.3 2.0 fusion.10
  133.3 4.8 %all-to-all-done.3.stats = f32[16,8,256]{2,1,0:T(8,128)S(1)} async-done(((f32[16,8,256]{2,1,0:T(8,128)}), f32[16,8,256]{2,1,0:T(8,128)S(1)}, u32[]{:S(2)}, u32[]{:S(2)}) %all-to-all-start.3) | async-done | bytes 131104 | tf_op jit(solution)/shard_map/all_to_all | solution.py:453
  138.1 4.9 %all-gather.6.cloned.1.call-done = bf16[2048,256]{1,0:T(8,128)(2,1)} async-done(((bf16[256,256]{1,0:T(8,128)(2,1)}), bf16[2048,256]{1,0:T(8,128)(2,1)}) %all-gather.6.cloned.1.call-update) | async-done | bytes 1048592 | tf_op jit(solution)/shard_map/all_gather | solution.py:450
  143.1 4.9 %collective-permute-start.3 = (bf16[8,256,256]{2,1,0:T(8,128)(2,1)}, bf16[8,256,256]{2,1,0:T(8,128)(2,1)}, u32[]{:S(2)}, u32[]{:S(2)}) collective-permute-start(bf16[8,256,256]{2,1,0:T(8,128)(2,1)} %bitcast.43), channel_id=1, source_target_pairs={{0,1},{1,0},{2,3},{3,2},{4,5},{5,4},{6,7},{7,6},{8,9},{9,8},{10,11... | collective-permute-start | bytes 3145736 | tf_op jit(solution)/shard_map/ppermute | solution.py:22
  154.7 3.8 %shard_map.135 = (f32[512,256]{1,0:T(8,128)}, bf16[8,512,256]{2,1,0:T(8,128)(2,1)S(1)}, f32[512,128]{1,0:T(8,128)S(1)}) custom-call(s32[4]{0:T(128)S(1)} %copy-done.18, bf16[8,256,256]{2,1,0:T(8,128)(2,1)S(1)} %slice.23.head, f32[16,256]{1,0:T(8,128)} %shard_map.134.known_mine, f32[16,256]{1,0:T(8,128)} %collective-permute-done.2.known_other, ...), custom_call_target="tpu_custom_call" | custom-call | tf_op jit(solution)/shard_map/pallas_call | solution.py:32
  159.9 6.4 %all-to-all-start.4 = ((f32[16,32,256]{2,1,0:T(8,128)}), f32[16,32,256]{2,1,0:T(8,128)S(1)}, u32[]{:S(2)}, u32[]{:S(2)}) async-start(f32[16,32,256]{2,1,0:T(8,128)} %bitcast.16), calls=%async_computation.5 | async-start | bytes 1048576 | tf_op jit(solution)/shard_map/all_to_all | solution.py:488
  171.0 2.7 %shard_map.136 = bf16[2000,256]{1,0:T(8,128)(2,1)} custom-call(s32[4]{0:T(128)S(1)} %copy-done.18, bf16[16,8,32,256]{3,2,1,0:T(8,128)(2,1)S(1)} %copy-done.3, f32[1,256]{1,0:T(1,128)S(1)} %bitcast.49, f32[16,256]{1,0:T(8,128)} %shard_map.134.known_mine, f32[16,256]{1,0:T(8,128)} %collective-permute-done.2.known_other, bf16[8,512,256]{2,1,0:T(8,128)(2,1)S(1)} %copy-done.7), custom_call_target="tpu_custom_call" | custom-call | tf_op jit(solution)/shard_map/pallas_call | solution.py:32
  173.7 3.1 %all-to-all-done.4.got = f32[16,32,256]{2,1,0:T(8,128)S(1)} async-done(((f32[16,32,256]{2,1,0:T(8,128)}), f32[16,32,256]{2,1,0:T(8,128)S(1)}, u32[]{:S(2)}, u32[]{:S(2)}) %all-to-all-start.4) | async-done | bytes 524320 | tf_op jit(solution)/shard_map/all_to_all | solution.py:488
  177.5 2.0 collective-permute-start.4
  180.3 1.6 copy-done.5
  182.0 2.5 %shard_map.138 = f32[8,2,4864]{2,1,0:T(2,128)} custom-call(s32[4]{0:T(128)S(1)} %copy-done.18, f32[16,256]{1,0:T(8,128)S(1)} %get-tuple-element.83.mine, f32[16,256]{1,0:T(8,128)S(1)} %collective-permute-done.4.other, bf16[4096,256]{1,0:T(8,128)(2,1)S(1)} %bitcast.42, bf16[4096,256]{1,0:T(8,128)(2,1)S(1)} %copy-done.5, ...), custom_call_target="tpu_custom_call" | custom-call | tf_op jit(solution)/shard_map/pallas_call | solution.py:32
  184.4 3.9 %all-to-all-start.5 = ((f32[8,2,4864]{2,1,0:T(2,128)}), f32[8,2,4864]{2,1,0:T(2,128)S(1)}, u32[]{:S(2)}, u32[]{:S(2)}) async-start(f32[8,2,4864]{2,1,0:T(2,128)} %shard_map.138), calls=%async_computation.6 | async-start | bytes 622592 | tf_op jit(solution)/shard_map/all_to_all | solution.py:524
  188.4 5.1 %convolution_convert_fusion = bf16[4096,256]{1,0:T(8,128)(2,1)} fusion(bf16[512,4096]{1,0:T(8,128)(2,1)} %fusion.2, bf16[32,256]{1,0:T(8,128)(2,1)S(1)} %get-tuple-element.90, pred[512]{0:T(512)(128)(4,1)S(1)} %copy-done.29, bf16[512,4096]{1,0:T(8,128)(2,1)} %bitcast.61, s32[]{:T(128)S(6)} %select_n.60, s32[32]{0:T(128)S(1)} %copy-done.26), kind=kOutput, calls=%fused_computation.5 | convolution fusion | flops 1083457536 | bytes 6570628 | tf_op jit(solution)/shard_map/dot_general | solution.py:530
  193.5 8.0 %all-to-all-done.5.got = f32[8,2,4864]{2,1,0:T(2,128)S(1)} async-done(((f32[8,2,4864]{2,1,0:T(2,128)}), f32[8,2,4864]{2,1,0:T(2,128)S(1)}, u32[]{:S(2)}, u32[]{:S(2)}) %all-to-all-start.5) | async-done | bytes 311328 | tf_op jit(solution)/shard_map/all_to_all | solution.py:524
  201.7 10.7 %all_to_all.35 = bf16[8,2,4864]{2,1,0:T(2,128)(2,1)S(1)} all-to-all(bf16[8,2,4864]{2,1,0:T(2,128)(2,1)S(1)} %shard_map.139), channel_id=1, replica_groups=mesh['pipe'=16,'z'=8,'core'=2] {'z'}, dimensions={0} | all-to-all | bytes 311296 | tf_op jit(solution)/shard_map/all_to_all | solution.py:540
  212.4 2.2 collective-permute-start.5
  217.6 7.6 %shard_map.140 = bf16[512,4096]{1,0:T(8,128)(2,1)} custom-call(bf16[512,4096]{1,0:T(8,128)(2,1)} %all-gather.4.cloned.1.call-done.main, bf16[32,4096]{1,0:T(8,128)(2,1)} %reshape.108.rows, s32[1,32]{1,0:T(1,128)} %constant_dynamic-slice_fusion.9.ids), custom_call_target="tpu_custom_call" | custom-call | tf_op jit(solution)/shard_map/pallas_call | solution.py:547
  (124 shorter events, 41.1 us)
Async XLA Ops:
  7.2 3.3 %copy-start = (s32[16,32]{1,0:T(8,128)S(1)}, s32[16,32]{1,0:T(8,128)}, u32[]{:S(2)}) copy-start(s32[16,32]{1,0:T(8,128)} %param.15) | copy-start | bytes 6148
  7.2 20.0 %collective-permute-start = (bf16[4096,256]{1,0:T(8,128)(2,1)}, bf16[4096,256]{1,0:T(8,128)(2,1)S(1)}, u32[]{:S(2)}, u32[]{:S(2)}) collective-permute-start(bf16[4096,256]{1,0:T(8,128)(2,1)} %bitcast.39), channel_id=1, source_target_pairs={{0,1},{1,0},{2,3},{3,2},{4,5},{5,4},{6,7},{7,6},{8,9},{9,8},{10,11... | collective-permute-start | bytes 6291464 | tf_op jit(solution)/shard_map/ppermute | solution.py:22
  20.1 38.5 %all-to-all-start = ((bf16[8,288,256]{2,1,0:T(8,128)(2,1)}), bf16[8,288,256]{2,1,0:T(8,128)(2,1)S(1)}, u32[]{:S(2)}, u32[]{:S(2)}) async-start(bf16[8,288,256]{2,1,0:T(8,128)(2,1)} %get-tuple-element.50), calls=%async_computation | async-start | bytes 2359296 | tf_op jit(solution)/shard_map/all_to_all | solution.py:352
  26.6 88.7 %reduce-scatter.2.cloned.1.call-start = ((), (), s32[]{:S(2)}) async-start(), calls=%async_computation.8 | async-start | bytes 2359296 | tf_op jit(solution)/shard_map/reduce_scatter | solution.py:386
  28.5 30.1 %copy-start.24 = (s32[16,32]{1,0:T(8,128)S(1)}, s32[16,32]{1,0:T(8,128)}, u32[]{:S(2)}) copy-start(s32[16,32]{1,0:T(8,128)} %param.17) | copy-start | bytes 6148
  28.5 30.2 %copy-start.27 = (f32[16]{0:T(128)S(1)}, f32[16]{0:T(128)}, u32[]{:S(2)}) copy-start(f32[16]{0:T(128)} %param.18) | copy-start | bytes 196
  28.5 30.4 %copy-start.28 = (s32[16]{0:T(128)S(1)}, s32[16]{0:T(128)}, u32[]{:S(2)}) copy-start(s32[16]{0:T(128)} %param.16) | copy-start | bytes 196
  28.5 30.8 %copy-start.23 = (f32[4096]{0:T(1024)S(1)}, f32[4096]{0:T(1024)}, u32[]{:S(2)}) copy-start(f32[4096]{0:T(1024)} %param.13) | copy-start | bytes 49156
  59.3 2.5 %copy-start.25 = (s32[32]{0:T(128)}, s32[32]{0:T(128)S(1)}, u32[]{:S(2)}) copy-start(s32[32]{0:T(128)S(1)} %fusion.27) | copy-start | bytes 388
  65.9 38.1 %all-to-all-start.1 = ((bf16[16,8,32,256]{3,2,1,0:T(8,128)(2,1)}), bf16[16,8,32,256]{3,2,1,0:T(8,128)(2,1)S(1)}, u32[]{:S(2)}, u32[]{:S(2)}) async-start(bf16[16,8,32,256]{3,2,1,0:T(8,128)(2,1)} %broadcast_in_dim.47), calls=%async_computation.1 | async-start | bytes 4194304 | tf_op jit(solution)/shard_map/all_to_all | solution.py:389
  72.7 70.4 %all-gather.6.cloned.1.call-start = ((), (), s32[]{:S(2)}) async-start(), calls=%async_computation.10 | async-start | bytes 1179648 | tf_op jit(solution)/shard_map/all_gather | solution.py:450
  74.7 5.1 %copy-start.10 = (f32[1,4096]{1,0:T(1,128)S(1)}, f32[1,4096]{1,0:T(1,128)}, u32[]{:S(2)}) copy-start(f32[1,4096]{1,0:T(1,128)} %gain.3) | copy-start | bytes 49156
  74.7 5.1 %copy-start.22 = (bf16[1,512,4096]{2,1,0:T(8,128)(2,1)S(1)}, bf16[1,512,4096]{2,1,0:T(8,128)(2,1)}, u32[]{:S(2)}) copy-start(bf16[1,512,4096]{2,1,0:T(8,128)(2,1)} %param.10) | copy-start | bytes 12582916
  79.8 24.3 %copy-start.18 = (s32[4]{0:T(128)S(1)}, s32[4]{0:T(128)}, u32[]{:S(2)}) copy-start(s32[4]{0:T(128)} %pad_add_fusion.place) | copy-start | bytes 52
  104.1 47.1 %copy-start.2 = (bf16[16,8,32,256]{3,2,1,0:T(8,128)(2,1)}, bf16[16,8,32,256]{3,2,1,0:T(8,128)(2,1)S(1)}, u32[]{:S(2)}) copy-start(bf16[16,8,32,256]{3,2,1,0:T(8,128)(2,1)S(1)} %all-to-all-done.1.rows) | copy-start | bytes 6291460
  107.7 3.2 %collective-permute-start.1 = (f32[256,384]{1,0:T(8,128)}, f32[256,384]{1,0:T(8,128)S(1)}, u32[]{:S(2)}, u32[]{:S(2)}) collective-permute-start(f32[256,384]{1,0:T(8,128)} %get-tuple-element.59), channel_id=1, source_target_pairs={{0,1},{1,0},{2,3},{3,2},{4,5},{5,4},{6,7},{7,6},{8,9},{9,8},{10,11... | collective-permute-start | bytes 1179656 | tf_op jit(solution)/shard_map/ppermute | solution.py:22
  115.3 11.2 %all-to-all-start.2 = ((f32[8,8,256]{2,1,0:T(8,128)}), f32[8,8,256]{2,1,0:T(8,128)S(1)}, u32[]{:S(2)}, u32[]{:S(2)}) async-start(f32[8,8,256]{2,1,0:T(8,128)} %get-tuple-element.65), calls=%async_computation.3 | async-start | bytes 131072 | tf_op jit(solution)/shard_map/all_to_all | solution.py:451
  127.7 10.4 %all-to-all-start.3 = ((f32[16,8,256]{2,1,0:T(8,128)}), f32[16,8,256]{2,1,0:T(8,128)S(1)}, u32[]{:S(2)}, u32[]{:S(2)}) async-start(f32[16,8,256]{2,1,0:T(8,128)} %shard_map.133), calls=%async_computation.4 | async-start | bytes 262144 | tf_op jit(solution)/shard_map/all_to_all | solution.py:453
  131.2 86.3 %all-gather.4.cloned.1.call-start = ((), (), s32[]{:S(2)}) async-start(), calls=%async_computation.9 | async-start | bytes 4456448 | tf_op jit(solution)/shard_map/all_gather | solution.py:469
  143.1 9.5 %collective-permute-start.3 = (bf16[8,256,256]{2,1,0:T(8,128)(2,1)}, bf16[8,256,256]{2,1,0:T(8,128)(2,1)}, u32[]{:S(2)}, u32[]{:S(2)}) collective-permute-start(bf16[8,256,256]{2,1,0:T(8,128)(2,1)} %bitcast.43), channel_id=1, source_target_pairs={{0,1},{1,0},{2,3},{3,2},{4,5},{5,4},{6,7},{7,6},{8,9},{9,8},{10,11... | collective-permute-start | bytes 3145736 | tf_op jit(solution)/shard_map/ppermute | solution.py:22
  149.8 2.8 %collective-permute-start.2 = (f32[16,256]{1,0:T(8,128)}, f32[16,256]{1,0:T(8,128)}, u32[]{:S(2)}, u32[]{:S(2)}) collective-permute-start(f32[16,256]{1,0:T(8,128)} %shard_map.134.known_mine), channel_id=1, source_target_pairs={{0,1},{1,0},{2,3},{3,2},{4,5},{5,4},{6,7},{7,6},{8,9},{9,8},{10,11... | collective-permute-start | bytes 49160 | tf_op jit(solution)/shard_map/ppermute | solution.py:22
  154.7 22.1 %copy-start.17 = (f32[32,256]{1,0:T(8,128)S(1)}, f32[32,256]{1,0:T(8,128)}, u32[]{:S(2)}) copy-start(f32[32,256]{1,0:T(8,128)} %fusion.14.grad_rows) | copy-start | bytes 98308
  154.7 25.6 %copy-start.20 = (f32[1,4096]{1,0:T(1,128)S(1)}, f32[1,4096]{1,0:T(1,128)}, u32[]{:S(2)}) copy-start(f32[1,4096]{1,0:T(1,128)} %get-tuple-element.86.gain_part) | copy-start | bytes 49156
  159.9 20.4 %copy-start.1 = (bf16[1,4096,256]{2,1,0:T(8,128)(2,1)S(1)}, bf16[1,4096,256]{2,1,0:T(8,128)(2,1)}, u32[]{:S(2)}) copy-start(bf16[1,4096,256]{2,1,0:T(8,128)(2,1)} %param.11) | copy-start | bytes 6291460
  159.9 16.9 %all-to-all-start.4 = ((f32[16,32,256]{2,1,0:T(8,128)}), f32[16,32,256]{2,1,0:T(8,128)S(1)}, u32[]{:S(2)}, u32[]{:S(2)}) async-start(f32[16,32,256]{2,1,0:T(8,128)} %bitcast.16), calls=%async_computation.5 | async-start | bytes 1048576 | tf_op jit(solution)/shard_map/all_to_all | solution.py:488
  173.7 14.7 %copy-start.26 = (s32[32]{0:T(128)S(1)}, s32[32]{0:T(128)}, u32[]{:S(2)}) copy-start(s32[32]{0:T(128)} %copy-done.25) | copy-start | bytes 388
  173.7 14.7 %copy-start.29 = (pred[512]{0:T(512)(128)(4,1)S(1)}, pred[512]{0:T(512)(128)(4,1)}, u32[]{:S(2)}) copy-start(pred[512]{0:T(512)(128)(4,1)} %compare_reduce_fusion) | copy-start | bytes 1540
  177.5 2.8 %collective-permute-start.4 = (f32[16,256]{1,0:T(8,128)S(1)}, f32[16,256]{1,0:T(8,128)S(1)}, u32[]{:S(2)}, u32[]{:S(2)}) collective-permute-start(f32[16,256]{1,0:T(8,128)S(1)} %get-tuple-element.84), channel_id=1, source_target_pairs={{0,1},{1,0},{2,3},{3,2},{4,5},{5,4},{6,7},{7,6},{8,9},{9,8},{10,11... | collective-permute-start | bytes 49160 | tf_op jit(solution)/shard_map/ppermute | solution.py:22
  184.4 17.1 %all-to-all-start.5 = ((f32[8,2,4864]{2,1,0:T(2,128)}), f32[8,2,4864]{2,1,0:T(2,128)S(1)}, u32[]{:S(2)}, u32[]{:S(2)}) async-start(f32[8,2,4864]{2,1,0:T(2,128)} %shard_map.138), calls=%async_computation.6 | async-start | bytes 622592 | tf_op jit(solution)/shard_map/all_to_all | solution.py:524
  188.4 13.2 %copy-start.11 = (f32[1,4096]{1,0:T(1,128)S(1)}, f32[1,4096]{1,0:T(1,128)}, u32[]{:S(2)}) copy-start(f32[1,4096]{1,0:T(1,128)} %gain.3) | copy-start | bytes 49156
  188.4 13.2 %copy-start.16 = (f32[2,4096]{1,0:T(2,128)S(1)}, f32[2,4096]{1,0:T(2,128)}, u32[]{:S(2)}) copy-start(f32[2,4096]{1,0:T(2,128)} %constant_dynamic-slice_fusion.7.unit) | copy-start | bytes 98308
  212.4 3.3 %collective-permute-start.5 = (bf16[8,2,4864]{2,1,0:T(2,128)(2,1)S(1)}, bf16[8,2,4864]{2,1,0:T(2,128)(2,1)S(1)}, u32[]{:S(2)}, u32[]{:S(2)}) collective-permute-start(bf16[8,2,4864]{2,1,0:T(2,128)(2,1)S(1)} %all_to_all.35), channel_id=1, source_target_pairs={{0,1},{1,0},{2,3},{3,2},{4,5},{5,4},{6,7},{7,6},{8,9},{9,8},{10,11... | collective-permute-start | bytes 466952 | tf_op jit(solution)/shard_map/ppermute | solution.py:22
  (13 other events, 14.6 us)
Sparse Core Ops, SparseCore 0:
  58.8 34.1 reduce-scatter.1
  115.4 27.5 all-gather.5
  144.9 45.0 all-gather.3

commit v7 on v5

v7 whole, which is shorter than its diff:
```python
import functools

import jax
import jax.numpy as jnp
from jax import lax
from jax.experimental import pallas as pl
from jax.experimental.pallas import tpu as pltpu
from jax.sharding import Mesh, PartitionSpec as P

F32 = jnp.float32
BF16 = jnp.bfloat16
EPSILON = 1e-05
SMALL = 20 * 1024 * 1024
VMEM = 32 * 1024 * 1024
LARGE = 56 * 1024 * 1024


def spread(values, axis, count):
    return lax.all_to_all(jnp.broadcast_to(values[None], (count,) + values.shape), axis, 0, 0)


def swap(values):
    return lax.ppermute(values, "core", [(0, 1), (1, 0)])


def pair(mine, other, core, axis):
    first = jnp.where(core == 0, mine, other)
    second = jnp.where(core == 0, other, mine)
    return jnp.concatenate([first, second], axis=axis)


def kernel_call(body, out, *operands):
    return pl.pallas_call(
        body,
        out_shape=out,
        in_specs=[
            pl.BlockSpec(memory_space=pltpu.SMEM if i == 0 else pltpu.VMEM) for i in range(len(operands))
        ],
        out_specs=jax.tree.map(lambda _: pl.BlockSpec(memory_space=pltpu.VMEM), out),
        compiler_params=pltpu.CompilerParams(vmem_limit_bytes=VMEM),
    )(*operands)


def vmem_call(body, out, *operands):
    return pl.pallas_call(
        body,
        out_shape=out,
        compiler_params=pltpu.CompilerParams(vmem_limit_bytes=VMEM),
    )(*operands)


def piped_call(body, out, *operands, limit=LARGE):
    specs = [pl.BlockSpec(memory_space=pltpu.SMEM)] + [
        pl.BlockSpec(value.shape, lambda i, n=value.ndim: (0,) * n) for value in operands[1:]
    ]
    return pl.pallas_call(
        body,
        grid=(1,),
        out_shape=out,
        in_specs=specs,
        out_specs=jax.tree.map(lambda value: pl.BlockSpec(value.shape, lambda i, n=len(value.shape): (0,) * n), out),
        compiler_params=pltpu.CompilerParams(vmem_limit_bytes=limit),
    )(*operands)


def shape(dims, dtype):
    return jax.ShapeDtypeStruct(dims, dtype)


def after(values, done):
    return lax.optimization_barrier((values, done))[0]


def pieces3(values):
    first = values.astype(BF16).astype(F32)
    rest = values - first
    second = rest.astype(BF16).astype(F32)
    return [first, second, rest - second]


def chip_term(core, grad, weight, weight_other):
    count, _, held, columns = grad.shape
    slab = columns // 2
    over = (((1,), (1,)), ((), ()))
    low = grad[:, 0, :, :slab].reshape(count * held, slab)
    high = grad[:, 0, :, slab:].reshape(count * held, slab)
    part = lax.dot_general(jnp.where(core == 0, low, high), weight[...], over, preferred_element_type=F32)
    return part + lax.dot_general(
        jnp.where(core == 0, high, low), weight_other[...], over, preferred_element_type=F32
    )


def main_kernel(place, grad, weight, weight_other, sent):
    sent[...] = chip_term(place[1], grad, weight, weight_other).astype(BF16)


def gain_kernel(place, grad, seg, ids, weight, weight_other, gain_out, inverse):
    core = place[1]
    step = pl.program_id(0)
    count, _, held, width = seg.shape
    tokens = count * held

    @pl.when(step == 0)
    def _():
        full = seg[...].reshape(tokens, width).astype(F32)
        inv = lax.rsqrt(jnp.mean(full * full, axis=-1, keepdims=True) + EPSILON)
        index = lax.broadcasted_iota(jnp.int32, (tokens, ids.shape[1]), 0)
        index = (index // held * 2 + core) * held + index % held
        found = jnp.max((index == ids[...]).astype(F32), axis=-1, keepdims=True) > 0.0
        inverse[...] = jnp.broadcast_to(jnp.where(found, 0.0, inv), inverse.shape)

    part = chip_term(core, grad, weight, weight_other)
    chunk = part.shape[1]
    unit = seg[:, 0, :, pl.ds(pl.multiple_of(step * chunk, chunk), chunk)].reshape(tokens, chunk).astype(F32)
    gain_out[...] = jnp.sum(part * (unit * inverse[:, :1]), axis=0, keepdims=True)


def logits_kernel(half, mine, other, gain_mine, gain_other, head_mine, head_other, out):
    squares = 0.0
    part = 0.0
    for row, gain, head in ((mine, gain_mine, head_mine), (other, gain_other, head_other)):
        row = row[...].reshape(-1, row.shape[-1]).astype(F32)
        squares += jnp.sum(row * row, axis=-1, keepdims=True)
        part += lax.dot_general(
            (row * gain[...]).astype(BF16), head[...], (((1,), (1,)), ((), ())), preferred_element_type=F32
        )
    column = lax.broadcasted_iota(jnp.int32, part.shape, 1)
    for i, piece in enumerate(pieces3(squares)):
        part = jnp.where(column == half + i, piece, part)
    out[...] = part.astype(BF16).reshape(out.shape)


def softmax_kernel(width, half, vocab, place, parts, targets, expo_out, stats):
    core, start = place[1], place[2]
    total = parts[0].astype(F32)
    for i in range(1, parts.shape[0]):
        total += parts[i].astype(F32)
    inv = lax.rsqrt(jnp.sum(total[:, half : half + 3], axis=-1, keepdims=True) / width + EPSILON)
    logits = total * inv
    column = lax.broadcasted_iota(jnp.int32, logits.shape, 1)
    live = (column < half) & (column + core * half < vocab)
    top = jnp.max(jnp.where(live, logits, -jnp.inf), axis=-1, keepdims=True)
    shifted = jnp.where(live, logits - top, -jnp.inf)
    expo = jnp.exp(shifted)
    expo_out[...] = expo.astype(BF16)
    hit = live & (column == targets[...] - start)
    values = [
        top,
        jnp.sum(expo, axis=-1, keepdims=True),
        jnp.sum(jnp.where(live, expo * shifted, 0.0), axis=-1, keepdims=True),
        jnp.sum(jnp.where(hit, logits, 0.0), axis=-1, keepdims=True),
        inv,
    ]
    lane = lax.broadcasted_iota(jnp.int32, (logits.shape[0], 128), 1)
    table = jnp.zeros(lane.shape, F32)
    for i, value in enumerate(values):
        table = jnp.where(lane == i, value, table)
    table = jnp.concatenate([table, jnp.zeros((128 - table.shape[0], 128), F32)])
    stats[...] = table.T[: stats.shape[0]]


def merged(stats):
    tops, totals, alongs, hits = [stats[:, i] for i in range(4)]
    top = jnp.max(tops, axis=0, keepdims=True)
    lower = jnp.exp(tops - top)
    total = jnp.sum(totals * lower, axis=0, keepdims=True)
    along = jnp.sum((alongs + (tops - top) * totals) * lower, axis=0, keepdims=True)
    return top, total, along, jnp.sum(hits, axis=0, keepdims=True)


def finish_kernel(width, stats, own, weights, known):
    top, total, along, hits = merged(stats[...])
    weight = weights[...]
    factor = weight * (jnp.exp(own[0:1] - top) / total)
    target = weight * (jnp.exp(hits - top) / total - 1.0)
    mean = weight * (along / total - (hits - top)) / width
    rest = jnp.zeros((known.shape[1] - 4, known.shape[2]), F32)
    known[...] = jnp.broadcast_to(jnp.concatenate([factor, target, mean, own[4:5], rest])[None], known.shape)


def logit_grads(half, vocab, which, start, expo, known, targets, grad, kept):
    count, rows, columns = expo.shape
    column = lax.broadcasted_iota(jnp.int32, (rows, columns), 1)
    lane = lax.broadcasted_iota(jnp.int32, (rows, 128), 1)
    live = (column < half) & (column + which * half < vocab)
    for i in range(count):
        table = jnp.concatenate([known[i], jnp.zeros((128 - known.shape[1], 128), F32)]).T[:rows]
        hit = (column + which * half == targets[i * rows : (i + 1) * rows, :] - start) & live
        grad[i] = jnp.where(hit, table[:, 1:2], expo[i].astype(F32) * table[:, 0:1]).astype(BF16)
        if kept is not None:
            kept[i * rows : (i + 1) * rows, :] = jnp.where(lane == 0, table[:, 2:3], table[:, 3:4])
    return grad[...].reshape(count * rows, columns)


def exit_kernel(half, vocab, place, expo, known, targets, head, part, grad, kept):
    rows = logit_grads(half, vocab, place[1], place[2], expo, known, targets, grad, kept)
    part[...] = jnp.dot(rows, head[...], preferred_element_type=F32)


def exit_rest_kernel(half, vocab, place, expo, known, targets, head, before, part, grad):
    rows = logit_grads(half, vocab, 1 - place[1], place[2], expo, known, targets, grad, None)
    total = before[...] + jnp.dot(rows, head[...], preferred_element_type=F32)
    part[...] = total.astype(BF16).reshape(part.shape)


def head_kernel(half, place, mine, gain, kept, dl_mine, dl_other, out):
    core = place[1]
    row = mine[...].reshape(-1, mine.shape[-1]).astype(F32)
    normed = (row * kept[:, 1:2] * gain[...]).astype(BF16)
    over_rows = (((0,), (0,)), ((), ()))
    low = lax.dot_general(
        dl_mine[...].reshape(row.shape[0], -1), normed, over_rows, preferred_element_type=F32
    )
    high = lax.dot_general(
        dl_other[...].reshape(row.shape[0], -1), normed, over_rows, preferred_element_type=F32
    )
    out[:half, :] = jnp.where(core == 0, low, high)[:half].astype(BF16)
    out[half:, :] = jnp.where(core == 0, high, low)[: out.shape[0] - half].astype(BF16)


def row_kernel(place, got, hidden, kept, gain, grad_rows, mine, other, whole):
    core = place[1]
    total = got[0].astype(F32)
    for i in range(1, got.shape[0]):
        total += got[i].astype(F32)
    mean, inv = kept[:, 0:1], kept[:, 1:2]
    back = (total * gain[...] - hidden[...].astype(F32) * inv * mean) * inv
    rows = grad_rows[...] + back
    whole[...] = rows.astype(BF16)
    half = mine.shape[0]
    mine[...] = jnp.where(core == 0, rows[:half], rows[half:])
    other[...] = jnp.where(core == 0, rows[half:], rows[:half])


def send_kernel(place, mine, other, weight, weight_other, unit, gain_part, out):
    core = place[1]
    columns = (((1,), (1,)), ((), ()))
    part = lax.dot_general(mine[...].astype(BF16), weight[...], columns, preferred_element_type=F32)
    part += lax.dot_general(other[...].astype(BF16), weight_other[...], columns, preferred_element_type=F32)
    gain = gain_part[...] + jnp.sum(part * unit[...], axis=0, keepdims=True)
    low = jnp.where(core == 0, mine[...], other[...])
    high = jnp.where(core == 0, other[...], mine[...])
    rows = jnp.concatenate([low, high], axis=1)
    rounded = rows.astype(BF16)
    rest = (rows - rounded.astype(F32)).astype(BF16)
    part = part.astype(BF16)
    gains = [values.astype(BF16) for values in pieces3(gain)]
    count, share, _ = out.shape
    width, slab = weight.shape
    piece = width // (count * share)
    for i in range(count):
        at = slice(i * share, (i + 1) * share)
        out[i, :, :width] = part[at]
        out[i, :, width : width + 2 * slab] = rounded[at]
        out[i, :, width + 2 * slab : width + 4 * slab] = rest[at]
        for j in range(share):
            first = (i * share + j) * piece
            for k in range(3):
                to = width + 4 * slab + k * piece
                out[i, j : j + 1, to : to + piece] = gains[k][:, first : first + piece]


def share_kernel(slabs, got, gain, unit, inv, out):
    total = got[0].astype(F32)
    for i in range(1, got.shape[0]):
        total += got[i].astype(F32)
    width = gain.shape[1]
    residual = jnp.concatenate(
        [
            got[i, :, width : width + slabs].astype(F32) + got[i, :, width + slabs : width + 2 * slabs].astype(F32)
            for i in range(got.shape[0])
        ],
        axis=1,
    )
    unit_grad = total[:, :width] * gain[...]
    centre = jnp.mean(unit_grad * unit[...], axis=-1, keepdims=True)
    rows = residual + (unit_grad - unit[...] * centre) * inv[...]
    gains = total[:, width + 2 * slabs :]
    piece = gains.shape[1] // 3
    gains = gains[:, :piece] + gains[:, piece : 2 * piece] + gains[:, 2 * piece :]
    whole = jnp.concatenate([rows] + pieces3(gains), axis=1)
    out[...] = jnp.broadcast_to(whole.astype(BF16)[None], out.shape)


def last_kernel(ids, main, rows, out):
    step = pl.program_id(0)
    count = out.shape[0]
    out[...] = main[pl.ds(pl.multiple_of(step * count, count), count), :]
    tile = lax.broadcasted_iota(jnp.int32, (16, out.shape[1]), 0)
    for i in range(rows.shape[0]):
        at = ids[i] - step * count

        @pl.when((at >= 0) & (at < count))
        def _():
            start = pl.multiple_of(at // 16 * 16, 16)
            out[pl.ds(start, 16), :] = jnp.where(tile == at - start, rows[i : i + 1, :], out[pl.ds(start, 16), :])


def local(
    segment_in,
    layer_weight,
    layer_gain,
    final_gain,
    head_weight,
    exit_rows,
    exit_count,
    exit_targets,
    exit_scale,
    out_grad,
):
    pipe = lax.axis_index("pipe")
    core = lax.axis_index("core")
    z = lax.axis_index("z")
    pipes = lax.axis_size("pipe")
    zs = lax.axis_size("z")
    block = z * 2 + core
    seg = segment_in[0]
    weight = layer_weight[0]
    gain = layer_gain[0]
    grad = out_grad[0]
    tokens, width = seg.shape
    slab = weight.shape[1]
    exits = exit_rows.shape[1]
    rows_all = pipes * exits
    vocab_part = head_weight.shape[0]
    half = -(-vocab_part // 32) * 16
    padded = -(-(half + 3) // 128) * 128
    place = jnp.stack([z, core, pipe * vocab_part, block]).astype(jnp.int32)
    whole = lambda *dims: pl.BlockSpec(dims, lambda i, *_: (0,) * len(dims))

    weight_other = swap(weight)
    halves = jnp.pad(head_weight, ((0, 2 * half - vocab_part), (0, 0))).reshape(2, half, slab)
    halves = jnp.pad(halves, ((0, 0), (0, padded - half), (0, 0)))
    head_mine = lax.dynamic_index_in_dim(halves, core, 0, keepdims=False)
    head_rest = lax.dynamic_index_in_dim(halves, 1 - core, 0, keepdims=False)
    head_other = swap(head_rest)

    my_rows = exit_rows[pipe]
    pick = (my_rows[:, None] == jnp.arange(tokens, dtype=jnp.int32)[None, :]).astype(BF16)
    row_in = jnp.dot(pick, seg, preferred_element_type=F32)
    row_inv = lax.rsqrt(jnp.mean(row_in * row_in, axis=-1, keepdims=True) + EPSILON)
    row_unit = row_in * row_inv
    row_normed = (row_unit * gain).astype(BF16)
    row_update = lax.reduce_precision(jnp.dot(row_normed, weight, preferred_element_type=F32), 8, 7)
    row_block = lax.dynamic_slice_in_dim(row_in, block * slab, slab, 1)
    hidden = (row_block + row_update).astype(BF16)

    held = tokens // (zs * 2)
    steps = 4
    chunk = width // steps
    grad_spec = pl.BlockSpec((zs, 1, held, 2 * slab), lambda i, at: (0, at[1], 0, at[0]))
    weight_spec = pl.BlockSpec((chunk, slab), lambda i, at: (i, 0))
    grad_view = grad.reshape(zs, 2, held, width)
    main_sent = pl.pallas_call(
        main_kernel,
        grid_spec=pltpu.PrefetchScalarGridSpec(
            num_scalar_prefetch=1,
            grid=(steps,),
            in_specs=[grad_spec, weight_spec, weight_spec],
            out_specs=pl.BlockSpec((zs * held, chunk), lambda i, at: (0, i)),
        ),
        out_shape=shape((zs * held, width), BF16),
        compiler_params=pltpu.CompilerParams(vmem_limit_bytes=LARGE),
    )(place, grad_view, weight, weight_other)
    hidden, main_sent = lax.optimization_barrier((hidden, main_sent))
    main_grad = lax.psum_scatter(main_sent, "z", scatter_dimension=0, tiled=True)

    all_mine = spread(hidden, "pipe", pipes)
    all_other = swap(all_mine)
    gain_mine = lax.dynamic_slice_in_dim(final_gain, block * slab, slab, 0)[None]
    gain_other = lax.dynamic_slice_in_dim(final_gain, (z * 2 + 1 - core) * slab, slab, 0)[None]
    own = rows_all // zs
    part = vmem_call(
        functools.partial(logits_kernel, half),
        shape((zs, own, padded), BF16),
        all_mine,
        all_other,
        gain_mine,
        gain_other,
        head_mine,
        head_other,
    )
    parts = lax.all_to_all(part, "z", 0, 0)

    gain_part = pl.pallas_call(
        gain_kernel,
        grid_spec=pltpu.PrefetchScalarGridSpec(
            num_scalar_prefetch=1,
            grid=(steps,),
            in_specs=[
                grad_spec,
                pl.BlockSpec((zs, 1, held, width), lambda i, at: (0, at[1], 0, 0)),
                whole(1, exits),
                weight_spec,
                weight_spec,
            ],
            out_specs=pl.BlockSpec((1, chunk), lambda i, at: (0, i)),
            scratch_shapes=[pltpu.VMEM((zs * held, 128), F32)],
        ),
        out_shape=shape((1, width), F32),
        compiler_params=pltpu.CompilerParams(vmem_limit_bytes=LARGE),
    )(
        place,
        after(grad, part).reshape(zs, 2, held, width),
        seg.reshape(zs, 2, held, width),
        my_rows[None],
        weight,
        weight_other,
    )
    all_targets = exit_targets.reshape(rows_all, 1)
    targets = lax.dynamic_slice_in_dim(all_targets, z * own, own, 0)
    slot = jnp.arange(exits, dtype=jnp.int32)[None, :]
    weights = jnp.where(slot < exit_count[:, None], exit_scale[:, None], F32(0.0)).reshape(1, rows_all)
    weights = jnp.pad(lax.dynamic_slice_in_dim(weights, z * own, own, 1), ((0, 0), (0, 128 - own)))
    parts, gain_part = lax.optimization_barrier((parts, gain_part))

    expo, stats = kernel_call(
        functools.partial(softmax_kernel, width, half, vocab_part),
        [shape((own, padded), BF16), shape((8, 128), F32)],
        place,
        parts,
        targets - core * half,
    )
    expo, stats, main_grad = lax.optimization_barrier((expo, stats, main_grad))
    ex_mine = lax.all_gather(expo, "z", axis=0)
    stats_other = swap(stats)
    all_stats = spread(jnp.stack([stats, stats_other]), "pipe", pipes).reshape(pipes * 2, 8, 128)
    known_mine = vmem_call(
        functools.partial(finish_kernel, width), shape((zs, 8, 128), F32), all_stats, stats, weights
    )
    known_sent = known_mine
    known_mine = lax.all_to_all(known_mine, "z", 0, 0)
    known_other = swap(known_mine)

    first = block * held
    held_in = lax.dynamic_slice_in_dim(after(seg, stats_other), first, held, 0).astype(F32)
    held_grad = lax.dynamic_slice_in_dim(after(grad, stats_other), first, held, 0).astype(F32)
    held_inv = lax.rsqrt(jnp.mean(held_in * held_in, axis=-1, keepdims=True) + EPSILON)
    held_unit = held_in * held_inv
    unit_grad = main_grad.astype(F32) * gain
    centre = jnp.mean(unit_grad * held_unit, axis=-1, keepdims=True)
    main_out = (held_grad + (unit_grad - held_unit * centre) * held_inv).astype(BF16)
    all_stats, main_out = lax.optimization_barrier((all_stats, main_out))
    inputs = after(seg, known_sent).astype(F32)
    inv_rms = lax.rsqrt(jnp.mean(inputs * inputs, axis=-1, keepdims=True) + EPSILON)
    normed = (inputs * inv_rms * gain).astype(BF16)
    grad_slab = lax.dynamic_slice_in_dim(after(grad, known_sent), block * slab, slab, 1)
    grad_rows = jnp.dot(pick, grad_slab, preferred_element_type=F32)
    core_rows = exits // 2
    share = core_rows // zs
    core_unit = lax.dynamic_slice_in_dim(after(row_unit, known_sent), core * core_rows, core_rows, 0)
    share_at = core * core_rows + z * share
    share_unit = lax.dynamic_slice_in_dim(core_unit, z * share, share, 0)
    share_inv = lax.dynamic_slice_in_dim(row_inv, share_at, share, 0)
    known_mine, normed, grad_rows, core_unit, share_unit, share_inv = lax.optimization_barrier(
        (known_mine, normed, grad_rows, core_unit, share_unit, share_inv)
    )
    ex_mine, main_out = lax.optimization_barrier((after(ex_mine, known_other), main_out))
    main_all = lax.all_gather(main_out, ("z", "core"), axis=0, tiled=True)
    ex_other = swap(ex_mine)

    exit_first, dl_mine, kept = piped_call(
        functools.partial(exit_kernel, half, vocab_part),
        [shape((rows_all, slab), F32), shape((zs, own, padded), BF16), shape((rows_all, 128), F32)],
        place,
        ex_mine,
        known_mine,
        all_targets,
        head_mine,
    )
    exit_part, dl_other = piped_call(
        functools.partial(exit_rest_kernel, half, vocab_part),
        [shape((pipes, exits, slab), BF16), shape((zs, own, padded), BF16)],
        place,
        ex_other,
        known_other,
        all_targets,
        head_rest,
        exit_first,
    )
    exit_got = lax.all_to_all(exit_part, "pipe", 0, 0)
    kept_all = kept
    kept = lax.dynamic_slice_in_dim(kept, pipe * exits, exits, 0)
    exit_got, kept = lax.optimization_barrier((exit_got, kept))
    row_mine, row_send, row_rounded = kernel_call(
        row_kernel,
        [shape((core_rows, slab), F32)] * 2 + [shape((exits, slab), BF16)],
        place,
        exit_got,
        hidden,
        kept,
        gain_mine,
        grad_rows,
    )

    piece = slab * 2 // share
    send = kernel_call(
        send_kernel,
        shape((zs, share, width + 4 * slab + 3 * piece), BF16),
        place,
        row_mine,
        swap(row_send),
        weight,
        weight_other,
        core_unit,
        gain_part,
    )
    got = lax.all_to_all(send, "z", 0, 0)
    put = pick.T
    is_exit = jnp.any(pick > 0, axis=0)
    slab_rounded = jnp.where(
        is_exit[:, None], jnp.dot(put, after(row_rounded, send), preferred_element_type=F32).astype(BF16), grad_slab
    )
    over_rows = (((0,), (0,)), ((), ()))
    weight_grad = lax.dot_general(normed, slab_rounded, over_rows, preferred_element_type=F32).astype(BF16)
    got, weight_grad = lax.optimization_barrier((got, weight_grad))
    last = vmem_call(
        functools.partial(share_kernel, 2 * slab),
        shape((zs, share, width + 3 * piece), BF16),
        got,
        gain[None],
        share_unit,
        share_inv,
    )
    last, main_all = lax.optimization_barrier((last, main_all))
    head_grad = piped_call(
        functools.partial(head_kernel, half),
        shape((vocab_part, slab), BF16),
        place,
        all_mine,
        gain_mine,
        after(kept_all, last),
        dl_mine,
        dl_other,
        limit=SMALL,
    )
    last = lax.all_to_all(last, "z", 0, 0)
    last, head_grad = lax.optimization_barrier((last, head_grad))
    last_other = swap(last)
    gain_grad = jnp.sum(
        (last[:, :, width:].astype(F32) + last_other[:, :, width:].astype(F32)).reshape(zs, share, 3, piece), axis=2
    ).reshape(width)
    row_out = pair(last, last_other, core, 0)[:, :, :width].reshape(exits, width)
    input_grad = pl.pallas_call(
        last_kernel,
        grid=(steps,),
        out_shape=shape((tokens, width), BF16),
        in_specs=[pl.BlockSpec(memory_space=pltpu.SMEM)] + [pl.BlockSpec(memory_space=pltpu.VMEM)] * 2,
        out_specs=pl.BlockSpec((tokens // steps, width), lambda i: (i, 0)),
        compiler_params=pltpu.CompilerParams(vmem_limit_bytes=SMALL),
    )(my_rows, main_all, row_out)
    return (input_grad[None], weight_grad[None], gain_grad[None], head_grad)


def solution(mesh):
    pipes, tensors = mesh.devices.shape
    fine = Mesh(mesh.devices.reshape(pipes, tensors // 2, 2), ("pipe", "z", "core"))
    tensor = ("z", "core")
    in_specs = (
        P("pipe", None, None),
        P("pipe", None, tensor),
        P("pipe", None),
        P(),
        P("pipe", tensor),
        P(),
        P(),
        P(),
        P(),
        P("pipe", None, None),
    )
    out_specs = (
        P("pipe", None, None),
        P("pipe", None, tensor),
        P("pipe", None),
        P("pipe", tensor),
    )
    return jax.shard_map(local, mesh=fine, in_specs=in_specs, out_specs=out_specs, check_vma=False)
```

time: 219 us -> 206 us (0.941)
  local copies, waits for them, and re-layouts: 25.6 us -> 7.7 us
  Pallas kernels: 22.6 us -> 35.6 us
  waiting for transfers between devices: 73.5 us -> 60.7 us
  starting transfers between devices: 41.8 us -> 51.1 us
  other arithmetic: 16.3 us -> 12.6 us
  matrix products: 12.3 us -> 10 us
    pallas_call x2 -> x6, Pallas kernels: 8.65 us -> 26.7 us  [the longest x3 9.55 us: piped_call(): pl.pallas_call(body, grid=(1,), out_shape=out, in_specs=specs, out_specs=...]
    unnamed x52 -> x44, local copies, waits for them, and re-layouts: 15.7 us -> 3.25 us
    ppermute x7 -> x8, starting transfers between devices: 9.92 us -> 19.4 us  [swap(): return lax.ppermute(values, 'core', [(0, 1), (1, 0)])]
    all_to_all x2, waiting for transfers between devices: 18.2 us -> 12.5 us  [the longest x1 6.76 us: local(): known_mine = lax.all_to_all(known_mine, 'z', 0, 0)]
    dynamic_slice x7 -> x4, local copies, waits for them, and re-layouts: 5.16 us -> 0.86 us  [the longest x1 0.72 us: local(): kept = lax.dynamic_slice_in_dim(kept, pipe * exits, exits, 0)]
    pallas_call x5 -> x3, Pallas kernels: 9.96 us -> 5.71 us  [kernel_call(): pl.pallas_call(body, out_shape=out, in_specs=[pl.BlockSpec(memory_space=p...]
    all_to_all x1, waiting for transfers between devices: 8.16 us -> 3.96 us  [local(): got = lax.all_to_all(send, 'z', 0, 0)]
    all_to_all x1, waiting for transfers between devices: 31 us -> 27.1 us  [local(): parts = lax.all_to_all(part, 'z', 0, 0)]
  transfers between devices with their start and end apart: 15 -> 17, of which waited for: 8 -> 11; matrix products, arithmetic and copies ran while one was open for 18% -> 13% of each run, Pallas kernels for 8% -> 12%
where the time goes in v7:
time: 206 us; the launch traced here: 205 us
  waiting for transfers between devices  60.7 us (29%)
  starting transfers between devices  51.1 us (25%)
  Pallas kernels  35.6 us (17%)
  between operations  14.2 us (7%)
  blocking collectives  13.3 us (6%)
  other arithmetic  12.6 us (6%)
  matrix products  10 us (5%)
  local copies, waits for them, and re-layouts  7.7 us (4%)
    all_to_all x1, waiting for transfers between devices, local(): parts = lax.all_to_all(part, 'z', 0, 0)  27.1 us
    ppermute x8, starting transfers between devices, swap(): return lax.ppermute(values, 'core', [(0, 1), (1, 0)])  19.4 us
    all_to_all x1, blocking collectives, spread(): lax.all_to_all(jnp.broadcast_to(values[None], (count,) + values.shape), a...  13.3 us
    pallas_call x3, Pallas kernels, piped_call(): pl.pallas_call(body, grid=(1,), out_shape=out, in_specs=specs, out_specs=...  9.55 us
    all_to_all x1, starting transfers between devices, local(): parts = lax.all_to_all(part, 'z', 0, 0)  8.19 us
    all_to_all x1, waiting for transfers between devices, local(): exit_got = lax.all_to_all(exit_part, 'pipe', 0, 0)  7.77 us
    pallas_call x1, Pallas kernels, local(): pl.pallas_call(gain_kernel, grid_spec=pltpu.PrefetchScalarGridSpec(num_sc...  6.84 us
    all_to_all x1, waiting for transfers between devices, local(): known_mine = lax.all_to_all(known_mine, 'z', 0, 0)  6.76 us
  transfers between devices with their start and end apart: 17, of which 11 were waited for; matrix products, arithmetic and copies ran while one was open for 13% of the time, Pallas kernels for 12%

profile of v7, /device:TPU:1, one launch (start us, length us, event | category | flops | bytes accessed | tf_op | source)
XLA Modules:
  0.0 205.3 jit_solution(17021991502003623749)
XLA Ops:
  7.2 3.3 %collective-permute-start = (bf16[4096,256]{1,0:T(8,128)(2,1)}, bf16[4096,256]{1,0:T(8,128)(2,1)}, u32[]{:S(2)}, u32[]{:S(2)}) collective-permute-start(bf16[4096,256]{1,0:T(8,128)(2,1)} %bitcast.42), channel_id=1, source_target_pairs={{0,1},{1,0},{2,3},{3,2},{4,5},{5,4},{6,7},{7,6},{8,9},{9,8},{10,11... | collective-permute-start | bytes 6291464 | tf_op jit(solution)/shard_map/ppermute | solution.py:23
  11.2 3.1 %multiply_reduce_fusion = (f32[32]{0:T(128)S(1)}, f32[32,4096]{1,0:T(8,128)S(1)}) fusion(bf16[1,512,4096]{2,1,0:T(8,128)(2,1)} %param.10, s32[32]{0:T(128)S(1)} %fusion.35.ids), kind=kOutput, calls=%fused_computation.27 | convolution fusion | flops 134496224 | bytes 4718848 | tf_op jit(solution)/shard_map/dot_general | solution.py:340
  15.0 5.9 %shard_map.129 = bf16[256,4096]{1,0:T(8,128)(2,1)} custom-call(s32[4]{0:T(128)} %pad_add_fusion.place, bf16[8,2,32,4096]{3,2,1,0:T(8,128)(2,1)} %bitcast.62, bf16[4096,256]{1,0:T(8,128)(2,1)} %bitcast.43, bf16[4096,256]{1,0:T(8,128)(2,1)} %collective-permute-done.weight_other), custom_call_target="tpu_custom_call" | custom-call | tf_op jit(solution)/shard_map/pallas_call | solution.py:354
  21.8 13.3 %all_to_all.35.mine = bf16[16,32,256]{2,1,0:T(8,128)(2,1)S(1)} all-to-all(bf16[16,32,256]{2,1,0:T(8,128)(2,1)S(1)} %broadcast_in_dim.29), channel_id=1, replica_groups=mesh['pipe'=16,'z'=8,'core'=2] {'pipe'}, dimensions={0} | all-to-all | bytes 524288 | tf_op jit(solution)/shard_map/all_to_all | solution.py:19
  39.1 8.2 %all-to-all-start.1 = ((bf16[8,64,1024]{2,1,0:T(8,128)(2,1)}), bf16[8,64,1024]{2,1,0:T(8,128)(2,1)S(1)}, u32[]{:S(2)}, u32[]{:S(2)}) async-start(bf16[8,64,1024]{2,1,0:T(8,128)(2,1)} %shard_map.130), calls=%async_computation.1 | async-start | bytes 2097152 | tf_op jit(solution)/shard_map/all_to_all | solution.py:383
  48.3 6.8 %shard_map.131.gain_part = f32[1,4096]{1,0:T(1,128)} custom-call(s32[4]{0:T(128)} %pad_add_fusion.place, bf16[8,2,32,4096]{3,2,1,0:T(8,128)(2,1)} %bitcast.63, bf16[8,2,32,4096]{3,2,1,0:T(8,128)(2,1)} %bitcast.56, s32[1,32]{1,0:T(1,128)} %constant_dynamic-slice_fusion.4.ids, bf16[4096,256]{1,0:T(8,128)(2,1)} %bitcast.44, ...), custom_call_target="tpu_custom_call" | custom-call | tf_op jit(solution)/shard_map/pallas_call | solution.py:385
  55.2 27.1 %all-to-all-done.1.parts = bf16[8,64,1024]{2,1,0:T(8,128)(2,1)S(1)} async-done(((bf16[8,64,1024]{2,1,0:T(8,128)(2,1)}), bf16[8,64,1024]{2,1,0:T(8,128)(2,1)S(1)}, u32[]{:S(2)}, u32[]{:S(2)}) %all-to-all-start.1) | async-done | bytes 1048608 | tf_op jit(solution)/shard_map/all_to_all | solution.py:383
  84.0 1.9 collective-permute-start.3
  87.4 6.0 %all-to-all-start.2 = ((f32[16,2,8,128]{3,2,1,0:T(8,128)}), f32[16,2,8,128]{3,2,1,0:T(8,128)S(1)}, u32[]{:S(2)}, u32[]{:S(2)}) async-start(f32[16,2,8,128]{3,2,1,0:T(8,128)} %broadcast_in_dim.56), calls=%async_computation.3 | async-start | bytes 262144 | tf_op jit(solution)/shard_map/all_to_all | solution.py:19
  95.8 4.4 %all-to-all-done.2 = f32[16,2,8,128]{3,2,1,0:T(8,128)S(1)} async-done(((f32[16,2,8,128]{3,2,1,0:T(8,128)}), f32[16,2,8,128]{3,2,1,0:T(8,128)S(1)}, u32[]{:S(2)}, u32[]{:S(2)}) %all-to-all-start.2) | async-done | bytes 131104 | tf_op jit(solution)/shard_map/all_to_all | solution.py:19
  100.9 3.3 %all-to-all-start.3 = ((f32[8,8,128]{2,1,0:T(8,128)}), f32[8,8,128]{2,1,0:T(8,128)S(1)}, u32[]{:S(2)}, u32[]{:S(2)}) async-start(f32[8,8,128]{2,1,0:T(8,128)} %shard_map.133), calls=%async_computation.4 | async-start | bytes 65536 | tf_op jit(solution)/shard_map/all_to_all | solution.py:432
  104.3 6.8 %all-to-all-done.3.known = f32[8,8,128]{2,1,0:T(8,128)S(1)} async-done(((f32[8,8,128]{2,1,0:T(8,128)}), f32[8,8,128]{2,1,0:T(8,128)S(1)}, u32[]{:S(2)}, u32[]{:S(2)}) %all-to-all-start.3) | async-done | bytes 32800 | tf_op jit(solution)/shard_map/all_to_all | solution.py:432
  111.1 2.9 %collective-permute-start.4 = (f32[8,8,128]{2,1,0:T(8,128)S(1)}, f32[8,8,128]{2,1,0:T(8,128)S(1)}, u32[]{:S(2)}, u32[]{:S(2)}) collective-permute-start(f32[8,8,128]{2,1,0:T(8,128)S(1)} %all-to-all-done.3.known), channel_id=1, source_target_pairs={{0,1},{1,0},{2,3},{3,2},{4,5},{5,4},{6,7},{7,6},{8,9},{9,8},{10,11... | collective-permute-start | bytes 98312 | tf_op jit(solution)/shard_map/ppermute | solution.py:23
  114.1 2.0 fusion.12
  116.1 2.1 %all-gather.6.cloned.1.call-done = bf16[512,1024]{1,0:T(8,128)(2,1)} async-done(((bf16[64,1024]{1,0:T(8,128)(2,1)}), bf16[512,1024]{1,0:T(8,128)(2,1)}) %all-gather.6.cloned.1.call-update) | async-done | bytes 1048592 | tf_op jit(solution)/shard_map/all_gather | solution.py:425
  118.3 3.2 %fusion = f32[512]{0:T(512)S(1)} fusion(bf16[512,4096]{1,0:T(8,128)(2,1)} %bitcast.60), kind=kLoop, calls=%fused_computation.2 | loop fusion | flops 6290944 | bytes 4196352 | tf_op jit(solution)/shard_map/reduce_sum | solution.py:445
  122.8 5.2 %collective-permute-start.5 = (bf16[8,64,1024]{2,1,0:T(8,128)(2,1)}, bf16[8,64,1024]{2,1,0:T(8,128)(2,1)S(1)}, u32[]{:S(2)}, u32[]{:S(2)}) collective-permute-start(bf16[8,64,1024]{2,1,0:T(8,128)(2,1)} %bitcast.17.expo), channel_id=1, source_target_pairs={{0,1},{1,0},{2,3},{3,2},{4,5},{5,4},{6,7},{7,6},{8,9},{9,8},{10,11... | collective-permute-start | bytes 3145736 | tf_op jit(solution)/shard_map/ppermute | solution.py:23
  127.9 3.6 %fusion.2 = bf16[512,4096]{1,0:T(8,128)(2,1)} fusion(bf16[512,4096]{1,0:T(8,128)(2,1)S(1)} %bitcast.61, f32[4096]{0:T(1024)S(1)} %bitcast.50, f32[512]{0:T(512)S(1)} %add_rsqrt_fusion), kind=kLoop, calls=%fused_computation.4 | loop fusion | flops 8388608 | bytes 8407040 | tf_op jit(solution)/shard_map/convert_element_type | solution.py:446
  131.6 3.7 %shard_map.134 = (f32[512,256]{1,0:T(8,128)}, bf16[8,64,1024]{2,1,0:T(8,128)(2,1)}, f32[512,128]{1,0:T(8,128)}) custom-call(s32[4]{0:T(128)} %pad_add_fusion.place, bf16[8,64,1024]{2,1,0:T(8,128)(2,1)} %bitcast.17.expo, f32[8,8,128]{2,1,0:T(8,128)} %copy-done.17, s32[512,1]{1,0:T(8,128)} %copy-done.13, bf16[1024,256]{1,0:T(8,128)(2,1)} %copy-done.3), custom_call_target="tpu_custom_call" | custom-call | tf_op jit(solution)/shard_map/pallas_call | solution.py:56
  136.3 3.5 %shard_map.135 = (bf16[16,32,256]{2,1,0:T(8,128)(2,1)}, bf16[8,64,1024]{2,1,0:T(8,128)(2,1)}) custom-call(s32[4]{0:T(128)} %pad_add_fusion.place, bf16[8,64,1024]{2,1,0:T(8,128)(2,1)} %copy-done.15, f32[8,8,128]{2,1,0:T(8,128)} %copy-done.18, s32[512,1]{1,0:T(8,128)} %copy-done.13, bf16[1024,256]{1,0:T(8,128)(2,1)} %copy-done.14, ...), custom_call_target="tpu_custom_call" | custom-call | tf_op jit(solution)/shard_map/pallas_call | solution.py:56
  139.8 6.4 %all-to-all-start.4 = ((bf16[16,32,256]{2,1,0:T(8,128)(2,1)}), bf16[16,32,256]{2,1,0:T(8,128)(2,1)S(1)}, u32[]{:S(2)}, u32[]{:S(2)}) async-start(bf16[16,32,256]{2,1,0:T(8,128)(2,1)} %get-tuple-element.66), calls=%async_computation.5 | async-start | bytes 524288 | tf_op jit(solution)/shard_map/all_to_all | solution.py:481
  147.0 7.8 %all-to-all-done.4.got = bf16[16,32,256]{2,1,0:T(8,128)(2,1)S(1)} async-done(((bf16[16,32,256]{2,1,0:T(8,128)(2,1)}), bf16[16,32,256]{2,1,0:T(8,128)(2,1)S(1)}, u32[]{:S(2)}, u32[]{:S(2)}) %all-to-all-start.4) | async-done | bytes 262176 | tf_op jit(solution)/shard_map/all_to_all | solution.py:481
  157.4 3.5 %shard_map.137 = bf16[8,2,5888]{2,1,0:T(2,128)(2,1)} custom-call(s32[4]{0:T(128)S(1)} %copy-done.11, f32[16,256]{1,0:T(8,128)S(1)} %get-tuple-element.71.mine, f32[16,256]{1,0:T(8,128)S(1)} %collective-permute-done.6.other, bf16[4096,256]{1,0:T(8,128)(2,1)S(1)} %bitcast.45, bf16[4096,256]{1,0:T(8,128)(2,1)} %collective-permute-done.weight_other, ...), custom_call_target="tpu_custom_call" | custom-call | tf_op jit(solution)/shard_map/pallas_call | solution.py:33
  161.0 4.3 %all-to-all-start.5 = ((bf16[8,2,5888]{2,1,0:T(2,128)(2,1)}), bf16[8,2,5888]{2,1,0:T(2,128)(2,1)S(1)}, u32[]{:S(2)}, u32[]{:S(2)}) async-start(bf16[8,2,5888]{2,1,0:T(2,128)(2,1)} %shard_map.137), calls=%async_computation.6 | async-start | bytes 376832 | tf_op jit(solution)/shard_map/all_to_all | solution.py:508
  165.3 5.3 %convolution_convert_fusion = bf16[4096,256]{1,0:T(8,128)(2,1)} fusion(bf16[512,4096]{1,0:T(8,128)(2,1)} %fusion.2, bf16[32,256]{1,0:T(8,128)(2,1)S(1)} %get-tuple-element.77, pred[512]{0:T(512)(128)(4,1)S(1)} %compare_reduce_fusion, bf16[512,4096]{1,0:T(8,128)(2,1)} %bitcast.66, s32[]{:T(128)S(6)} %select_n.73, s32[32]{0:T(128)S(1)} %fusion.35.ids), kind=kOutput, calls=%fused_computation.5 | convolution fusion | flops 1083457536 | bytes 6570628 | tf_op jit(solution)/shard_map/dot_general | solution.py:515
  170.5 4.0 %all-to-all-done.5.got = bf16[8,2,5888]{2,1,0:T(2,128)(2,1)S(1)} async-done(((bf16[8,2,5888]{2,1,0:T(2,128)(2,1)}), bf16[8,2,5888]{2,1,0:T(2,128)(2,1)S(1)}, u32[]{:S(2)}, u32[]{:S(2)}) %all-to-all-start.5) | async-done | bytes 188448 | tf_op jit(solution)/shard_map/all_to_all | solution.py:508
  175.3 3.4 %all-to-all-start.6 = ((bf16[8,2,4864]{2,1,0:T(2,128)(2,1)}), bf16[8,2,4864]{2,1,0:T(2,128)(2,1)S(1)}, u32[]{:S(2)}, u32[]{:S(2)}) async-start(bf16[8,2,4864]{2,1,0:T(2,128)(2,1)} %shard_map.138), calls=%async_computation.7 | async-start | bytes 311296 | tf_op jit(solution)/shard_map/all_to_all | solution.py:537
  178.8 2.4 %shard_map.139 = bf16[2000,256]{1,0:T(8,128)(2,1)} custom-call(s32[4]{0:T(128)S(1)} %copy-done.11, bf16[16,32,256]{2,1,0:T(8,128)(2,1)S(1)} %all_to_all.35.mine, f32[1,256]{1,0:T(1,128)S(1)} %bitcast.53, f32[512,128]{1,0:T(8,128)S(1)} %copy-done.8, bf16[8,64,1024]{2,1,0:T(8,128)(2,1)S(1)} %copy-done.5, bf16[8,64,1024]{2,1,0:T(8,128)(2,1)S(1)} %copy-done.6), custom_call_target="tpu_custom_call" | custom-call | tf_op jit(solution)/shard_map/pallas_call | solution.py:56
  181.1 5.8 %all-to-all-done.6 = bf16[8,2,4864]{2,1,0:T(2,128)(2,1)S(1)} async-done(((bf16[8,2,4864]{2,1,0:T(2,128)(2,1)}), bf16[8,2,4864]{2,1,0:T(2,128)(2,1)S(1)}, u32[]{:S(2)}, u32[]{:S(2)}) %all-to-all-start.6) | async-done | bytes 155680 | tf_op jit(solution)/shard_map/all_to_all | solution.py:537
  186.9 3.1 %collective-permute-start.7 = (bf16[8,2,4864]{2,1,0:T(2,128)(2,1)S(1)}, bf16[8,2,4864]{2,1,0:T(2,128)(2,1)S(1)}, u32[]{:S(2)}, u32[]{:S(2)}) collective-permute-start(bf16[8,2,4864]{2,1,0:T(2,128)(2,1)S(1)} %all-to-all-done.6), channel_id=1, source_target_pairs={{0,1},{1,0},{2,3},{3,2},{4,5},{5,4},{6,7},{7,6},{8,9},{9,8},{10,11... | collective-permute-start | bytes 466952 | tf_op jit(solution)/shard_map/ppermute | solution.py:23
  192.2 2.2 %copy-done.4 = bf16[512,4096]{1,0:T(8,128)(2,1)S(1)} copy-done((bf16[512,4096]{1,0:T(8,128)(2,1)S(1)}, bf16[512,4096]{1,0:T(8,128)(2,1)}, u32[]{:S(2)}) %copy-start.4) | copy-done | bytes 4194328
  194.4 4.4 %shard_map.140 = bf16[512,4096]{1,0:T(8,128)(2,1)} custom-call(s32[32]{0:T(128)S(1)} %fusion.35.ids, bf16[512,4096]{1,0:T(8,128)(2,1)S(1)} %copy-done.4, bf16[32,4096]{1,0:T(8,128)(2,1)S(1)} %reshape.115.rows), custom_call_target="tpu_custom_call" | custom-call | tf_op jit(solution)/shard_map/pallas_call | solution.py:544
  (106 shorter events, 22.1 us)
Async XLA Ops:
  7.2 76.6 %reduce-scatter.2.cloned.1.call-start = ((), (), s32[]{:S(2)}) async-start(), calls=%async_computation.8 | async-start | bytes 2359296 | tf_op jit(solution)/shard_map/reduce_scatter | solution.py:366
  7.2 7.7 %collective-permute-start = (bf16[4096,256]{1,0:T(8,128)(2,1)}, bf16[4096,256]{1,0:T(8,128)(2,1)}, u32[]{:S(2)}, u32[]{:S(2)}) collective-permute-start(bf16[4096,256]{1,0:T(8,128)(2,1)} %bitcast.42), channel_id=1, source_target_pairs={{0,1},{1,0},{2,3},{3,2},{4,5},{5,4},{6,7},{7,6},{8,9},{9,8},{10,11... | collective-permute-start | bytes 6291464 | tf_op jit(solution)/shard_map/ppermute | solution.py:23
  21.0 26.3 %copy-start.19 = (s32[16,32]{1,0:T(8,128)S(1)}, s32[16,32]{1,0:T(8,128)}, u32[]{:S(2)}) copy-start(s32[16,32]{1,0:T(8,128)} %param.17) | copy-start | bytes 6148
  21.1 18.0 %copy-start.14 = (bf16[1024,256]{1,0:T(8,128)(2,1)}, bf16[1024,256]{1,0:T(8,128)(2,1)S(1)}, u32[]{:S(2)}) copy-start(bf16[1024,256]{1,0:T(8,128)(2,1)S(1)} %get-tuple-element.90.head) | copy-start | bytes 1572868
  21.1 34.0 %copy-start.3 = (bf16[1024,256]{1,0:T(8,128)(2,1)}, bf16[1024,256]{1,0:T(8,128)(2,1)S(1)}, u32[]{:S(2)}) copy-start(bf16[1024,256]{1,0:T(8,128)(2,1)S(1)} %get-tuple-element.91.head_mine.head) | copy-start | bytes 1572868
  21.1 15.9 %collective-permute-start.2 = (bf16[1024,256]{1,0:T(8,128)(2,1)S(1)}, bf16[1024,256]{1,0:T(8,128)(2,1)S(1)}, u32[]{:S(2)}, u32[]{:S(2)}) collective-permute-start(bf16[1024,256]{1,0:T(8,128)(2,1)S(1)} %get-tuple-element.90.head), channel_id=1, source_target_pairs={{0,1},{1,0},{2,3},{3,2},{4,5},{5,4},{6,7},{7,6},{8,9},{9,8},{10,11... | collective-permute-start | bytes 1572872 | tf_op jit(solution)/shard_map/ppermute | solution.py:23
  35.1 2.3 %collective-permute-start.1 = (bf16[16,32,256]{2,1,0:T(8,128)(2,1)S(1)}, bf16[16,32,256]{2,1,0:T(8,128)(2,1)S(1)}, u32[]{:S(2)}, u32[]{:S(2)}) collective-permute-start(bf16[16,32,256]{2,1,0:T(8,128)(2,1)S(1)} %all_to_all.35.mine), channel_id=1, source_target_pairs={{0,1},{1,0},{2,3},{3,2},{4,5},{5,4},{6,7},{7,6},{8,9},{9,8},{10,11... | collective-permute-start | bytes 786440 | tf_op jit(solution)/shard_map/ppermute | solution.py:23
  39.1 43.1 %all-to-all-start.1 = ((bf16[8,64,1024]{2,1,0:T(8,128)(2,1)}), bf16[8,64,1024]{2,1,0:T(8,128)(2,1)S(1)}, u32[]{:S(2)}, u32[]{:S(2)}) async-start(bf16[8,64,1024]{2,1,0:T(8,128)(2,1)} %shard_map.130), calls=%async_computation.1 | async-start | bytes 2097152 | tf_op jit(solution)/shard_map/all_to_all | solution.py:383
  47.3 70.9 %all-gather.6.cloned.1.call-start = ((), (), s32[]{:S(2)}) async-start(), calls=%async_computation.10 | async-start | bytes 1179648 | tf_op jit(solution)/shard_map/all_gather | solution.py:425
  48.3 34.0 %copy-start.10 = (s32[4]{0:T(128)S(1)}, s32[4]{0:T(128)}, u32[]{:S(2)}) copy-start(s32[4]{0:T(128)} %pad_add_fusion.place) | copy-start | bytes 52
  48.3 35.5 %copy-start.20 = (f32[16]{0:T(128)S(1)}, f32[16]{0:T(128)}, u32[]{:S(2)}) copy-start(f32[16]{0:T(128)} %param.18) | copy-start | bytes 196
  48.3 35.5 %copy-start.21 = (s32[16]{0:T(128)S(1)}, s32[16]{0:T(128)}, u32[]{:S(2)}) copy-start(s32[16]{0:T(128)} %param.16) | copy-start | bytes 196
  84.0 2.7 %collective-permute-start.3 = (f32[8,128]{1,0:T(8,128)S(1)}, f32[8,128]{1,0:T(8,128)S(1)}, u32[]{:S(2)}, u32[]{:S(2)}) collective-permute-start(f32[8,128]{1,0:T(8,128)S(1)} %get-tuple-element.54.own), channel_id=1, source_target_pairs={{0,1},{1,0},{2,3},{3,2},{4,5},{5,4},{6,7},{7,6},{8,9},{9,8},{10,11... | collective-permute-start | bytes 12296 | tf_op jit(solution)/shard_map/ppermute | solution.py:23
  87.4 12.9 %all-to-all-start.2 = ((f32[16,2,8,128]{3,2,1,0:T(8,128)}), f32[16,2,8,128]{3,2,1,0:T(8,128)S(1)}, u32[]{:S(2)}, u32[]{:S(2)}) async-start(f32[16,2,8,128]{3,2,1,0:T(8,128)} %broadcast_in_dim.56), calls=%async_computation.3 | async-start | bytes 262144 | tf_op jit(solution)/shard_map/all_to_all | solution.py:19
  100.9 10.2 %all-to-all-start.3 = ((f32[8,8,128]{2,1,0:T(8,128)}), f32[8,8,128]{2,1,0:T(8,128)S(1)}, u32[]{:S(2)}, u32[]{:S(2)}) async-start(f32[8,8,128]{2,1,0:T(8,128)} %shard_map.133), calls=%async_computation.4 | async-start | bytes 65536 | tf_op jit(solution)/shard_map/all_to_all | solution.py:432
  104.3 71.1 %all-gather.4.cloned.1.call-start = ((), (), s32[]{:S(2)}) async-start(), calls=%async_computation.9 | async-start | bytes 4456448 | tf_op jit(solution)/shard_map/all_gather | solution.py:459
  111.1 20.5 %copy-start.17 = (f32[8,8,128]{2,1,0:T(8,128)}, f32[8,8,128]{2,1,0:T(8,128)S(1)}, u32[]{:S(2)}) copy-start(f32[8,8,128]{2,1,0:T(8,128)S(1)} %all-to-all-done.3.known) | copy-start | bytes 98308
  111.1 5.0 %collective-permute-start.4 = (f32[8,8,128]{2,1,0:T(8,128)S(1)}, f32[8,8,128]{2,1,0:T(8,128)S(1)}, u32[]{:S(2)}, u32[]{:S(2)}) collective-permute-start(f32[8,8,128]{2,1,0:T(8,128)S(1)} %all-to-all-done.3.known), channel_id=1, source_target_pairs={{0,1},{1,0},{2,3},{3,2},{4,5},{5,4},{6,7},{7,6},{8,9},{9,8},{10,11... | collective-permute-start | bytes 98312 | tf_op jit(solution)/shard_map/ppermute | solution.py:23
  116.1 15.5 %copy-start.18 = (f32[8,8,128]{2,1,0:T(8,128)}, f32[8,8,128]{2,1,0:T(8,128)S(1)}, u32[]{:S(2)}) copy-start(f32[8,8,128]{2,1,0:T(8,128)S(1)} %collective-permute-done.4.known) | copy-start | bytes 98308
  118.2 9.7 %copy-start.12 = (bf16[1,512,4096]{2,1,0:T(8,128)(2,1)S(1)}, bf16[1,512,4096]{2,1,0:T(8,128)(2,1)}, u32[]{:S(2)}) copy-start(bf16[1,512,4096]{2,1,0:T(8,128)(2,1)} %param.10) | copy-start | bytes 12582916
  122.8 12.5 %collective-permute-start.5 = (bf16[8,64,1024]{2,1,0:T(8,128)(2,1)}, bf16[8,64,1024]{2,1,0:T(8,128)(2,1)S(1)}, u32[]{:S(2)}, u32[]{:S(2)}) collective-permute-start(bf16[8,64,1024]{2,1,0:T(8,128)(2,1)} %bitcast.17.expo), channel_id=1, source_target_pairs={{0,1},{1,0},{2,3},{3,2},{4,5},{5,4},{6,7},{7,6},{8,9},{9,8},{10,11... | collective-permute-start | bytes 3145736 | tf_op jit(solution)/shard_map/ppermute | solution.py:23
  131.6 23.1 %copy-start.11 = (s32[4]{0:T(128)S(1)}, s32[4]{0:T(128)}, u32[]{:S(2)}) copy-start(s32[4]{0:T(128)} %pad_add_fusion.place) | copy-start | bytes 52
  131.6 25.8 %copy-start.2 = (bf16[1,4096,256]{2,1,0:T(8,128)(2,1)S(1)}, bf16[1,4096,256]{2,1,0:T(8,128)(2,1)}, u32[]{:S(2)}) copy-start(bf16[1,4096,256]{2,1,0:T(8,128)(2,1)} %param.11) | copy-start | bytes 6291460
  131.6 25.8 %copy-start.9 = (f32[1,4096]{1,0:T(1,128)S(1)}, f32[1,4096]{1,0:T(1,128)}, u32[]{:S(2)}) copy-start(f32[1,4096]{1,0:T(1,128)} %shard_map.131.gain_part) | copy-start | bytes 49156
  139.8 14.9 %all-to-all-start.4 = ((bf16[16,32,256]{2,1,0:T(8,128)(2,1)}), bf16[16,32,256]{2,1,0:T(8,128)(2,1)S(1)}, u32[]{:S(2)}, u32[]{:S(2)}) async-start(bf16[16,32,256]{2,1,0:T(8,128)(2,1)} %get-tuple-element.66), calls=%async_computation.5 | async-start | bytes 524288 | tf_op jit(solution)/shard_map/all_to_all | solution.py:481
  155.4 2.1 %collective-permute-start.6 = (f32[16,256]{1,0:T(8,128)S(1)}, f32[16,256]{1,0:T(8,128)S(1)}, u32[]{:S(2)}, u32[]{:S(2)}) collective-permute-start(f32[16,256]{1,0:T(8,128)S(1)} %get-tuple-element.72), channel_id=1, source_target_pairs={{0,1},{1,0},{2,3},{3,2},{4,5},{5,4},{6,7},{7,6},{8,9},{9,8},{10,11... | collective-permute-start | bytes 49160 | tf_op jit(solution)/shard_map/ppermute | solution.py:23
  161.0 13.5 %all-to-all-start.5 = ((bf16[8,2,5888]{2,1,0:T(2,128)(2,1)}), bf16[8,2,5888]{2,1,0:T(2,128)(2,1)S(1)}, u32[]{:S(2)}, u32[]{:S(2)}) async-start(bf16[8,2,5888]{2,1,0:T(2,128)(2,1)} %shard_map.137), calls=%async_computation.6 | async-start | bytes 376832 | tf_op jit(solution)/shard_map/all_to_all | solution.py:508
  165.2 13.5 %copy-start.5 = (bf16[8,64,1024]{2,1,0:T(8,128)(2,1)S(1)}, bf16[8,64,1024]{2,1,0:T(8,128)(2,1)}, u32[]{:S(2)}) copy-start(bf16[8,64,1024]{2,1,0:T(8,128)(2,1)} %get-tuple-element.85.dl_mine) | copy-start | bytes 3145732
  165.2 13.5 %copy-start.6 = (bf16[8,64,1024]{2,1,0:T(8,128)(2,1)S(1)}, bf16[8,64,1024]{2,1,0:T(8,128)(2,1)}, u32[]{:S(2)}) copy-start(bf16[8,64,1024]{2,1,0:T(8,128)(2,1)} %get-tuple-element.86.dl_other) | copy-start | bytes 3145732
  165.2 13.5 %copy-start.8 = (f32[512,128]{1,0:T(8,128)S(1)}, f32[512,128]{1,0:T(8,128)}, u32[]{:S(2)}) copy-start(f32[512,128]{1,0:T(8,128)} %get-tuple-element.84.kept) | copy-start | bytes 786436
  175.3 11.5 %all-to-all-start.6 = ((bf16[8,2,4864]{2,1,0:T(2,128)(2,1)}), bf16[8,2,4864]{2,1,0:T(2,128)(2,1)S(1)}, u32[]{:S(2)}, u32[]{:S(2)}) async-start(bf16[8,2,4864]{2,1,0:T(2,128)(2,1)} %shard_map.138), calls=%async_computation.7 | async-start | bytes 311296 | tf_op jit(solution)/shard_map/all_to_all | solution.py:537
  186.9 4.1 %collective-permute-start.7 = (bf16[8,2,4864]{2,1,0:T(2,128)(2,1)S(1)}, bf16[8,2,4864]{2,1,0:T(2,128)(2,1)S(1)}, u32[]{:S(2)}, u32[]{:S(2)}) collective-permute-start(bf16[8,2,4864]{2,1,0:T(2,128)(2,1)S(1)} %all-to-all-done.6), channel_id=1, source_target_pairs={{0,1},{1,0},{2,3},{3,2},{4,5},{5,4},{6,7},{7,6},{8,9},{9,8},{10,11... | collective-permute-start | bytes 466952 | tf_op jit(solution)/shard_map/ppermute | solution.py:23
  (7 other events, 34.7 us)
Sparse Core Ops, SparseCore 0:
  21.1 53.3 reduce-scatter.1
  83.9 34.2 all-gather.5
  120.0 45.2 all-gather.3

commit v8 on v7

--- a/solution.py
+++ b/solution.py
@@ -21,12 +21,6 @@
 
 def swap(values):
     return lax.ppermute(values, "core", [(0, 1), (1, 0)])
-
-
-def pair(mine, other, core, axis):
-    first = jnp.where(core == 0, mine, other)
-    second = jnp.where(core == 0, other, mine)
-    return jnp.concatenate([first, second], axis=axis)
 
 
 def kernel_call(body, out, *operands):
@@ -49,9 +43,12 @@
     )(*operands)
 
 
-def piped_call(body, out, *operands, limit=LARGE):
+def piped_call(body, out, *operands, held=(), scratch=(), limit=LARGE):
     specs = [pl.BlockSpec(memory_space=pltpu.SMEM)] + [
-        pl.BlockSpec(value.shape, lambda i, n=value.ndim: (0,) * n) for value in operands[1:]
+        pl.BlockSpec(memory_space=pltpu.VMEM)
+        if i in held
+        else pl.BlockSpec(value.shape, lambda i, n=value.ndim: (0,) * n)
+        for i, value in enumerate(operands[1:], 1)
     ]
     return pl.pallas_call(
         body,
@@ -59,6 +56,7 @@
         out_shape=out,
         in_specs=specs,
         out_specs=jax.tree.map(lambda value: pl.BlockSpec(value.shape, lambda i, n=len(value.shape): (0,) * n), out),
+        scratch_shapes=list(scratch),
         compiler_params=pltpu.CompilerParams(vmem_limit_bytes=limit),
     )(*operands)
 
@@ -192,7 +190,7 @@
     return grad[...].reshape(count * rows, columns)
 
 
-def exit_kernel(half, vocab, place, expo, known, targets, head, part, grad, kept):
+def exit_kernel(half, vocab, place, expo, known, targets, head, part, kept, grad):
     rows = logit_grads(half, vocab, place[1], place[2], expo, known, targets, grad, kept)
     part[...] = jnp.dot(rows, head[...], preferred_element_type=F32)
 
@@ -203,17 +201,16 @@
     part[...] = total.astype(BF16).reshape(part.shape)
 
 
-def head_kernel(half, place, mine, gain, kept, dl_mine, dl_other, out):
-    core = place[1]
-    row = mine[...].reshape(-1, mine.shape[-1]).astype(F32)
+def head_kernel(half, vocab, place, row, gain, kept, targets, ex_mine, ex_other, known_mine, known_other, out, grad):
+    core, start = place[1], place[2]
+    row = row[...].reshape(-1, row.shape[-1]).astype(F32)
     normed = (row * kept[:, 1:2] * gain[...]).astype(BF16)
     over_rows = (((0,), (0,)), ((), ()))
-    low = lax.dot_general(
-        dl_mine[...].reshape(row.shape[0], -1), normed, over_rows, preferred_element_type=F32
-    )
-    high = lax.dot_general(
-        dl_other[...].reshape(row.shape[0], -1), normed, over_rows, preferred_element_type=F32
-    )
+    parts = []
+    for which, expo, known in ((core, ex_mine, known_mine), (1 - core, ex_other, known_other)):
+        rows = logit_grads(half, vocab, which, start, expo, known, targets, grad, None)
+        parts.append(lax.dot_general(rows, normed, over_rows, preferred_element_type=F32))
+    low, high = parts
     out[:half, :] = jnp.where(core == 0, low, high)[:half].astype(BF16)
     out[half:, :] = jnp.where(core == 0, high, low)[: out.shape[0] - half].astype(BF16)
 
@@ -282,18 +279,48 @@
     out[...] = jnp.broadcast_to(whole.astype(BF16)[None], out.shape)
 
 
-def last_kernel(ids, main, rows, out):
-    step = pl.program_id(0)
-    count = out.shape[0]
-    out[...] = main[pl.ds(pl.multiple_of(step * count, count), count), :]
-    tile = lax.broadcasted_iota(jnp.int32, (16, out.shape[1]), 0)
-    for i in range(rows.shape[0]):
-        at = ids[i] - step * count
-
-        @pl.when((at >= 0) & (at < count))
-        def _():
-            start = pl.multiple_of(at // 16 * 16, 16)
-            out[pl.ds(start, 16), :] = jnp.where(tile == at - start, rows[i : i + 1, :], out[pl.ds(start, 16), :])
+def last_kernel(parts, place, ids, mine, other, main, out, gain_out, block, into, outof):
+    core = place[1]
+    tokens, width = block.shape
+    count = tokens // parts
+
+    def copies(source, target, done):
+        return [
+            pltpu.make_async_copy(
+                source.at[pl.ds(i * count, count)], target.at[pl.ds(i * count, count)], done.at[i]
+            )
+            for i in range(parts)
+        ]
+
+    loads = copies(main, block, into)
+    stores = copies(block, out, outof)
+    for load in loads:
+        load.start()
+    groups, share = mine.shape[:2]
+    piece = (mine.shape[2] - width) // 3
+    total = mine[:, :, width:].astype(F32) + other[:, :, width:].astype(F32)
+    total = total[:, :, :piece] + total[:, :, piece : 2 * piece] + total[:, :, 2 * piece :]
+    for i in range(groups):
+        for j in range(share):
+            at = (i * share + j) * piece
+            gain_out[:, at : at + piece] = total[i, j : j + 1]
+    tile = lax.broadcasted_iota(jnp.int32, (16, width), 0)
+    for k in range(parts):
+        loads[k].wait()
+        for rows, first in ((mine, core), (other, 1 - core)):
+            for i in range(groups):
+                for j in range(share):
+                    at = ids[first * groups * share + i * share + j]
+
+                    @pl.when(at // count == k)
+                    def _():
+                        start = pl.multiple_of(at // 16 * 16, 16)
+                        row = rows[i, j : j + 1, :width]
+                        block[pl.ds(start, 16), :] = jnp.where(tile == at - start, row, block[pl.ds(start, 16), :])
+
+        stores[k].start()
+    for store in stores:
+        store.wait()
 
 
 def local(
@@ -430,7 +457,6 @@
     )
     known_sent = known_mine
     known_mine = lax.all_to_all(known_mine, "z", 0, 0)
-    known_other = swap(known_mine)
 
     first = block * held
     held_in = lax.dynamic_slice_in_dim(after(seg, stats_other), first, held, 0).astype(F32)
@@ -455,28 +481,33 @@
     known_mine, normed, grad_rows, core_unit, share_unit, share_inv = lax.optimization_barrier(
         (known_mine, normed, grad_rows, core_unit, share_unit, share_inv)
     )
+    known_other = swap(known_mine)
     ex_mine, main_out = lax.optimization_barrier((after(ex_mine, known_other), main_out))
     main_all = lax.all_gather(main_out, ("z", "core"), axis=0, tiled=True)
     ex_other = swap(ex_mine)
 
-    exit_first, dl_mine, kept = piped_call(
+    grads = [pltpu.VMEM((zs, own, padded), BF16)]
+    exit_first, kept = piped_call(
         functools.partial(exit_kernel, half, vocab_part),
-        [shape((rows_all, slab), F32), shape((zs, own, padded), BF16), shape((rows_all, 128), F32)],
+        [shape((rows_all, slab), F32), shape((rows_all, 128), F32)],
         place,
         ex_mine,
         known_mine,
         all_targets,
         head_mine,
-    )
-    exit_part, dl_other = piped_call(
+        scratch=grads,
+    )
+    exit_part = piped_call(
         functools.partial(exit_rest_kernel, half, vocab_part),
-        [shape((pipes, exits, slab), BF16), shape((zs, own, padded), BF16)],
+        shape((pipes, exits, slab), BF16),
         place,
         ex_other,
         known_other,
         all_targets,
         head_rest,
         exit_first,
+        held=(1, 5),
+        scratch=grads,
     )
     exit_got = lax.all_to_all(exit_part, "pipe", 0, 0)
     kept_all = kept
@@ -524,32 +555,38 @@
     )
     last, main_all = lax.optimization_barrier((last, main_all))
     head_grad = piped_call(
-        functools.partial(head_kernel, half),
+        functools.partial(head_kernel, half, vocab_part),
         shape((vocab_part, slab), BF16),
         place,
         all_mine,
         gain_mine,
         after(kept_all, last),
-        dl_mine,
-        dl_other,
-        limit=SMALL,
+        all_targets,
+        ex_mine,
+        ex_other,
+        known_mine,
+        known_other,
+        scratch=grads,
     )
     last = lax.all_to_all(last, "z", 0, 0)
     last, head_grad = lax.optimization_barrier((last, head_grad))
     last_other = swap(last)
-    gain_grad = jnp.sum(
-        (last[:, :, width:].astype(F32) + last_other[:, :, width:].astype(F32)).reshape(zs, share, 3, piece), axis=2
-    ).reshape(width)
-    row_out = pair(last, last_other, core, 0)[:, :, :width].reshape(exits, width)
-    input_grad = pl.pallas_call(
-        last_kernel,
-        grid=(steps,),
-        out_shape=shape((tokens, width), BF16),
-        in_specs=[pl.BlockSpec(memory_space=pltpu.SMEM)] + [pl.BlockSpec(memory_space=pltpu.VMEM)] * 2,
-        out_specs=pl.BlockSpec((tokens // steps, width), lambda i: (i, 0)),
-        compiler_params=pltpu.CompilerParams(vmem_limit_bytes=SMALL),
-    )(my_rows, main_all, row_out)
-    return (input_grad[None], weight_grad[None], gain_grad[None], head_grad)
+    parts = 4
+    input_grad, gain_grad = pl.pallas_call(
+        functools.partial(last_kernel, parts),
+        in_specs=[pl.BlockSpec(memory_space=pltpu.SMEM)] * 2
+        + [pl.BlockSpec(memory_space=pltpu.VMEM)] * 2
+        + [pl.BlockSpec(memory_space=pl.ANY)],
+        out_specs=[pl.BlockSpec(memory_space=pl.ANY), pl.BlockSpec(memory_space=pltpu.VMEM)],
+        out_shape=[shape((tokens, width), BF16), shape((1, width), F32)],
+        scratch_shapes=[
+            pltpu.VMEM((tokens, width), BF16),
+            pltpu.SemaphoreType.DMA((parts,)),
+            pltpu.SemaphoreType.DMA((parts,)),
+        ],
+        compiler_params=pltpu.CompilerParams(vmem_limit_bytes=LARGE),
+    )(place, my_rows, last, last_other, main_all)
+    return (input_grad[None], weight_grad[None], gain_grad, head_grad)
 
 
 def solution(mesh):

time: 206 us -> 197 us (0.956)
  waiting for transfers between devices: 60.7 us -> 52.5 us
  Pallas kernels: 35.6 us -> 39.6 us
  starting transfers between devices: 51.1 us -> 49 us
    all_to_all x1, waiting for transfers between devices: 6.76 us -> 0.01 us  [local(): known_mine = lax.all_to_all(known_mine, 'z', 0, 0)]
    ppermute x8, starting transfers between devices: 19.4 us -> 16.7 us  [swap(): return lax.ppermute(values, 'core', [(0, 1), (1, 0)])]
    all_to_all x1, waiting for transfers between devices: 3.96 us -> 6.42 us  [local(): got = lax.all_to_all(send, 'z', 0, 0)]
    pallas_call x1, Pallas kernels: 4.37 us -> 6.81 us  [local(): pl.pallas_call(functools.partial(last_kernel, parts), in_specs=[pl.BlockS...]
    all_to_all x1, waiting for transfers between devices: 5.76 us -> 3.44 us  [local(): last = lax.all_to_all(last, 'z', 0, 0)]
    all_gather x1, waiting for transfers between devices: 2.13 us -> 0.01 us  [local(): ex_mine = lax.all_gather(expo, 'z', axis=0)]
  transfers between devices with their start and end apart: 17 -> 17, of which waited for: 11 -> 9; matrix products, arithmetic and copies ran while one was open for 13% -> 13% of each run, Pallas kernels for 12% -> 14%
where the time goes in v8:
time: 197 us; the launch traced here: 196 us
  waiting for transfers between devices  52.5 us (27%)
  starting transfers between devices  49 us (25%)
  Pallas kernels  39.6 us (20%)
  between operations  14.1 us (7%)
  blocking collectives  13.3 us (7%)
  other arithmetic  12.1 us (6%)
  matrix products  10.1 us (5%)
  local copies, waits for them, and re-layouts  5.65 us (3%)
    all_to_all x1, waiting for transfers between devices, local(): parts = lax.all_to_all(part, 'z', 0, 0)  26.5 us
    ppermute x8, starting transfers between devices, swap(): return lax.ppermute(values, 'core', [(0, 1), (1, 0)])  16.7 us
    all_to_all x1, blocking collectives, spread(): lax.all_to_all(jnp.broadcast_to(values[None], (count,) + values.shape), a...  13.3 us
    pallas_call x3, Pallas kernels, piped_call(): pl.pallas_call(body, grid=(1,), out_shape=out, in_specs=specs, out_specs=...  11.1 us
    all_to_all x1, starting transfers between devices, local(): parts = lax.all_to_all(part, 'z', 0, 0)  8.18 us
    all_to_all x1, waiting for transfers between devices, local(): exit_got = lax.all_to_all(exit_part, 'pipe', 0, 0)  7.79 us
    pallas_call x1, Pallas kernels, local(): pl.pallas_call(gain_kernel, grid_spec=pltpu.PrefetchScalarGridSpec(num_sc...  6.83 us
    pallas_call x1, Pallas kernels, local(): pl.pallas_call(functools.partial(last_kernel, parts), in_specs=[pl.BlockS...  6.81 us
  transfers between devices with their start and end apart: 17, of which 9 were waited for; matrix products, arithmetic and copies ran while one was open for 13% of the time, Pallas kernels for 14%

profile of v8, /device:TPU:1, one launch (start us, length us, event | category | flops | bytes accessed | tf_op | source)
XLA Modules:
  0.0 196.4 jit_solution(15357794259995043433)
XLA Ops:
  7.2 3.3 %collective-permute-start = (bf16[4096,256]{1,0:T(8,128)(2,1)}, bf16[4096,256]{1,0:T(8,128)(2,1)}, u32[]{:S(2)}, u32[]{:S(2)}) collective-permute-start(bf16[4096,256]{1,0:T(8,128)(2,1)} %bitcast.36), channel_id=1, source_target_pairs={{0,1},{1,0},{2,3},{3,2},{4,5},{5,4},{6,7},{7,6},{8,9},{9,8},{10,11... | collective-permute-start | bytes 6291464 | tf_op jit(solution)/shard_map/ppermute | solution.py:23
  11.2 3.1 %multiply_reduce_fusion = (f32[32]{0:T(128)S(1)}, f32[32,4096]{1,0:T(8,128)S(1)}) fusion(bf16[1,512,4096]{2,1,0:T(8,128)(2,1)} %param.10, s32[32]{0:T(128)S(1)} %fusion.35.ids), kind=kOutput, calls=%fused_computation.27 | convolution fusion | flops 134496224 | bytes 4718848 | tf_op jit(solution)/shard_map/dot_general | solution.py:367
  15.0 5.9 %shard_map.129 = bf16[256,4096]{1,0:T(8,128)(2,1)} custom-call(s32[4]{0:T(128)} %pad_add_fusion.place, bf16[8,2,32,4096]{3,2,1,0:T(8,128)(2,1)} %bitcast.56, bf16[4096,256]{1,0:T(8,128)(2,1)} %bitcast.37, bf16[4096,256]{1,0:T(8,128)(2,1)} %collective-permute-done.weight_other), custom_call_target="tpu_custom_call" | custom-call | tf_op jit(solution)/shard_map/pallas_call | solution.py:381
  21.8 13.3 %all_to_all.35.mine.row = bf16[16,32,256]{2,1,0:T(8,128)(2,1)S(1)} all-to-all(bf16[16,32,256]{2,1,0:T(8,128)(2,1)S(1)} %broadcast_in_dim.29), channel_id=1, replica_groups=mesh['pipe'=16,'z'=8,'core'=2] {'pipe'}, dimensions={0} | all-to-all | bytes 524288 | tf_op jit(solution)/shard_map/all_to_all | solution.py:19
  37.4 1.7 shard_map.130
  39.1 8.2 %all-to-all-start.1 = ((bf16[8,64,1024]{2,1,0:T(8,128)(2,1)}), bf16[8,64,1024]{2,1,0:T(8,128)(2,1)S(1)}, u32[]{:S(2)}, u32[]{:S(2)}) async-start(bf16[8,64,1024]{2,1,0:T(8,128)(2,1)} %shard_map.130), calls=%async_computation.1 | async-start | bytes 2097152 | tf_op jit(solution)/shard_map/all_to_all | solution.py:410
  48.5 6.8 %shard_map.131.gain_part = f32[1,4096]{1,0:T(1,128)} custom-call(s32[4]{0:T(128)} %pad_add_fusion.place, bf16[8,2,32,4096]{3,2,1,0:T(8,128)(2,1)} %bitcast.57, bf16[8,2,32,4096]{3,2,1,0:T(8,128)(2,1)} %bitcast.50, s32[1,32]{1,0:T(1,128)} %constant_dynamic-slice_fusion.4.ids, bf16[4096,256]{1,0:T(8,128)(2,1)} %bitcast.38, ...), custom_call_target="tpu_custom_call" | custom-call | tf_op jit(solution)/shard_map/pallas_call | solution.py:412
  55.3 26.5 %all-to-all-done.1.parts = bf16[8,64,1024]{2,1,0:T(8,128)(2,1)S(1)} async-done(((bf16[8,64,1024]{2,1,0:T(8,128)(2,1)}), bf16[8,64,1024]{2,1,0:T(8,128)(2,1)S(1)}, u32[]{:S(2)}, u32[]{:S(2)}) %all-to-all-start.1) | async-done | bytes 1048608 | tf_op jit(solution)/shard_map/all_to_all | solution.py:410
  81.8 1.5 shard_map.132
  83.3 1.7 collective-permute-start.3
  87.7 6.5 %all-to-all-start.2 = ((f32[16,2,8,128]{3,2,1,0:T(8,128)}), f32[16,2,8,128]{3,2,1,0:T(8,128)S(1)}, u32[]{:S(2)}, u32[]{:S(2)}) async-start(f32[16,2,8,128]{3,2,1,0:T(8,128)} %broadcast_in_dim.56), calls=%async_computation.3 | async-start | bytes 262144 | tf_op jit(solution)/shard_map/all_to_all | solution.py:19
  95.4 5.6 %all-to-all-done.2 = f32[16,2,8,128]{3,2,1,0:T(8,128)S(1)} async-done(((f32[16,2,8,128]{3,2,1,0:T(8,128)}), f32[16,2,8,128]{3,2,1,0:T(8,128)S(1)}, u32[]{:S(2)}, u32[]{:S(2)}) %all-to-all-start.2) | async-done | bytes 131104 | tf_op jit(solution)/shard_map/all_to_all | solution.py:19
  101.7 3.3 %all-to-all-start.3 = ((f32[8,8,128]{2,1,0:T(8,128)}), f32[8,8,128]{2,1,0:T(8,128)S(1)}, u32[]{:S(2)}, u32[]{:S(2)}) async-start(f32[8,8,128]{2,1,0:T(8,128)} %shard_map.133), calls=%async_computation.4 | async-start | bytes 65536 | tf_op jit(solution)/shard_map/all_to_all | solution.py:459
  105.1 3.2 %fusion = f32[512]{0:T(512)S(1)} fusion(bf16[512,4096]{1,0:T(8,128)(2,1)} %bitcast.53), kind=kLoop, calls=%fused_computation.2 | loop fusion | flops 6290944 | bytes 4196352 | tf_op jit(solution)/shard_map/reduce_sum | solution.py:471
  108.6 3.6 %fusion.2 = bf16[512,4096]{1,0:T(8,128)(2,1)} fusion(bf16[512,4096]{1,0:T(8,128)(2,1)S(1)} %bitcast.55, f32[4096]{0:T(1024)S(1)} %bitcast.43, f32[512]{0:T(512)S(1)} %add_rsqrt_fusion), kind=kLoop, calls=%fused_computation.4 | loop fusion | flops 8388608 | bytes 8407040 | tf_op jit(solution)/shard_map/convert_element_type | solution.py:472
  112.2 1.3 fusion.19.grad_rows
  113.5 1.8 collective-permute-start.4
  115.4 1.9 fusion.12
  117.3 4.6 %collective-permute-start.5 = (bf16[8,64,1024]{2,1,0:T(8,128)(2,1)}, bf16[8,64,1024]{2,1,0:T(8,128)(2,1)S(1)}, u32[]{:S(2)}, u32[]{:S(2)}) collective-permute-start(bf16[8,64,1024]{2,1,0:T(8,128)(2,1)} %bitcast.61), channel_id=1, source_target_pairs={{0,1},{1,0},{2,3},{3,2},{4,5},{5,4},{6,7},{7,6},{8,9},{9,8},{10,11... | collective-permute-start | bytes 3145736 | tf_op jit(solution)/shard_map/ppermute | solution.py:23
  122.0 3.2 %shard_map.134 = (f32[512,256]{1,0:T(8,128)}, f32[512,128]{1,0:T(8,128)}) custom-call(s32[4]{0:T(128)} %pad_add_fusion.place, bf16[8,64,1024]{2,1,0:T(8,128)(2,1)} %bitcast.62, f32[8,8,128]{2,1,0:T(8,128)} %copy-done.17, s32[512,1]{1,0:T(8,128)} %copy-done.11, bf16[1024,256]{1,0:T(8,128)(2,1)} %copy-done.3), custom_call_target="tpu_custom_call" | custom-call | tf_op jit(solution)/shard_map/pallas_call | solution.py:53
  126.3 3.2 %shard_map.135 = bf16[16,32,256]{2,1,0:T(8,128)(2,1)} custom-call(s32[4]{0:T(128)} %pad_add_fusion.place, bf16[8,64,1024]{2,1,0:T(8,128)(2,1)} %copy-done.12, f32[8,8,128]{2,1,0:T(8,128)} %copy-done.19, s32[512,1]{1,0:T(8,128)} %copy-done.11, bf16[1024,256]{1,0:T(8,128)(2,1)} %copy-done.13, f32[512,256]{1,0:T(8,128)} %get-tuple-element.64.before), custom_call_target="tpu_custom_call" | custom-call | tf_op jit(solution)/shard_map/pallas_call | solution.py:53
  129.5 6.5 %all-to-all-start.4 = ((bf16[16,32,256]{2,1,0:T(8,128)(2,1)}), bf16[16,32,256]{2,1,0:T(8,128)(2,1)S(1)}, u32[]{:S(2)}, u32[]{:S(2)}) async-start(bf16[16,32,256]{2,1,0:T(8,128)(2,1)} %shard_map.135), calls=%async_computation.5 | async-start | bytes 524288 | tf_op jit(solution)/shard_map/all_to_all | solution.py:512
  136.7 7.8 %all-to-all-done.4.got = bf16[16,32,256]{2,1,0:T(8,128)(2,1)S(1)} async-done(((bf16[16,32,256]{2,1,0:T(8,128)(2,1)}), bf16[16,32,256]{2,1,0:T(8,128)(2,1)S(1)}, u32[]{:S(2)}, u32[]{:S(2)}) %all-to-all-start.4) | async-done | bytes 262176 | tf_op jit(solution)/shard_map/all_to_all | solution.py:512
  147.2 3.5 %shard_map.137 = bf16[8,2,5888]{2,1,0:T(2,128)(2,1)} custom-call(s32[4]{0:T(128)S(1)} %copy-done.8, f32[16,256]{1,0:T(8,128)S(1)} %get-tuple-element.69.mine, f32[16,256]{1,0:T(8,128)S(1)} %collective-permute-done.6.other, bf16[4096,256]{1,0:T(8,128)(2,1)S(1)} %bitcast.39, bf16[4096,256]{1,0:T(8,128)(2,1)} %collective-permute-done.weight_other, ...), custom_call_target="tpu_custom_call" | custom-call | tf_op jit(solution)/shard_map/pallas_call | solution.py:27
  150.8 4.3 %all-to-all-start.5 = ((bf16[8,2,5888]{2,1,0:T(2,128)(2,1)}), bf16[8,2,5888]{2,1,0:T(2,128)(2,1)S(1)}, u32[]{:S(2)}, u32[]{:S(2)}) async-start(bf16[8,2,5888]{2,1,0:T(2,128)(2,1)} %shard_map.137), calls=%async_computation.6 | async-start | bytes 376832 | tf_op jit(solution)/shard_map/all_to_all | solution.py:539
  155.0 5.2 %convolution_convert_fusion = bf16[4096,256]{1,0:T(8,128)(2,1)} fusion(bf16[512,4096]{1,0:T(8,128)(2,1)} %fusion.2, bf16[32,256]{1,0:T(8,128)(2,1)S(1)} %get-tuple-element.75, pred[512]{0:T(512)(128)(4,1)S(1)} %compare_reduce_fusion, bf16[512,4096]{1,0:T(8,128)(2,1)} %bitcast.60, s32[]{:T(128)S(6)} %select_n.61, s32[32]{0:T(128)S(1)} %fusion.35.ids), kind=kOutput, calls=%fused_computation.5 | convolution fusion | flops 1083457536 | bytes 6570628 | tf_op jit(solution)/shard_map/dot_general | solution.py:546
  160.2 6.4 %all-to-all-done.5.got = bf16[8,2,5888]{2,1,0:T(2,128)(2,1)S(1)} async-done(((bf16[8,2,5888]{2,1,0:T(2,128)(2,1)}), bf16[8,2,5888]{2,1,0:T(2,128)(2,1)S(1)}, u32[]{:S(2)}, u32[]{:S(2)}) %all-to-all-start.5) | async-done | bytes 188448 | tf_op jit(solution)/shard_map/all_to_all | solution.py:539
  167.5 3.4 %all-to-all-start.6 = ((bf16[8,2,4864]{2,1,0:T(2,128)(2,1)}), bf16[8,2,4864]{2,1,0:T(2,128)(2,1)S(1)}, u32[]{:S(2)}, u32[]{:S(2)}) async-start(bf16[8,2,4864]{2,1,0:T(2,128)(2,1)} %shard_map.138), calls=%async_computation.7 | async-start | bytes 311296 | tf_op jit(solution)/shard_map/all_to_all | solution.py:571
  170.9 4.7 %shard_map.139 = bf16[2000,256]{1,0:T(8,128)(2,1)} custom-call(s32[4]{0:T(128)} %pad_add_fusion.place, bf16[16,32,256]{2,1,0:T(8,128)(2,1)} %copy-done.4, f32[1,256]{1,0:T(1,128)} %bitcast.47, f32[512,128]{1,0:T(8,128)} %get-tuple-element.81.kept, s32[512,1]{1,0:T(8,128)} %copy-done.11, bf16[8,64,1024]{2,1,0:T(8,128)(2,1)} %bitcast.63, ...), custom_call_target="tpu_custom_call" | custom-call | tf_op jit(solution)/shard_map/pallas_call | solution.py:53
  175.6 3.4 %all-to-all-done.6.mine = bf16[8,2,4864]{2,1,0:T(2,128)(2,1)S(1)} async-done(((bf16[8,2,4864]{2,1,0:T(2,128)(2,1)}), bf16[8,2,4864]{2,1,0:T(2,128)(2,1)S(1)}, u32[]{:S(2)}, u32[]{:S(2)}) %all-to-all-start.6) | async-done | bytes 155680 | tf_op jit(solution)/shard_map/all_to_all | solution.py:571
  179.0 2.3 %collective-permute-start.7 = (bf16[8,2,4864]{2,1,0:T(2,128)(2,1)S(1)}, bf16[8,2,4864]{2,1,0:T(2,128)(2,1)S(1)}, u32[]{:S(2)}, u32[]{:S(2)}) collective-permute-start(bf16[8,2,4864]{2,1,0:T(2,128)(2,1)S(1)} %all-to-all-done.6.mine), channel_id=1, source_target_pairs={{0,1},{1,0},{2,3},{3,2},{4,5},{5,4},{6,7},{7,6},{8,9},{9,8},{10,11... | collective-permute-start | bytes 466952 | tf_op jit(solution)/shard_map/ppermute | solution.py:23
  183.0 6.8 %shard_map.140 = (bf16[512,4096]{1,0:T(8,128)(2,1)}, f32[1,4096]{1,0:T(1,128)}) custom-call(s32[4]{0:T(128)} %pad_add_fusion.place, s32[32]{0:T(128)} %copy-done.21, bf16[8,2,4864]{2,1,0:T(2,128)(2,1)} %copy-done.16, bf16[8,2,4864]{2,1,0:T(2,128)(2,1)} %copy-done.18, bf16[512,4096]{1,0:T(8,128)(2,1)} %all-gather.4.cloned.1.call-done.main), custom_call_target="tpu_custom_call" | custom-call | tf_op jit(solution)/shard_map/pallas_call | solution.py:575
  (101 shorter events, 17.4 us)
Async XLA Ops:
  7.2 76.1 %reduce-scatter.2.cloned.1.call-start = ((), (), s32[]{:S(2)}) async-start(), calls=%async_computation.8 | async-start | bytes 2359296 | tf_op jit(solution)/shard_map/reduce_scatter | solution.py:393
  7.2 7.7 %collective-permute-start = (bf16[4096,256]{1,0:T(8,128)(2,1)}, bf16[4096,256]{1,0:T(8,128)(2,1)}, u32[]{:S(2)}, u32[]{:S(2)}) collective-permute-start(bf16[4096,256]{1,0:T(8,128)(2,1)} %bitcast.36), channel_id=1, source_target_pairs={{0,1},{1,0},{2,3},{3,2},{4,5},{5,4},{6,7},{7,6},{8,9},{9,8},{10,11... | collective-permute-start | bytes 6291464 | tf_op jit(solution)/shard_map/ppermute | solution.py:23
  10.6 144.4 %copy-start.21 = (s32[32]{0:T(128)}, s32[32]{0:T(128)S(1)}, u32[]{:S(2)}) copy-start(s32[32]{0:T(128)S(1)} %fusion.35.ids) | copy-start | bytes 388
  21.0 26.4 %copy-start.20 = (s32[16,32]{1,0:T(8,128)S(1)}, s32[16,32]{1,0:T(8,128)}, u32[]{:S(2)}) copy-start(s32[16,32]{1,0:T(8,128)} %param.17) | copy-start | bytes 6148
  21.0 26.6 %copy-start.22 = (f32[16]{0:T(128)S(1)}, f32[16]{0:T(128)}, u32[]{:S(2)}) copy-start(f32[16]{0:T(128)} %param.18) | copy-start | bytes 196
  21.0 26.6 %copy-start.23 = (s32[16]{0:T(128)S(1)}, s32[16]{0:T(128)}, u32[]{:S(2)}) copy-start(s32[16]{0:T(128)} %param.16) | copy-start | bytes 196
  21.1 34.1 %copy-start.3 = (bf16[1024,256]{1,0:T(8,128)(2,1)}, bf16[1024,256]{1,0:T(8,128)(2,1)S(1)}, u32[]{:S(2)}) copy-start(bf16[1024,256]{1,0:T(8,128)(2,1)S(1)} %get-tuple-element.89.head_mine.head) | copy-start | bytes 1572868
  21.2 34.1 %copy-start.13 = (bf16[1024,256]{1,0:T(8,128)(2,1)}, bf16[1024,256]{1,0:T(8,128)(2,1)S(1)}, u32[]{:S(2)}) copy-start(bf16[1024,256]{1,0:T(8,128)(2,1)S(1)} %get-tuple-element.88.head) | copy-start | bytes 1572868
  21.2 15.9 %collective-permute-start.2 = (bf16[1024,256]{1,0:T(8,128)(2,1)S(1)}, bf16[1024,256]{1,0:T(8,128)(2,1)S(1)}, u32[]{:S(2)}, u32[]{:S(2)}) collective-permute-start(bf16[1024,256]{1,0:T(8,128)(2,1)S(1)} %get-tuple-element.88.head), channel_id=1, source_target_pairs={{0,1},{1,0},{2,3},{3,2},{4,5},{5,4},{6,7},{7,6},{8,9},{9,8},{10,11... | collective-permute-start | bytes 1572872 | tf_op jit(solution)/shard_map/ppermute | solution.py:23
  35.1 20.1 %copy-start.4 = (bf16[16,32,256]{2,1,0:T(8,128)(2,1)}, bf16[16,32,256]{2,1,0:T(8,128)(2,1)S(1)}, u32[]{:S(2)}) copy-start(bf16[16,32,256]{2,1,0:T(8,128)(2,1)S(1)} %all_to_all.35.mine.row) | copy-start | bytes 786436
  35.1 2.3 %collective-permute-start.1 = (bf16[16,32,256]{2,1,0:T(8,128)(2,1)S(1)}, bf16[16,32,256]{2,1,0:T(8,128)(2,1)S(1)}, u32[]{:S(2)}, u32[]{:S(2)}) collective-permute-start(bf16[16,32,256]{2,1,0:T(8,128)(2,1)S(1)} %all_to_all.35.mine.row), channel_id=1, source_target_pairs={{0,1},{1,0},{2,3},{3,2},{4,5},{5,4},{6,7},{7,6},{8,9},{9,8},{10,11... | collective-permute-start | bytes 786440 | tf_op jit(solution)/shard_map/ppermute | solution.py:23
  37.1 107.4 %copy-start.9 = (f32[256]{0:T(256)}, f32[256]{0:T(256)S(1)}, u32[]{:S(2)}) copy-start(f32[256]{0:T(256)S(1)} %get-tuple-element.91) | copy-start | bytes 3076
  39.1 42.7 %all-to-all-start.1 = ((bf16[8,64,1024]{2,1,0:T(8,128)(2,1)}), bf16[8,64,1024]{2,1,0:T(8,128)(2,1)S(1)}, u32[]{:S(2)}, u32[]{:S(2)}) async-start(bf16[8,64,1024]{2,1,0:T(8,128)(2,1)} %shard_map.130), calls=%async_computation.1 | async-start | bytes 2097152 | tf_op jit(solution)/shard_map/all_to_all | solution.py:410
  47.3 70.0 %all-gather.6.cloned.1.call-start = ((), (), s32[]{:S(2)}) async-start(), calls=%async_computation.10 | async-start | bytes 1179648 | tf_op jit(solution)/shard_map/all_gather | solution.py:452
  47.7 7.6 %copy-start.11 = (s32[512,1]{1,0:T(8,128)}, s32[512,1]{1,0:T(8,128)S(1)}, u32[]{:S(2)}) copy-start(s32[512,1]{1,0:T(8,128)S(1)} %reshape.110.targets) | copy-start | bytes 6148
  48.4 33.4 %copy-start.7 = (s32[4]{0:T(128)S(1)}, s32[4]{0:T(128)}, u32[]{:S(2)}) copy-start(s32[4]{0:T(128)} %pad_add_fusion.place) | copy-start | bytes 52
  83.3 2.5 %collective-permute-start.3 = (f32[8,128]{1,0:T(8,128)S(1)}, f32[8,128]{1,0:T(8,128)S(1)}, u32[]{:S(2)}, u32[]{:S(2)}) collective-permute-start(f32[8,128]{1,0:T(8,128)S(1)} %get-tuple-element.53.own), channel_id=1, source_target_pairs={{0,1},{1,0},{2,3},{3,2},{4,5},{5,4},{6,7},{7,6},{8,9},{9,8},{10,11... | collective-permute-start | bytes 12296 | tf_op jit(solution)/shard_map/ppermute | solution.py:23
  87.7 13.3 %all-to-all-start.2 = ((f32[16,2,8,128]{3,2,1,0:T(8,128)}), f32[16,2,8,128]{3,2,1,0:T(8,128)S(1)}, u32[]{:S(2)}, u32[]{:S(2)}) async-start(f32[16,2,8,128]{3,2,1,0:T(8,128)} %broadcast_in_dim.56), calls=%async_computation.3 | async-start | bytes 262144 | tf_op jit(solution)/shard_map/all_to_all | solution.py:19
  101.7 11.8 %all-to-all-start.3 = ((f32[8,8,128]{2,1,0:T(8,128)}), f32[8,8,128]{2,1,0:T(8,128)S(1)}, u32[]{:S(2)}, u32[]{:S(2)}) async-start(f32[8,8,128]{2,1,0:T(8,128)} %shard_map.133), calls=%async_computation.4 | async-start | bytes 65536 | tf_op jit(solution)/shard_map/all_to_all | solution.py:459
  105.0 62.5 %all-gather.4.cloned.1.call-start = ((), (), s32[]{:S(2)}) async-start(), calls=%async_computation.9 | async-start | bytes 4456448 | tf_op jit(solution)/shard_map/all_gather | solution.py:486
  112.1 32.4 %copy-start.8 = (s32[4]{0:T(128)S(1)}, s32[4]{0:T(128)}, u32[]{:S(2)}) copy-start(s32[4]{0:T(128)} %pad_add_fusion.place) | copy-start | bytes 52
  112.1 35.1 %copy-start.2 = (bf16[1,4096,256]{2,1,0:T(8,128)(2,1)S(1)}, bf16[1,4096,256]{2,1,0:T(8,128)(2,1)}, u32[]{:S(2)}) copy-start(bf16[1,4096,256]{2,1,0:T(8,128)(2,1)} %param.11) | copy-start | bytes 6291460
  112.2 35.1 %copy-start.6 = (f32[1,4096]{1,0:T(1,128)S(1)}, f32[1,4096]{1,0:T(1,128)}, u32[]{:S(2)}) copy-start(f32[1,4096]{1,0:T(1,128)} %shard_map.131.gain_part) | copy-start | bytes 49156
  113.5 8.5 %copy-start.17 = (f32[8,8,128]{2,1,0:T(8,128)}, f32[8,8,128]{2,1,0:T(8,128)S(1)}, u32[]{:S(2)}) copy-start(f32[8,8,128]{2,1,0:T(8,128)S(1)} %all-to-all-done.3.known.known_mine) | copy-start | bytes 98308
  113.5 3.8 %collective-permute-start.4 = (f32[8,8,128]{2,1,0:T(8,128)S(1)}, f32[8,8,128]{2,1,0:T(8,128)S(1)}, u32[]{:S(2)}, u32[]{:S(2)}) collective-permute-start(f32[8,8,128]{2,1,0:T(8,128)S(1)} %all-to-all-done.3.known.known_mine), channel_id=1, source_target_pairs={{0,1},{1,0},{2,3},{3,2},{4,5},{5,4},{6,7},{7,6},{8,9},{9,8},{10,11... | collective-permute-start | bytes 98312 | tf_op jit(solution)/shard_map/ppermute | solution.py:23
  117.3 7.9 %copy-start.19 = (f32[8,8,128]{2,1,0:T(8,128)}, f32[8,8,128]{2,1,0:T(8,128)S(1)}, u32[]{:S(2)}) copy-start(f32[8,8,128]{2,1,0:T(8,128)S(1)} %collective-permute-done.4.known.known_other) | copy-start | bytes 98308
  117.3 7.9 %collective-permute-start.5 = (bf16[8,64,1024]{2,1,0:T(8,128)(2,1)}, bf16[8,64,1024]{2,1,0:T(8,128)(2,1)S(1)}, u32[]{:S(2)}, u32[]{:S(2)}) collective-permute-start(bf16[8,64,1024]{2,1,0:T(8,128)(2,1)} %bitcast.61), channel_id=1, source_target_pairs={{0,1},{1,0},{2,3},{3,2},{4,5},{5,4},{6,7},{7,6},{8,9},{9,8},{10,11... | collective-permute-start | bytes 3145736 | tf_op jit(solution)/shard_map/ppermute | solution.py:23
  129.5 15.0 %all-to-all-start.4 = ((bf16[16,32,256]{2,1,0:T(8,128)(2,1)}), bf16[16,32,256]{2,1,0:T(8,128)(2,1)S(1)}, u32[]{:S(2)}, u32[]{:S(2)}) async-start(bf16[16,32,256]{2,1,0:T(8,128)(2,1)} %shard_map.135), calls=%async_computation.5 | async-start | bytes 524288 | tf_op jit(solution)/shard_map/all_to_all | solution.py:512
  145.2 2.0 %collective-permute-start.6 = (f32[16,256]{1,0:T(8,128)S(1)}, f32[16,256]{1,0:T(8,128)S(1)}, u32[]{:S(2)}, u32[]{:S(2)}) collective-permute-start(f32[16,256]{1,0:T(8,128)S(1)} %get-tuple-element.70), channel_id=1, source_target_pairs={{0,1},{1,0},{2,3},{3,2},{4,5},{5,4},{6,7},{7,6},{8,9},{9,8},{10,11... | collective-permute-start | bytes 49160 | tf_op jit(solution)/shard_map/ppermute | solution.py:23
  150.8 15.9 %all-to-all-start.5 = ((bf16[8,2,5888]{2,1,0:T(2,128)(2,1)}), bf16[8,2,5888]{2,1,0:T(2,128)(2,1)S(1)}, u32[]{:S(2)}, u32[]{:S(2)}) async-start(bf16[8,2,5888]{2,1,0:T(2,128)(2,1)} %shard_map.137), calls=%async_computation.6 | async-start | bytes 376832 | tf_op jit(solution)/shard_map/all_to_all | solution.py:539
  167.5 11.5 %all-to-all-start.6 = ((bf16[8,2,4864]{2,1,0:T(2,128)(2,1)}), bf16[8,2,4864]{2,1,0:T(2,128)(2,1)S(1)}, u32[]{:S(2)}, u32[]{:S(2)}) async-start(bf16[8,2,4864]{2,1,0:T(2,128)(2,1)} %shard_map.138), calls=%async_computation.7 | async-start | bytes 311296 | tf_op jit(solution)/shard_map/all_to_all | solution.py:571
  179.0 3.3 %collective-permute-start.7 = (bf16[8,2,4864]{2,1,0:T(2,128)(2,1)S(1)}, bf16[8,2,4864]{2,1,0:T(2,128)(2,1)S(1)}, u32[]{:S(2)}, u32[]{:S(2)}) collective-permute-start(bf16[8,2,4864]{2,1,0:T(2,128)(2,1)S(1)} %all-to-all-done.6.mine), channel_id=1, source_target_pairs={{0,1},{1,0},{2,3},{3,2},{4,5},{5,4},{6,7},{7,6},{8,9},{9,8},{10,11... | collective-permute-start | bytes 466952 | tf_op jit(solution)/shard_map/ppermute | solution.py:23
  (9 other events, 39.4 us)
Sparse Core Ops, SparseCore 0:
  21.1 53.2 reduce-scatter.1
  85.3 31.2 all-gather.5
  118.4 47.6 all-gather.3

commit v9 on v8

--- a/solution.py
+++ b/solution.py
@@ -43,19 +43,19 @@
     )(*operands)
 
 
-def piped_call(body, out, *operands, held=(), scratch=(), limit=LARGE):
-    specs = [pl.BlockSpec(memory_space=pltpu.SMEM)] + [
-        pl.BlockSpec(memory_space=pltpu.VMEM)
-        if i in held
-        else pl.BlockSpec(value.shape, lambda i, n=value.ndim: (0,) * n)
-        for i, value in enumerate(operands[1:], 1)
-    ]
+def piped_call(body, out, *operands, held=(), kept=(), scratch=(), limit=LARGE):
+    def spec(value, stays):
+        if stays:
+            return pl.BlockSpec(memory_space=pltpu.VMEM)
+        return pl.BlockSpec(value.shape, lambda i: (0,) * len(value.shape))
+
     return pl.pallas_call(
         body,
         grid=(1,),
         out_shape=out,
-        in_specs=specs,
-        out_specs=jax.tree.map(lambda value: pl.BlockSpec(value.shape, lambda i, n=len(value.shape): (0,) * n), out),
+        in_specs=[pl.BlockSpec(memory_space=pltpu.SMEM)]
+        + [spec(value, i in held) for i, value in enumerate(operands[1:], 1)],
+        out_specs=[spec(value, i in kept) for i, value in enumerate(out)],
         scratch_shapes=list(scratch),
         compiler_params=pltpu.CompilerParams(vmem_limit_bytes=limit),
     )(*operands)
@@ -86,10 +86,6 @@
     return part + lax.dot_general(
         jnp.where(core == 0, high, low), weight_other[...], over, preferred_element_type=F32
     )
-
-
-def main_kernel(place, grad, weight, weight_other, sent):
-    sent[...] = chip_term(place[1], grad, weight, weight_other).astype(BF16)
 
 
 def gain_kernel(place, grad, seg, ids, weight, weight_other, gain_out, inverse):
@@ -229,11 +225,9 @@
     other[...] = jnp.where(core == 0, rows[half:], rows[:half])
 
 
-def send_kernel(place, mine, other, weight, weight_other, unit, gain_part, out):
+def send_kernel(place, part, mine, other, unit, gain_part, out):
     core = place[1]
-    columns = (((1,), (1,)), ((), ()))
-    part = lax.dot_general(mine[...].astype(BF16), weight[...], columns, preferred_element_type=F32)
-    part += lax.dot_general(other[...].astype(BF16), weight_other[...], columns, preferred_element_type=F32)
+    part = part[...]
     gain = gain_part[...] + jnp.sum(part * unit[...], axis=0, keepdims=True)
     low = jnp.where(core == 0, mine[...], other[...])
     high = jnp.where(core == 0, other[...], mine[...])
@@ -243,7 +237,7 @@
     part = part.astype(BF16)
     gains = [values.astype(BF16) for values in pieces3(gain)]
     count, share, _ = out.shape
-    width, slab = weight.shape
+    width, slab = part.shape[1], mine.shape[1]
     piece = width // (count * share)
     for i in range(count):
         at = slice(i * share, (i + 1) * share)
@@ -279,24 +273,39 @@
     out[...] = jnp.broadcast_to(whole.astype(BF16)[None], out.shape)
 
 
-def last_kernel(parts, place, ids, mine, other, main, out, gain_out, block, into, outof):
+def fetch_kernel(source, out, done):
+    parts = done.shape[0]
+    count = out.shape[0] // parts
+    copies = [
+        pltpu.make_async_copy(source.at[pl.ds(i * count, count)], out.at[pl.ds(i * count, count)], done.at[i])
+        for i in range(parts)
+    ]
+    for copy in copies:
+        copy.start()
+    for copy in copies:
+        copy.wait()
+
+
+def last_kernel(place, ids, mine, other, main, out, gain_out, block, done):
     core = place[1]
     tokens, width = block.shape
+    groups, share = mine.shape[:2]
+    tile = lax.broadcasted_iota(jnp.int32, (16, width), 0)
+    for rows, first in ((mine, core), (other, 1 - core)):
+        for i in range(groups):
+            for j in range(share):
+                at = ids[first * groups * share + i * share + j]
+                start = pl.multiple_of(at // 16 * 16, 16)
+                row = rows[i, j : j + 1, :width]
+                block[pl.ds(start, 16), :] = jnp.where(tile == at - start, row, block[pl.ds(start, 16), :])
+    parts = done.shape[0]
     count = tokens // parts
-
-    def copies(source, target, done):
-        return [
-            pltpu.make_async_copy(
-                source.at[pl.ds(i * count, count)], target.at[pl.ds(i * count, count)], done.at[i]
-            )
-            for i in range(parts)
-        ]
-
-    loads = copies(main, block, into)
-    stores = copies(block, out, outof)
-    for load in loads:
-        load.start()
-    groups, share = mine.shape[:2]
+    copies = [
+        pltpu.make_async_copy(block.at[pl.ds(i * count, count)], out.at[pl.ds(i * count, count)], done.at[i])
+        for i in range(parts)
+    ]
+    for copy in copies:
+        copy.start()
     piece = (mine.shape[2] - width) // 3
     total = mine[:, :, width:].astype(F32) + other[:, :, width:].astype(F32)
     total = total[:, :, :piece] + total[:, :, piece : 2 * piece] + total[:, :, 2 * piece :]
@@ -304,23 +313,8 @@
         for j in range(share):
             at = (i * share + j) * piece
             gain_out[:, at : at + piece] = total[i, j : j + 1]
-    tile = lax.broadcasted_iota(jnp.int32, (16, width), 0)
-    for k in range(parts):
-        loads[k].wait()
-        for rows, first in ((mine, core), (other, 1 - core)):
-            for i in range(groups):
-                for j in range(share):
-                    at = ids[first * groups * share + i * share + j]
-
-                    @pl.when(at // count == k)
-                    def _():
-                        start = pl.multiple_of(at // 16 * 16, 16)
-                        row = rows[i, j : j + 1, :width]
-                        block[pl.ds(start, 16), :] = jnp.where(tile == at - start, row, block[pl.ds(start, 16), :])
-
-        stores[k].start()
-    for store in stores:
-        store.wait()
+    for copy in copies:
+        copy.wait()
 
 
 def local(
@@ -378,17 +372,16 @@
     grad_spec = pl.BlockSpec((zs, 1, held, 2 * slab), lambda i, at: (0, at[1], 0, at[0]))
     weight_spec = pl.BlockSpec((chunk, slab), lambda i, at: (i, 0))
     grad_view = grad.reshape(zs, 2, held, width)
-    main_sent = pl.pallas_call(
-        main_kernel,
-        grid_spec=pltpu.PrefetchScalarGridSpec(
-            num_scalar_prefetch=1,
-            grid=(steps,),
-            in_specs=[grad_spec, weight_spec, weight_spec],
-            out_specs=pl.BlockSpec((zs * held, chunk), lambda i, at: (0, i)),
-        ),
-        out_shape=shape((zs * held, width), BF16),
-        compiler_params=pltpu.CompilerParams(vmem_limit_bytes=LARGE),
-    )(place, grad_view, weight, weight_other)
+    joined = jnp.concatenate([weight, weight_other], axis=1)
+    chip_grad = lax.dynamic_slice(grad_view, (0, core, 0, z * 2 * slab), (zs, 1, held, 2 * slab))
+    on_columns = (((1,), (1,)), ((), ()))
+
+    def own_first(values):
+        return jnp.where(core == 0, values, jnp.roll(values, slab, axis=1))
+
+    main_sent = lax.dot_general(
+        own_first(chip_grad.reshape(zs * held, 2 * slab)), joined, on_columns, preferred_element_type=F32
+    ).astype(BF16)
     hidden, main_sent = lax.optimization_barrier((hidden, main_sent))
     main_grad = lax.psum_scatter(main_sent, "z", scatter_dimension=0, tiled=True)
 
@@ -495,11 +488,12 @@
         known_mine,
         all_targets,
         head_mine,
+        kept=(0,),
         scratch=grads,
     )
-    exit_part = piped_call(
+    (exit_part,) = piped_call(
         functools.partial(exit_rest_kernel, half, vocab_part),
-        shape((pipes, exits, slab), BF16),
+        [shape((pipes, exits, slab), BF16)],
         place,
         ex_other,
         known_other,
@@ -525,14 +519,17 @@
     )
 
     piece = slab * 2 // share
+    row_other = swap(row_send)
+    row_part = lax.dot_general(
+        jnp.concatenate([row_mine, row_other], axis=1).astype(BF16), joined, on_columns, preferred_element_type=F32
+    )
     send = kernel_call(
         send_kernel,
         shape((zs, share, width + 4 * slab + 3 * piece), BF16),
         place,
+        row_part,
         row_mine,
-        swap(row_send),
-        weight,
-        weight_other,
+        row_other,
         core_unit,
         gain_part,
     )
@@ -554,9 +551,9 @@
         share_inv,
     )
     last, main_all = lax.optimization_barrier((last, main_all))
-    head_grad = piped_call(
+    (head_grad,) = piped_call(
         functools.partial(head_kernel, half, vocab_part),
-        shape((vocab_part, slab), BF16),
+        [shape((vocab_part, slab), BF16)],
         place,
         all_mine,
         gain_mine,
@@ -569,23 +566,26 @@
         scratch=grads,
     )
     last = lax.all_to_all(last, "z", 0, 0)
-    last, head_grad = lax.optimization_barrier((last, head_grad))
+    main_near = pl.pallas_call(
+        fetch_kernel,
+        in_specs=[pl.BlockSpec(memory_space=pl.ANY)],
+        out_specs=pl.BlockSpec(memory_space=pltpu.VMEM),
+        out_shape=shape((tokens, width), BF16),
+        scratch_shapes=[pltpu.SemaphoreType.DMA((4,))],
+        compiler_params=pltpu.CompilerParams(vmem_limit_bytes=SMALL),
+    )(main_all)
+    last, head_grad, main_near = lax.optimization_barrier((last, head_grad, main_near))
     last_other = swap(last)
-    parts = 4
-    input_grad, gain_grad = pl.pallas_call(
-        functools.partial(last_kernel, parts),
-        in_specs=[pl.BlockSpec(memory_space=pltpu.SMEM)] * 2
-        + [pl.BlockSpec(memory_space=pltpu.VMEM)] * 2
-        + [pl.BlockSpec(memory_space=pl.ANY)],
-        out_specs=[pl.BlockSpec(memory_space=pl.ANY), pl.BlockSpec(memory_space=pltpu.VMEM)],
-        out_shape=[shape((tokens, width), BF16), shape((1, width), F32)],
-        scratch_shapes=[
-            pltpu.VMEM((tokens, width), BF16),
-            pltpu.SemaphoreType.DMA((parts,)),
-            pltpu.SemaphoreType.DMA((parts,)),
-        ],
-        compiler_params=pltpu.CompilerParams(vmem_limit_bytes=LARGE),
-    )(place, my_rows, last, last_other, main_all)
+    in_vmem = pl.BlockSpec(memory_space=pltpu.VMEM)
+    input_grad, gain_grad, _ = pl.pallas_call(
+        last_kernel,
+        in_specs=[pl.BlockSpec(memory_space=pltpu.SMEM)] * 2 + [in_vmem] * 3,
+        out_specs=[pl.BlockSpec(memory_space=pl.ANY), in_vmem, in_vmem],
+        out_shape=[shape((tokens, width), BF16), shape((1, width), F32), shape((tokens, width), BF16)],
+        input_output_aliases={4: 2},
+        scratch_shapes=[pltpu.SemaphoreType.DMA((4,))],
+        compiler_params=pltpu.CompilerParams(vmem_limit_bytes=SMALL),
+    )(place, my_rows, last, last_other, main_near)
     return (input_grad[None], weight_grad[None], gain_grad, head_grad)
 
 

time: 197 us -> 196 us (level)
  Pallas kernels: 39.6 us -> 29.3 us
  local copies, waits for them, and re-layouts: 5.65 us -> 13.6 us
  matrix products: 10.1 us -> 17.1 us
  starting transfers between devices: 49 us -> 45.7 us
  waiting for transfers between devices: 52.5 us -> 49.5 us
    pallas_call x5, Pallas kernels: 23.8 us -> 15.6 us  [the longest x3 11.1 us: piped_call(): pl.pallas_call(body, grid=(1,), out_shape=out, in_specs=[pl.BlockSpec(mem...]
    dot_general x0 -> x2, matrix products: none -> 7.04 us  [the longest x1 4.22 us: local(): lax.dot_general(own_first(chip_grad.reshape(zs * held, 2 * slab)), joined...]
    unnamed x48, local copies, waits for them, and re-layouts: 2.09 us -> 7.76 us
    all_to_all x1, waiting for transfers between devices: 3.44 us -> 0.01 us  [local(): last = lax.all_to_all(last, 'z', 0, 0)]
    pallas_call x3, Pallas kernels: 5.71 us -> 3.59 us  [kernel_call(): pl.pallas_call(body, out_shape=out, in_specs=[pl.BlockSpec(memory_space=p...]
    all_to_all x1, starting transfers between devices: 6.48 us -> 4.47 us  [spread(): lax.all_to_all(jnp.broadcast_to(values[None], (count,) + values.shape), a...]
  transfers between devices with their start and end apart: 17 -> 17, of which waited for: 9 -> 9; matrix products, arithmetic and copies ran while one was open for 13% -> 16% of each run, Pallas kernels for 14% -> 13%
where the time goes in v9:
time: 196 us; the launch traced here: 194 us
  waiting for transfers between devices  49.5 us (25%)
  starting transfers between devices  45.7 us (23%)
  Pallas kernels  29.3 us (15%)
  matrix products  17.1 us (9%)
  between operations  14.1 us (7%)
  local copies, waits for them, and re-layouts  13.6 us (7%)
  blocking collectives  13 us (7%)
  other arithmetic  12.1 us (6%)
    all_to_all x1, waiting for transfers between devices, local(): parts = lax.all_to_all(part, 'z', 0, 0)  27.5 us
    ppermute x8, starting transfers between devices, swap(): return lax.ppermute(values, 'core', [(0, 1), (1, 0)])  15.4 us
    all_to_all x1, blocking collectives, spread(): lax.all_to_all(jnp.broadcast_to(values[None], (count,) + values.shape), a...  13 us
    pallas_call x3, Pallas kernels, piped_call(): pl.pallas_call(body, grid=(1,), out_shape=out, in_specs=[pl.BlockSpec(mem...  11.1 us
    all_to_all x1, starting transfers between devices, local(): parts = lax.all_to_all(part, 'z', 0, 0)  8.19 us
    all_to_all x1, waiting for transfers between devices, local(): exit_got = lax.all_to_all(exit_part, 'pipe', 0, 0)  7.78 us
    unnamed x48, local copies, waits for them, and re-layouts  7.76 us
    pallas_call x1, Pallas kernels, local(): pl.pallas_call(gain_kernel, grid_spec=pltpu.PrefetchScalarGridSpec(num_sc...  6.82 us
  transfers between devices with their start and end apart: 17, of which 9 were waited for; matrix products, arithmetic and copies ran while one was open for 16% of the time, Pallas kernels for 13%

profile of v9, /device:TPU:1, one launch (start us, length us, event | category | flops | bytes accessed | tf_op | source)
XLA Modules:
  0.0 194.3 jit_solution(18131691995715026066)
XLA Ops:
  7.2 3.3 %collective-permute-start = (bf16[4096,256]{1,0:T(8,128)(2,1)}, bf16[4096,256]{1,0:T(8,128)(2,1)}, u32[]{:S(2)}, u32[]{:S(2)}) collective-permute-start(bf16[4096,256]{1,0:T(8,128)(2,1)} %bitcast.53), channel_id=1, source_target_pairs={{0,1},{1,0},{2,3},{3,2},{4,5},{5,4},{6,7},{7,6},{8,9},{9,8},{10,11... | collective-permute-start | bytes 6291464 | tf_op jit(solution)/shard_map/ppermute | solution.py:23
  11.6 3.1 %multiply_reduce_fusion = (f32[32]{0:T(128)S(1)}, f32[32,4096]{1,0:T(8,128)S(1)}) fusion(bf16[1,512,4096]{2,1,0:T(8,128)(2,1)} %param.10, s32[32]{0:T(128)S(1)} %fusion.45.ids), kind=kOutput, calls=%fused_computation.30 | convolution fusion | flops 134496224 | bytes 4718848 | tf_op jit(solution)/shard_map/dot_general | solution.py:361
  15.4 4.2 %convolution_convert_fusion.1 = bf16[256,4096]{1,0:T(8,128)(2,1)} fusion(bf16[4096,256]{1,0:T(8,128)(2,1)} %collective-permute-done.weight_other, bf16[4096,256]{1,0:T(8,128)(2,1)S(1)} %bitcast.55, bf16[256,512]{1,0:T(8,128)(2,1)S(1)} %bitcast.67, bf16[256,256]{1,0:T(8,128)(2,1)S(1)} %get-tuple-element.93, bf16[256,256]{1,0:T(8,128)(2,1)S(1)} %get-tuple-element.92, ...), kind=kOutput, calls=%fused_computation.6 | convolution fusion | flops 1083834368 | bytes 6815745 | tf_op jit(solution)/shard_map/dot_general | solution.py:382
  21.3 13.0 %all_to_all.35.mine.row = bf16[16,32,256]{2,1,0:T(8,128)(2,1)S(1)} all-to-all(bf16[16,32,256]{2,1,0:T(8,128)(2,1)S(1)} %broadcast_in_dim.29), channel_id=1, replica_groups=mesh['pipe'=16,'z'=8,'core'=2] {'pipe'}, dimensions={0} | all-to-all | bytes 524288 | tf_op jit(solution)/shard_map/all_to_all | solution.py:19
  34.3 1.5 collective-permute-start.1
  36.9 1.7 shard_map.129
  38.7 8.2 %all-to-all-start.1 = ((bf16[8,64,1024]{2,1,0:T(8,128)(2,1)}), bf16[8,64,1024]{2,1,0:T(8,128)(2,1)S(1)}, u32[]{:S(2)}, u32[]{:S(2)}) async-start(bf16[8,64,1024]{2,1,0:T(8,128)(2,1)} %shard_map.129), calls=%async_computation.1 | async-start | bytes 2097152 | tf_op jit(solution)/shard_map/all_to_all | solution.py:403
  48.6 6.8 %shard_map.130.gain_part = f32[1,4096]{1,0:T(1,128)} custom-call(s32[4]{0:T(128)} %pad_add_fusion.place, bf16[8,2,32,4096]{3,2,1,0:T(8,128)(2,1)} %bitcast.58, bf16[8,2,32,4096]{3,2,1,0:T(8,128)(2,1)} %bitcast.47, s32[1,32]{1,0:T(1,128)} %constant_dynamic-slice_fusion.5.ids, bf16[4096,256]{1,0:T(8,128)(2,1)} %bitcast.54, ...), custom_call_target="tpu_custom_call" | custom-call | tf_op jit(solution)/shard_map/pallas_call | solution.py:405
  55.4 27.5 %all-to-all-done.1.parts = bf16[8,64,1024]{2,1,0:T(8,128)(2,1)S(1)} async-done(((bf16[8,64,1024]{2,1,0:T(8,128)(2,1)}), bf16[8,64,1024]{2,1,0:T(8,128)(2,1)S(1)}, u32[]{:S(2)}, u32[]{:S(2)}) %all-to-all-start.1) | async-done | bytes 1048608 | tf_op jit(solution)/shard_map/all_to_all | solution.py:403
  82.9 1.5 shard_map.131
  87.7 4.5 %all-to-all-start.2 = ((f32[16,2,8,128]{3,2,1,0:T(8,128)}), f32[16,2,8,128]{3,2,1,0:T(8,128)S(1)}, u32[]{:S(2)}, u32[]{:S(2)}) async-start(f32[16,2,8,128]{3,2,1,0:T(8,128)} %broadcast_in_dim.56), calls=%async_computation.3 | async-start | bytes 262144 | tf_op jit(solution)/shard_map/all_to_all | solution.py:19
  93.4 5.6 %all-to-all-done.2 = f32[16,2,8,128]{3,2,1,0:T(8,128)S(1)} async-done(((f32[16,2,8,128]{3,2,1,0:T(8,128)}), f32[16,2,8,128]{3,2,1,0:T(8,128)S(1)}, u32[]{:S(2)}, u32[]{:S(2)}) %all-to-all-start.2) | async-done | bytes 131104 | tf_op jit(solution)/shard_map/all_to_all | solution.py:19
  99.7 3.3 %all-to-all-start.3 = ((f32[8,8,128]{2,1,0:T(8,128)}), f32[8,8,128]{2,1,0:T(8,128)S(1)}, u32[]{:S(2)}, u32[]{:S(2)}) async-start(f32[8,8,128]{2,1,0:T(8,128)} %shard_map.132), calls=%async_computation.4 | async-start | bytes 65536 | tf_op jit(solution)/shard_map/all_to_all | solution.py:452
  103.1 3.2 %fusion = f32[512]{0:T(512)S(1)} fusion(bf16[512,4096]{1,0:T(8,128)(2,1)} %bitcast.50), kind=kLoop, calls=%fused_computation.2 | loop fusion | flops 6290944 | bytes 4196352 | tf_op jit(solution)/shard_map/reduce_sum | solution.py:464
  106.6 3.6 %fusion.2 = bf16[512,4096]{1,0:T(8,128)(2,1)} fusion(bf16[512,4096]{1,0:T(8,128)(2,1)S(1)} %bitcast.52, f32[4096]{0:T(1024)S(1)} %bitcast.40, f32[512]{0:T(512)S(1)} %add_rsqrt_fusion), kind=kLoop, calls=%fused_computation.4 | loop fusion | flops 8388608 | bytes 8407040 | tf_op jit(solution)/shard_map/convert_element_type | solution.py:465
  111.6 2.0 %collective-permute-start.4 = (f32[8,8,128]{2,1,0:T(8,128)S(1)}, f32[8,8,128]{2,1,0:T(8,128)S(1)}, u32[]{:S(2)}, u32[]{:S(2)}) collective-permute-start(f32[8,8,128]{2,1,0:T(8,128)S(1)} %all-to-all-done.3.known.known_mine), channel_id=1, source_target_pairs={{0,1},{1,0},{2,3},{3,2},{4,5},{5,4},{6,7},{7,6},{8,9},{9,8},{10,11... | collective-permute-start | bytes 98312 | tf_op jit(solution)/shard_map/ppermute | solution.py:23
  113.6 1.9 fusion.13
  115.6 5.2 %collective-permute-start.5 = (bf16[8,64,1024]{2,1,0:T(8,128)(2,1)}, bf16[8,64,1024]{2,1,0:T(8,128)(2,1)S(1)}, u32[]{:S(2)}, u32[]{:S(2)}) collective-permute-start(bf16[8,64,1024]{2,1,0:T(8,128)(2,1)} %bitcast.62), channel_id=1, source_target_pairs={{0,1},{1,0},{2,3},{3,2},{4,5},{5,4},{6,7},{7,6},{8,9},{9,8},{10,11... | collective-permute-start | bytes 3145736 | tf_op jit(solution)/shard_map/ppermute | solution.py:23
  120.8 3.2 %shard_map.133 = (f32[512,256]{1,0:T(8,128)}, f32[512,128]{1,0:T(8,128)}) custom-call(s32[4]{0:T(128)} %pad_add_fusion.place, bf16[8,64,1024]{2,1,0:T(8,128)(2,1)} %bitcast.63, f32[8,8,128]{2,1,0:T(8,128)} %copy-done.19, s32[512,1]{1,0:T(8,128)} %copy-done.15, bf16[1024,256]{1,0:T(8,128)(2,1)} %copy-done.3), custom_call_target="tpu_custom_call" | custom-call | tf_op jit(solution)/shard_map/pallas_call | solution.py:52
  125.2 3.2 %shard_map.134 = bf16[16,32,256]{2,1,0:T(8,128)(2,1)} custom-call(s32[4]{0:T(128)} %pad_add_fusion.place, bf16[8,64,1024]{2,1,0:T(8,128)(2,1)} %copy-done.16, f32[8,8,128]{2,1,0:T(8,128)} %copy-done.20, s32[512,1]{1,0:T(8,128)} %copy-done.15, bf16[1024,256]{1,0:T(8,128)(2,1)} %copy-done.17, f32[512,256]{1,0:T(8,128)} %get-tuple-element.65.before), custom_call_target="tpu_custom_call" | custom-call | tf_op jit(solution)/shard_map/pallas_call | solution.py:52
  128.3 6.5 %all-to-all-start.4 = ((bf16[16,32,256]{2,1,0:T(8,128)(2,1)}), bf16[16,32,256]{2,1,0:T(8,128)(2,1)S(1)}, u32[]{:S(2)}, u32[]{:S(2)}) async-start(bf16[16,32,256]{2,1,0:T(8,128)(2,1)} %shard_map.134), calls=%async_computation.5 | async-start | bytes 524288 | tf_op jit(solution)/shard_map/all_to_all | solution.py:506
  135.6 7.8 %all-to-all-done.4.got = bf16[16,32,256]{2,1,0:T(8,128)(2,1)S(1)} async-done(((bf16[16,32,256]{2,1,0:T(8,128)(2,1)}), bf16[16,32,256]{2,1,0:T(8,128)(2,1)S(1)}, u32[]{:S(2)}, u32[]{:S(2)}) %all-to-all-start.4) | async-done | bytes 262176 | tf_op jit(solution)/shard_map/all_to_all | solution.py:506
  146.1 2.8 %fusion.3.part = f32[16,4096]{1,0:T(8,128)S(1)} fusion(bf16[4096,256]{1,0:T(8,128)(2,1)} %collective-permute-done.weight_other, bf16[4096,256]{1,0:T(8,128)(2,1)S(1)} %bitcast.56, bf16[16,256]{1,0:T(8,128)(2,1)S(1)} %convert.7, bf16[16,256]{1,0:T(8,128)(2,1)S(1)} %convert.6), kind=kOutput, calls=%fused_computation.8 | convolution fusion | flops 75530240 | bytes 4472832 | tf_op jit(solution)/shard_map/dot_general | solution.py:523
  150.3 4.2 %all-to-all-start.5 = ((bf16[8,2,5888]{2,1,0:T(2,128)(2,1)}), bf16[8,2,5888]{2,1,0:T(2,128)(2,1)S(1)}, u32[]{:S(2)}, u32[]{:S(2)}) async-start(bf16[8,2,5888]{2,1,0:T(2,128)(2,1)} %shard_map.136), calls=%async_computation.6 | async-start | bytes 376832 | tf_op jit(solution)/shard_map/all_to_all | solution.py:536
  154.5 5.2 %convolution_convert_fusion = bf16[4096,256]{1,0:T(8,128)(2,1)} fusion(bf16[512,4096]{1,0:T(8,128)(2,1)} %fusion.2, bf16[32,256]{1,0:T(8,128)(2,1)S(1)} %get-tuple-element.76, pred[512]{0:T(512)(128)(4,1)S(1)} %compare_reduce_fusion, bf16[512,4096]{1,0:T(8,128)(2,1)} %bitcast.61, s32[]{:T(128)S(6)} %select_n.73, s32[32]{0:T(128)S(1)} %fusion.45.ids), kind=kOutput, calls=%fused_computation.5 | convolution fusion | flops 1083457536 | bytes 6570628 | tf_op jit(solution)/shard_map/dot_general | solution.py:543
  159.7 5.8 %all-to-all-done.5.got = bf16[8,2,5888]{2,1,0:T(2,128)(2,1)S(1)} async-done(((bf16[8,2,5888]{2,1,0:T(2,128)(2,1)}), bf16[8,2,5888]{2,1,0:T(2,128)(2,1)S(1)}, u32[]{:S(2)}, u32[]{:S(2)}) %all-to-all-start.5) | async-done | bytes 188448 | tf_op jit(solution)/shard_map/all_to_all | solution.py:536
  166.3 3.4 %all-to-all-start.6 = ((bf16[8,2,4864]{2,1,0:T(2,128)(2,1)}), bf16[8,2,4864]{2,1,0:T(2,128)(2,1)S(1)}, u32[]{:S(2)}, u32[]{:S(2)}) async-start(bf16[8,2,4864]{2,1,0:T(2,128)(2,1)} %shard_map.137), calls=%async_computation.7 | async-start | bytes 311296 | tf_op jit(solution)/shard_map/all_to_all | solution.py:568
  169.8 2.2 %copy-done.4 = bf16[512,4096]{1,0:T(8,128)(2,1)S(1)} copy-done((bf16[512,4096]{1,0:T(8,128)(2,1)S(1)}, bf16[512,4096]{1,0:T(8,128)(2,1)}, u32[]{:S(2)}) %copy-start.4) | copy-done | bytes 4194328
  172.3 2.0 %copy-done.1 = bf16[512,4096]{1,0:T(8,128)(2,1)} copy-done((bf16[512,4096]{1,0:T(8,128)(2,1)}, bf16[512,4096]{1,0:T(8,128)(2,1)S(1)}, u32[]{:S(2)}) %copy-start.1) | copy-done | bytes 4194328
  174.3 4.7 %shard_map.138 = bf16[2000,256]{1,0:T(8,128)(2,1)} custom-call(s32[4]{0:T(128)} %pad_add_fusion.place, bf16[16,32,256]{2,1,0:T(8,128)(2,1)} %copy-done.5, f32[1,256]{1,0:T(1,128)} %bitcast.44, f32[512,128]{1,0:T(8,128)} %get-tuple-element.82.kept, s32[512,1]{1,0:T(8,128)} %copy-done.15, bf16[8,64,1024]{2,1,0:T(8,128)(2,1)} %bitcast.64, ...), custom_call_target="tpu_custom_call" | custom-call | tf_op jit(solution)/shard_map/pallas_call | solution.py:52
  181.4 2.2 %copy-done.2 = bf16[512,4096]{1,0:T(8,128)(2,1)S(1)} copy-done((bf16[512,4096]{1,0:T(8,128)(2,1)S(1)}, bf16[512,4096]{1,0:T(8,128)(2,1)}, u32[]{:S(2)}) %copy-start.2) | copy-done | bytes 4194328
  183.6 4.2 %shard_map.140 = (bf16[512,4096]{1,0:T(8,128)(2,1)}, f32[1,4096]{1,0:T(1,128)}, bf16[512,4096]{1,0:T(8,128)(2,1)S(1)}) custom-call(s32[4]{0:T(128)S(1)} %copy-done.10, s32[32]{0:T(128)S(1)} %fusion.45.ids, bf16[8,2,4864]{2,1,0:T(2,128)(2,1)S(1)} %all-to-all-done.6.mine, ...), custom_call_target="tpu_custom_call", output_to_operand_aliasing={{2}: (4, {})} | custom-call | tf_op jit(solution)/shard_map/pallas_call | solution.py:580
  (107 shorter events, 22.5 us)
Async XLA Ops:
  7.2 77.2 %reduce-scatter.2.cloned.1.call-start = ((), (), s32[]{:S(2)}) async-start(), calls=%async_computation.8 | async-start | bytes 2359296 | tf_op jit(solution)/shard_map/reduce_scatter | solution.py:386
  7.2 8.1 %collective-permute-start = (bf16[4096,256]{1,0:T(8,128)(2,1)}, bf16[4096,256]{1,0:T(8,128)(2,1)}, u32[]{:S(2)}, u32[]{:S(2)}) collective-permute-start(bf16[4096,256]{1,0:T(8,128)(2,1)} %bitcast.53), channel_id=1, source_target_pairs={{0,1},{1,0},{2,3},{3,2},{4,5},{5,4},{6,7},{7,6},{8,9},{9,8},{10,11... | collective-permute-start | bytes 6291464 | tf_op jit(solution)/shard_map/ppermute | solution.py:23
  20.9 26.0 %copy-start.22 = (f32[16]{0:T(128)S(1)}, f32[16]{0:T(128)}, u32[]{:S(2)}) copy-start(f32[16]{0:T(128)} %param.18) | copy-start | bytes 196
  20.9 26.0 %copy-start.23 = (s32[16]{0:T(128)S(1)}, s32[16]{0:T(128)}, u32[]{:S(2)}) copy-start(s32[16]{0:T(128)} %param.16) | copy-start | bytes 196
  20.9 26.2 %copy-start.21 = (s32[16,32]{1,0:T(8,128)S(1)}, s32[16,32]{1,0:T(8,128)}, u32[]{:S(2)}) copy-start(s32[16,32]{1,0:T(8,128)} %param.17) | copy-start | bytes 6148
  21.0 34.4 %copy-start.3 = (bf16[1024,256]{1,0:T(8,128)(2,1)}, bf16[1024,256]{1,0:T(8,128)(2,1)S(1)}, u32[]{:S(2)}) copy-start(bf16[1024,256]{1,0:T(8,128)(2,1)S(1)} %get-tuple-element.91.head_mine.head) | copy-start | bytes 1572868
  21.0 34.4 %copy-start.17 = (bf16[1024,256]{1,0:T(8,128)(2,1)}, bf16[1024,256]{1,0:T(8,128)(2,1)S(1)}, u32[]{:S(2)}) copy-start(bf16[1024,256]{1,0:T(8,128)(2,1)S(1)} %get-tuple-element.90.head) | copy-start | bytes 1572868
  21.0 15.6 %collective-permute-start.2 = (bf16[1024,256]{1,0:T(8,128)(2,1)S(1)}, bf16[1024,256]{1,0:T(8,128)(2,1)S(1)}, u32[]{:S(2)}, u32[]{:S(2)}) collective-permute-start(bf16[1024,256]{1,0:T(8,128)(2,1)S(1)} %get-tuple-element.90.head), channel_id=1, source_target_pairs={{0,1},{1,0},{2,3},{3,2},{4,5},{5,4},{6,7},{7,6},{8,9},{9,8},{10,11... | collective-permute-start | bytes 1572872 | tf_op jit(solution)/shard_map/ppermute | solution.py:23
  34.3 21.1 %copy-start.5 = (bf16[16,32,256]{2,1,0:T(8,128)(2,1)}, bf16[16,32,256]{2,1,0:T(8,128)(2,1)S(1)}, u32[]{:S(2)}) copy-start(bf16[16,32,256]{2,1,0:T(8,128)(2,1)S(1)} %all_to_all.35.mine.row) | copy-start | bytes 786436
  34.3 2.7 %collective-permute-start.1 = (bf16[16,32,256]{2,1,0:T(8,128)(2,1)S(1)}, bf16[16,32,256]{2,1,0:T(8,128)(2,1)S(1)}, u32[]{:S(2)}, u32[]{:S(2)}) collective-permute-start(bf16[16,32,256]{2,1,0:T(8,128)(2,1)S(1)} %all_to_all.35.mine.row), channel_id=1, source_target_pairs={{0,1},{1,0},{2,3},{3,2},{4,5},{5,4},{6,7},{7,6},{8,9},{9,8},{10,11... | collective-permute-start | bytes 786440 | tf_op jit(solution)/shard_map/ppermute | solution.py:23
  36.6 106.8 %copy-start.11 = (f32[256]{0:T(256)}, f32[256]{0:T(256)S(1)}, u32[]{:S(2)}) copy-start(f32[256]{0:T(256)S(1)} %get-tuple-element.95) | copy-start | bytes 3076
  38.7 44.3 %all-to-all-start.1 = ((bf16[8,64,1024]{2,1,0:T(8,128)(2,1)}), bf16[8,64,1024]{2,1,0:T(8,128)(2,1)S(1)}, u32[]{:S(2)}, u32[]{:S(2)}) async-start(bf16[8,64,1024]{2,1,0:T(8,128)(2,1)} %shard_map.129), calls=%async_computation.1 | async-start | bytes 2097152 | tf_op jit(solution)/shard_map/all_to_all | solution.py:403
  46.8 68.8 %all-gather.6.cloned.1.call-start = ((), (), s32[]{:S(2)}) async-start(), calls=%async_computation.10 | async-start | bytes 1179648 | tf_op jit(solution)/shard_map/all_gather | solution.py:445
  47.3 8.1 %copy-start.15 = (s32[512,1]{1,0:T(8,128)}, s32[512,1]{1,0:T(8,128)S(1)}, u32[]{:S(2)}) copy-start(s32[512,1]{1,0:T(8,128)S(1)} %reshape.114.targets) | copy-start | bytes 6148
  48.6 34.3 %copy-start.8 = (s32[4]{0:T(128)S(1)}, s32[4]{0:T(128)}, u32[]{:S(2)}) copy-start(s32[4]{0:T(128)} %pad_add_fusion.place) | copy-start | bytes 52
  84.4 1.4 collective-permute-start.3
  87.7 11.3 %all-to-all-start.2 = ((f32[16,2,8,128]{3,2,1,0:T(8,128)}), f32[16,2,8,128]{3,2,1,0:T(8,128)S(1)}, u32[]{:S(2)}, u32[]{:S(2)}) async-start(f32[16,2,8,128]{3,2,1,0:T(8,128)} %broadcast_in_dim.56), calls=%async_computation.3 | async-start | bytes 262144 | tf_op jit(solution)/shard_map/all_to_all | solution.py:19
  99.7 11.9 %all-to-all-start.3 = ((f32[8,8,128]{2,1,0:T(8,128)}), f32[8,8,128]{2,1,0:T(8,128)S(1)}, u32[]{:S(2)}, u32[]{:S(2)}) async-start(f32[8,8,128]{2,1,0:T(8,128)} %shard_map.132), calls=%async_computation.4 | async-start | bytes 65536 | tf_op jit(solution)/shard_map/all_to_all | solution.py:452
  103.0 63.3 %all-gather.4.cloned.1.call-start = ((), (), s32[]{:S(2)}) async-start(), calls=%async_computation.9 | async-start | bytes 4456448 | tf_op jit(solution)/shard_map/all_gather | solution.py:479
  110.2 33.2 %copy-start.9 = (s32[4]{0:T(128)S(1)}, s32[4]{0:T(128)}, u32[]{:S(2)}) copy-start(s32[4]{0:T(128)} %pad_add_fusion.place) | copy-start | bytes 52
  110.2 35.9 %copy-start.14 = (bf16[1,4096,256]{2,1,0:T(8,128)(2,1)S(1)}, bf16[1,4096,256]{2,1,0:T(8,128)(2,1)}, u32[]{:S(2)}) copy-start(bf16[1,4096,256]{2,1,0:T(8,128)(2,1)} %param.11) | copy-start | bytes 6291460
  111.6 9.3 %copy-start.19 = (f32[8,8,128]{2,1,0:T(8,128)}, f32[8,8,128]{2,1,0:T(8,128)S(1)}, u32[]{:S(2)}) copy-start(f32[8,8,128]{2,1,0:T(8,128)S(1)} %all-to-all-done.3.known.known_mine) | copy-start | bytes 98308
  111.6 3.9 %collective-permute-start.4 = (f32[8,8,128]{2,1,0:T(8,128)S(1)}, f32[8,8,128]{2,1,0:T(8,128)S(1)}, u32[]{:S(2)}, u32[]{:S(2)}) collective-permute-start(f32[8,8,128]{2,1,0:T(8,128)S(1)} %all-to-all-done.3.known.known_mine), channel_id=1, source_target_pairs={{0,1},{1,0},{2,3},{3,2},{4,5},{5,4},{6,7},{7,6},{8,9},{9,8},{10,11... | collective-permute-start | bytes 98312 | tf_op jit(solution)/shard_map/ppermute | solution.py:23
  115.5 8.6 %copy-start.20 = (f32[8,8,128]{2,1,0:T(8,128)}, f32[8,8,128]{2,1,0:T(8,128)S(1)}, u32[]{:S(2)}) copy-start(f32[8,8,128]{2,1,0:T(8,128)S(1)} %collective-permute-done.4.known.known_other) | copy-start | bytes 98308
  115.6 8.4 %collective-permute-start.5 = (bf16[8,64,1024]{2,1,0:T(8,128)(2,1)}, bf16[8,64,1024]{2,1,0:T(8,128)(2,1)S(1)}, u32[]{:S(2)}, u32[]{:S(2)}) collective-permute-start(bf16[8,64,1024]{2,1,0:T(8,128)(2,1)} %bitcast.62), channel_id=1, source_target_pairs={{0,1},{1,0},{2,3},{3,2},{4,5},{5,4},{6,7},{7,6},{8,9},{9,8},{10,11... | collective-permute-start | bytes 3145736 | tf_op jit(solution)/shard_map/ppermute | solution.py:23
  128.3 20.6 %copy-start.7 = (f32[1,4096]{1,0:T(1,128)S(1)}, f32[1,4096]{1,0:T(1,128)}, u32[]{:S(2)}) copy-start(f32[1,4096]{1,0:T(1,128)} %shard_map.130.gain_part) | copy-start | bytes 49156
  128.3 15.0 %all-to-all-start.4 = ((bf16[16,32,256]{2,1,0:T(8,128)(2,1)}), bf16[16,32,256]{2,1,0:T(8,128)(2,1)S(1)}, u32[]{:S(2)}, u32[]{:S(2)}) async-start(bf16[16,32,256]{2,1,0:T(8,128)(2,1)} %shard_map.134), calls=%async_computation.5 | async-start | bytes 524288 | tf_op jit(solution)/shard_map/all_to_all | solution.py:506
  144.0 2.1 %collective-permute-start.6 = (f32[16,256]{1,0:T(8,128)S(1)}, f32[16,256]{1,0:T(8,128)S(1)}, u32[]{:S(2)}, u32[]{:S(2)}) collective-permute-start(f32[16,256]{1,0:T(8,128)S(1)} %get-tuple-element.71), channel_id=1, source_target_pairs={{0,1},{1,0},{2,3},{3,2},{4,5},{5,4},{6,7},{7,6},{8,9},{9,8},{10,11... | collective-permute-start | bytes 49160 | tf_op jit(solution)/shard_map/ppermute | solution.py:23
  150.3 15.2 %all-to-all-start.5 = ((bf16[8,2,5888]{2,1,0:T(2,128)(2,1)}), bf16[8,2,5888]{2,1,0:T(2,128)(2,1)S(1)}, u32[]{:S(2)}, u32[]{:S(2)}) async-start(bf16[8,2,5888]{2,1,0:T(2,128)(2,1)} %shard_map.136), calls=%async_computation.6 | async-start | bytes 376832 | tf_op jit(solution)/shard_map/all_to_all | solution.py:536
  166.3 12.7 %all-to-all-start.6 = ((bf16[8,2,4864]{2,1,0:T(2,128)(2,1)}), bf16[8,2,4864]{2,1,0:T(2,128)(2,1)S(1)}, u32[]{:S(2)}, u32[]{:S(2)}) async-start(bf16[8,2,4864]{2,1,0:T(2,128)(2,1)} %shard_map.137), calls=%async_computation.7 | async-start | bytes 311296 | tf_op jit(solution)/shard_map/all_to_all | solution.py:568
  172.0 9.4 %copy-start.10 = (s32[4]{0:T(128)S(1)}, s32[4]{0:T(128)}, u32[]{:S(2)}) copy-start(s32[4]{0:T(128)} %pad_add_fusion.place) | copy-start | bytes 52
  179.0 2.3 %collective-permute-start.7 = (bf16[8,2,4864]{2,1,0:T(2,128)(2,1)S(1)}, bf16[8,2,4864]{2,1,0:T(2,128)(2,1)S(1)}, u32[]{:S(2)}, u32[]{:S(2)}) collective-permute-start(bf16[8,2,4864]{2,1,0:T(2,128)(2,1)S(1)} %all-to-all-done.6.mine), channel_id=1, source_target_pairs={{0,1},{1,0},{2,3},{3,2},{4,5},{5,4},{6,7},{7,6},{8,9},{9,8},{10,11... | collective-permute-start | bytes 466952 | tf_op jit(solution)/shard_map/ppermute | solution.py:23
  (9 other events, 37.7 us)
Sparse Core Ops, SparseCore 0:
  19.7 52.2 reduce-scatter.1
  85.3 30.3 all-gather.5
  117.5 47.2 all-gather.3

commit v10 on v9

--- a/solution.py
+++ b/solution.py
@@ -225,9 +225,11 @@
     other[...] = jnp.where(core == 0, rows[half:], rows[:half])
 
 
-def send_kernel(place, part, mine, other, unit, gain_part, out):
+def send_kernel(place, mine, other, weight, weight_other, unit, gain_part, out):
     core = place[1]
-    part = part[...]
+    columns = (((1,), (1,)), ((), ()))
+    part = lax.dot_general(mine[...].astype(BF16), weight[...], columns, preferred_element_type=F32)
+    part += lax.dot_general(other[...].astype(BF16), weight_other[...], columns, preferred_element_type=F32)
     gain = gain_part[...] + jnp.sum(part * unit[...], axis=0, keepdims=True)
     low = jnp.where(core == 0, mine[...], other[...])
     high = jnp.where(core == 0, other[...], mine[...])
@@ -237,7 +239,7 @@
     part = part.astype(BF16)
     gains = [values.astype(BF16) for values in pieces3(gain)]
     count, share, _ = out.shape
-    width, slab = part.shape[1], mine.shape[1]
+    width, slab = weight.shape
     piece = width // (count * share)
     for i in range(count):
         at = slice(i * share, (i + 1) * share)
@@ -350,12 +352,6 @@
     whole = lambda *dims: pl.BlockSpec(dims, lambda i, *_: (0,) * len(dims))
 
     weight_other = swap(weight)
-    halves = jnp.pad(head_weight, ((0, 2 * half - vocab_part), (0, 0))).reshape(2, half, slab)
-    halves = jnp.pad(halves, ((0, 0), (0, padded - half), (0, 0)))
-    head_mine = lax.dynamic_index_in_dim(halves, core, 0, keepdims=False)
-    head_rest = lax.dynamic_index_in_dim(halves, 1 - core, 0, keepdims=False)
-    head_other = swap(head_rest)
-
     my_rows = exit_rows[pipe]
     pick = (my_rows[:, None] == jnp.arange(tokens, dtype=jnp.int32)[None, :]).astype(BF16)
     row_in = jnp.dot(pick, seg, preferred_element_type=F32)
@@ -384,6 +380,12 @@
     ).astype(BF16)
     hidden, main_sent = lax.optimization_barrier((hidden, main_sent))
     main_grad = lax.psum_scatter(main_sent, "z", scatter_dimension=0, tiled=True)
+
+    halves = jnp.pad(after(head_weight, hidden), ((0, 2 * half - vocab_part), (0, 0))).reshape(2, half, slab)
+    halves = jnp.pad(halves, ((0, 0), (0, padded - half), (0, 0)))
+    head_mine = lax.dynamic_index_in_dim(halves, core, 0, keepdims=False)
+    head_rest = lax.dynamic_index_in_dim(halves, 1 - core, 0, keepdims=False)
+    head_other = swap(head_rest)
 
     all_mine = spread(hidden, "pipe", pipes)
     all_other = swap(all_mine)
@@ -502,11 +504,27 @@
         exit_first,
         held=(1, 5),
         scratch=grads,
+        limit=SMALL,
     )
     exit_got = lax.all_to_all(exit_part, "pipe", 0, 0)
     kept_all = kept
     kept = lax.dynamic_slice_in_dim(kept, pipe * exits, exits, 0)
-    exit_got, kept = lax.optimization_barrier((exit_got, kept))
+    (head_grad,) = piped_call(
+        functools.partial(head_kernel, half, vocab_part),
+        [shape((vocab_part, slab), BF16)],
+        place,
+        all_mine,
+        gain_mine,
+        after(kept_all, exit_part),
+        all_targets,
+        ex_mine,
+        ex_other,
+        known_mine,
+        known_other,
+        scratch=grads,
+        limit=SMALL,
+    )
+    exit_got, kept, head_grad = lax.optimization_barrier((exit_got, kept, head_grad))
     row_mine, row_send, row_rounded = kernel_call(
         row_kernel,
         [shape((core_rows, slab), F32)] * 2 + [shape((exits, slab), BF16)],
@@ -519,17 +537,14 @@
     )
 
     piece = slab * 2 // share
-    row_other = swap(row_send)
-    row_part = lax.dot_general(
-        jnp.concatenate([row_mine, row_other], axis=1).astype(BF16), joined, on_columns, preferred_element_type=F32
-    )
     send = kernel_call(
         send_kernel,
         shape((zs, share, width + 4 * slab + 3 * piece), BF16),
         place,
-        row_part,
         row_mine,
-        row_other,
+        swap(row_send),
+        weight,
+        weight_other,
         core_unit,
         gain_part,
     )
@@ -551,20 +566,6 @@
         share_inv,
     )
     last, main_all = lax.optimization_barrier((last, main_all))
-    (head_grad,) = piped_call(
-        functools.partial(head_kernel, half, vocab_part),
-        [shape((vocab_part, slab), BF16)],
-        place,
-        all_mine,
-        gain_mine,
-        after(kept_all, last),
-        all_targets,
-        ex_mine,
-        ex_other,
-        known_mine,
-        known_other,
-        scratch=grads,
-    )
     last = lax.all_to_all(last, "z", 0, 0)
     main_near = pl.pallas_call(
         fetch_kernel,
@@ -574,7 +575,7 @@
         scratch_shapes=[pltpu.SemaphoreType.DMA((4,))],
         compiler_params=pltpu.CompilerParams(vmem_limit_bytes=SMALL),
     )(main_all)
-    last, head_grad, main_near = lax.optimization_barrier((last, head_grad, main_near))
+    last, main_near = lax.optimization_barrier((last, main_near))
     last_other = swap(last)
     in_vmem = pl.BlockSpec(memory_space=pltpu.VMEM)
     input_grad, gain_grad, _ = pl.pallas_call(

time: 196 us -> 197 us (level)
  local copies, waits for them, and re-layouts: 13.6 us -> 23.9 us
  waiting for transfers between devices: 49.5 us -> 43.5 us
  matrix products: 17.1 us -> 14.1 us
    unnamed x48 -> x68, local copies, waits for them, and re-layouts: 7.76 us -> 15.5 us
    all_to_all x1, waiting for transfers between devices: 7.78 us -> 0.43 us  [local(): exit_got = lax.all_to_all(exit_part, 'pipe', 0, 0)]
    all_to_all x1, waiting for transfers between devices: 0.01 us -> 3.58 us  [local(): last = lax.all_to_all(last, 'z', 0, 0)]
    pallas_call x3, Pallas kernels: 11.1 us -> 8.11 us  [piped_call(): pl.pallas_call(body, grid=(1,), out_shape=out, in_specs=[pl.BlockSpec(mem...]
    dot_general x1 -> x0, matrix products: 2.82 us -> none  [local(): lax.dot_general(jnp.concatenate([row_mine, row_other], axis=1).astype(BF1...]
    pallas_call x3, Pallas kernels: 3.59 us -> 6.17 us  [kernel_call(): pl.pallas_call(body, out_shape=out, in_specs=[pl.BlockSpec(memory_space=p...]
  transfers between devices with their start and end apart: 17 -> 17, of which waited for: 9 -> 8; matrix products, arithmetic and copies ran while one was open for 16% -> 16% of each run, Pallas kernels for 13% -> 13%
where the time goes in v10:
time: 197 us; the launch traced here: 196 us
  starting transfers between devices  45.6 us (23%)
  waiting for transfers between devices  43.5 us (22%)
  Pallas kernels  28.8 us (15%)
  local copies, waits for them, and re-layouts  23.9 us (12%)
  between operations  14.2 us (7%)
  matrix products  14.1 us (7%)
  blocking collectives  13 us (7%)
  other arithmetic  12.7 us (6%)
    all_to_all x1, waiting for transfers between devices, local(): parts = lax.all_to_all(part, 'z', 0, 0)  27.4 us
    unnamed x68, local copies, waits for them, and re-layouts  15.5 us
    ppermute x8, starting transfers between devices, swap(): return lax.ppermute(values, 'core', [(0, 1), (1, 0)])  15.4 us
    all_to_all x1, blocking collectives, spread(): lax.all_to_all(jnp.broadcast_to(values[None], (count,) + values.shape), a...  13 us
    all_to_all x1, starting transfers between devices, local(): parts = lax.all_to_all(part, 'z', 0, 0)  8.19 us
    pallas_call x3, Pallas kernels, piped_call(): pl.pallas_call(body, grid=(1,), out_shape=out, in_specs=[pl.BlockSpec(mem...  8.11 us
    pallas_call x1, Pallas kernels, local(): pl.pallas_call(gain_kernel, grid_spec=pltpu.PrefetchScalarGridSpec(num_sc...  6.82 us
    all_to_all x1, starting transfers between devices, local(): exit_got = lax.all_to_all(exit_part, 'pipe', 0, 0)  6.4 us
  transfers between devices with their start and end apart: 17, of which 8 were waited for; matrix products, arithmetic and copies ran while one was open for 16% of the time, Pallas kernels for 13%

profile of v10, /device:TPU:1, one launch (start us, length us, event | category | flops | bytes accessed | tf_op | source)
XLA Modules:
  0.0 195.8 jit_solution(16421222053133505618)
XLA Ops:
  7.2 3.3 %collective-permute-start = (bf16[4096,256]{1,0:T(8,128)(2,1)}, bf16[4096,256]{1,0:T(8,128)(2,1)}, u32[]{:S(2)}, u32[]{:S(2)}) collective-permute-start(bf16[4096,256]{1,0:T(8,128)(2,1)} %bitcast.37), channel_id=1, source_target_pairs={{0,1},{1,0},{2,3},{3,2},{4,5},{5,4},{6,7},{7,6},{8,9},{9,8},{10,11... | collective-permute-start | bytes 6291464 | tf_op jit(solution)/shard_map/ppermute | solution.py:23
  11.6 3.1 %multiply_reduce_fusion = (f32[32]{0:T(128)S(1)}, f32[32,4096]{1,0:T(8,128)S(1)}) fusion(bf16[1,512,4096]{2,1,0:T(8,128)(2,1)} %param.10, s32[32]{0:T(128)S(1)} %fusion.43.ids), kind=kOutput, calls=%fused_computation.31 | convolution fusion | flops 134496224 | bytes 4718848 | tf_op jit(solution)/shard_map/dot_general | solution.py:357
  15.4 4.2 %convolution_convert_fusion.1 = bf16[256,4096]{1,0:T(8,128)(2,1)} fusion(bf16[4096,256]{1,0:T(8,128)(2,1)} %collective-permute-done.weight_other, bf16[4096,256]{1,0:T(8,128)(2,1)S(1)} %bitcast.39, bf16[256,512]{1,0:T(8,128)(2,1)S(1)} %bitcast.67, bf16[256,256]{1,0:T(8,128)(2,1)S(1)} %get-tuple-element.95, bf16[256,256]{1,0:T(8,128)(2,1)S(1)} %get-tuple-element.94, ...), kind=kOutput, calls=%fused_computation.6 | convolution fusion | flops 1083834368 | bytes 6815745 | tf_op jit(solution)/shard_map/dot_general | solution.py:378
  21.3 13.0 %all_to_all.35.mine.row = bf16[16,32,256]{2,1,0:T(8,128)(2,1)S(1)} all-to-all(bf16[16,32,256]{2,1,0:T(8,128)(2,1)S(1)} %broadcast_in_dim.29), channel_id=1, replica_groups=mesh['pipe'=16,'z'=8,'core'=2] {'pipe'}, dimensions={0} | all-to-all | bytes 524288 | tf_op jit(solution)/shard_map/all_to_all | solution.py:19
  34.3 1.5 collective-permute-start.1
  36.9 1.7 shard_map.129
  38.7 8.2 %all-to-all-start.1 = ((bf16[8,64,1024]{2,1,0:T(8,128)(2,1)}), bf16[8,64,1024]{2,1,0:T(8,128)(2,1)S(1)}, u32[]{:S(2)}, u32[]{:S(2)}) async-start(bf16[8,64,1024]{2,1,0:T(8,128)(2,1)} %shard_map.129), calls=%async_computation.1 | async-start | bytes 2097152 | tf_op jit(solution)/shard_map/all_to_all | solution.py:405
  48.7 6.8 %shard_map.130.gain_part = f32[1,4096]{1,0:T(1,128)} custom-call(s32[4]{0:T(128)} %pad_add_fusion.place, bf16[8,2,32,4096]{3,2,1,0:T(8,128)(2,1)} %bitcast.61, bf16[8,2,32,4096]{3,2,1,0:T(8,128)(2,1)} %bitcast.54, s32[1,32]{1,0:T(1,128)} %constant_dynamic-slice_fusion.5.ids, bf16[4096,256]{1,0:T(8,128)(2,1)} %bitcast.38, ...), custom_call_target="tpu_custom_call" | custom-call | tf_op jit(solution)/shard_map/pallas_call | solution.py:407
  55.6 27.4 %all-to-all-done.1.parts = bf16[8,64,1024]{2,1,0:T(8,128)(2,1)S(1)} async-done(((bf16[8,64,1024]{2,1,0:T(8,128)(2,1)}), bf16[8,64,1024]{2,1,0:T(8,128)(2,1)S(1)}, u32[]{:S(2)}, u32[]{:S(2)}) %all-to-all-start.1) | async-done | bytes 1048608 | tf_op jit(solution)/shard_map/all_to_all | solution.py:405
  82.9 1.5 shard_map.131
  87.7 4.5 %all-to-all-start.2 = ((f32[16,2,8,128]{3,2,1,0:T(8,128)}), f32[16,2,8,128]{3,2,1,0:T(8,128)S(1)}, u32[]{:S(2)}, u32[]{:S(2)}) async-start(f32[16,2,8,128]{3,2,1,0:T(8,128)} %broadcast_in_dim.56), calls=%async_computation.3 | async-start | bytes 262144 | tf_op jit(solution)/shard_map/all_to_all | solution.py:19
  93.5 5.6 %all-to-all-done.2 = f32[16,2,8,128]{3,2,1,0:T(8,128)S(1)} async-done(((f32[16,2,8,128]{3,2,1,0:T(8,128)}), f32[16,2,8,128]{3,2,1,0:T(8,128)S(1)}, u32[]{:S(2)}, u32[]{:S(2)}) %all-to-all-start.2) | async-done | bytes 131104 | tf_op jit(solution)/shard_map/all_to_all | solution.py:19
  99.8 3.3 %all-to-all-start.3 = ((f32[8,8,128]{2,1,0:T(8,128)}), f32[8,8,128]{2,1,0:T(8,128)S(1)}, u32[]{:S(2)}, u32[]{:S(2)}) async-start(f32[8,8,128]{2,1,0:T(8,128)} %shard_map.132), calls=%async_computation.4 | async-start | bytes 65536 | tf_op jit(solution)/shard_map/all_to_all | solution.py:454
  103.2 3.2 %fusion = f32[512]{0:T(512)S(1)} fusion(bf16[512,4096]{1,0:T(8,128)(2,1)} %bitcast.57), kind=kLoop, calls=%fused_computation.2 | loop fusion | flops 6290944 | bytes 4196352 | tf_op jit(solution)/shard_map/reduce_sum | solution.py:466
  106.7 3.6 %fusion.2 = bf16[512,4096]{1,0:T(8,128)(2,1)} fusion(bf16[512,4096]{1,0:T(8,128)(2,1)S(1)} %bitcast.59, f32[4096]{0:T(1024)S(1)} %bitcast.47, f32[512]{0:T(512)S(1)} %add_rsqrt_fusion), kind=kLoop, calls=%fused_computation.4 | loop fusion | flops 8388608 | bytes 8407040 | tf_op jit(solution)/shard_map/convert_element_type | solution.py:467
  112.7 1.9 collective-permute-start.4
  114.6 2.0 fusion.15
  116.6 4.3 %collective-permute-start.5 = (bf16[8,64,1024]{2,1,0:T(8,128)(2,1)}, bf16[8,64,1024]{2,1,0:T(8,128)(2,1)S(1)}, u32[]{:S(2)}, u32[]{:S(2)}) collective-permute-start(bf16[8,64,1024]{2,1,0:T(8,128)(2,1)} %bitcast.41), channel_id=1, source_target_pairs={{0,1},{1,0},{2,3},{3,2},{4,5},{5,4},{6,7},{7,6},{8,9},{9,8},{10,11... | collective-permute-start | bytes 3145736 | tf_op jit(solution)/shard_map/ppermute | solution.py:23
  120.9 3.2 %shard_map.133 = (f32[512,256]{1,0:T(8,128)}, f32[512,128]{1,0:T(8,128)}) custom-call(s32[4]{0:T(128)} %pad_add_fusion.place, bf16[8,64,1024]{2,1,0:T(8,128)(2,1)} %bitcast.42, f32[8,8,128]{2,1,0:T(8,128)} %copy-done.21, s32[512,1]{1,0:T(8,128)} %copy-done.6, bf16[1024,256]{1,0:T(8,128)(2,1)} %copy-done.5), custom_call_target="tpu_custom_call" | custom-call | tf_op jit(solution)/shard_map/pallas_call | solution.py:52
  129.5 6.4 %all-to-all-start.4 = ((bf16[16,32,256]{2,1,0:T(8,128)(2,1)}), bf16[16,32,256]{2,1,0:T(8,128)(2,1)}, u32[]{:S(2)}, u32[]{:S(2)}) async-start(bf16[16,32,256]{2,1,0:T(8,128)(2,1)} %copy-done.17), calls=%async_computation.5 | async-start | bytes 524288 | tf_op jit(solution)/shard_map/all_to_all | solution.py:509
  140.6 3.5 %shard_map.135 = bf16[2000,256]{1,0:T(8,128)(2,1)} custom-call(s32[4]{0:T(128)S(1)} %copy-done.26, bf16[16,32,256]{2,1,0:T(8,128)(2,1)S(1)} %copy-done.13, f32[1,256]{1,0:T(1,128)S(1)} %bitcast.50, f32[512,128]{1,0:T(8,128)S(1)} %copy-done.20, s32[512,1]{1,0:T(8,128)S(1)} %copy-done.7, bf16[8,64,1024]{2,1,0:T(8,128)(2,1)S(1)} %bitcast.43, ...), custom_call_target="tpu_custom_call" | custom-call | tf_op jit(solution)/shard_map/pallas_call | solution.py:52
  149.1 3.6 %shard_map.137 = bf16[8,2,5888]{2,1,0:T(2,128)(2,1)} custom-call(s32[4]{0:T(128)S(1)} %copy-done.26, f32[16,256]{1,0:T(8,128)S(1)} %get-tuple-element.73.mine, f32[16,256]{1,0:T(8,128)S(1)} %collective-permute-done.6.other, bf16[4096,256]{1,0:T(8,128)(2,1)S(1)} %bitcast.40, bf16[4096,256]{1,0:T(8,128)(2,1)} %collective-permute-done.weight_other, ...), custom_call_target="tpu_custom_call" | custom-call | tf_op jit(solution)/shard_map/pallas_call | solution.py:27
  152.7 4.3 %all-to-all-start.5 = ((bf16[8,2,5888]{2,1,0:T(2,128)(2,1)}), bf16[8,2,5888]{2,1,0:T(2,128)(2,1)S(1)}, u32[]{:S(2)}, u32[]{:S(2)}) async-start(bf16[8,2,5888]{2,1,0:T(2,128)(2,1)} %shard_map.137), calls=%async_computation.6 | async-start | bytes 376832 | tf_op jit(solution)/shard_map/all_to_all | solution.py:551
  157.0 5.2 %convolution_convert_fusion = bf16[4096,256]{1,0:T(8,128)(2,1)} fusion(bf16[512,4096]{1,0:T(8,128)(2,1)} %fusion.2, bf16[32,256]{1,0:T(8,128)(2,1)S(1)} %get-tuple-element.79, pred[512]{0:T(512)(128)(4,1)S(1)} %compare_reduce_fusion, bf16[512,4096]{1,0:T(8,128)(2,1)} %bitcast.64, s32[]{:T(128)S(6)} %select_n.73, s32[32]{0:T(128)S(1)} %copy-done.28), kind=kOutput, calls=%fused_computation.5 | convolution fusion | flops 1083457536 | bytes 6570628 | tf_op jit(solution)/shard_map/dot_general | solution.py:558
  162.2 5.0 %all-to-all-done.5.got = bf16[8,2,5888]{2,1,0:T(2,128)(2,1)S(1)} async-done(((bf16[8,2,5888]{2,1,0:T(2,128)(2,1)}), bf16[8,2,5888]{2,1,0:T(2,128)(2,1)S(1)}, u32[]{:S(2)}, u32[]{:S(2)}) %all-to-all-start.5) | async-done | bytes 188448 | tf_op jit(solution)/shard_map/all_to_all | solution.py:551
  168.0 3.4 %all-to-all-start.6 = ((bf16[8,2,4864]{2,1,0:T(2,128)(2,1)}), bf16[8,2,4864]{2,1,0:T(2,128)(2,1)S(1)}, u32[]{:S(2)}, u32[]{:S(2)}) async-start(bf16[8,2,4864]{2,1,0:T(2,128)(2,1)} %shard_map.138), calls=%async_computation.7 | async-start | bytes 311296 | tf_op jit(solution)/shard_map/all_to_all | solution.py:569
  171.4 2.2 %copy-done.11 = bf16[512,4096]{1,0:T(8,128)(2,1)S(1)} copy-done((bf16[512,4096]{1,0:T(8,128)(2,1)S(1)}, bf16[512,4096]{1,0:T(8,128)(2,1)}, u32[]{:S(2)}) %copy-start.11) | copy-done | bytes 4194328
  173.9 2.0 %copy-done.3 = bf16[512,4096]{1,0:T(8,128)(2,1)} copy-done((bf16[512,4096]{1,0:T(8,128)(2,1)}, bf16[512,4096]{1,0:T(8,128)(2,1)S(1)}, u32[]{:S(2)}) %copy-start.3) | copy-done | bytes 4194328
  175.9 3.6 %all-to-all-done.6.mine = bf16[8,2,4864]{2,1,0:T(2,128)(2,1)S(1)} async-done(((bf16[8,2,4864]{2,1,0:T(2,128)(2,1)}), bf16[8,2,4864]{2,1,0:T(2,128)(2,1)S(1)}, u32[]{:S(2)}, u32[]{:S(2)}) %all-to-all-start.6) | async-done | bytes 155680 | tf_op jit(solution)/shard_map/all_to_all | solution.py:569
  179.5 2.3 %collective-permute-start.7 = (bf16[8,2,4864]{2,1,0:T(2,128)(2,1)S(1)}, bf16[8,2,4864]{2,1,0:T(2,128)(2,1)S(1)}, u32[]{:S(2)}, u32[]{:S(2)}) collective-permute-start(bf16[8,2,4864]{2,1,0:T(2,128)(2,1)S(1)} %all-to-all-done.6.mine), channel_id=1, source_target_pairs={{0,1},{1,0},{2,3},{3,2},{4,5},{5,4},{6,7},{7,6},{8,9},{9,8},{10,11... | collective-permute-start | bytes 466952 | tf_op jit(solution)/shard_map/ppermute | solution.py:23
  182.9 2.2 %copy-done.4 = bf16[512,4096]{1,0:T(8,128)(2,1)S(1)} copy-done((bf16[512,4096]{1,0:T(8,128)(2,1)S(1)}, bf16[512,4096]{1,0:T(8,128)(2,1)}, u32[]{:S(2)}) %copy-start.4) | copy-done | bytes 4194328
  185.1 4.2 %shard_map.140 = (bf16[512,4096]{1,0:T(8,128)(2,1)}, f32[1,4096]{1,0:T(1,128)}, bf16[512,4096]{1,0:T(8,128)(2,1)S(1)}) custom-call(s32[4]{0:T(128)S(1)} %copy-done.26, s32[32]{0:T(128)S(1)} %copy-done.28, bf16[8,2,4864]{2,1,0:T(2,128)(2,1)S(1)} %all-to-all-done.6.mine, ...), custom_call_target="tpu_custom_call", output_to_operand_aliasing={{2}: (4, {})} | custom-call | tf_op jit(solution)/shard_map/pallas_call | solution.py:581
  (124 shorter events, 31.5 us)
Async XLA Ops:
  7.2 77.3 %reduce-scatter.2.cloned.1.call-start = ((), (), s32[]{:S(2)}) async-start(), calls=%async_computation.8 | async-start | bytes 2359296 | tf_op jit(solution)/shard_map/reduce_scatter | solution.py:382
  7.2 8.1 %collective-permute-start = (bf16[4096,256]{1,0:T(8,128)(2,1)}, bf16[4096,256]{1,0:T(8,128)(2,1)}, u32[]{:S(2)}, u32[]{:S(2)}) collective-permute-start(bf16[4096,256]{1,0:T(8,128)(2,1)} %bitcast.37), channel_id=1, source_target_pairs={{0,1},{1,0},{2,3},{3,2},{4,5},{5,4},{6,7},{7,6},{8,9},{9,8},{10,11... | collective-permute-start | bytes 6291464 | tf_op jit(solution)/shard_map/ppermute | solution.py:23
  11.6 100.0 %copy-start.27 = (s32[32]{0:T(128)}, s32[32]{0:T(128)S(1)}, u32[]{:S(2)}) copy-start(s32[32]{0:T(128)S(1)} %fusion.43.ids) | copy-start | bytes 388
  20.9 26.0 %copy-start.32 = (f32[16]{0:T(128)S(1)}, f32[16]{0:T(128)}, u32[]{:S(2)}) copy-start(f32[16]{0:T(128)} %param.18) | copy-start | bytes 196
  20.9 26.0 %copy-start.33 = (s32[16]{0:T(128)S(1)}, s32[16]{0:T(128)}, u32[]{:S(2)}) copy-start(s32[16]{0:T(128)} %param.16) | copy-start | bytes 196
  20.9 26.2 %copy-start.31 = (s32[16,32]{1,0:T(8,128)S(1)}, s32[16,32]{1,0:T(8,128)}, u32[]{:S(2)}) copy-start(s32[16,32]{1,0:T(8,128)} %param.17) | copy-start | bytes 6148
  21.0 17.6 %copy-start.14 = (bf16[1024,256]{1,0:T(8,128)(2,1)}, bf16[1024,256]{1,0:T(8,128)(2,1)S(1)}, u32[]{:S(2)}) copy-start(bf16[1024,256]{1,0:T(8,128)(2,1)S(1)} %get-tuple-element.92.head) | copy-start | bytes 1572868
  21.0 34.5 %copy-start.5 = (bf16[1024,256]{1,0:T(8,128)(2,1)}, bf16[1024,256]{1,0:T(8,128)(2,1)S(1)}, u32[]{:S(2)}) copy-start(bf16[1024,256]{1,0:T(8,128)(2,1)S(1)} %get-tuple-element.93.head_mine.head) | copy-start | bytes 1572868
  21.0 15.9 %collective-permute-start.2 = (bf16[1024,256]{1,0:T(8,128)(2,1)S(1)}, bf16[1024,256]{1,0:T(8,128)(2,1)S(1)}, u32[]{:S(2)}, u32[]{:S(2)}) collective-permute-start(bf16[1024,256]{1,0:T(8,128)(2,1)S(1)} %get-tuple-element.92.head), channel_id=1, source_target_pairs={{0,1},{1,0},{2,3},{3,2},{4,5},{5,4},{6,7},{7,6},{8,9},{9,8},{10,11... | collective-permute-start | bytes 1572872 | tf_op jit(solution)/shard_map/ppermute | solution.py:23
  34.3 2.7 %collective-permute-start.1 = (bf16[16,32,256]{2,1,0:T(8,128)(2,1)S(1)}, bf16[16,32,256]{2,1,0:T(8,128)(2,1)S(1)}, u32[]{:S(2)}, u32[]{:S(2)}) collective-permute-start(bf16[16,32,256]{2,1,0:T(8,128)(2,1)S(1)} %all_to_all.35.mine.row), channel_id=1, source_target_pairs={{0,1},{1,0},{2,3},{3,2},{4,5},{5,4},{6,7},{7,6},{8,9},{9,8},{10,11... | collective-permute-start | bytes 786440 | tf_op jit(solution)/shard_map/ppermute | solution.py:23
  38.7 44.2 %all-to-all-start.1 = ((bf16[8,64,1024]{2,1,0:T(8,128)(2,1)}), bf16[8,64,1024]{2,1,0:T(8,128)(2,1)S(1)}, u32[]{:S(2)}, u32[]{:S(2)}) async-start(bf16[8,64,1024]{2,1,0:T(8,128)(2,1)} %shard_map.129), calls=%async_computation.1 | async-start | bytes 2097152 | tf_op jit(solution)/shard_map/all_to_all | solution.py:405
  46.9 69.7 %all-gather.6.cloned.1.call-start = ((), (), s32[]{:S(2)}) async-start(), calls=%async_computation.10 | async-start | bytes 1179648 | tf_op jit(solution)/shard_map/all_gather | solution.py:447
  47.3 8.2 %copy-start.6 = (s32[512,1]{1,0:T(8,128)}, s32[512,1]{1,0:T(8,128)S(1)}, u32[]{:S(2)}) copy-start(s32[512,1]{1,0:T(8,128)S(1)} %reshape.114.targets) | copy-start | bytes 6148
  48.7 34.2 %copy-start.25 = (s32[4]{0:T(128)S(1)}, s32[4]{0:T(128)}, u32[]{:S(2)}) copy-start(s32[4]{0:T(128)} %pad_add_fusion.place) | copy-start | bytes 52
  84.5 1.4 collective-permute-start.3
  87.7 11.4 %all-to-all-start.2 = ((f32[16,2,8,128]{3,2,1,0:T(8,128)}), f32[16,2,8,128]{3,2,1,0:T(8,128)S(1)}, u32[]{:S(2)}, u32[]{:S(2)}) async-start(f32[16,2,8,128]{3,2,1,0:T(8,128)} %broadcast_in_dim.56), calls=%async_computation.3 | async-start | bytes 262144 | tf_op jit(solution)/shard_map/all_to_all | solution.py:19
  99.8 13.0 %all-to-all-start.3 = ((f32[8,8,128]{2,1,0:T(8,128)}), f32[8,8,128]{2,1,0:T(8,128)S(1)}, u32[]{:S(2)}, u32[]{:S(2)}) async-start(f32[8,8,128]{2,1,0:T(8,128)} %shard_map.132), calls=%async_computation.4 | async-start | bytes 65536 | tf_op jit(solution)/shard_map/all_to_all | solution.py:454
  103.1 64.9 %all-gather.4.cloned.1.call-start = ((), (), s32[]{:S(2)}) async-start(), calls=%async_computation.9 | async-start | bytes 4456448 | tf_op jit(solution)/shard_map/all_gather | solution.py:481
  106.7 17.5 %copy-start.7 = (s32[512,1]{1,0:T(8,128)S(1)}, s32[512,1]{1,0:T(8,128)}, u32[]{:S(2)}) copy-start(s32[512,1]{1,0:T(8,128)} %copy-done.6) | copy-start | bytes 6148
  106.7 17.5 %copy-start.26 = (s32[4]{0:T(128)S(1)}, s32[4]{0:T(128)}, u32[]{:S(2)}) copy-start(s32[4]{0:T(128)} %pad_add_fusion.place) | copy-start | bytes 52
  112.7 3.8 %collective-permute-start.4 = (f32[8,8,128]{2,1,0:T(8,128)S(1)}, f32[8,8,128]{2,1,0:T(8,128)S(1)}, u32[]{:S(2)}, u32[]{:S(2)}) collective-permute-start(f32[8,8,128]{2,1,0:T(8,128)S(1)} %all-to-all-done.3.known.known_mine), channel_id=1, source_target_pairs={{0,1},{1,0},{2,3},{3,2},{4,5},{5,4},{6,7},{7,6},{8,9},{9,8},{10,11... | collective-permute-start | bytes 98312 | tf_op jit(solution)/shard_map/ppermute | solution.py:23
  116.6 20.1 %copy-start.8 = (bf16[512,1024]{1,0:T(8,128)(2,1)S(1)}, bf16[512,1024]{1,0:T(8,128)(2,1)}, u32[]{:S(2)}) copy-start(bf16[512,1024]{1,0:T(8,128)(2,1)} %all-gather.6.cloned.1.call-done) | copy-start | bytes 3145732
  116.6 7.5 %collective-permute-start.5 = (bf16[8,64,1024]{2,1,0:T(8,128)(2,1)}, bf16[8,64,1024]{2,1,0:T(8,128)(2,1)S(1)}, u32[]{:S(2)}, u32[]{:S(2)}) collective-permute-start(bf16[8,64,1024]{2,1,0:T(8,128)(2,1)} %bitcast.41), channel_id=1, source_target_pairs={{0,1},{1,0},{2,3},{3,2},{4,5},{5,4},{6,7},{7,6},{8,9},{9,8},{10,11... | collective-permute-start | bytes 3145736 | tf_op jit(solution)/shard_map/ppermute | solution.py:23
  124.1 24.1 %copy-start.2 = (bf16[1,4096,256]{2,1,0:T(8,128)(2,1)S(1)}, bf16[1,4096,256]{2,1,0:T(8,128)(2,1)}, u32[]{:S(2)}) copy-start(bf16[1,4096,256]{2,1,0:T(8,128)(2,1)} %param.11) | copy-start | bytes 6291460
  126.4 21.8 %copy-start.24 = (f32[1,4096]{1,0:T(1,128)S(1)}, f32[1,4096]{1,0:T(1,128)}, u32[]{:S(2)}) copy-start(f32[1,4096]{1,0:T(1,128)} %shard_map.130.gain_part) | copy-start | bytes 49156
  129.5 15.0 %all-to-all-start.4 = ((bf16[16,32,256]{2,1,0:T(8,128)(2,1)}), bf16[16,32,256]{2,1,0:T(8,128)(2,1)}, u32[]{:S(2)}, u32[]{:S(2)}) async-start(bf16[16,32,256]{2,1,0:T(8,128)(2,1)} %copy-done.17), calls=%async_computation.5 | async-start | bytes 524288 | tf_op jit(solution)/shard_map/all_to_all | solution.py:509
  144.0 13.0 %copy-start.28 = (s32[32]{0:T(128)S(1)}, s32[32]{0:T(128)}, u32[]{:S(2)}) copy-start(s32[32]{0:T(128)} %copy-done.27) | copy-start | bytes 388
  145.5 2.6 %collective-permute-start.6 = (f32[16,256]{1,0:T(8,128)S(1)}, f32[16,256]{1,0:T(8,128)S(1)}, u32[]{:S(2)}, u32[]{:S(2)}) collective-permute-start(f32[16,256]{1,0:T(8,128)S(1)} %get-tuple-element.74), channel_id=1, source_target_pairs={{0,1},{1,0},{2,3},{3,2},{4,5},{5,4},{6,7},{7,6},{8,9},{9,8},{10,11... | collective-permute-start | bytes 49160 | tf_op jit(solution)/shard_map/ppermute | solution.py:23
  152.7 14.5 %all-to-all-start.5 = ((bf16[8,2,5888]{2,1,0:T(2,128)(2,1)}), bf16[8,2,5888]{2,1,0:T(2,128)(2,1)S(1)}, u32[]{:S(2)}, u32[]{:S(2)}) async-start(bf16[8,2,5888]{2,1,0:T(2,128)(2,1)} %shard_map.137), calls=%async_computation.6 | async-start | bytes 376832 | tf_op jit(solution)/shard_map/all_to_all | solution.py:551
  157.0 10.2 %copy-start.23 = (f32[2,4096]{1,0:T(2,128)S(1)}, f32[2,4096]{1,0:T(2,128)}, u32[]{:S(2)}) copy-start(f32[2,4096]{1,0:T(2,128)} %constant_dynamic-slice_fusion.1.unit) | copy-start | bytes 98308
  168.0 11.5 %all-to-all-start.6 = ((bf16[8,2,4864]{2,1,0:T(2,128)(2,1)}), bf16[8,2,4864]{2,1,0:T(2,128)(2,1)S(1)}, u32[]{:S(2)}, u32[]{:S(2)}) async-start(bf16[8,2,4864]{2,1,0:T(2,128)(2,1)} %shard_map.138), calls=%async_computation.7 | async-start | bytes 311296 | tf_op jit(solution)/shard_map/all_to_all | solution.py:569
  179.5 3.4 %collective-permute-start.7 = (bf16[8,2,4864]{2,1,0:T(2,128)(2,1)S(1)}, bf16[8,2,4864]{2,1,0:T(2,128)(2,1)S(1)}, u32[]{:S(2)}, u32[]{:S(2)}) collective-permute-start(bf16[8,2,4864]{2,1,0:T(2,128)(2,1)S(1)} %all-to-all-done.6.mine), channel_id=1, source_target_pairs={{0,1},{1,0},{2,3},{3,2},{4,5},{5,4},{6,7},{7,6},{8,9},{9,8},{10,11... | collective-permute-start | bytes 466952 | tf_op jit(solution)/shard_map/ppermute | solution.py:23
  (19 other events, 59.0 us)
Sparse Core Ops, SparseCore 0:
  19.7 52.2 reduce-scatter.1
  85.8 30.1 all-gather.5
  117.8 45.5 all-gather.3

commit v11 on v10

--- a/solution.py
+++ b/solution.py
@@ -10,9 +10,8 @@
 F32 = jnp.float32
 BF16 = jnp.bfloat16
 EPSILON = 1e-05
-SMALL = 20 * 1024 * 1024
 VMEM = 32 * 1024 * 1024
-LARGE = 56 * 1024 * 1024
+LARGE = 63 * 1024 * 1024
 
 
 def spread(values, axis, count):
@@ -275,24 +274,35 @@
     out[...] = jnp.broadcast_to(whole.astype(BF16)[None], out.shape)
 
 
-def fetch_kernel(source, out, done):
-    parts = done.shape[0]
-    count = out.shape[0] // parts
-    copies = [
-        pltpu.make_async_copy(source.at[pl.ds(i * count, count)], out.at[pl.ds(i * count, count)], done.at[i])
-        for i in range(parts)
-    ]
-    for copy in copies:
-        copy.start()
-    for copy in copies:
-        copy.wait()
-
-
-def last_kernel(place, ids, mine, other, main, out, gain_out, block, done):
+def last_kernel(place, ids, mine, other, main, out, gain_out, block, into, outof):
     core = place[1]
     tokens, width = block.shape
+    parts = into.shape[0]
+    count = tokens // parts
+
+    def copies(source, target, done):
+        return [
+            pltpu.make_async_copy(
+                source.at[pl.ds(i * count, count)], target.at[pl.ds(i * count, count)], done.at[i]
+            )
+            for i in range(parts)
+        ]
+
+    loads = copies(main, block, into)
+    stores = copies(block, out, outof)
+    for load in loads:
+        load.start()
     groups, share = mine.shape[:2]
+    piece = (mine.shape[2] - width) // 3
+    total = mine[:, :, width:].astype(F32) + other[:, :, width:].astype(F32)
+    total = total[:, :, :piece] + total[:, :, piece : 2 * piece] + total[:, :, 2 * piece :]
+    for i in range(groups):
+        for j in range(share):
+            at = (i * share + j) * piece
+            gain_out[:, at : at + piece] = total[i, j : j + 1]
     tile = lax.broadcasted_iota(jnp.int32, (16, width), 0)
+    for load in loads:
+        load.wait()
     for rows, first in ((mine, core), (other, 1 - core)):
         for i in range(groups):
             for j in range(share):
@@ -300,23 +310,10 @@
                 start = pl.multiple_of(at // 16 * 16, 16)
                 row = rows[i, j : j + 1, :width]
                 block[pl.ds(start, 16), :] = jnp.where(tile == at - start, row, block[pl.ds(start, 16), :])
-    parts = done.shape[0]
-    count = tokens // parts
-    copies = [
-        pltpu.make_async_copy(block.at[pl.ds(i * count, count)], out.at[pl.ds(i * count, count)], done.at[i])
-        for i in range(parts)
-    ]
-    for copy in copies:
-        copy.start()
-    piece = (mine.shape[2] - width) // 3
-    total = mine[:, :, width:].astype(F32) + other[:, :, width:].astype(F32)
-    total = total[:, :, :piece] + total[:, :, piece : 2 * piece] + total[:, :, 2 * piece :]
-    for i in range(groups):
-        for j in range(share):
-            at = (i * share + j) * piece
-            gain_out[:, at : at + piece] = total[i, j : j + 1]
-    for copy in copies:
-        copy.wait()
+    for store in stores:
+        store.start()
+    for store in stores:
+        store.wait()
 
 
 def local(
@@ -369,7 +366,7 @@
     weight_spec = pl.BlockSpec((chunk, slab), lambda i, at: (i, 0))
     grad_view = grad.reshape(zs, 2, held, width)
     joined = jnp.concatenate([weight, weight_other], axis=1)
-    chip_grad = lax.dynamic_slice(grad_view, (0, core, 0, z * 2 * slab), (zs, 1, held, 2 * slab))
+    chip_grad = lax.dynamic_slice(after(grad_view, hidden), (0, core, 0, z * 2 * slab), (zs, 1, held, 2 * slab))
     on_columns = (((1,), (1,)), ((), ()))
 
     def own_first(values):
@@ -378,8 +375,6 @@
     main_sent = lax.dot_general(
         own_first(chip_grad.reshape(zs * held, 2 * slab)), joined, on_columns, preferred_element_type=F32
     ).astype(BF16)
-    hidden, main_sent = lax.optimization_barrier((hidden, main_sent))
-    main_grad = lax.psum_scatter(main_sent, "z", scatter_dimension=0, tiled=True)
 
     halves = jnp.pad(after(head_weight, hidden), ((0, 2 * half - vocab_part), (0, 0))).reshape(2, half, slab)
     halves = jnp.pad(halves, ((0, 0), (0, padded - half), (0, 0)))
@@ -388,6 +383,8 @@
     head_other = swap(head_rest)
 
     all_mine = spread(hidden, "pipe", pipes)
+    all_mine, main_sent, head_other = lax.optimization_barrier((all_mine, main_sent, head_other))
+    main_grad = lax.psum_scatter(main_sent, "z", scatter_dimension=0, tiled=True)
     all_other = swap(all_mine)
     gain_mine = lax.dynamic_slice_in_dim(final_gain, block * slab, slab, 0)[None]
     gain_other = lax.dynamic_slice_in_dim(final_gain, (z * 2 + 1 - core) * slab, slab, 0)[None]
@@ -502,9 +499,8 @@
         all_targets,
         head_rest,
         exit_first,
-        held=(1, 5),
+        held=(5,),
         scratch=grads,
-        limit=SMALL,
     )
     exit_got = lax.all_to_all(exit_part, "pipe", 0, 0)
     kept_all = kept
@@ -522,7 +518,6 @@
         known_mine,
         known_other,
         scratch=grads,
-        limit=SMALL,
     )
     exit_got, kept, head_grad = lax.optimization_barrier((exit_got, kept, head_grad))
     row_mine, row_send, row_rounded = kernel_call(
@@ -567,26 +562,21 @@
     )
     last, main_all = lax.optimization_barrier((last, main_all))
     last = lax.all_to_all(last, "z", 0, 0)
-    main_near = pl.pallas_call(
-        fetch_kernel,
-        in_specs=[pl.BlockSpec(memory_space=pl.ANY)],
-        out_specs=pl.BlockSpec(memory_space=pltpu.VMEM),
-        out_shape=shape((tokens, width), BF16),
-        scratch_shapes=[pltpu.SemaphoreType.DMA((4,))],
-        compiler_params=pltpu.CompilerParams(vmem_limit_bytes=SMALL),
-    )(main_all)
-    last, main_near = lax.optimization_barrier((last, main_near))
     last_other = swap(last)
     in_vmem = pl.BlockSpec(memory_space=pltpu.VMEM)
-    input_grad, gain_grad, _ = pl.pallas_call(
+    parts = 4
+    input_grad, gain_grad = pl.pallas_call(
         last_kernel,
-        in_specs=[pl.BlockSpec(memory_space=pltpu.SMEM)] * 2 + [in_vmem] * 3,
-        out_specs=[pl.BlockSpec(memory_space=pl.ANY), in_vmem, in_vmem],
-        out_shape=[shape((tokens, width), BF16), shape((1, width), F32), shape((tokens, width), BF16)],
-        input_output_aliases={4: 2},
-        scratch_shapes=[pltpu.SemaphoreType.DMA((4,))],
-        compiler_params=pltpu.CompilerParams(vmem_limit_bytes=SMALL),
-    )(place, my_rows, last, last_other, main_near)
+        in_specs=[pl.BlockSpec(memory_space=pltpu.SMEM)] * 2 + [in_vmem] * 2 + [pl.BlockSpec(memory_space=pl.ANY)],
+        out_specs=[pl.BlockSpec(memory_space=pl.ANY), in_vmem],
+        out_shape=[shape((tokens, width), BF16), shape((1, width), F32)],
+        scratch_shapes=[
+            pltpu.VMEM((tokens, width), BF16),
+            pltpu.SemaphoreType.DMA((parts,)),
+            pltpu.SemaphoreType.DMA((parts,)),
+        ],
+        compiler_params=pltpu.CompilerParams(vmem_limit_bytes=LARGE),
+    )(place, my_rows, last, last_other, main_all)
     return (input_grad[None], weight_grad[None], gain_grad, head_grad)
 
 

time: 197 us -> 211 us (1.071)
  waiting for transfers between devices: 43.5 us -> 55.1 us
  local copies, waits for them, and re-layouts: 23.9 us -> 12.9 us
  starting transfers between devices: 45.6 us -> 53.7 us
  Pallas kernels: 28.8 us -> 34.9 us
    unnamed x68 -> x48, local copies, waits for them, and re-layouts: 15.5 us -> 3.44 us
    all_to_all x1 -> x2, starting transfers between devices: 4.55 us -> 12.5 us  [spread(): lax.all_to_all(jnp.broadcast_to(values[None], (count,) + values.shape), a...]
    all_to_all x1, waiting for transfers between devices: 27.4 us -> 31.8 us  [local(): parts = lax.all_to_all(part, 'z', 0, 0)]
    all_to_all x1 -> x0, waiting for transfers between devices: 3.58 us -> none  [local(): last = lax.all_to_all(last, 'z', 0, 0)]
    all_to_all x1 -> x0, starting transfers between devices: 3.38 us -> none  [local(): last = lax.all_to_all(last, 'z', 0, 0)]
    all_to_all x1 -> x2, waiting for transfers between devices: 5.55 us -> 8.7 us  [spread(): lax.all_to_all(jnp.broadcast_to(values[None], (count,) + values.shape), a...]
    pallas_call x3, Pallas kernels: 8.11 us -> 11.1 us  [piped_call(): pl.pallas_call(body, grid=(1,), out_shape=out, in_specs=[pl.BlockSpec(mem...]
    pallas_call x1, Pallas kernels: 4.18 us -> 6.85 us  [local(): pl.pallas_call(last_kernel, in_specs=[pl.BlockSpec(memory_space=pltpu.SME...]
  transfers between devices with their start and end apart: 17 -> 17, of which waited for: 8 -> 11; matrix products, arithmetic and copies ran while one was open for 16% -> 17% of each run, Pallas kernels for 13% -> 13%
where the time goes in v11:
time: 211 us; the launch traced here: 210 us
  waiting for transfers between devices  55.1 us (26%)
  starting transfers between devices  53.7 us (25%)
  Pallas kernels  34.9 us (17%)
  matrix products  14.1 us (7%)
  between operations  14.1 us (7%)
  local copies, waits for them, and re-layouts  12.9 us (6%)
  blocking collectives  12.7 us (6%)
  other arithmetic  12.2 us (6%)
    all_to_all x1, waiting for transfers between devices, local(): parts = lax.all_to_all(part, 'z', 0, 0)  31.8 us
    ppermute x8, starting transfers between devices, swap(): return lax.ppermute(values, 'core', [(0, 1), (1, 0)])  16.8 us
    all_to_all x1, blocking collectives, local(): last = lax.all_to_all(last, 'z', 0, 0)  12.7 us
    all_to_all x2, starting transfers between devices, spread(): lax.all_to_all(jnp.broadcast_to(values[None], (count,) + values.shape), a...  12.5 us
    pallas_call x3, Pallas kernels, piped_call(): pl.pallas_call(body, grid=(1,), out_shape=out, in_specs=[pl.BlockSpec(mem...  11.1 us
    all_to_all x2, waiting for transfers between devices, spread(): lax.all_to_all(jnp.broadcast_to(values[None], (count,) + values.shape), a...  8.7 us
    all_to_all x1, starting transfers between devices, local(): parts = lax.all_to_all(part, 'z', 0, 0)  8.19 us
    pallas_call x1, Pallas kernels, local(): pl.pallas_call(last_kernel, in_specs=[pl.BlockSpec(memory_space=pltpu.SME...  6.85 us
  transfers between devices with their start and end apart: 17, of which 11 were waited for; matrix products, arithmetic and copies ran while one was open for 17% of the time, Pallas kernels for 13%

profile of v11, /device:TPU:1, one launch (start us, length us, event | category | flops | bytes accessed | tf_op | source)
XLA Modules:
  0.0 209.7 jit_solution(18286575175993952295)
XLA Ops:
  7.2 3.3 %collective-permute-start = (bf16[4096,256]{1,0:T(8,128)(2,1)}, bf16[4096,256]{1,0:T(8,128)(2,1)}, u32[]{:S(2)}, u32[]{:S(2)}) collective-permute-start(bf16[4096,256]{1,0:T(8,128)(2,1)} %bitcast.37), channel_id=1, source_target_pairs={{0,1},{1,0},{2,3},{3,2},{4,5},{5,4},{6,7},{7,6},{8,9},{9,8},{10,11... | collective-permute-start | bytes 6291464 | tf_op jit(solution)/shard_map/ppermute | solution.py:22
  10.5 3.1 %multiply_reduce_fusion = (f32[32]{0:T(128)S(1)}, f32[32,4096]{1,0:T(8,128)S(1)}) fusion(bf16[1,512,4096]{2,1,0:T(8,128)(2,1)} %param.10, s32[32]{0:T(128)S(1)} %fusion.43.ids), kind=kOutput, calls=%fused_computation.31 | convolution fusion | flops 134496224 | bytes 4718848 | tf_op jit(solution)/shard_map/dot_general | solution.py:354
  15.1 2.2 %pad.12 = bf16[2016,256]{1,0:T(8,128)(2,1)} pad(bf16[2000,256]{1,0:T(8,128)(2,1)} %param.14, bf16[]{:T(256)} %constant.64.clone.1), padding=0_16x0_0 | pad | bytes 2056194 | tf_op jit(solution)/shard_map/jit(_pad)/pad | solution.py:379
  17.4 2.1 fusion.18
  20.7 5.0 %all-to-all-start = ((bf16[16,32,256]{2,1,0:T(8,128)(2,1)}), bf16[16,32,256]{2,1,0:T(8,128)(2,1)S(1)}, u32[]{:S(2)}, u32[]{:S(2)}) async-start(bf16[16,32,256]{2,1,0:T(8,128)(2,1)} %broadcast_in_dim.29), calls=%async_computation | async-start | bytes 524288 | tf_op jit(solution)/shard_map/all_to_all | solution.py:18
  26.8 4.2 %convolution_convert_fusion.1 = bf16[256,4096]{1,0:T(8,128)(2,1)} fusion(bf16[4096,256]{1,0:T(8,128)(2,1)} %collective-permute-done.weight_other, bf16[4096,256]{1,0:T(8,128)(2,1)S(1)} %bitcast.39, bf16[256,512]{1,0:T(8,128)(2,1)S(1)} %bitcast.67, bf16[256,256]{1,0:T(8,128)(2,1)S(1)} %get-tuple-element.95, bf16[256,256]{1,0:T(8,128)(2,1)S(1)} %get-tuple-element.94, ...), kind=kOutput, calls=%fused_computation.6 | convolution fusion | flops 1083834368 | bytes 6815745 | tf_op jit(solution)/shard_map/dot_general | solution.py:375
  31.1 3.2 %all-to-all-done.mine.row = bf16[16,32,256]{2,1,0:T(8,128)(2,1)S(1)} async-done(((bf16[16,32,256]{2,1,0:T(8,128)(2,1)}), bf16[16,32,256]{2,1,0:T(8,128)(2,1)S(1)}, u32[]{:S(2)}, u32[]{:S(2)}) %all-to-all-start) | async-done | bytes 262176 | tf_op jit(solution)/shard_map/all_to_all | solution.py:18
  36.7 2.8 %shard_map.129 = bf16[8,64,1024]{2,1,0:T(8,128)(2,1)} custom-call(bf16[16,32,256]{2,1,0:T(8,128)(2,1)S(1)} %all-to-all-done.mine.row, bf16[16,32,256]{2,1,0:T(8,128)(2,1)S(1)} %collective-permute-done.2.other, f32[1,256]{1,0:T(1,128)S(1)} %bitcast.46, f32[1,256]{1,0:T(1,128)S(1)} %bitcast.50, bf16[1024,256]{1,0:T(8,128)(2,1)S(1)} %get-tuple-element.92.head_mine.head, ...), custom_call_target="tpu_custom_call" | custom-call | tf_op jit(solution)/shard_map/pallas_call | solution.py:38
  39.4 8.2 %all-to-all-start.1 = ((bf16[8,64,1024]{2,1,0:T(8,128)(2,1)}), bf16[8,64,1024]{2,1,0:T(8,128)(2,1)}, u32[]{:S(2)}, u32[]{:S(2)}) async-start(bf16[8,64,1024]{2,1,0:T(8,128)(2,1)} %shard_map.129), calls=%async_computation.1 | async-start | bytes 2097152 | tf_op jit(solution)/shard_map/all_to_all | solution.py:402
  49.4 6.8 %shard_map.130.gain_part = f32[1,4096]{1,0:T(1,128)} custom-call(s32[4]{0:T(128)} %pad_add_fusion.place, bf16[8,2,32,4096]{3,2,1,0:T(8,128)(2,1)} %bitcast.58, bf16[8,2,32,4096]{3,2,1,0:T(8,128)(2,1)} %bitcast.51, s32[1,32]{1,0:T(1,128)} %constant_dynamic-slice_fusion.5.ids, bf16[4096,256]{1,0:T(8,128)(2,1)} %bitcast.38, ...), custom_call_target="tpu_custom_call" | custom-call | tf_op jit(solution)/shard_map/pallas_call | solution.py:404
  56.3 31.8 %all-to-all-done.1.parts = bf16[8,64,1024]{2,1,0:T(8,128)(2,1)} async-done(((bf16[8,64,1024]{2,1,0:T(8,128)(2,1)}), bf16[8,64,1024]{2,1,0:T(8,128)(2,1)}, u32[]{:S(2)}, u32[]{:S(2)}) %all-to-all-start.1) | async-done | bytes 1048608 | tf_op jit(solution)/shard_map/all_to_all | solution.py:402
  88.1 2.2 %shard_map.131 = (bf16[64,1024]{1,0:T(8,128)(2,1)}, f32[8,128]{1,0:T(8,128)S(1)}) custom-call(s32[4]{0:T(128)S(1)} %copy-done.7, bf16[8,64,1024]{2,1,0:T(8,128)(2,1)} %all-to-all-done.1.parts, s32[64,1]{1,0:T(8,128)S(1)} %dynamic-slice_subtract_fusion.targets), custom_call_target="tpu_custom_call" | custom-call | tf_op jit(solution)/shard_map/pallas_call | solution.py:26
  90.4 1.9 reduce-scatter.2.cloned.1.call-done
  96.3 7.4 %all-to-all-start.2 = ((f32[16,2,8,128]{3,2,1,0:T(8,128)}), f32[16,2,8,128]{3,2,1,0:T(8,128)S(1)}, u32[]{:S(2)}, u32[]{:S(2)}) async-start(f32[16,2,8,128]{3,2,1,0:T(8,128)} %broadcast_in_dim.56), calls=%async_computation.3 | async-start | bytes 262144 | tf_op jit(solution)/shard_map/all_to_all | solution.py:18
  105.1 5.6 %all-to-all-done.2 = f32[16,2,8,128]{3,2,1,0:T(8,128)S(1)} async-done(((f32[16,2,8,128]{3,2,1,0:T(8,128)}), f32[16,2,8,128]{3,2,1,0:T(8,128)S(1)}, u32[]{:S(2)}, u32[]{:S(2)}) %all-to-all-start.2) | async-done | bytes 131104 | tf_op jit(solution)/shard_map/all_to_all | solution.py:18
  111.3 5.7 %all-to-all-start.3 = ((f32[8,8,128]{2,1,0:T(8,128)}), f32[8,8,128]{2,1,0:T(8,128)S(1)}, u32[]{:S(2)}, u32[]{:S(2)}) async-start(f32[8,8,128]{2,1,0:T(8,128)} %shard_map.132), calls=%async_computation.4 | async-start | bytes 65536 | tf_op jit(solution)/shard_map/all_to_all | solution.py:451
  117.1 3.3 %fusion = f32[512]{0:T(512)S(1)} fusion(bf16[512,4096]{1,0:T(8,128)(2,1)} %bitcast.54), kind=kLoop, calls=%fused_computation.2 | loop fusion | flops 6290944 | bytes 4196352 | tf_op jit(solution)/shard_map/reduce_sum | solution.py:463
  120.6 3.6 %fusion.2 = bf16[512,4096]{1,0:T(8,128)(2,1)} fusion(bf16[512,4096]{1,0:T(8,128)(2,1)S(1)} %bitcast.56, f32[4096]{0:T(1024)S(1)} %bitcast.44, f32[512]{0:T(512)S(1)} %add_rsqrt_fusion), kind=kLoop, calls=%fused_computation.4 | loop fusion | flops 8388608 | bytes 8407040 | tf_op jit(solution)/shard_map/convert_element_type | solution.py:464
  125.4 2.2 %collective-permute-start.4 = (f32[8,8,128]{2,1,0:T(8,128)S(1)}, f32[8,8,128]{2,1,0:T(8,128)S(1)}, u32[]{:S(2)}, u32[]{:S(2)}) collective-permute-start(f32[8,8,128]{2,1,0:T(8,128)S(1)} %all-to-all-done.3.known.known_mine), channel_id=1, source_target_pairs={{0,1},{1,0},{2,3},{3,2},{4,5},{5,4},{6,7},{7,6},{8,9},{9,8},{10,11... | collective-permute-start | bytes 98312 | tf_op jit(solution)/shard_map/ppermute | solution.py:22
  127.6 1.9 fusion.15
  130.7 5.0 %collective-permute-start.5 = (bf16[8,64,1024]{2,1,0:T(8,128)(2,1)}, bf16[8,64,1024]{2,1,0:T(8,128)(2,1)}, u32[]{:S(2)}, u32[]{:S(2)}) collective-permute-start(bf16[8,64,1024]{2,1,0:T(8,128)(2,1)} %bitcast.62), channel_id=1, source_target_pairs={{0,1},{1,0},{2,3},{3,2},{4,5},{5,4},{6,7},{7,6},{8,9},{9,8},{10,11... | collective-permute-start | bytes 3145736 | tf_op jit(solution)/shard_map/ppermute | solution.py:22
  135.7 3.2 %shard_map.133 = (f32[512,256]{1,0:T(8,128)}, f32[512,128]{1,0:T(8,128)}) custom-call(s32[4]{0:T(128)} %pad_add_fusion.place, bf16[8,64,1024]{2,1,0:T(8,128)(2,1)} %bitcast.63, f32[8,8,128]{2,1,0:T(8,128)} %copy-done.17, s32[512,1]{1,0:T(8,128)} %copy-done.12, bf16[1024,256]{1,0:T(8,128)(2,1)} %copy-done.3), custom_call_target="tpu_custom_call" | custom-call | tf_op jit(solution)/shard_map/pallas_call | solution.py:51
  138.9 3.2 %shard_map.134 = bf16[16,32,256]{2,1,0:T(8,128)(2,1)} custom-call(s32[4]{0:T(128)} %pad_add_fusion.place, bf16[8,64,1024]{2,1,0:T(8,128)(2,1)} %collective-permute-done.5.expo.ex_other, f32[8,8,128]{2,1,0:T(8,128)} %copy-done.19, s32[512,1]{1,0:T(8,128)} %copy-done.12, bf16[1024,256]{1,0:T(8,128)(2,1)} %get-tuple-element.93.head, ...), custom_call_target="tpu_custom_call" | custom-call | tf_op jit(solution)/shard_map/pallas_call | solution.py:51
  142.1 6.6 %all-to-all-start.4 = ((bf16[16,32,256]{2,1,0:T(8,128)(2,1)}), bf16[16,32,256]{2,1,0:T(8,128)(2,1)S(1)}, u32[]{:S(2)}, u32[]{:S(2)}) async-start(bf16[16,32,256]{2,1,0:T(8,128)(2,1)} %shard_map.134), calls=%async_computation.5 | async-start | bytes 524288 | tf_op jit(solution)/shard_map/all_to_all | solution.py:505
  149.4 4.7 %shard_map.135 = bf16[2000,256]{1,0:T(8,128)(2,1)} custom-call(s32[4]{0:T(128)} %pad_add_fusion.place, bf16[16,32,256]{2,1,0:T(8,128)(2,1)} %copy-done.4, f32[1,256]{1,0:T(1,128)} %bitcast.47, f32[512,128]{1,0:T(8,128)} %get-tuple-element.71.kept, s32[512,1]{1,0:T(8,128)} %copy-done.12, bf16[8,64,1024]{2,1,0:T(8,128)(2,1)} %bitcast.64, ...), custom_call_target="tpu_custom_call" | custom-call | tf_op jit(solution)/shard_map/pallas_call | solution.py:51
  154.1 3.1 %all-to-all-done.4.got = bf16[16,32,256]{2,1,0:T(8,128)(2,1)S(1)} async-done(((bf16[16,32,256]{2,1,0:T(8,128)(2,1)}), bf16[16,32,256]{2,1,0:T(8,128)(2,1)S(1)}, u32[]{:S(2)}, u32[]{:S(2)}) %all-to-all-start.4) | async-done | bytes 262176 | tf_op jit(solution)/shard_map/all_to_all | solution.py:505
  161.5 3.6 %shard_map.137 = bf16[8,2,5888]{2,1,0:T(2,128)(2,1)} custom-call(s32[4]{0:T(128)S(1)} %copy-done.8, f32[16,256]{1,0:T(8,128)S(1)} %get-tuple-element.75.mine, f32[16,256]{1,0:T(8,128)S(1)} %collective-permute-done.6.other, bf16[4096,256]{1,0:T(8,128)(2,1)S(1)} %bitcast.40, bf16[4096,256]{1,0:T(8,128)(2,1)} %collective-permute-done.weight_other, ...), custom_call_target="tpu_custom_call" | custom-call | tf_op jit(solution)/shard_map/pallas_call | solution.py:26
  165.1 3.9 %all-to-all-start.5 = ((bf16[8,2,5888]{2,1,0:T(2,128)(2,1)}), bf16[8,2,5888]{2,1,0:T(2,128)(2,1)S(1)}, u32[]{:S(2)}, u32[]{:S(2)}) async-start(bf16[8,2,5888]{2,1,0:T(2,128)(2,1)} %shard_map.137), calls=%async_computation.6 | async-start | bytes 376832 | tf_op jit(solution)/shard_map/all_to_all | solution.py:546
  169.0 5.2 %convolution_convert_fusion = bf16[4096,256]{1,0:T(8,128)(2,1)} fusion(bf16[512,4096]{1,0:T(8,128)(2,1)} %fusion.2, bf16[32,256]{1,0:T(8,128)(2,1)S(1)} %get-tuple-element.81, pred[512]{0:T(512)(128)(4,1)S(1)} %compare_reduce_fusion, bf16[512,4096]{1,0:T(8,128)(2,1)} %bitcast.61, s32[]{:T(128)S(6)} %select_n.73, s32[32]{0:T(128)S(1)} %fusion.43.ids), kind=kOutput, calls=%fused_computation.5 | convolution fusion | flops 1083457536 | bytes 6570628 | tf_op jit(solution)/shard_map/dot_general | solution.py:553
  174.1 5.7 %all-to-all-done.5.got = bf16[8,2,5888]{2,1,0:T(2,128)(2,1)S(1)} async-done(((bf16[8,2,5888]{2,1,0:T(2,128)(2,1)}), bf16[8,2,5888]{2,1,0:T(2,128)(2,1)S(1)}, u32[]{:S(2)}, u32[]{:S(2)}) %all-to-all-start.5) | async-done | bytes 188448 | tf_op jit(solution)/shard_map/all_to_all | solution.py:546
  180.1 12.7 %all_to_all.35.mine = bf16[8,2,4864]{2,1,0:T(2,128)(2,1)S(1)} all-to-all(bf16[8,2,4864]{2,1,0:T(2,128)(2,1)S(1)} %shard_map.138), channel_id=1, replica_groups=mesh['pipe'=16,'z'=8,'core'=2] {'z'}, dimensions={0} | all-to-all | bytes 311296 | tf_op jit(solution)/shard_map/all_to_all | solution.py:564
  196.3 6.8 %shard_map.139 = (bf16[512,4096]{1,0:T(8,128)(2,1)}, f32[1,4096]{1,0:T(1,128)}) custom-call(s32[4]{0:T(128)} %pad_add_fusion.place, s32[32]{0:T(128)} %copy-done.21, bf16[8,2,4864]{2,1,0:T(2,128)(2,1)} %copy-done.16, bf16[8,2,4864]{2,1,0:T(2,128)(2,1)} %copy-done.18, bf16[512,4096]{1,0:T(8,128)(2,1)} %all-gather.4.cloned.1.call-done.main), custom_call_target="tpu_custom_call" | custom-call | tf_op jit(solution)/shard_map/pallas_call | solution.py:568
  (103 shorter events, 25.3 us)
Async XLA Ops:
  7.2 7.5 %copy-start.1 = (bf16[1,4096,256]{2,1,0:T(8,128)(2,1)S(1)}, bf16[1,4096,256]{2,1,0:T(8,128)(2,1)}, u32[]{:S(2)}) copy-start(bf16[1,4096,256]{2,1,0:T(8,128)(2,1)} %param.11) | copy-start | bytes 6291460
  7.2 19.6 %collective-permute-start = (bf16[4096,256]{1,0:T(8,128)(2,1)}, bf16[4096,256]{1,0:T(8,128)(2,1)}, u32[]{:S(2)}, u32[]{:S(2)}) collective-permute-start(bf16[4096,256]{1,0:T(8,128)(2,1)} %bitcast.37), channel_id=1, source_target_pairs={{0,1},{1,0},{2,3},{3,2},{4,5},{5,4},{6,7},{7,6},{8,9},{9,8},{10,11... | collective-permute-start | bytes 6291464 | tf_op jit(solution)/shard_map/ppermute | solution.py:22
  10.5 158.4 %copy-start.21 = (s32[32]{0:T(128)}, s32[32]{0:T(128)S(1)}, u32[]{:S(2)}) copy-start(s32[32]{0:T(128)S(1)} %fusion.43.ids) | copy-start | bytes 388
  19.4 17.3 %copy-start.3 = (bf16[1024,256]{1,0:T(8,128)(2,1)}, bf16[1024,256]{1,0:T(8,128)(2,1)S(1)}, u32[]{:S(2)}) copy-start(bf16[1024,256]{1,0:T(8,128)(2,1)S(1)} %get-tuple-element.92.head_mine.head) | copy-start | bytes 1572868
  19.4 14.8 %collective-permute-start.1 = (bf16[1024,256]{1,0:T(8,128)(2,1)}, bf16[1024,256]{1,0:T(8,128)(2,1)}, u32[]{:S(2)}, u32[]{:S(2)}) collective-permute-start(bf16[1024,256]{1,0:T(8,128)(2,1)} %get-tuple-element.93.head), channel_id=1, source_target_pairs={{0,1},{1,0},{2,3},{3,2},{4,5},{5,4},{6,7},{7,6},{8,9},{9,8},{10,11... | collective-permute-start | bytes 1572872 | tf_op jit(solution)/shard_map/ppermute | solution.py:22
  20.7 13.5 %all-to-all-start = ((bf16[16,32,256]{2,1,0:T(8,128)(2,1)}), bf16[16,32,256]{2,1,0:T(8,128)(2,1)S(1)}, u32[]{:S(2)}, u32[]{:S(2)}) async-start(bf16[16,32,256]{2,1,0:T(8,128)(2,1)} %broadcast_in_dim.29), calls=%async_computation | async-start | bytes 524288 | tf_op jit(solution)/shard_map/all_to_all | solution.py:18
  25.8 66.5 %reduce-scatter.2.cloned.1.call-start = ((), (), s32[]{:S(2)}) async-start(), calls=%async_computation.8 | async-start | bytes 2359296 | tf_op jit(solution)/shard_map/reduce_scatter | solution.py:387
  31.1 16.6 %copy-start.20 = (s32[16,32]{1,0:T(8,128)S(1)}, s32[16,32]{1,0:T(8,128)}, u32[]{:S(2)}) copy-start(s32[16,32]{1,0:T(8,128)} %param.17) | copy-start | bytes 6148
  31.1 16.9 %copy-start.22 = (f32[16]{0:T(128)S(1)}, f32[16]{0:T(128)}, u32[]{:S(2)}) copy-start(f32[16]{0:T(128)} %param.18) | copy-start | bytes 196
  31.1 16.9 %copy-start.23 = (s32[16]{0:T(128)S(1)}, s32[16]{0:T(128)}, u32[]{:S(2)}) copy-start(s32[16]{0:T(128)} %param.16) | copy-start | bytes 196
  34.2 22.0 %copy-start.4 = (bf16[16,32,256]{2,1,0:T(8,128)(2,1)}, bf16[16,32,256]{2,1,0:T(8,128)(2,1)S(1)}, u32[]{:S(2)}) copy-start(bf16[16,32,256]{2,1,0:T(8,128)(2,1)S(1)} %all-to-all-done.mine.row) | copy-start | bytes 786436
  34.2 2.4 %collective-permute-start.2 = (bf16[16,32,256]{2,1,0:T(8,128)(2,1)S(1)}, bf16[16,32,256]{2,1,0:T(8,128)(2,1)S(1)}, u32[]{:S(2)}, u32[]{:S(2)}) collective-permute-start(bf16[16,32,256]{2,1,0:T(8,128)(2,1)S(1)} %all-to-all-done.mine.row), channel_id=1, source_target_pairs={{0,1},{1,0},{2,3},{3,2},{4,5},{5,4},{6,7},{7,6},{8,9},{9,8},{10,11... | collective-permute-start | bytes 786440 | tf_op jit(solution)/shard_map/ppermute | solution.py:22
  36.3 19.9 %copy-start.9 = (f32[256]{0:T(256)}, f32[256]{0:T(256)S(1)}, u32[]{:S(2)}) copy-start(f32[256]{0:T(256)S(1)} %get-tuple-element.97) | copy-start | bytes 3076
  39.4 48.7 %all-to-all-start.1 = ((bf16[8,64,1024]{2,1,0:T(8,128)(2,1)}), bf16[8,64,1024]{2,1,0:T(8,128)(2,1)}, u32[]{:S(2)}, u32[]{:S(2)}) async-start(bf16[8,64,1024]{2,1,0:T(8,128)(2,1)} %shard_map.129), calls=%async_computation.1 | async-start | bytes 2097152 | tf_op jit(solution)/shard_map/all_to_all | solution.py:402
  47.6 83.0 %all-gather.6.cloned.1.call-start = ((), (), s32[]{:S(2)}) async-start(), calls=%async_computation.10 | async-start | bytes 1179648 | tf_op jit(solution)/shard_map/all_gather | solution.py:444
  48.0 8.3 %copy-start.12 = (s32[512,1]{1,0:T(8,128)}, s32[512,1]{1,0:T(8,128)S(1)}, u32[]{:S(2)}) copy-start(s32[512,1]{1,0:T(8,128)S(1)} %reshape.114.targets) | copy-start | bytes 6148
  49.4 38.7 %copy-start.7 = (s32[4]{0:T(128)S(1)}, s32[4]{0:T(128)}, u32[]{:S(2)}) copy-start(s32[4]{0:T(128)} %pad_add_fusion.place) | copy-start | bytes 52
  92.2 2.3 %collective-permute-start.3 = (f32[8,128]{1,0:T(8,128)S(1)}, f32[8,128]{1,0:T(8,128)S(1)}, u32[]{:S(2)}, u32[]{:S(2)}) collective-permute-start(f32[8,128]{1,0:T(8,128)S(1)} %get-tuple-element.58.own), channel_id=1, source_target_pairs={{0,1},{1,0},{2,3},{3,2},{4,5},{5,4},{6,7},{7,6},{8,9},{9,8},{10,11... | collective-permute-start | bytes 12296 | tf_op jit(solution)/shard_map/ppermute | solution.py:22
  96.3 14.3 %all-to-all-start.2 = ((f32[16,2,8,128]{3,2,1,0:T(8,128)}), f32[16,2,8,128]{3,2,1,0:T(8,128)S(1)}, u32[]{:S(2)}, u32[]{:S(2)}) async-start(f32[16,2,8,128]{3,2,1,0:T(8,128)} %broadcast_in_dim.56), calls=%async_computation.3 | async-start | bytes 262144 | tf_op jit(solution)/shard_map/all_to_all | solution.py:18
  111.3 14.1 %all-to-all-start.3 = ((f32[8,8,128]{2,1,0:T(8,128)}), f32[8,8,128]{2,1,0:T(8,128)S(1)}, u32[]{:S(2)}, u32[]{:S(2)}) async-start(f32[8,8,128]{2,1,0:T(8,128)} %shard_map.132), calls=%async_computation.4 | async-start | bytes 65536 | tf_op jit(solution)/shard_map/all_to_all | solution.py:451
  117.0 63.0 %all-gather.4.cloned.1.call-start = ((), (), s32[]{:S(2)}) async-start(), calls=%async_computation.9 | async-start | bytes 4456448 | tf_op jit(solution)/shard_map/all_gather | solution.py:478
  125.4 10.2 %copy-start.17 = (f32[8,8,128]{2,1,0:T(8,128)}, f32[8,8,128]{2,1,0:T(8,128)S(1)}, u32[]{:S(2)}) copy-start(f32[8,8,128]{2,1,0:T(8,128)S(1)} %all-to-all-done.3.known.known_mine) | copy-start | bytes 98308
  125.4 4.1 %collective-permute-start.4 = (f32[8,8,128]{2,1,0:T(8,128)S(1)}, f32[8,8,128]{2,1,0:T(8,128)S(1)}, u32[]{:S(2)}, u32[]{:S(2)}) collective-permute-start(f32[8,8,128]{2,1,0:T(8,128)S(1)} %all-to-all-done.3.known.known_mine), channel_id=1, source_target_pairs={{0,1},{1,0},{2,3},{3,2},{4,5},{5,4},{6,7},{7,6},{8,9},{9,8},{10,11... | collective-permute-start | bytes 98312 | tf_op jit(solution)/shard_map/ppermute | solution.py:22
  129.5 9.4 %copy-start.19 = (f32[8,8,128]{2,1,0:T(8,128)}, f32[8,8,128]{2,1,0:T(8,128)S(1)}, u32[]{:S(2)}) copy-start(f32[8,8,128]{2,1,0:T(8,128)S(1)} %collective-permute-done.4.known.known_other) | copy-start | bytes 98308
  130.7 26.5 %copy-start.8 = (s32[4]{0:T(128)S(1)}, s32[4]{0:T(128)}, u32[]{:S(2)}) copy-start(s32[4]{0:T(128)} %pad_add_fusion.place) | copy-start | bytes 52
  130.7 26.5 %copy-start.10 = (f32[256]{0:T(256)S(1)}, f32[256]{0:T(256)}, u32[]{:S(2)}) copy-start(f32[256]{0:T(256)} %copy-done.9) | copy-start | bytes 3076
  130.7 8.2 %collective-permute-start.5 = (bf16[8,64,1024]{2,1,0:T(8,128)(2,1)}, bf16[8,64,1024]{2,1,0:T(8,128)(2,1)}, u32[]{:S(2)}, u32[]{:S(2)}) collective-permute-start(bf16[8,64,1024]{2,1,0:T(8,128)(2,1)} %bitcast.62), channel_id=1, source_target_pairs={{0,1},{1,0},{2,3},{3,2},{4,5},{5,4},{6,7},{7,6},{8,9},{9,8},{10,11... | collective-permute-start | bytes 3145736 | tf_op jit(solution)/shard_map/ppermute | solution.py:22
  138.9 21.0 %copy-start.6 = (f32[1,4096]{1,0:T(1,128)S(1)}, f32[1,4096]{1,0:T(1,128)}, u32[]{:S(2)}) copy-start(f32[1,4096]{1,0:T(1,128)} %shard_map.130.gain_part) | copy-start | bytes 49156
  142.1 15.1 %all-to-all-start.4 = ((bf16[16,32,256]{2,1,0:T(8,128)(2,1)}), bf16[16,32,256]{2,1,0:T(8,128)(2,1)S(1)}, u32[]{:S(2)}, u32[]{:S(2)}) async-start(bf16[16,32,256]{2,1,0:T(8,128)(2,1)} %shard_map.134), calls=%async_computation.5 | async-start | bytes 524288 | tf_op jit(solution)/shard_map/all_to_all | solution.py:505
  157.8 2.1 collective-permute-start.6
  165.1 14.8 %all-to-all-start.5 = ((bf16[8,2,5888]{2,1,0:T(2,128)(2,1)}), bf16[8,2,5888]{2,1,0:T(2,128)(2,1)S(1)}, u32[]{:S(2)}, u32[]{:S(2)}) async-start(bf16[8,2,5888]{2,1,0:T(2,128)(2,1)} %shard_map.137), calls=%async_computation.6 | async-start | bytes 376832 | tf_op jit(solution)/shard_map/all_to_all | solution.py:546
  192.8 2.9 %collective-permute-start.7 = (bf16[8,2,4864]{2,1,0:T(2,128)(2,1)S(1)}, bf16[8,2,4864]{2,1,0:T(2,128)(2,1)S(1)}, u32[]{:S(2)}, u32[]{:S(2)}) collective-permute-start(bf16[8,2,4864]{2,1,0:T(2,128)(2,1)S(1)} %all_to_all.35.mine), channel_id=1, source_target_pairs={{0,1},{1,0},{2,3},{3,2},{4,5},{5,4},{6,7},{7,6},{8,9},{9,8},{10,11... | collective-permute-start | bytes 466952 | tf_op jit(solution)/shard_map/ppermute | solution.py:22
  (9 other events, 31.0 us)
Sparse Core Ops, SparseCore 0:
  34.4 57.8 reduce-scatter.1
  94.0 36.5 all-gather.5
  132.5 46.8 all-gather.3

commit v12 on v9

--- a/solution.py
+++ b/solution.py
@@ -13,6 +13,7 @@
 SMALL = 20 * 1024 * 1024
 VMEM = 32 * 1024 * 1024
 LARGE = 56 * 1024 * 1024
+LARGEST = 63 * 1024 * 1024
 
 
 def spread(values, axis, count):
@@ -43,7 +44,7 @@
     )(*operands)
 
 
-def piped_call(body, out, *operands, held=(), kept=(), scratch=(), limit=LARGE):
+def piped_call(body, out, *operands, held=(), kept=(), scratch=(), limit=LARGEST):
     def spec(value, stays):
         if stays:
             return pl.BlockSpec(memory_space=pltpu.VMEM)
@@ -225,9 +226,11 @@
     other[...] = jnp.where(core == 0, rows[half:], rows[:half])
 
 
-def send_kernel(place, part, mine, other, unit, gain_part, out):
+def send_kernel(place, mine, other, weight, weight_other, unit, gain_part, out):
     core = place[1]
-    part = part[...]
+    columns = (((1,), (1,)), ((), ()))
+    part = lax.dot_general(mine[...].astype(BF16), weight[...], columns, preferred_element_type=F32)
+    part += lax.dot_general(other[...].astype(BF16), weight_other[...], columns, preferred_element_type=F32)
     gain = gain_part[...] + jnp.sum(part * unit[...], axis=0, keepdims=True)
     low = jnp.where(core == 0, mine[...], other[...])
     high = jnp.where(core == 0, other[...], mine[...])
@@ -237,7 +240,7 @@
     part = part.astype(BF16)
     gains = [values.astype(BF16) for values in pieces3(gain)]
     count, share, _ = out.shape
-    width, slab = part.shape[1], mine.shape[1]
+    width, slab = weight.shape
     piece = width // (count * share)
     for i in range(count):
         at = slice(i * share, (i + 1) * share)
@@ -500,7 +503,7 @@
         all_targets,
         head_rest,
         exit_first,
-        held=(1, 5),
+        held=(5,),
         scratch=grads,
     )
     exit_got = lax.all_to_all(exit_part, "pipe", 0, 0)
@@ -519,17 +522,14 @@
     )
 
     piece = slab * 2 // share
-    row_other = swap(row_send)
-    row_part = lax.dot_general(
-        jnp.concatenate([row_mine, row_other], axis=1).astype(BF16), joined, on_columns, preferred_element_type=F32
-    )
     send = kernel_call(
         send_kernel,
         shape((zs, share, width + 4 * slab + 3 * piece), BF16),
         place,
-        row_part,
         row_mine,
-        row_other,
+        swap(row_send),
+        weight,
+        weight_other,
         core_unit,
         gain_part,
     )

time: 196 us -> 195 us (level)
  matrix products: 17.1 us -> 14.1 us
  Pallas kernels: 29.3 us -> 31.4 us
    dot_general x1 -> x0, matrix products: 2.82 us -> none  [local(): lax.dot_general(jnp.concatenate([row_mine, row_other], axis=1).astype(BF1...]
    pallas_call x3, Pallas kernels: 3.59 us -> 5.73 us  [kernel_call(): pl.pallas_call(body, out_shape=out, in_specs=[pl.BlockSpec(memory_space=p...]
    unnamed x48 -> x46, local copies, waits for them, and re-layouts: 7.76 us -> 8.33 us
  transfers between devices with their start and end apart: 17 -> 17, of which waited for: 9 -> 9; matrix products, arithmetic and copies ran while one was open for 16% -> 14% of each run, Pallas kernels for 13% -> 14%
where the time goes in v12:
time: 195 us; the launch traced here: 194 us
  waiting for transfers between devices  49.1 us (25%)
  starting transfers between devices  46 us (24%)
  Pallas kernels  31.4 us (16%)
  local copies, waits for them, and re-layouts  14.2 us (7%)
  matrix products  14.1 us (7%)
  between operations  14.1 us (7%)
  blocking collectives  13 us (7%)
  other arithmetic  12.2 us (6%)
    all_to_all x1, waiting for transfers between devices, local(): parts = lax.all_to_all(part, 'z', 0, 0)  27.4 us
    ppermute x8, starting transfers between devices, swap(): return lax.ppermute(values, 'core', [(0, 1), (1, 0)])  15.4 us
    all_to_all x1, blocking collectives, spread(): lax.all_to_all(jnp.broadcast_to(values[None], (count,) + values.shape), a...  13 us
    pallas_call x3, Pallas kernels, piped_call(): pl.pallas_call(body, grid=(1,), out_shape=out, in_specs=[pl.BlockSpec(mem...  11.1 us
    unnamed x46, local copies, waits for them, and re-layouts  8.33 us
    all_to_all x1, starting transfers between devices, local(): parts = lax.all_to_all(part, 'z', 0, 0)  8.19 us
    all_to_all x1, waiting for transfers between devices, local(): exit_got = lax.all_to_all(exit_part, 'pipe', 0, 0)  7.78 us
    pallas_call x1, Pallas kernels, local(): pl.pallas_call(gain_kernel, grid_spec=pltpu.PrefetchScalarGridSpec(num_sc...  6.83 us
  transfers between devices with their start and end apart: 17, of which 9 were waited for; matrix products, arithmetic and copies ran while one was open for 14% of the time, Pallas kernels for 14%

profile of v12, /device:TPU:1, one launch (start us, length us, event | category | flops | bytes accessed | tf_op | source)
XLA Modules:
  0.0 194.1 jit_solution(5258139279279769225)
XLA Ops:
  7.2 3.3 %collective-permute-start = (bf16[4096,256]{1,0:T(8,128)(2,1)}, bf16[4096,256]{1,0:T(8,128)(2,1)}, u32[]{:S(2)}, u32[]{:S(2)}) collective-permute-start(bf16[4096,256]{1,0:T(8,128)(2,1)} %bitcast.37), channel_id=1, source_target_pairs={{0,1},{1,0},{2,3},{3,2},{4,5},{5,4},{6,7},{7,6},{8,9},{9,8},{10,11... | collective-permute-start | bytes 6291464 | tf_op jit(solution)/shard_map/ppermute | solution.py:24
  11.6 3.1 %multiply_reduce_fusion = (f32[32]{0:T(128)S(1)}, f32[32,4096]{1,0:T(8,128)S(1)}) fusion(bf16[1,512,4096]{2,1,0:T(8,128)(2,1)} %param.10, s32[32]{0:T(128)S(1)} %fusion.43.ids), kind=kOutput, calls=%fused_computation.31 | convolution fusion | flops 134496224 | bytes 4718848 | tf_op jit(solution)/shard_map/dot_general | solution.py:364
  15.4 4.2 %convolution_convert_fusion.1 = bf16[256,4096]{1,0:T(8,128)(2,1)} fusion(bf16[4096,256]{1,0:T(8,128)(2,1)} %collective-permute-done.weight_other, bf16[4096,256]{1,0:T(8,128)(2,1)S(1)} %bitcast.39, bf16[256,512]{1,0:T(8,128)(2,1)S(1)} %bitcast.67, bf16[256,256]{1,0:T(8,128)(2,1)S(1)} %get-tuple-element.93, bf16[256,256]{1,0:T(8,128)(2,1)S(1)} %get-tuple-element.92, ...), kind=kOutput, calls=%fused_computation.6 | convolution fusion | flops 1083834368 | bytes 6815745 | tf_op jit(solution)/shard_map/dot_general | solution.py:385
  21.3 13.0 %all_to_all.35.mine.row = bf16[16,32,256]{2,1,0:T(8,128)(2,1)S(1)} all-to-all(bf16[16,32,256]{2,1,0:T(8,128)(2,1)S(1)} %broadcast_in_dim.29), channel_id=1, replica_groups=mesh['pipe'=16,'z'=8,'core'=2] {'pipe'}, dimensions={0} | all-to-all | bytes 524288 | tf_op jit(solution)/shard_map/all_to_all | solution.py:20
  36.9 1.7 shard_map.129
  38.7 8.2 %all-to-all-start.1 = ((bf16[8,64,1024]{2,1,0:T(8,128)(2,1)}), bf16[8,64,1024]{2,1,0:T(8,128)(2,1)S(1)}, u32[]{:S(2)}, u32[]{:S(2)}) async-start(bf16[8,64,1024]{2,1,0:T(8,128)(2,1)} %shard_map.129), calls=%async_computation.1 | async-start | bytes 2097152 | tf_op jit(solution)/shard_map/all_to_all | solution.py:406
  48.7 6.8 %shard_map.130.gain_part = f32[1,4096]{1,0:T(1,128)} custom-call(s32[4]{0:T(128)} %pad_add_fusion.place, bf16[8,2,32,4096]{3,2,1,0:T(8,128)(2,1)} %bitcast.58, bf16[8,2,32,4096]{3,2,1,0:T(8,128)(2,1)} %bitcast.51, s32[1,32]{1,0:T(1,128)} %constant_dynamic-slice_fusion.5.ids, bf16[4096,256]{1,0:T(8,128)(2,1)} %bitcast.38, ...), custom_call_target="tpu_custom_call" | custom-call | tf_op jit(solution)/shard_map/pallas_call | solution.py:408
  55.5 27.4 %all-to-all-done.1.parts = bf16[8,64,1024]{2,1,0:T(8,128)(2,1)S(1)} async-done(((bf16[8,64,1024]{2,1,0:T(8,128)(2,1)}), bf16[8,64,1024]{2,1,0:T(8,128)(2,1)S(1)}, u32[]{:S(2)}, u32[]{:S(2)}) %all-to-all-start.1) | async-done | bytes 1048608 | tf_op jit(solution)/shard_map/all_to_all | solution.py:406
  82.9 1.5 shard_map.131
  87.7 4.5 %all-to-all-start.2 = ((f32[16,2,8,128]{3,2,1,0:T(8,128)}), f32[16,2,8,128]{3,2,1,0:T(8,128)S(1)}, u32[]{:S(2)}, u32[]{:S(2)}) async-start(f32[16,2,8,128]{3,2,1,0:T(8,128)} %broadcast_in_dim.56), calls=%async_computation.3 | async-start | bytes 262144 | tf_op jit(solution)/shard_map/all_to_all | solution.py:20
  93.4 5.6 %all-to-all-done.2 = f32[16,2,8,128]{3,2,1,0:T(8,128)S(1)} async-done(((f32[16,2,8,128]{3,2,1,0:T(8,128)}), f32[16,2,8,128]{3,2,1,0:T(8,128)S(1)}, u32[]{:S(2)}, u32[]{:S(2)}) %all-to-all-start.2) | async-done | bytes 131104 | tf_op jit(solution)/shard_map/all_to_all | solution.py:20
  99.7 3.3 %all-to-all-start.3 = ((f32[8,8,128]{2,1,0:T(8,128)}), f32[8,8,128]{2,1,0:T(8,128)S(1)}, u32[]{:S(2)}, u32[]{:S(2)}) async-start(f32[8,8,128]{2,1,0:T(8,128)} %shard_map.132), calls=%async_computation.4 | async-start | bytes 65536 | tf_op jit(solution)/shard_map/all_to_all | solution.py:455
  103.1 3.2 %fusion = f32[512]{0:T(512)S(1)} fusion(bf16[512,4096]{1,0:T(8,128)(2,1)} %bitcast.54), kind=kLoop, calls=%fused_computation.2 | loop fusion | flops 6290944 | bytes 4196352 | tf_op jit(solution)/shard_map/reduce_sum | solution.py:467
  106.6 3.6 %fusion.2 = bf16[512,4096]{1,0:T(8,128)(2,1)} fusion(bf16[512,4096]{1,0:T(8,128)(2,1)S(1)} %bitcast.56, f32[4096]{0:T(1024)S(1)} %bitcast.44, f32[512]{0:T(512)S(1)} %add_rsqrt_fusion), kind=kLoop, calls=%fused_computation.4 | loop fusion | flops 8388608 | bytes 8407040 | tf_op jit(solution)/shard_map/convert_element_type | solution.py:468
  111.5 2.0 %collective-permute-start.4 = (f32[8,8,128]{2,1,0:T(8,128)S(1)}, f32[8,8,128]{2,1,0:T(8,128)S(1)}, u32[]{:S(2)}, u32[]{:S(2)}) collective-permute-start(f32[8,8,128]{2,1,0:T(8,128)S(1)} %all-to-all-done.3.known.known_mine), channel_id=1, source_target_pairs={{0,1},{1,0},{2,3},{3,2},{4,5},{5,4},{6,7},{7,6},{8,9},{9,8},{10,11... | collective-permute-start | bytes 98312 | tf_op jit(solution)/shard_map/ppermute | solution.py:24
  113.4 2.0 %fusion.15 = bf16[32,4096]{1,0:T(8,128)(2,1)} fusion(bf16[32,4096]{1,0:T(8,128)(2,1)S(1)} %copy-done.17, f32[32]{0:T(128)S(1)} %broadcast_multiply_fusion.1, f32[32]{0:T(128)S(1)} %add_rsqrt_fusion.1, bf16[512,4096]{1,0:T(8,128)(2,1)} %bitcast.60, s32[]{:T(128)S(6)} %select_n.88, f32[4096]{0:T(1024)S(1)} %bitcast.45, bf16[512,4096]{1,0:T(8,128)(2,1)} %bitcast.55), kind=kLoop, calls=%fused_computation.25 | loop fusion | flops 1310720 | bytes 1065220 | tf_op jit(solution)/shard_map/convert_element_type | solution.py:464
  115.6 5.2 %collective-permute-start.5 = (bf16[8,64,1024]{2,1,0:T(8,128)(2,1)}, bf16[8,64,1024]{2,1,0:T(8,128)(2,1)}, u32[]{:S(2)}, u32[]{:S(2)}) collective-permute-start(bf16[8,64,1024]{2,1,0:T(8,128)(2,1)} %bitcast.62), channel_id=1, source_target_pairs={{0,1},{1,0},{2,3},{3,2},{4,5},{5,4},{6,7},{7,6},{8,9},{9,8},{10,11... | collective-permute-start | bytes 3145736 | tf_op jit(solution)/shard_map/ppermute | solution.py:24
  120.8 3.2 %shard_map.133 = (f32[512,256]{1,0:T(8,128)}, f32[512,128]{1,0:T(8,128)}) custom-call(s32[4]{0:T(128)} %pad_add_fusion.place, bf16[8,64,1024]{2,1,0:T(8,128)(2,1)} %bitcast.63, f32[8,8,128]{2,1,0:T(8,128)} %copy-done.18, s32[512,1]{1,0:T(8,128)} %copy-done.15, bf16[1024,256]{1,0:T(8,128)(2,1)} %copy-done.5), custom_call_target="tpu_custom_call" | custom-call | tf_op jit(solution)/shard_map/pallas_call | solution.py:53
  124.1 3.2 %shard_map.134 = bf16[16,32,256]{2,1,0:T(8,128)(2,1)} custom-call(s32[4]{0:T(128)} %pad_add_fusion.place, bf16[8,64,1024]{2,1,0:T(8,128)(2,1)} %collective-permute-done.5.expo.ex_other, f32[8,8,128]{2,1,0:T(8,128)} %copy-done.19, s32[512,1]{1,0:T(8,128)} %copy-done.15, bf16[1024,256]{1,0:T(8,128)(2,1)} %copy-done.16, f32[512,256]{1,0:T(8,128)} %get-tuple-element.65.before), custom_call_target="tpu_custom_call" | custom-call | tf_op jit(solution)/shard_map/pallas_call | solution.py:53
  127.3 6.4 %all-to-all-start.4 = ((bf16[16,32,256]{2,1,0:T(8,128)(2,1)}), bf16[16,32,256]{2,1,0:T(8,128)(2,1)S(1)}, u32[]{:S(2)}, u32[]{:S(2)}) async-start(bf16[16,32,256]{2,1,0:T(8,128)(2,1)} %shard_map.134), calls=%async_computation.5 | async-start | bytes 524288 | tf_op jit(solution)/shard_map/all_to_all | solution.py:509
  134.4 7.8 %all-to-all-done.4.got = bf16[16,32,256]{2,1,0:T(8,128)(2,1)S(1)} async-done(((bf16[16,32,256]{2,1,0:T(8,128)(2,1)}), bf16[16,32,256]{2,1,0:T(8,128)(2,1)S(1)}, u32[]{:S(2)}, u32[]{:S(2)}) %all-to-all-start.4) | async-done | bytes 262176 | tf_op jit(solution)/shard_map/all_to_all | solution.py:509
  144.9 1.6 copy-done.2
  146.5 3.6 %shard_map.136 = bf16[8,2,5888]{2,1,0:T(2,128)(2,1)} custom-call(s32[4]{0:T(128)S(1)} %copy-done.11, f32[16,256]{1,0:T(8,128)S(1)} %get-tuple-element.70.mine, f32[16,256]{1,0:T(8,128)S(1)} %collective-permute-done.6.other, bf16[4096,256]{1,0:T(8,128)(2,1)S(1)} %bitcast.40, bf16[4096,256]{1,0:T(8,128)(2,1)} %collective-permute-done.weight_other, ...), custom_call_target="tpu_custom_call" | custom-call | tf_op jit(solution)/shard_map/pallas_call | solution.py:28
  150.1 4.2 %all-to-all-start.5 = ((bf16[8,2,5888]{2,1,0:T(2,128)(2,1)}), bf16[8,2,5888]{2,1,0:T(2,128)(2,1)S(1)}, u32[]{:S(2)}, u32[]{:S(2)}) async-start(bf16[8,2,5888]{2,1,0:T(2,128)(2,1)} %shard_map.136), calls=%async_computation.6 | async-start | bytes 376832 | tf_op jit(solution)/shard_map/all_to_all | solution.py:536
  154.3 5.2 %convolution_convert_fusion = bf16[4096,256]{1,0:T(8,128)(2,1)} fusion(bf16[512,4096]{1,0:T(8,128)(2,1)} %fusion.2, bf16[32,256]{1,0:T(8,128)(2,1)S(1)} %get-tuple-element.76, pred[512]{0:T(512)(128)(4,1)S(1)} %compare_reduce_fusion, bf16[512,4096]{1,0:T(8,128)(2,1)} %bitcast.61, s32[]{:T(128)S(6)} %select_n.73, s32[32]{0:T(128)S(1)} %fusion.43.ids), kind=kOutput, calls=%fused_computation.5 | convolution fusion | flops 1083457536 | bytes 6570628 | tf_op jit(solution)/shard_map/dot_general | solution.py:543
  159.5 5.4 %all-to-all-done.5.got = bf16[8,2,5888]{2,1,0:T(2,128)(2,1)S(1)} async-done(((bf16[8,2,5888]{2,1,0:T(2,128)(2,1)}), bf16[8,2,5888]{2,1,0:T(2,128)(2,1)S(1)}, u32[]{:S(2)}, u32[]{:S(2)}) %all-to-all-start.5) | async-done | bytes 188448 | tf_op jit(solution)/shard_map/all_to_all | solution.py:536
  165.7 3.9 %all-to-all-start.6 = ((bf16[8,2,4864]{2,1,0:T(2,128)(2,1)}), bf16[8,2,4864]{2,1,0:T(2,128)(2,1)S(1)}, u32[]{:S(2)}, u32[]{:S(2)}) async-start(bf16[8,2,4864]{2,1,0:T(2,128)(2,1)} %shard_map.137), calls=%async_computation.7 | async-start | bytes 311296 | tf_op jit(solution)/shard_map/all_to_all | solution.py:568
  169.7 2.2 %copy-done.6 = bf16[512,4096]{1,0:T(8,128)(2,1)S(1)} copy-done((bf16[512,4096]{1,0:T(8,128)(2,1)S(1)}, bf16[512,4096]{1,0:T(8,128)(2,1)}, u32[]{:S(2)}) %copy-start.6) | copy-done | bytes 4194328
  172.2 2.0 %copy-done.3 = bf16[512,4096]{1,0:T(8,128)(2,1)} copy-done((bf16[512,4096]{1,0:T(8,128)(2,1)}, bf16[512,4096]{1,0:T(8,128)(2,1)S(1)}, u32[]{:S(2)}) %copy-start.3) | copy-done | bytes 4194328
  174.2 4.7 %shard_map.138 = bf16[2000,256]{1,0:T(8,128)(2,1)} custom-call(s32[4]{0:T(128)} %pad_add_fusion.place, bf16[16,32,256]{2,1,0:T(8,128)(2,1)} %copy-done.7, f32[1,256]{1,0:T(1,128)} %bitcast.48, f32[512,128]{1,0:T(8,128)} %get-tuple-element.82.kept, s32[512,1]{1,0:T(8,128)} %copy-done.15, bf16[8,64,1024]{2,1,0:T(8,128)(2,1)} %bitcast.64, ...), custom_call_target="tpu_custom_call" | custom-call | tf_op jit(solution)/shard_map/pallas_call | solution.py:53
  181.2 2.2 %copy-done.4 = bf16[512,4096]{1,0:T(8,128)(2,1)S(1)} copy-done((bf16[512,4096]{1,0:T(8,128)(2,1)S(1)}, bf16[512,4096]{1,0:T(8,128)(2,1)}, u32[]{:S(2)}) %copy-start.4) | copy-done | bytes 4194328
  183.4 4.2 %shard_map.140 = (bf16[512,4096]{1,0:T(8,128)(2,1)}, f32[1,4096]{1,0:T(1,128)}, bf16[512,4096]{1,0:T(8,128)(2,1)S(1)}) custom-call(s32[4]{0:T(128)S(1)} %copy-done.12, s32[32]{0:T(128)S(1)} %fusion.43.ids, bf16[8,2,4864]{2,1,0:T(2,128)(2,1)S(1)} %all-to-all-done.6.mine, ...), custom_call_target="tpu_custom_call", output_to_operand_aliasing={{2}: (4, {})} | custom-call | tf_op jit(solution)/shard_map/pallas_call | solution.py:580
  (102 shorter events, 21.5 us)
Async XLA Ops:
  7.2 7.7 %copy-start.1 = (bf16[1,4096,256]{2,1,0:T(8,128)(2,1)S(1)}, bf16[1,4096,256]{2,1,0:T(8,128)(2,1)}, u32[]{:S(2)}) copy-start(bf16[1,4096,256]{2,1,0:T(8,128)(2,1)} %param.11) | copy-start | bytes 6291460
  7.2 77.3 %reduce-scatter.2.cloned.1.call-start = ((), (), s32[]{:S(2)}) async-start(), calls=%async_computation.8 | async-start | bytes 2359296 | tf_op jit(solution)/shard_map/reduce_scatter | solution.py:389
  7.2 8.1 %collective-permute-start = (bf16[4096,256]{1,0:T(8,128)(2,1)}, bf16[4096,256]{1,0:T(8,128)(2,1)}, u32[]{:S(2)}, u32[]{:S(2)}) collective-permute-start(bf16[4096,256]{1,0:T(8,128)(2,1)} %bitcast.37), channel_id=1, source_target_pairs={{0,1},{1,0},{2,3},{3,2},{4,5},{5,4},{6,7},{7,6},{8,9},{9,8},{10,11... | collective-permute-start | bytes 6291464 | tf_op jit(solution)/shard_map/ppermute | solution.py:24
  20.9 26.0 %copy-start.21 = (f32[16]{0:T(128)S(1)}, f32[16]{0:T(128)}, u32[]{:S(2)}) copy-start(f32[16]{0:T(128)} %param.18) | copy-start | bytes 196
  20.9 26.0 %copy-start.22 = (s32[16]{0:T(128)S(1)}, s32[16]{0:T(128)}, u32[]{:S(2)}) copy-start(s32[16]{0:T(128)} %param.16) | copy-start | bytes 196
  20.9 26.2 %copy-start.20 = (s32[16,32]{1,0:T(8,128)S(1)}, s32[16,32]{1,0:T(8,128)}, u32[]{:S(2)}) copy-start(s32[16,32]{1,0:T(8,128)} %param.17) | copy-start | bytes 6148
  21.0 17.6 %copy-start.16 = (bf16[1024,256]{1,0:T(8,128)(2,1)}, bf16[1024,256]{1,0:T(8,128)(2,1)S(1)}, u32[]{:S(2)}) copy-start(bf16[1024,256]{1,0:T(8,128)(2,1)S(1)} %get-tuple-element.90.head) | copy-start | bytes 1572868
  21.0 34.5 %copy-start.5 = (bf16[1024,256]{1,0:T(8,128)(2,1)}, bf16[1024,256]{1,0:T(8,128)(2,1)S(1)}, u32[]{:S(2)}) copy-start(bf16[1024,256]{1,0:T(8,128)(2,1)S(1)} %get-tuple-element.91.head_mine.head) | copy-start | bytes 1572868
  21.0 15.6 %collective-permute-start.2 = (bf16[1024,256]{1,0:T(8,128)(2,1)S(1)}, bf16[1024,256]{1,0:T(8,128)(2,1)S(1)}, u32[]{:S(2)}, u32[]{:S(2)}) collective-permute-start(bf16[1024,256]{1,0:T(8,128)(2,1)S(1)} %get-tuple-element.90.head), channel_id=1, source_target_pairs={{0,1},{1,0},{2,3},{3,2},{4,5},{5,4},{6,7},{7,6},{8,9},{9,8},{10,11... | collective-permute-start | bytes 1572872 | tf_op jit(solution)/shard_map/ppermute | solution.py:24
  34.3 21.2 %copy-start.7 = (bf16[16,32,256]{2,1,0:T(8,128)(2,1)}, bf16[16,32,256]{2,1,0:T(8,128)(2,1)S(1)}, u32[]{:S(2)}) copy-start(bf16[16,32,256]{2,1,0:T(8,128)(2,1)S(1)} %all_to_all.35.mine.row) | copy-start | bytes 786436
  34.3 2.7 %collective-permute-start.1 = (bf16[16,32,256]{2,1,0:T(8,128)(2,1)S(1)}, bf16[16,32,256]{2,1,0:T(8,128)(2,1)S(1)}, u32[]{:S(2)}, u32[]{:S(2)}) collective-permute-start(bf16[16,32,256]{2,1,0:T(8,128)(2,1)S(1)} %all_to_all.35.mine.row), channel_id=1, source_target_pairs={{0,1},{1,0},{2,3},{3,2},{4,5},{5,4},{6,7},{7,6},{8,9},{9,8},{10,11... | collective-permute-start | bytes 786440 | tf_op jit(solution)/shard_map/ppermute | solution.py:24
  36.6 105.6 %copy-start.13 = (f32[256]{0:T(256)}, f32[256]{0:T(256)S(1)}, u32[]{:S(2)}) copy-start(f32[256]{0:T(256)S(1)} %get-tuple-element.95) | copy-start | bytes 3076
  38.7 44.3 %all-to-all-start.1 = ((bf16[8,64,1024]{2,1,0:T(8,128)(2,1)}), bf16[8,64,1024]{2,1,0:T(8,128)(2,1)S(1)}, u32[]{:S(2)}, u32[]{:S(2)}) async-start(bf16[8,64,1024]{2,1,0:T(8,128)(2,1)} %shard_map.129), calls=%async_computation.1 | async-start | bytes 2097152 | tf_op jit(solution)/shard_map/all_to_all | solution.py:406
  46.8 68.8 %all-gather.6.cloned.1.call-start = ((), (), s32[]{:S(2)}) async-start(), calls=%async_computation.10 | async-start | bytes 1179648 | tf_op jit(solution)/shard_map/all_gather | solution.py:448
  47.3 8.2 %copy-start.15 = (s32[512,1]{1,0:T(8,128)}, s32[512,1]{1,0:T(8,128)S(1)}, u32[]{:S(2)}) copy-start(s32[512,1]{1,0:T(8,128)S(1)} %reshape.114.targets) | copy-start | bytes 6148
  48.7 34.2 %copy-start.10 = (s32[4]{0:T(128)S(1)}, s32[4]{0:T(128)}, u32[]{:S(2)}) copy-start(s32[4]{0:T(128)} %pad_add_fusion.place) | copy-start | bytes 52
  84.5 1.4 collective-permute-start.3
  87.7 11.3 %all-to-all-start.2 = ((f32[16,2,8,128]{3,2,1,0:T(8,128)}), f32[16,2,8,128]{3,2,1,0:T(8,128)S(1)}, u32[]{:S(2)}, u32[]{:S(2)}) async-start(f32[16,2,8,128]{3,2,1,0:T(8,128)} %broadcast_in_dim.56), calls=%async_computation.3 | async-start | bytes 262144 | tf_op jit(solution)/shard_map/all_to_all | solution.py:20
  99.7 11.8 %all-to-all-start.3 = ((f32[8,8,128]{2,1,0:T(8,128)}), f32[8,8,128]{2,1,0:T(8,128)S(1)}, u32[]{:S(2)}, u32[]{:S(2)}) async-start(f32[8,8,128]{2,1,0:T(8,128)} %shard_map.132), calls=%async_computation.4 | async-start | bytes 65536 | tf_op jit(solution)/shard_map/all_to_all | solution.py:455
  103.0 62.7 %all-gather.4.cloned.1.call-start = ((), (), s32[]{:S(2)}) async-start(), calls=%async_computation.9 | async-start | bytes 4456448 | tf_op jit(solution)/shard_map/all_gather | solution.py:482
  110.2 32.0 %copy-start.11 = (s32[4]{0:T(128)S(1)}, s32[4]{0:T(128)}, u32[]{:S(2)}) copy-start(s32[4]{0:T(128)} %pad_add_fusion.place) | copy-start | bytes 52
  110.2 34.7 %copy-start.9 = (f32[1,4096]{1,0:T(1,128)S(1)}, f32[1,4096]{1,0:T(1,128)}, u32[]{:S(2)}) copy-start(f32[1,4096]{1,0:T(1,128)} %shard_map.130.gain_part) | copy-start | bytes 49156
  111.4 9.4 %copy-start.18 = (f32[8,8,128]{2,1,0:T(8,128)}, f32[8,8,128]{2,1,0:T(8,128)S(1)}, u32[]{:S(2)}) copy-start(f32[8,8,128]{2,1,0:T(8,128)S(1)} %all-to-all-done.3.known.known_mine) | copy-start | bytes 98308
  111.5 3.9 %collective-permute-start.4 = (f32[8,8,128]{2,1,0:T(8,128)S(1)}, f32[8,8,128]{2,1,0:T(8,128)S(1)}, u32[]{:S(2)}, u32[]{:S(2)}) collective-permute-start(f32[8,8,128]{2,1,0:T(8,128)S(1)} %all-to-all-done.3.known.known_mine), channel_id=1, source_target_pairs={{0,1},{1,0},{2,3},{3,2},{4,5},{5,4},{6,7},{7,6},{8,9},{9,8},{10,11... | collective-permute-start | bytes 98312 | tf_op jit(solution)/shard_map/ppermute | solution.py:24
  115.4 8.7 %copy-start.19 = (f32[8,8,128]{2,1,0:T(8,128)}, f32[8,8,128]{2,1,0:T(8,128)S(1)}, u32[]{:S(2)}) copy-start(f32[8,8,128]{2,1,0:T(8,128)S(1)} %collective-permute-done.4.known.known_other) | copy-start | bytes 98308
  115.6 8.4 %collective-permute-start.5 = (bf16[8,64,1024]{2,1,0:T(8,128)(2,1)}, bf16[8,64,1024]{2,1,0:T(8,128)(2,1)}, u32[]{:S(2)}, u32[]{:S(2)}) collective-permute-start(bf16[8,64,1024]{2,1,0:T(8,128)(2,1)} %bitcast.62), channel_id=1, source_target_pairs={{0,1},{1,0},{2,3},{3,2},{4,5},{5,4},{6,7},{7,6},{8,9},{9,8},{10,11... | collective-permute-start | bytes 3145736 | tf_op jit(solution)/shard_map/ppermute | solution.py:24
  127.3 14.9 %all-to-all-start.4 = ((bf16[16,32,256]{2,1,0:T(8,128)(2,1)}), bf16[16,32,256]{2,1,0:T(8,128)(2,1)S(1)}, u32[]{:S(2)}, u32[]{:S(2)}) async-start(bf16[16,32,256]{2,1,0:T(8,128)(2,1)} %shard_map.134), calls=%async_computation.5 | async-start | bytes 524288 | tf_op jit(solution)/shard_map/all_to_all | solution.py:509
  142.8 2.1 %collective-permute-start.6 = (f32[16,256]{1,0:T(8,128)S(1)}, f32[16,256]{1,0:T(8,128)S(1)}, u32[]{:S(2)}, u32[]{:S(2)}) collective-permute-start(f32[16,256]{1,0:T(8,128)S(1)} %get-tuple-element.71), channel_id=1, source_target_pairs={{0,1},{1,0},{2,3},{3,2},{4,5},{5,4},{6,7},{7,6},{8,9},{9,8},{10,11... | collective-permute-start | bytes 49160 | tf_op jit(solution)/shard_map/ppermute | solution.py:24
  150.1 14.8 %all-to-all-start.5 = ((bf16[8,2,5888]{2,1,0:T(2,128)(2,1)}), bf16[8,2,5888]{2,1,0:T(2,128)(2,1)S(1)}, u32[]{:S(2)}, u32[]{:S(2)}) async-start(bf16[8,2,5888]{2,1,0:T(2,128)(2,1)} %shard_map.136), calls=%async_computation.6 | async-start | bytes 376832 | tf_op jit(solution)/shard_map/all_to_all | solution.py:536
  165.7 13.2 %all-to-all-start.6 = ((bf16[8,2,4864]{2,1,0:T(2,128)(2,1)}), bf16[8,2,4864]{2,1,0:T(2,128)(2,1)S(1)}, u32[]{:S(2)}, u32[]{:S(2)}) async-start(bf16[8,2,4864]{2,1,0:T(2,128)(2,1)} %shard_map.137), calls=%async_computation.7 | async-start | bytes 311296 | tf_op jit(solution)/shard_map/all_to_all | solution.py:568
  171.8 9.4 %copy-start.12 = (s32[4]{0:T(128)S(1)}, s32[4]{0:T(128)}, u32[]{:S(2)}) copy-start(s32[4]{0:T(128)} %pad_add_fusion.place) | copy-start | bytes 52
  178.9 2.3 %collective-permute-start.7 = (bf16[8,2,4864]{2,1,0:T(2,128)(2,1)S(1)}, bf16[8,2,4864]{2,1,0:T(2,128)(2,1)S(1)}, u32[]{:S(2)}, u32[]{:S(2)}) collective-permute-start(bf16[8,2,4864]{2,1,0:T(2,128)(2,1)S(1)} %all-to-all-done.6.mine), channel_id=1, source_target_pairs={{0,1},{1,0},{2,3},{3,2},{4,5},{5,4},{6,7},{7,6},{8,9},{9,8},{10,11... | collective-permute-start | bytes 466952 | tf_op jit(solution)/shard_map/ppermute | solution.py:24
  (8 other events, 30.5 us)
Sparse Core Ops, SparseCore 0:
  19.7 52.2 reduce-scatter.1
  85.3 30.2 all-gather.5
  117.5 47.2 all-gather.3

commit v13 on v11

--- a/solution.py
+++ b/solution.py
@@ -10,8 +10,10 @@
 F32 = jnp.float32
 BF16 = jnp.bfloat16
 EPSILON = 1e-05
+SMALL = 20 * 1024 * 1024
 VMEM = 32 * 1024 * 1024
-LARGE = 63 * 1024 * 1024
+LARGE = 56 * 1024 * 1024
+LARGEST = 63 * 1024 * 1024
 
 
 def spread(values, axis, count):
@@ -42,7 +44,7 @@
     )(*operands)
 
 
-def piped_call(body, out, *operands, held=(), kept=(), scratch=(), limit=LARGE):
+def piped_call(body, out, *operands, held=(), kept=(), scratch=(), limit=LARGEST):
     def spec(value, stays):
         if stays:
             return pl.BlockSpec(memory_space=pltpu.VMEM)
@@ -224,11 +226,9 @@
     other[...] = jnp.where(core == 0, rows[half:], rows[:half])
 
 
-def send_kernel(place, mine, other, weight, weight_other, unit, gain_part, out):
+def send_kernel(place, part, mine, other, unit, gain_part, out):
     core = place[1]
-    columns = (((1,), (1,)), ((), ()))
-    part = lax.dot_general(mine[...].astype(BF16), weight[...], columns, preferred_element_type=F32)
-    part += lax.dot_general(other[...].astype(BF16), weight_other[...], columns, preferred_element_type=F32)
+    part = part[...]
     gain = gain_part[...] + jnp.sum(part * unit[...], axis=0, keepdims=True)
     low = jnp.where(core == 0, mine[...], other[...])
     high = jnp.where(core == 0, other[...], mine[...])
@@ -238,7 +238,7 @@
     part = part.astype(BF16)
     gains = [values.astype(BF16) for values in pieces3(gain)]
     count, share, _ = out.shape
-    width, slab = weight.shape
+    width, slab = part.shape[1], mine.shape[1]
     piece = width // (count * share)
     for i in range(count):
         at = slice(i * share, (i + 1) * share)
@@ -276,23 +276,28 @@
 
 def last_kernel(place, ids, mine, other, main, out, gain_out, block, into, outof):
     core = place[1]
-    tokens, width = block.shape
+    width = block.shape[1]
     parts = into.shape[0]
-    count = tokens // parts
-
-    def copies(source, target, done):
-        return [
-            pltpu.make_async_copy(
-                source.at[pl.ds(i * count, count)], target.at[pl.ds(i * count, count)], done.at[i]
-            )
-            for i in range(parts)
-        ]
-
-    loads = copies(main, block, into)
-    stores = copies(block, out, outof)
+    count = width // parts
+    columns = [slice(k * count, (k + 1) * count) for k in range(parts)]
+    loads = [pltpu.make_async_copy(main.at[:, c], block.at[:, c], into.at[k]) for k, c in enumerate(columns)]
+    stores = [pltpu.make_async_copy(block.at[:, c], out.at[:, c], outof.at[k]) for k, c in enumerate(columns)]
     for load in loads:
         load.start()
     groups, share = mine.shape[:2]
+    spots = []
+    for rows, first in ((mine, core), (other, 1 - core)):
+        for i in range(groups):
+            for j in range(share):
+                at = ids[first * groups * share + i * share + j]
+                start = pl.multiple_of(at // 16 * 16, 16)
+                spots.append((rows, i, j, start, at - start))
+    tile = lax.broadcasted_iota(jnp.int32, (16, count), 0)
+    for k, c in enumerate(columns):
+        loads[k].wait()
+        for rows, i, j, start, at in spots:
+            block[pl.ds(start, 16), c] = jnp.where(tile == at, rows[i, j : j + 1, c], block[pl.ds(start, 16), c])
+        stores[k].start()
     piece = (mine.shape[2] - width) // 3
     total = mine[:, :, width:].astype(F32) + other[:, :, width:].astype(F32)
     total = total[:, :, :piece] + total[:, :, piece : 2 * piece] + total[:, :, 2 * piece :]
@@ -300,18 +305,6 @@
         for j in range(share):
             at = (i * share + j) * piece
             gain_out[:, at : at + piece] = total[i, j : j + 1]
-    tile = lax.broadcasted_iota(jnp.int32, (16, width), 0)
-    for load in loads:
-        load.wait()
-    for rows, first in ((mine, core), (other, 1 - core)):
-        for i in range(groups):
-            for j in range(share):
-                at = ids[first * groups * share + i * share + j]
-                start = pl.multiple_of(at // 16 * 16, 16)
-                row = rows[i, j : j + 1, :width]
-                block[pl.ds(start, 16), :] = jnp.where(tile == at - start, row, block[pl.ds(start, 16), :])
-    for store in stores:
-        store.start()
     for store in stores:
         store.wait()
 
@@ -349,6 +342,12 @@
     whole = lambda *dims: pl.BlockSpec(dims, lambda i, *_: (0,) * len(dims))
 
     weight_other = swap(weight)
+    halves = jnp.pad(head_weight, ((0, 2 * half - vocab_part), (0, 0))).reshape(2, half, slab)
+    halves = jnp.pad(halves, ((0, 0), (0, padded - half), (0, 0)))
+    head_mine = lax.dynamic_index_in_dim(halves, core, 0, keepdims=False)
+    head_rest = lax.dynamic_index_in_dim(halves, 1 - core, 0, keepdims=False)
+    head_other = swap(head_rest)
+
     my_rows = exit_rows[pipe]
     pick = (my_rows[:, None] == jnp.arange(tokens, dtype=jnp.int32)[None, :]).astype(BF16)
     row_in = jnp.dot(pick, seg, preferred_element_type=F32)
@@ -366,7 +365,7 @@
     weight_spec = pl.BlockSpec((chunk, slab), lambda i, at: (i, 0))
     grad_view = grad.reshape(zs, 2, held, width)
     joined = jnp.concatenate([weight, weight_other], axis=1)
-    chip_grad = lax.dynamic_slice(after(grad_view, hidden), (0, core, 0, z * 2 * slab), (zs, 1, held, 2 * slab))
+    chip_grad = lax.dynamic_slice(grad_view, (0, core, 0, z * 2 * slab), (zs, 1, held, 2 * slab))
     on_columns = (((1,), (1,)), ((), ()))
 
     def own_first(values):
@@ -375,16 +374,10 @@
     main_sent = lax.dot_general(
         own_first(chip_grad.reshape(zs * held, 2 * slab)), joined, on_columns, preferred_element_type=F32
     ).astype(BF16)
-
-    halves = jnp.pad(after(head_weight, hidden), ((0, 2 * half - vocab_part), (0, 0))).reshape(2, half, slab)
-    halves = jnp.pad(halves, ((0, 0), (0, padded - half), (0, 0)))
-    head_mine = lax.dynamic_index_in_dim(halves, core, 0, keepdims=False)
-    head_rest = lax.dynamic_index_in_dim(halves, 1 - core, 0, keepdims=False)
-    head_other = swap(head_rest)
+    hidden, main_sent = lax.optimization_barrier((hidden, main_sent))
+    main_grad = lax.psum_scatter(main_sent, "z", scatter_dimension=0, tiled=True)
 
     all_mine = spread(hidden, "pipe", pipes)
-    all_mine, main_sent, head_other = lax.optimization_barrier((all_mine, main_sent, head_other))
-    main_grad = lax.psum_scatter(main_sent, "z", scatter_dimension=0, tiled=True)
     all_other = swap(all_mine)
     gain_mine = lax.dynamic_slice_in_dim(final_gain, block * slab, slab, 0)[None]
     gain_other = lax.dynamic_slice_in_dim(final_gain, (z * 2 + 1 - core) * slab, slab, 0)[None]
@@ -532,14 +525,17 @@
     )
 
     piece = slab * 2 // share
+    row_other = swap(row_send)
+    row_part = lax.dot_general(
+        jnp.concatenate([row_mine, row_other], axis=1).astype(BF16), joined, on_columns, preferred_element_type=F32
+    )
     send = kernel_call(
         send_kernel,
         shape((zs, share, width + 4 * slab + 3 * piece), BF16),
         place,
+        row_part,
         row_mine,
-        swap(row_send),
-        weight,
-        weight_other,
+        row_other,
         core_unit,
         gain_part,
     )

time: 211 us -> 195 us (0.924)
  blocking collectives: 12.7 us -> 26.1 us
  starting transfers between devices: 53.7 us -> 42.9 us
  waiting for transfers between devices: 55.1 us -> 44.5 us
  local copies, waits for them, and re-layouts: 12.9 us -> 6.79 us
  Pallas kernels: 34.9 us -> 29.3 us
  matrix products: 14.1 us -> 17.6 us
    all_to_all x0 -> x1, blocking collectives: none -> 13 us  [spread(): lax.all_to_all(jnp.broadcast_to(values[None], (count,) + values.shape), a...]
    all_to_all x2 -> x1, starting transfers between devices: 12.5 us -> 4.67 us  [spread(): lax.all_to_all(jnp.broadcast_to(values[None], (count,) + values.shape), a...]
    all_to_all x1, waiting for transfers between devices: 31.8 us -> 27.3 us  [local(): parts = lax.all_to_all(part, 'z', 0, 0)]
    dot_general x0 -> x1, matrix products: none -> 3.5 us  [local(): lax.dot_general(jnp.concatenate([row_mine, row_other], axis=1).astype(BF1...]
    all_to_all x2 -> x1, waiting for transfers between devices: 8.7 us -> 5.55 us  [spread(): lax.all_to_all(jnp.broadcast_to(values[None], (count,) + values.shape), a...]
    pallas_call x3, Pallas kernels: 6.42 us -> 3.61 us  [kernel_call(): pl.pallas_call(body, out_shape=out, in_specs=[pl.BlockSpec(memory_space=p...]
    unnamed x48 -> x44, local copies, waits for them, and re-layouts: 3.44 us -> 1 us
    all_to_all x1, starting transfers between devices: 5.72 us -> 3.34 us  [local(): known_mine = lax.all_to_all(known_mine, 'z', 0, 0)]
  transfers between devices with their start and end apart: 17 -> 16, of which waited for: 11 -> 9; matrix products, arithmetic and copies ran while one was open for 17% -> 16% of each run, Pallas kernels for 13% -> 12%
where the time goes in v13:
time: 195 us; the launch traced here: 193 us
  waiting for transfers between devices  44.5 us (23%)
  starting transfers between devices  42.9 us (22%)
  Pallas kernels  29.3 us (15%)
  blocking collectives  26.1 us (13%)
  matrix products  17.6 us (9%)
  between operations  14.1 us (7%)
  other arithmetic  12.1 us (6%)
  local copies, waits for them, and re-layouts  6.79 us (3%)
    all_to_all x1, waiting for transfers between devices, local(): parts = lax.all_to_all(part, 'z', 0, 0)  27.3 us
    ppermute x8, starting transfers between devices, swap(): return lax.ppermute(values, 'core', [(0, 1), (1, 0)])  16 us
    all_to_all x1, blocking collectives, local(): last = lax.all_to_all(last, 'z', 0, 0)  13.1 us
    all_to_all x1, blocking collectives, spread(): lax.all_to_all(jnp.broadcast_to(values[None], (count,) + values.shape), a...  13 us
    pallas_call x3, Pallas kernels, piped_call(): pl.pallas_call(body, grid=(1,), out_shape=out, in_specs=[pl.BlockSpec(mem...  11.1 us
    all_to_all x1, starting transfers between devices, local(): parts = lax.all_to_all(part, 'z', 0, 0)  8.19 us
    pallas_call x1, Pallas kernels, local(): pl.pallas_call(gain_kernel, grid_spec=pltpu.PrefetchScalarGridSpec(num_sc...  6.83 us
    all_to_all x1, starting transfers between devices, local(): exit_got = lax.all_to_all(exit_part, 'pipe', 0, 0)  6.39 us
  transfers between devices with their start and end apart: 16, of which 9 were waited for; matrix products, arithmetic and copies ran while one was open for 16% of the time, Pallas kernels for 12%

profile of v13, /device:TPU:1, one launch (start us, length us, event | category | flops | bytes accessed | tf_op | source)
XLA Modules:
  0.0 193.5 jit_solution(4737351505817399875)
XLA Ops:
  7.2 3.3 %collective-permute-start = (bf16[4096,256]{1,0:T(8,128)(2,1)}, bf16[4096,256]{1,0:T(8,128)(2,1)}, u32[]{:S(2)}, u32[]{:S(2)}) collective-permute-start(bf16[4096,256]{1,0:T(8,128)(2,1)} %bitcast.53), channel_id=1, source_target_pairs={{0,1},{1,0},{2,3},{3,2},{4,5},{5,4},{6,7},{7,6},{8,9},{9,8},{10,11... | collective-permute-start | bytes 6291464 | tf_op jit(solution)/shard_map/ppermute | solution.py:24
  11.6 3.1 %multiply_reduce_fusion = (f32[32]{0:T(128)S(1)}, f32[32,4096]{1,0:T(8,128)S(1)}) fusion(bf16[1,512,4096]{2,1,0:T(8,128)(2,1)} %param.10, s32[32]{0:T(128)S(1)} %fusion.45.ids), kind=kOutput, calls=%fused_computation.30 | convolution fusion | flops 134496224 | bytes 4718848 | tf_op jit(solution)/shard_map/dot_general | solution.py:353
  15.4 4.2 %convolution_convert_fusion.1 = bf16[256,4096]{1,0:T(8,128)(2,1)} fusion(bf16[4096,256]{1,0:T(8,128)(2,1)} %collective-permute-done.weight_other, bf16[4096,256]{1,0:T(8,128)(2,1)S(1)} %bitcast.56, bf16[256,512]{1,0:T(8,128)(2,1)S(1)} %bitcast.67, bf16[256,256]{1,0:T(8,128)(2,1)S(1)} %get-tuple-element.89, bf16[256,256]{1,0:T(8,128)(2,1)S(1)} %get-tuple-element.88, ...), kind=kOutput, calls=%fused_computation.6 | convolution fusion | flops 1083834368 | bytes 6815745 | tf_op jit(solution)/shard_map/dot_general | solution.py:374
  19.6 1.3 pad.12
  21.3 13.0 %all_to_all.35.mine.row = bf16[16,32,256]{2,1,0:T(8,128)(2,1)S(1)} all-to-all(bf16[16,32,256]{2,1,0:T(8,128)(2,1)S(1)} %broadcast_in_dim.29), channel_id=1, replica_groups=mesh['pipe'=16,'z'=8,'core'=2] {'pipe'}, dimensions={0} | all-to-all | bytes 524288 | tf_op jit(solution)/shard_map/all_to_all | solution.py:20
  34.3 1.5 collective-permute-start.1
  36.9 1.7 shard_map.129
  38.7 8.2 %all-to-all-start.1 = ((bf16[8,64,1024]{2,1,0:T(8,128)(2,1)}), bf16[8,64,1024]{2,1,0:T(8,128)(2,1)S(1)}, u32[]{:S(2)}, u32[]{:S(2)}) async-start(bf16[8,64,1024]{2,1,0:T(8,128)(2,1)} %shard_map.129), calls=%async_computation.1 | async-start | bytes 2097152 | tf_op jit(solution)/shard_map/all_to_all | solution.py:395
  48.6 6.8 %shard_map.130.gain_part = f32[1,4096]{1,0:T(1,128)} custom-call(s32[4]{0:T(128)} %pad_add_fusion.place, bf16[8,2,32,4096]{3,2,1,0:T(8,128)(2,1)} %bitcast.58, bf16[8,2,32,4096]{3,2,1,0:T(8,128)(2,1)} %bitcast.47, s32[1,32]{1,0:T(1,128)} %constant_dynamic-slice_fusion.5.ids, bf16[4096,256]{1,0:T(8,128)(2,1)} %bitcast.54, ...), custom_call_target="tpu_custom_call" | custom-call | tf_op jit(solution)/shard_map/pallas_call | solution.py:397
  55.4 27.3 %all-to-all-done.1.parts = bf16[8,64,1024]{2,1,0:T(8,128)(2,1)S(1)} async-done(((bf16[8,64,1024]{2,1,0:T(8,128)(2,1)}), bf16[8,64,1024]{2,1,0:T(8,128)(2,1)S(1)}, u32[]{:S(2)}, u32[]{:S(2)}) %all-to-all-start.1) | async-done | bytes 1048608 | tf_op jit(solution)/shard_map/all_to_all | solution.py:395
  82.7 1.6 shard_map.131
  87.5 4.7 %all-to-all-start.2 = ((f32[16,2,8,128]{3,2,1,0:T(8,128)}), f32[16,2,8,128]{3,2,1,0:T(8,128)S(1)}, u32[]{:S(2)}, u32[]{:S(2)}) async-start(f32[16,2,8,128]{3,2,1,0:T(8,128)} %broadcast_in_dim.56), calls=%async_computation.3 | async-start | bytes 262144 | tf_op jit(solution)/shard_map/all_to_all | solution.py:20
  93.5 5.6 %all-to-all-done.2 = f32[16,2,8,128]{3,2,1,0:T(8,128)S(1)} async-done(((f32[16,2,8,128]{3,2,1,0:T(8,128)}), f32[16,2,8,128]{3,2,1,0:T(8,128)S(1)}, u32[]{:S(2)}, u32[]{:S(2)}) %all-to-all-start.2) | async-done | bytes 131104 | tf_op jit(solution)/shard_map/all_to_all | solution.py:20
  99.7 3.3 %all-to-all-start.3 = ((f32[8,8,128]{2,1,0:T(8,128)}), f32[8,8,128]{2,1,0:T(8,128)S(1)}, u32[]{:S(2)}, u32[]{:S(2)}) async-start(f32[8,8,128]{2,1,0:T(8,128)} %shard_map.132), calls=%async_computation.4 | async-start | bytes 65536 | tf_op jit(solution)/shard_map/all_to_all | solution.py:444
  103.1 3.2 %fusion = f32[512]{0:T(512)S(1)} fusion(bf16[512,4096]{1,0:T(8,128)(2,1)} %bitcast.50), kind=kLoop, calls=%fused_computation.2 | loop fusion | flops 6290944 | bytes 4196352 | tf_op jit(solution)/shard_map/reduce_sum | solution.py:456
  106.6 3.6 %fusion.2 = bf16[512,4096]{1,0:T(8,128)(2,1)} fusion(bf16[512,4096]{1,0:T(8,128)(2,1)S(1)} %bitcast.52, f32[4096]{0:T(1024)S(1)} %bitcast.40, f32[512]{0:T(512)S(1)} %add_rsqrt_fusion), kind=kLoop, calls=%fused_computation.4 | loop fusion | flops 8388608 | bytes 8407040 | tf_op jit(solution)/shard_map/convert_element_type | solution.py:457
  111.5 2.0 %collective-permute-start.4 = (f32[8,8,128]{2,1,0:T(8,128)S(1)}, f32[8,8,128]{2,1,0:T(8,128)S(1)}, u32[]{:S(2)}, u32[]{:S(2)}) collective-permute-start(f32[8,8,128]{2,1,0:T(8,128)S(1)} %all-to-all-done.3.known.known_mine), channel_id=1, source_target_pairs={{0,1},{1,0},{2,3},{3,2},{4,5},{5,4},{6,7},{7,6},{8,9},{9,8},{10,11... | collective-permute-start | bytes 98312 | tf_op jit(solution)/shard_map/ppermute | solution.py:24
  113.5 1.9 fusion.13
  115.7 5.2 %collective-permute-start.5 = (bf16[8,64,1024]{2,1,0:T(8,128)(2,1)}, bf16[8,64,1024]{2,1,0:T(8,128)(2,1)}, u32[]{:S(2)}, u32[]{:S(2)}) collective-permute-start(bf16[8,64,1024]{2,1,0:T(8,128)(2,1)} %bitcast.62), channel_id=1, source_target_pairs={{0,1},{1,0},{2,3},{3,2},{4,5},{5,4},{6,7},{7,6},{8,9},{9,8},{10,11... | collective-permute-start | bytes 3145736 | tf_op jit(solution)/shard_map/ppermute | solution.py:24
  120.9 3.2 %shard_map.133 = (f32[512,256]{1,0:T(8,128)}, f32[512,128]{1,0:T(8,128)}) custom-call(s32[4]{0:T(128)} %pad_add_fusion.place, bf16[8,64,1024]{2,1,0:T(8,128)(2,1)} %bitcast.63, f32[8,8,128]{2,1,0:T(8,128)} %copy-done.15, s32[512,1]{1,0:T(8,128)} %copy-done.11, bf16[1024,256]{1,0:T(8,128)(2,1)} %copy-done.1), custom_call_target="tpu_custom_call" | custom-call | tf_op jit(solution)/shard_map/pallas_call | solution.py:53
  124.1 3.2 %shard_map.134 = bf16[16,32,256]{2,1,0:T(8,128)(2,1)} custom-call(s32[4]{0:T(128)} %pad_add_fusion.place, bf16[8,64,1024]{2,1,0:T(8,128)(2,1)} %collective-permute-done.5.expo.ex_other, f32[8,8,128]{2,1,0:T(8,128)} %copy-done.17, s32[512,1]{1,0:T(8,128)} %copy-done.11, bf16[1024,256]{1,0:T(8,128)(2,1)} %copy-done.12, f32[512,256]{1,0:T(8,128)} %get-tuple-element.63.before), custom_call_target="tpu_custom_call" | custom-call | tf_op jit(solution)/shard_map/pallas_call | solution.py:53
  127.3 6.4 %all-to-all-start.4 = ((bf16[16,32,256]{2,1,0:T(8,128)(2,1)}), bf16[16,32,256]{2,1,0:T(8,128)(2,1)S(1)}, u32[]{:S(2)}, u32[]{:S(2)}) async-start(bf16[16,32,256]{2,1,0:T(8,128)(2,1)} %shard_map.134), calls=%async_computation.5 | async-start | bytes 524288 | tf_op jit(solution)/shard_map/all_to_all | solution.py:498
  134.4 4.7 %shard_map.135 = bf16[2000,256]{1,0:T(8,128)(2,1)} custom-call(s32[4]{0:T(128)} %pad_add_fusion.place, bf16[16,32,256]{2,1,0:T(8,128)(2,1)} %copy-done.2, f32[1,256]{1,0:T(1,128)} %bitcast.43, f32[512,128]{1,0:T(8,128)} %get-tuple-element.65.kept, s32[512,1]{1,0:T(8,128)} %copy-done.11, bf16[8,64,1024]{2,1,0:T(8,128)(2,1)} %bitcast.64, ...), custom_call_target="tpu_custom_call" | custom-call | tf_op jit(solution)/shard_map/pallas_call | solution.py:53
  139.2 3.1 %all-to-all-done.4.got = bf16[16,32,256]{2,1,0:T(8,128)(2,1)S(1)} async-done(((bf16[16,32,256]{2,1,0:T(8,128)(2,1)}), bf16[16,32,256]{2,1,0:T(8,128)(2,1)S(1)}, u32[]{:S(2)}, u32[]{:S(2)}) %all-to-all-start.4) | async-done | bytes 262176 | tf_op jit(solution)/shard_map/all_to_all | solution.py:498
  144.9 3.5 %fusion.3.part = f32[16,4096]{1,0:T(8,128)S(1)} fusion(bf16[4096,256]{1,0:T(8,128)(2,1)} %collective-permute-done.weight_other, bf16[4096,256]{1,0:T(8,128)(2,1)} %bitcast.55, bf16[16,256]{1,0:T(8,128)(2,1)S(1)} %convert.7, bf16[16,256]{1,0:T(8,128)(2,1)S(1)} %convert.6), kind=kOutput, calls=%fused_computation.8 | convolution fusion | flops 75530240 | bytes 4472832 | tf_op jit(solution)/shard_map/dot_general | solution.py:529
  148.4 1.4 shard_map.137
  149.8 4.3 %all-to-all-start.5 = ((bf16[8,2,5888]{2,1,0:T(2,128)(2,1)}), bf16[8,2,5888]{2,1,0:T(2,128)(2,1)S(1)}, u32[]{:S(2)}, u32[]{:S(2)}) async-start(bf16[8,2,5888]{2,1,0:T(2,128)(2,1)} %shard_map.137), calls=%async_computation.6 | async-start | bytes 376832 | tf_op jit(solution)/shard_map/all_to_all | solution.py:542
  154.1 5.2 %convolution_convert_fusion = bf16[4096,256]{1,0:T(8,128)(2,1)} fusion(bf16[512,4096]{1,0:T(8,128)(2,1)} %fusion.2, bf16[32,256]{1,0:T(8,128)(2,1)S(1)} %get-tuple-element.75, pred[512]{0:T(512)(128)(4,1)S(1)} %compare_reduce_fusion, bf16[512,4096]{1,0:T(8,128)(2,1)} %bitcast.61, s32[]{:T(128)S(6)} %select_n.73, s32[32]{0:T(128)S(1)} %fusion.45.ids), kind=kOutput, calls=%fused_computation.5 | convolution fusion | flops 1083457536 | bytes 6570628 | tf_op jit(solution)/shard_map/dot_general | solution.py:549
  159.3 5.6 %all-to-all-done.5.got = bf16[8,2,5888]{2,1,0:T(2,128)(2,1)S(1)} async-done(((bf16[8,2,5888]{2,1,0:T(2,128)(2,1)}), bf16[8,2,5888]{2,1,0:T(2,128)(2,1)S(1)}, u32[]{:S(2)}, u32[]{:S(2)}) %all-to-all-start.5) | async-done | bytes 188448 | tf_op jit(solution)/shard_map/all_to_all | solution.py:542
  165.1 13.1 %all_to_all.36.mine = bf16[8,2,4864]{2,1,0:T(2,128)(2,1)S(1)} all-to-all(bf16[8,2,4864]{2,1,0:T(2,128)(2,1)S(1)} %shard_map.138), channel_id=1, replica_groups=mesh['pipe'=16,'z'=8,'core'=2] {'z'}, dimensions={0} | all-to-all | bytes 311296 | tf_op jit(solution)/shard_map/all_to_all | solution.py:560
  178.2 1.9 collective-permute-start.7
  181.7 5.2 %shard_map.139 = (bf16[512,4096]{1,0:T(8,128)(2,1)}, f32[1,4096]{1,0:T(1,128)}) custom-call(s32[4]{0:T(128)} %pad_add_fusion.place, s32[32]{0:T(128)} %copy-done.19, bf16[8,2,4864]{2,1,0:T(2,128)(2,1)} %copy-done.14, bf16[8,2,4864]{2,1,0:T(2,128)(2,1)} %copy-done.16, bf16[512,4096]{1,0:T(8,128)(2,1)} %all-gather.4.cloned.1.call-done.main), custom_call_target="tpu_custom_call" | custom-call | tf_op jit(solution)/shard_map/pallas_call | solution.py:564
  (101 shorter events, 17.1 us)
Async XLA Ops:
  7.2 7.7 %copy-start.10 = (bf16[1,4096,256]{2,1,0:T(8,128)(2,1)S(1)}, bf16[1,4096,256]{2,1,0:T(8,128)(2,1)}, u32[]{:S(2)}) copy-start(bf16[1,4096,256]{2,1,0:T(8,128)(2,1)} %param.11) | copy-start | bytes 6291460
  7.2 77.0 %reduce-scatter.2.cloned.1.call-start = ((), (), s32[]{:S(2)}) async-start(), calls=%async_computation.8 | async-start | bytes 2359296 | tf_op jit(solution)/shard_map/reduce_scatter | solution.py:378
  7.2 8.1 %collective-permute-start = (bf16[4096,256]{1,0:T(8,128)(2,1)}, bf16[4096,256]{1,0:T(8,128)(2,1)}, u32[]{:S(2)}, u32[]{:S(2)}) collective-permute-start(bf16[4096,256]{1,0:T(8,128)(2,1)} %bitcast.53), channel_id=1, source_target_pairs={{0,1},{1,0},{2,3},{3,2},{4,5},{5,4},{6,7},{7,6},{8,9},{9,8},{10,11... | collective-permute-start | bytes 6291464 | tf_op jit(solution)/shard_map/ppermute | solution.py:24
  11.6 142.5 %copy-start.19 = (s32[32]{0:T(128)}, s32[32]{0:T(128)S(1)}, u32[]{:S(2)}) copy-start(s32[32]{0:T(128)S(1)} %fusion.45.ids) | copy-start | bytes 388
  20.9 26.0 %copy-start.18 = (s32[16,32]{1,0:T(8,128)S(1)}, s32[16,32]{1,0:T(8,128)}, u32[]{:S(2)}) copy-start(s32[16,32]{1,0:T(8,128)} %param.17) | copy-start | bytes 6148
  20.9 26.3 %copy-start.20 = (f32[16]{0:T(128)S(1)}, f32[16]{0:T(128)}, u32[]{:S(2)}) copy-start(f32[16]{0:T(128)} %param.18) | copy-start | bytes 196
  20.9 26.3 %copy-start.21 = (s32[16]{0:T(128)S(1)}, s32[16]{0:T(128)}, u32[]{:S(2)}) copy-start(s32[16]{0:T(128)} %param.16) | copy-start | bytes 196
  21.0 17.6 %copy-start.12 = (bf16[1024,256]{1,0:T(8,128)(2,1)}, bf16[1024,256]{1,0:T(8,128)(2,1)S(1)}, u32[]{:S(2)}) copy-start(bf16[1024,256]{1,0:T(8,128)(2,1)S(1)} %get-tuple-element.86.head) | copy-start | bytes 1572868
  21.0 34.4 %copy-start.1 = (bf16[1024,256]{1,0:T(8,128)(2,1)}, bf16[1024,256]{1,0:T(8,128)(2,1)S(1)}, u32[]{:S(2)}) copy-start(bf16[1024,256]{1,0:T(8,128)(2,1)S(1)} %get-tuple-element.87.head_mine.head) | copy-start | bytes 1572868
  21.0 15.6 %collective-permute-start.2 = (bf16[1024,256]{1,0:T(8,128)(2,1)S(1)}, bf16[1024,256]{1,0:T(8,128)(2,1)S(1)}, u32[]{:S(2)}, u32[]{:S(2)}) collective-permute-start(bf16[1024,256]{1,0:T(8,128)(2,1)S(1)} %get-tuple-element.86.head), channel_id=1, source_target_pairs={{0,1},{1,0},{2,3},{3,2},{4,5},{5,4},{6,7},{7,6},{8,9},{9,8},{10,11... | collective-permute-start | bytes 1572872 | tf_op jit(solution)/shard_map/ppermute | solution.py:24
  34.3 21.1 %copy-start.2 = (bf16[16,32,256]{2,1,0:T(8,128)(2,1)}, bf16[16,32,256]{2,1,0:T(8,128)(2,1)S(1)}, u32[]{:S(2)}) copy-start(bf16[16,32,256]{2,1,0:T(8,128)(2,1)S(1)} %all_to_all.35.mine.row) | copy-start | bytes 786436
  34.3 2.7 %collective-permute-start.1 = (bf16[16,32,256]{2,1,0:T(8,128)(2,1)S(1)}, bf16[16,32,256]{2,1,0:T(8,128)(2,1)S(1)}, u32[]{:S(2)}, u32[]{:S(2)}) collective-permute-start(bf16[16,32,256]{2,1,0:T(8,128)(2,1)S(1)} %all_to_all.35.mine.row), channel_id=1, source_target_pairs={{0,1},{1,0},{2,3},{3,2},{4,5},{5,4},{6,7},{7,6},{8,9},{9,8},{10,11... | collective-permute-start | bytes 786440 | tf_op jit(solution)/shard_map/ppermute | solution.py:24
  36.6 18.8 %copy-start.7 = (f32[256]{0:T(256)}, f32[256]{0:T(256)S(1)}, u32[]{:S(2)}) copy-start(f32[256]{0:T(256)S(1)} %get-tuple-element.91) | copy-start | bytes 3076
  38.7 44.0 %all-to-all-start.1 = ((bf16[8,64,1024]{2,1,0:T(8,128)(2,1)}), bf16[8,64,1024]{2,1,0:T(8,128)(2,1)S(1)}, u32[]{:S(2)}, u32[]{:S(2)}) async-start(bf16[8,64,1024]{2,1,0:T(8,128)(2,1)} %shard_map.129), calls=%async_computation.1 | async-start | bytes 2097152 | tf_op jit(solution)/shard_map/all_to_all | solution.py:395
  46.8 68.8 %all-gather.6.cloned.1.call-start = ((), (), s32[]{:S(2)}) async-start(), calls=%async_computation.10 | async-start | bytes 1179648 | tf_op jit(solution)/shard_map/all_gather | solution.py:437
  47.2 8.2 %copy-start.11 = (s32[512,1]{1,0:T(8,128)}, s32[512,1]{1,0:T(8,128)S(1)}, u32[]{:S(2)}) copy-start(s32[512,1]{1,0:T(8,128)S(1)} %reshape.114.targets) | copy-start | bytes 6148
  48.6 34.1 %copy-start.5 = (s32[4]{0:T(128)S(1)}, s32[4]{0:T(128)}, u32[]{:S(2)}) copy-start(s32[4]{0:T(128)} %pad_add_fusion.place) | copy-start | bytes 52
  84.3 1.5 collective-permute-start.3
  87.5 11.5 %all-to-all-start.2 = ((f32[16,2,8,128]{3,2,1,0:T(8,128)}), f32[16,2,8,128]{3,2,1,0:T(8,128)S(1)}, u32[]{:S(2)}, u32[]{:S(2)}) async-start(f32[16,2,8,128]{3,2,1,0:T(8,128)} %broadcast_in_dim.56), calls=%async_computation.3 | async-start | bytes 262144 | tf_op jit(solution)/shard_map/all_to_all | solution.py:20
  99.7 11.8 %all-to-all-start.3 = ((f32[8,8,128]{2,1,0:T(8,128)}), f32[8,8,128]{2,1,0:T(8,128)S(1)}, u32[]{:S(2)}, u32[]{:S(2)}) async-start(f32[8,8,128]{2,1,0:T(8,128)} %shard_map.132), calls=%async_computation.4 | async-start | bytes 65536 | tf_op jit(solution)/shard_map/all_to_all | solution.py:444
  103.1 62.0 %all-gather.4.cloned.1.call-start = ((), (), s32[]{:S(2)}) async-start(), calls=%async_computation.9 | async-start | bytes 4456448 | tf_op jit(solution)/shard_map/all_gather | solution.py:471
  111.5 9.4 %copy-start.15 = (f32[8,8,128]{2,1,0:T(8,128)}, f32[8,8,128]{2,1,0:T(8,128)S(1)}, u32[]{:S(2)}) copy-start(f32[8,8,128]{2,1,0:T(8,128)S(1)} %all-to-all-done.3.known.known_mine) | copy-start | bytes 98308
  111.5 3.9 %collective-permute-start.4 = (f32[8,8,128]{2,1,0:T(8,128)S(1)}, f32[8,8,128]{2,1,0:T(8,128)S(1)}, u32[]{:S(2)}, u32[]{:S(2)}) collective-permute-start(f32[8,8,128]{2,1,0:T(8,128)S(1)} %all-to-all-done.3.known.known_mine), channel_id=1, source_target_pairs={{0,1},{1,0},{2,3},{3,2},{4,5},{5,4},{6,7},{7,6},{8,9},{9,8},{10,11... | collective-permute-start | bytes 98312 | tf_op jit(solution)/shard_map/ppermute | solution.py:24
  115.4 8.7 %copy-start.17 = (f32[8,8,128]{2,1,0:T(8,128)}, f32[8,8,128]{2,1,0:T(8,128)S(1)}, u32[]{:S(2)}) copy-start(f32[8,8,128]{2,1,0:T(8,128)S(1)} %collective-permute-done.4.known.known_other) | copy-start | bytes 98308
  115.7 26.6 %copy-start.6 = (s32[4]{0:T(128)S(1)}, s32[4]{0:T(128)}, u32[]{:S(2)}) copy-start(s32[4]{0:T(128)} %pad_add_fusion.place) | copy-start | bytes 52
  115.7 26.6 %copy-start.8 = (f32[256]{0:T(256)S(1)}, f32[256]{0:T(256)}, u32[]{:S(2)}) copy-start(f32[256]{0:T(256)} %copy-done.7) | copy-start | bytes 3076
  115.7 8.4 %collective-permute-start.5 = (bf16[8,64,1024]{2,1,0:T(8,128)(2,1)}, bf16[8,64,1024]{2,1,0:T(8,128)(2,1)}, u32[]{:S(2)}, u32[]{:S(2)}) collective-permute-start(bf16[8,64,1024]{2,1,0:T(8,128)(2,1)} %bitcast.62), channel_id=1, source_target_pairs={{0,1},{1,0},{2,3},{3,2},{4,5},{5,4},{6,7},{7,6},{8,9},{9,8},{10,11... | collective-permute-start | bytes 3145736 | tf_op jit(solution)/shard_map/ppermute | solution.py:24
  127.3 14.9 %all-to-all-start.4 = ((bf16[16,32,256]{2,1,0:T(8,128)(2,1)}), bf16[16,32,256]{2,1,0:T(8,128)(2,1)S(1)}, u32[]{:S(2)}, u32[]{:S(2)}) async-start(bf16[16,32,256]{2,1,0:T(8,128)(2,1)} %shard_map.134), calls=%async_computation.5 | async-start | bytes 524288 | tf_op jit(solution)/shard_map/all_to_all | solution.py:498
  139.2 9.3 %copy-start.4 = (f32[1,4096]{1,0:T(1,128)S(1)}, f32[1,4096]{1,0:T(1,128)}, u32[]{:S(2)}) copy-start(f32[1,4096]{1,0:T(1,128)} %shard_map.130.gain_part) | copy-start | bytes 49156
  142.9 2.1 %collective-permute-start.6 = (f32[16,256]{1,0:T(8,128)S(1)}, f32[16,256]{1,0:T(8,128)S(1)}, u32[]{:S(2)}, u32[]{:S(2)}) collective-permute-start(f32[16,256]{1,0:T(8,128)S(1)} %get-tuple-element.70), channel_id=1, source_target_pairs={{0,1},{1,0},{2,3},{3,2},{4,5},{5,4},{6,7},{7,6},{8,9},{9,8},{10,11... | collective-permute-start | bytes 49160 | tf_op jit(solution)/shard_map/ppermute | solution.py:24
  149.8 15.0 %all-to-all-start.5 = ((bf16[8,2,5888]{2,1,0:T(2,128)(2,1)}), bf16[8,2,5888]{2,1,0:T(2,128)(2,1)S(1)}, u32[]{:S(2)}, u32[]{:S(2)}) async-start(bf16[8,2,5888]{2,1,0:T(2,128)(2,1)} %shard_map.137), calls=%async_computation.6 | async-start | bytes 376832 | tf_op jit(solution)/shard_map/all_to_all | solution.py:542
  178.2 2.9 %collective-permute-start.7 = (bf16[8,2,4864]{2,1,0:T(2,128)(2,1)S(1)}, bf16[8,2,4864]{2,1,0:T(2,128)(2,1)S(1)}, u32[]{:S(2)}, u32[]{:S(2)}) collective-permute-start(bf16[8,2,4864]{2,1,0:T(2,128)(2,1)S(1)} %all_to_all.36.mine), channel_id=1, source_target_pairs={{0,1},{1,0},{2,3},{3,2},{4,5},{5,4},{6,7},{7,6},{8,9},{9,8},{10,11... | collective-permute-start | bytes 466952 | tf_op jit(solution)/shard_map/ppermute | solution.py:24
  (6 other events, 26.0 us)
Sparse Core Ops, SparseCore 0:
  19.7 52.3 reduce-scatter.1
  85.1 30.4 all-gather.5
  117.5 47.2 all-gather.3
